TPU v7x, 32 devices: a whole 2x2x4 slice. The times are simulated.
32 devices in a mesh: seq: 8 (over z, x), mp: 4 (over y, core).
Axes of the slice: x: 2, y: 2, z: 4, core: 2. Of those that a mesh axis runs over, the one named last changes fastest.
Arguments:
- tokens: bfloat16 [4096, 2048], P('mp', 'seq'), may hold values from -24 to 24
- packing: int32 [2048], replicated, may hold values from 0 to 2047, as said below
- norm_gain: float32 [4096], replicated, may hold values from 0.5 to 1.5
- w_value: bfloat16 [4096, 4096], P('seq', 'mp'), may hold values from -0.09375 to 0.09375
- w_gate: bfloat16 [4096, 4096], P('seq', 'mp'), may hold values from -0.09375 to 0.09375
- filters: bfloat16 [4096, 256], P('mp'), may hold values from -3 to 3
- skip_gain: float32 [4096], P('mp'), may hold values from -1 to 1
- lengths: int32 [4], replicated, may hold values from 1 to 4, 8 in all
Outputs:
- mixed: bfloat16 [4096, 2048], P('mp', 'seq')
Inputs may be any that keep to these rules, and one draw needn't show every extreme that they name: Each of 0 to 2047 appears once. Of the 256 corpus rows j with the same j // 256, at most 64 have the same packing[j] // 256, and in every draw some group reaches 64.
All inputs are finite; a program needn't handle non-finite values.
Results may differ from a plain program's by a relative error of at most 0.0052.
Values may be sent and summed in bfloat16 or wider, within the bound.
No kernel may reach another device: no remote copies, remote signals or barrier semaphores. Data moves between devices by JAX's collectives and lax.ppermute only.
A program may use at most 128 MiB of HBM per device.

v0:
```python
import math

import jax
import jax.numpy as jnp
from jax import lax
from jax.sharding import PartitionSpec as P

epsilon = 1e-05


def toeplitz(filter_taps):
    chan_count, tap_count = filter_taps.shape
    padding = jnp.zeros((chan_count, tap_count), filter_taps.dtype)
    line_row = jnp.concatenate([padding, filter_taps[:, ::-1], padding], axis=1)
    tiled = jnp.tile(line_row, (1, tap_count))[:, : tap_count * (3 * tap_count - 1)]
    return tiled.reshape(chan_count, tap_count, 3 * tap_count - 1)[
        :, :, tap_count - 1 : 3 * tap_count - 1
    ]


def doc_flags(lengths, block_count, dtype):
    starts = jnp.cumsum(lengths, dtype=jnp.int32) - lengths
    block_index = jnp.arange(block_count, dtype=jnp.int32)
    is_start = jnp.any(block_index[:, None] == starts[None, :], axis=1)
    return jnp.where(is_start, 0.0, 1.0).astype(dtype)


def band_product(values, prior_rim, filter_taps, link_flags):
    chan_count, seq_length = values.shape
    tap_count = filter_taps.shape[1]
    block_count = seq_length // tap_count
    group_size = math.gcd(chan_count, 64)
    groups = chan_count // group_size

    def one_group(group_args):
        part_values, part_rim, part_taps = group_args
        blocks = part_values.reshape(group_size, block_count, tap_count)
        earlier = jnp.concatenate([part_rim[:, None, :], blocks[:, :-1, :]], axis=1)
        earlier = earlier * link_flags[None, :, None]
        joined = jnp.concatenate([earlier, blocks], axis=2)
        banded = jnp.einsum(
            "cpq,cbq->cbp", toeplitz(part_taps), joined, preferred_element_type=jnp.float32
        )
        return banded.reshape(group_size, seq_length)

    result = lax.map(
        one_group,
        (
            values.reshape(groups, group_size, seq_length),
            prior_rim.reshape(groups, group_size, tap_count),
            filter_taps.reshape(groups, group_size, tap_count),
        ),
    )
    return result.reshape(chan_count, seq_length)


def project(all_features, norm_gain, weight_pair):
    widened = all_features.astype(jnp.float32)
    inv_scale = lax.rsqrt(jnp.mean(widened * widened, axis=0, keepdims=True) + epsilon)
    normed = (widened * inv_scale * norm_gain[:, None]).astype(jnp.bfloat16)
    contract = (((0,), (0,)), ((), ()))
    value_part = lax.dot_general(
        weight_pair[0], normed, contract, preferred_element_type=jnp.float32
    ).astype(jnp.bfloat16)
    gate_part = lax.dot_general(
        weight_pair[1], normed, contract, preferred_element_type=jnp.float32
    ).astype(jnp.bfloat16)
    return (value_part, gate_part)


def on_device(tokens, packing, norm_gain, w_value, w_gate, filters, skip_gain, lengths):
    row_count = tokens.shape[1]
    shards = lax.axis_size("seq")
    my_index = lax.axis_index("seq")
    all_count = packing.shape[0]
    tap_count = filters.shape[1]
    chan_count = tokens.shape[0] // shards
    weight_pair = (
        lax.all_gather(w_value, "seq", axis=0, tiled=True),
        lax.all_gather(w_gate, "seq", axis=0, tiled=True),
    )
    inverse = (
        jnp.zeros((all_count,), jnp.int32).at[packing].set(jnp.arange(all_count, dtype=jnp.int32))
    )
    chan_taps = lax.dynamic_slice_in_dim(filters, my_index * chan_count, chan_count, 0)
    chan_skip = lax.dynamic_slice_in_dim(skip_gain, my_index * chan_count, chan_count, 0)
    slot_cap = 2 * (row_count // shards)
    own_packing = lax.dynamic_slice_in_dim(packing, my_index * row_count, row_count)
    dest_owner = own_packing // row_count
    onehot = (dest_owner[:, None] == jnp.arange(shards, dtype=jnp.int32)[None, :]).astype(jnp.int32)
    slot_rank = jnp.sum((jnp.cumsum(onehot, axis=0, dtype=jnp.int32) - onehot) * onehot, axis=1)
    slot_index = dest_owner * slot_cap + slot_rank
    send_buffer = (
        jnp.zeros((tokens.shape[0], shards * slot_cap), jnp.bfloat16).at[:, slot_index].set(tokens)
    )
    received = lax.all_to_all(send_buffer, "seq", split_axis=1, concat_axis=1, tiled=True)
    my_sources = lax.dynamic_slice_in_dim(inverse, my_index * row_count, row_count)
    to_me = (packing // row_count == my_index).astype(jnp.int32).reshape(shards, row_count)
    arrival_rank = (jnp.cumsum(to_me, axis=1, dtype=jnp.int32) - to_me).reshape(all_count)
    packed = received[:, my_sources // row_count * slot_cap + arrival_rank[my_sources]]
    all_features = lax.all_gather(packed, "mp", axis=0, tiled=True)
    value_part, gate_part = project(all_features, norm_gain, weight_pair)
    value_chan = lax.all_to_all(value_part, "seq", split_axis=0, concat_axis=1, tiled=True)
    link_flags = doc_flags(lengths, all_count // tap_count, jnp.bfloat16)
    prior_rim = jnp.zeros((chan_count, tap_count), jnp.bfloat16)
    banded = band_product(value_chan, prior_rim, chan_taps, link_flags)
    chan_band = (banded + chan_skip[:, None] * value_chan.astype(jnp.float32)).astype(jnp.bfloat16)
    mixed_band = lax.all_to_all(chan_band, "seq", split_axis=1, concat_axis=0, tiled=True)
    mixed_band = lax.optimization_barrier(mixed_band)
    gate_wide = lax.optimization_barrier(gate_part).astype(jnp.float32)
    return (packed.astype(jnp.float32) + gate_wide * mixed_band.astype(jnp.float32)).astype(
        jnp.bfloat16
    )


def solution(mesh):
    placed = (P("mp", "seq"), P(), P(), P("seq", "mp"), P("seq", "mp"), P("mp", None), P("mp"), P())
    return jax.shard_map(
        on_device, mesh=mesh, in_specs=placed, out_specs=P("mp", "seq"), check_vma=False
    )
```

profile of v0, /device:TPU:0, one launch (start us, length us, event | category | flops | bytes accessed | tf_op | source)
XLA Modules:
  0.0 501.1 jit_solution(2563866235025709923)
XLA Ops:
  6.5 0.8 add_select_fusion.1
  7.3 8.0 %scatter_custom_fusion.1 = s32[2048]{0:T(1024)S(1)} fusion(s32[2048]{0:T(1024)S(1)} %add_select_fusion.1, s32[2048]{0:T(1024)S(1)} %iota.15, s32[]{:T(128)} %copy.63), kind=kCustom, calls=%fused_computation.52 | custom fusion | bytes 8196 | tf_op jit(solution)/shard_map/scatter | solution.py:83
  15.4 0.8 and_select_fusion.1
  16.1 0.6 reduce-window.24
  16.7 0.2 slice_reduce_fusion.1
  17.1 1.2 copy.35
  18.4 2.7 scatter_custom_fusion
  21.0 7.3 %all-to-all-start = ((bf16[1024,8,64]{0,2,1:T(8,128)(2,1)}), bf16[1024,8,64]{0,2,1:T(8,128)(2,1)S(1)}, u32[]{:S(2)}, u32[]{:S(2)}) async-start(bf16[1024,8,64]{0,2,1:T(8,128)(2,1)} %bitcast.5), calls=%async_computation | async-start | bytes 2097152 | tf_op jit(solution)/shard_map/all_to_all | solution.py:96
  28.4 0.6 reduce-window.31
  28.9 0.2 slice_reduce_fusion
  29.3 1.7 gather_fusion
  31.1 22.9 %all-to-all-done = bf16[1024,8,64]{0,2,1:T(8,128)(2,1)S(1)} async-done(((bf16[1024,8,64]{0,2,1:T(8,128)(2,1)}), bf16[1024,8,64]{0,2,1:T(8,128)(2,1)S(1)}, u32[]{:S(2)}, u32[]{:S(2)}) %all-to-all-start) | async-done | bytes 1048608 | tf_op jit(solution)/shard_map/all_to_all | solution.py:96
  54.0 2.0 gather_fusion.1
  56.1 0.7 all-gather.7.cloned.1.call-update
  56.8 0.7 all-gather.5.cloned.1.call-update
  57.5 20.3 %all-gather.9.cloned.1.call-done = bf16[4096,256]{0,1:T(8,128)(2,1)} async-done(((bf16[1024,256]{0,1:T(8,128)(2,1)}), bf16[4096,256]{0,1:T(8,128)(2,1)}) %all-gather.9.cloned.1.call-update) | async-done | bytes 2097168 | tf_op jit(solution)/shard_map/all_gather | solution.py:101
  77.8 2.1 fusion.6
  79.9 125.0 %all-gather.7.cloned.1.call-done = bf16[4096,1024]{1,0:T(8,128)(2,1)} async-done(((bf16[512,1024]{1,0:T(8,128)(2,1)}), bf16[4096,1024]{1,0:T(8,128)(2,1)}) %all-gather.7.cloned.1.call-update) | async-done | bytes 8388624 | tf_op jit(solution)/shard_map/all_gather | solution.py:79
  204.9 6.4 %fusion.10 = bf16[32,8,8,128]{3,2,1,0:T(8,128)(2,1)S(1)} fusion(bf16[4096,1024]{1,0:T(8,128)(2,1)} %all-gather.7.cloned.1.call-done, bf16[4096,256]{0,1:T(8,128)(2,1)} %all-gather.9.cloned.1.call-done, f32[4096]{0:T(1024)S(1)} %copy-done.9, f32[256]{0:T(256)S(1)} %add_rsqrt_fusion), kind=kOutput, calls=%fused_computation.23 | convolution fusion | flops 2151940096 | bytes 11027456 | tf_op jit(solution)/shard_map/dot_general | solution.py:62
  211.3 0.9 copy.50
  212.2 3.7 all-to-all-start.1
  216.1 1.4 dynamic_slice.24
  217.6 27.8 %all-to-all-done.1 = bf16[8,128,256]{1,2,0:T(8,128)(2,1)S(1)} async-done(((bf16[8,128,256]{1,2,0:T(8,128)(2,1)}), bf16[8,128,256]{1,2,0:T(8,128)(2,1)S(1)}, u32[]{:S(2)}, u32[]{:S(2)}) %all-to-all-start.1) | async-done | bytes 524320 | tf_op jit(solution)/shard_map/all_to_all | solution.py:103
  245.4 0.4 copy.39
  245.8 0.2 reshape.110
  246.0 0.5 copy-done.2
  246.6 222.9 %while.10 = (s32[]{:T(128)}, f32[2,64,2048]{2,1,0:T(8,128)}, bf16[2,64,2048]{2,1,0:T(8,128)(2,1)S(1)}, bf16[8]{0:T(256)(128)(2,1)S(1)}, bf16[2,64,256]{2,1,0:T(8,128)(2,1)S(1)}, /*index=5*/s32[]{:T(128)}, bf16[]{:T(256)}) while((s32[]{:T(128)}, f32[2,64,2048]{2,1,0:T(8,128)}, bf16[2,64,2048]{2,1,0:T(8,128)(2,1)S(1)}, ...), condition=%wide.region_11.12_spmd, body=%wide.region_10.11_spmd.sunk | while | flops 136085504 | bytes 197918832 | solution.py:46
  247.0 1.9 tile.10
  248.9 15.9 %copy.53 = bf16[8,8,256,768]{3,1,2,0:T(8,128)(2,1)} copy(bf16[8,8,256,768]{3,2,1,0:T(8,128)(2,1)S(1)} %bitcast.66) | data formatting | bytes 50331648 | tf_op jit(solution)/shard_map/while
  264.8 20.6 %slice.41 = bf16[64,196352]{1,0:T(8,128)(2,1)} slice(bf16[64,196608]{1,0:T(8,128)(2,1)} %bitcast.67), slice={[0:64], [0:196352]} | slice | bytes 50266112 | tf_op jit(solution)/shard_map/while/body/eval_jaxpr/slice | solution.py:15
  285.4 62.0 %reshape.159 = bf16[64,256,767]{2,1,0:T(8,128)(2,1)} reshape(bf16[64,196352]{1,0:T(8,128)(2,1)} %slice.41) | data formatting | bytes 50266112 | tf_op jit(solution)/shard_map/while/body/eval_jaxpr/reshape | solution.py:16
  347.4 9.8 %fusion.35 = f32[64,8,256]{2,1,0:T(8,128)S(1)} fusion(bf16[64,256,767]{2,1,0:T(8,128)(2,1)} %reshape.159, bf16[64,8,256]{2,1,0:T(8,128)(2,1)S(1)} %bitcast.69, bf16[64,8,256]{2,1,0:T(8,128)(2,1)S(1)} %pad_multiply_fusion.2), kind=kOutput, calls=%fused_computation.4.clone.1 | convolution fusion | flops 135266304 | bytes 17825792 | tf_op jit(solution)/shard_map/while/body/eval_jaxpr/cpq,cbq->cbp/dot_general | solution.py:41
  357.3 0.8 constant_dynamic-update-slice_fusion.2
  358.5 1.9 tile.10
  360.5 15.9 %copy.53 = bf16[8,8,256,768]{3,1,2,0:T(8,128)(2,1)} copy(bf16[8,8,256,768]{3,2,1,0:T(8,128)(2,1)S(1)} %bitcast.66) | data formatting | bytes 50331648 | tf_op jit(solution)/shard_map/while
  376.3 20.5 %slice.41 = bf16[64,196352]{1,0:T(8,128)(2,1)} slice(bf16[64,196608]{1,0:T(8,128)(2,1)} %bitcast.67), slice={[0:64], [0:196352]} | slice | bytes 50266112 | tf_op jit(solution)/shard_map/while/body/eval_jaxpr/slice | solution.py:15
  396.8 62.0 %reshape.159 = bf16[64,256,767]{2,1,0:T(8,128)(2,1)} reshape(bf16[64,196352]{1,0:T(8,128)(2,1)} %slice.41) | data formatting | bytes 50266112 | tf_op jit(solution)/shard_map/while/body/eval_jaxpr/reshape | solution.py:16
  458.8 9.8 %fusion.35 = f32[64,8,256]{2,1,0:T(8,128)S(1)} fusion(bf16[64,256,767]{2,1,0:T(8,128)(2,1)} %reshape.159, bf16[64,8,256]{2,1,0:T(8,128)(2,1)S(1)} %bitcast.69, bf16[64,8,256]{2,1,0:T(8,128)(2,1)S(1)} %pad_multiply_fusion.2), kind=kOutput, calls=%fused_computation.4.clone.1 | convolution fusion | flops 135266304 | bytes 17825792 | tf_op jit(solution)/shard_map/while/body/eval_jaxpr/cpq,cbq->cbp/dot_general | solution.py:41
  468.6 0.8 constant_dynamic-update-slice_fusion.2
  469.5 1.7 copy.47
  471.2 1.4 fusion.11
  472.6 1.2 copy.40
  473.8 4.1 all-to-all-start.2
  478.0 6.7 %fusion.9 = bf16[1024,256]{0,1:T(8,128)(2,1)} fusion(bf16[4096,1024]{1,0:T(8,128)(2,1)} %all-gather.5.cloned.1.call-done, bf16[4096,256]{0,1:T(8,128)(2,1)S(1)} %copy-done.4, f32[4096]{0:T(1024)S(1)} %copy-done.10, f32[256]{0:T(256)S(1)} %copy-done.7), kind=kOutput, calls=%fused_computation.22 | convolution fusion | flops 2151940096 | bytes 11027456 | tf_op jit(solution)/shard_map/dot_general | solution.py:65
  484.7 6.4 %all-to-all-done.2 = bf16[128,8,256]{0,2,1:T(8,128)(2,1)} async-done(((bf16[128,8,256]{0,2,1:T(8,128)(2,1)}), bf16[128,8,256]{0,2,1:T(8,128)(2,1)}, u32[]{:S(2)}, u32[]{:S(2)}) %all-to-all-start.2) | async-done | bytes 524320 | tf_op jit(solution)/shard_map/all_to_all | solution.py:108
  491.1 1.1 copy_bitcast_fusion
  492.2 1.3 add_convert_fusion
  493.5 1.0 copy.42
  (67 shorter events, 1.9 us)
Async XLA Ops:
  6.5 211.0 %copy-start = (bf16[1024,256]{1,0:T(8,128)(2,1)S(1)}, bf16[1024,256]{1,0:T(8,128)(2,1)}, u32[]{:S(2)}) copy-start(bf16[1024,256]{1,0:T(8,128)(2,1)} %param.15) | copy-start | bytes 1572868
  6.5 21.8 %copy-start.5 = (s32[2048]{0:T(1024)S(1)}, s32[2048]{0:T(1024)}, u32[]{:S(2)}) copy-start(s32[2048]{0:T(1024)} %param.11) | copy-start | bytes 24580
  21.0 33.0 %all-to-all-start = ((bf16[1024,8,64]{0,2,1:T(8,128)(2,1)}), bf16[1024,8,64]{0,2,1:T(8,128)(2,1)S(1)}, u32[]{:S(2)}, u32[]{:S(2)}) async-start(bf16[1024,8,64]{0,2,1:T(8,128)(2,1)} %bitcast.5), calls=%async_computation | async-start | bytes 2097152 | tf_op jit(solution)/shard_map/all_to_all | solution.py:96
  28.3 49.5 %all-gather.9.cloned.1.call-start = ((), (), s32[]{:S(2)}) async-start(), calls=%async_computation.5 | async-start | bytes 2621440 | tf_op jit(solution)/shard_map/all_gather | solution.py:101
  54.0 150.9 %copy-start.9 = (f32[4096]{0:T(1024)S(1)}, f32[4096]{0:T(1024)}, u32[]{:S(2)}) copy-start(f32[4096]{0:T(1024)} %param.12) | copy-start | bytes 49156
  56.0 148.9 %all-gather.7.cloned.1.call-start = ((), (), s32[]{:S(2)}) async-start(), calls=%async_computation.4 | async-start | bytes 9437184 | tf_op jit(solution)/shard_map/all_gather | solution.py:79
  56.8 421.2 %all-gather.5.cloned.1.call-start = ((), (), s32[]{:S(2)}) async-start(), calls=%async_computation.3 | async-start | bytes 9437184 | tf_op jit(solution)/shard_map/all_gather | solution.py:80
  79.9 131.4 %copy-start.6 = (f32[256]{0:T(256)}, f32[256]{0:T(256)S(1)}, u32[]{:S(2)}) copy-start(f32[256]{0:T(256)S(1)} %add_rsqrt_fusion) | copy-start | bytes 3076
  79.9 136.0 %copy-start.11 = (s32[4]{0:T(128)S(1)}, s32[4]{0:T(128)}, u32[]{:S(2)}) copy-start(s32[4]{0:T(128)} %param.17) | copy-start | bytes 52
  212.2 33.2 %all-to-all-start.1 = ((bf16[8,128,256]{1,2,0:T(8,128)(2,1)}), bf16[8,128,256]{1,2,0:T(8,128)(2,1)S(1)}, u32[]{:S(2)}, u32[]{:S(2)}) async-start(bf16[8,128,256]{1,2,0:T(8,128)(2,1)} %bitcast.50), calls=%async_computation.1 | async-start | bytes 1048576 | tf_op jit(solution)/shard_map/all_to_all | solution.py:103
  245.8 0.8 copy-start.2
  246.0 225.1 %copy-start.8 = (f32[128]{0:T(128)S(1)}, f32[128]{0:T(128)}, u32[]{:S(2)}) copy-start(f32[128]{0:T(128)} %dynamic_slice.24) | copy-start | bytes 1540
  469.5 8.5 %copy-start.4 = (bf16[4096,256]{0,1:T(8,128)(2,1)S(1)}, bf16[4096,256]{0,1:T(8,128)(2,1)}, u32[]{:S(2)}) copy-start(bf16[4096,256]{0,1:T(8,128)(2,1)} %all-gather.9.cloned.1.call-done) | copy-start | bytes 6291460
  469.5 8.5 %copy-start.7 = (f32[256]{0:T(256)S(1)}, f32[256]{0:T(256)}, u32[]{:S(2)}) copy-start(f32[256]{0:T(256)} %copy-done.6) | copy-start | bytes 3076
  469.5 8.5 %copy-start.10 = (f32[4096]{0:T(1024)S(1)}, f32[4096]{0:T(1024)}, u32[]{:S(2)}) copy-start(f32[4096]{0:T(1024)} %param.12) | copy-start | bytes 49156
  473.8 17.3 %all-to-all-start.2 = ((bf16[128,8,256]{0,2,1:T(8,128)(2,1)}), bf16[128,8,256]{0,2,1:T(8,128)(2,1)}, u32[]{:S(2)}, u32[]{:S(2)}) async-start(bf16[128,8,256]{0,2,1:T(8,128)(2,1)} %copy.40), calls=%async_computation.2 | async-start | bytes 1048576 | tf_op jit(solution)/shard_map/all_to_all | solution.py:108
  477.9 14.3 %copy-start.3 = (bf16[256,1024]{1,0:T(8,128)(2,1)S(1)}, bf16[256,1024]{1,0:T(8,128)(2,1)}, u32[]{:S(2)}) copy-start(bf16[256,1024]{1,0:T(8,128)(2,1)} %gather_fusion.1) | copy-start | bytes 1572868
  478.0 16.6 %copy-start.1 = (bf16[1024,256]{1,0:T(8,128)(2,1)S(1)}, bf16[1024,256]{1,0:T(8,128)(2,1)}, u32[]{:S(2)}) copy-start(bf16[1024,256]{1,0:T(8,128)(2,1)} %param.15) | copy-start | bytes 1572868
Sparse Core Ops, SparseCore 0:
  56.1 21.6 all-gather.8
  79.9 124.9 all-gather.6
  207.0 134.1 all-gather.4
where the time goes:
time: 502 us; the launch traced here: 501 us
  local copies, waits for them, and re-layouts  228 us (45%)
  waiting for transfers between devices  204 us (41%)
  matrix products  32.6 us (6%)
  starting transfers between devices  15.2 us (3%)
  between operations  13.4 us (3%)
  other arithmetic  8.4 us (2%)
    all_gather x1, waiting for transfers between devices, on_device(): lax.all_gather(w_value, 'seq', axis=0, tiled=True)  125 us
    reshape x2, local copies, waits for them, and re-layouts, toeplitz(): tiled.reshape(chan_count, tap_count, 3 * tap_count - 1)  124 us
    slice x2, local copies, waits for them, and re-layouts, toeplitz(): jnp.tile(line_row, (1, tap_count))[:, :tap_count * (3 * tap_count - 1)]  41.1 us
    while x4, local copies, waits for them, and re-layouts  31.8 us
    all_to_all x1, waiting for transfers between devices, on_device(): lax.all_to_all(value_part, 'seq', split_axis=0, concat_axis=1, tiled=True)  27.8 us
    all_to_all x1, waiting for transfers between devices, on_device(): lax.all_to_all(send_buffer, 'seq', split_axis=1, concat_axis=1, tiled=True)  22.9 us
    all_gather x1, waiting for transfers between devices, on_device(): all_features = lax.all_gather(packed, 'mp', axis=0, tiled=True)  20.3 us
    dot_general x2, matrix products, one_group(): jnp.einsum('cpq,cbq->cbp', toeplitz(part_taps), joined, preferred_element...  19.5 us
  transfers between devices with their start and end apart: 6, of which 5 were waited for; matrix products, arithmetic and copies ran while one was open for 50% of the time, Pallas kernels for 0%

commit v1 on v0

--- a/solution.py
+++ b/solution.py
@@ -1,11 +1,20 @@
+import functools
 import math
 
 import jax
 import jax.numpy as jnp
 from jax import lax
+from jax.experimental import pallas as pl
+from jax.experimental.pallas import tpu as pltpu
 from jax.sharding import PartitionSpec as P
 
 epsilon = 1e-05
+AXES = ("seq", "mp")
+LANES = 128
+SUBLANES = 8
+VMEM = pl.BlockSpec(memory_space=pltpu.VMEM)
+SMEM = pl.BlockSpec(memory_space=pltpu.SMEM)
+PARAMS = pltpu.CompilerParams(vmem_limit_bytes=48 * 1024 * 1024)
 
 
 def toeplitz(filter_taps):
@@ -54,7 +63,7 @@
     return result.reshape(chan_count, seq_length)
 
 
-def project(all_features, norm_gain, weight_pair):
+def project_all(all_features, norm_gain, weight_pair):
     widened = all_features.astype(jnp.float32)
     inv_scale = lax.rsqrt(jnp.mean(widened * widened, axis=0, keepdims=True) + epsilon)
     normed = (widened * inv_scale * norm_gain[:, None]).astype(jnp.bfloat16)
@@ -99,7 +108,7 @@
     arrival_rank = (jnp.cumsum(to_me, axis=1, dtype=jnp.int32) - to_me).reshape(all_count)
     packed = received[:, my_sources // row_count * slot_cap + arrival_rank[my_sources]]
     all_features = lax.all_gather(packed, "mp", axis=0, tiled=True)
-    value_part, gate_part = project(all_features, norm_gain, weight_pair)
+    value_part, gate_part = project_all(all_features, norm_gain, weight_pair)
     value_chan = lax.all_to_all(value_part, "seq", split_axis=0, concat_axis=1, tiled=True)
     link_flags = doc_flags(lengths, all_count // tap_count, jnp.bfloat16)
     prior_rim = jnp.zeros((chan_count, tap_count), jnp.bfloat16)
@@ -113,8 +122,298 @@
     )
 
 
+def pack_kernel(line, place_ref, value_ref, gate_ref, *out_refs):
+    height, columns = value_ref.shape
+    width = columns // (2 * line)
+    z = place_ref[0]
+    for d in range(line):
+        target = lax.rem(z + d, line)
+        for half in range(2):
+            first = pl.multiple_of(half * (columns // 2) + target * width, width)
+            for which, ref in enumerate((value_ref, gate_ref)):
+                out_refs[d][half, which] = ref[:, pl.ds(first, width)].T
+
+
+def pack_weights(place, w_value, w_gate, line):
+    height, columns = w_value.shape
+    width = columns // (2 * line)
+    return pl.pallas_call(
+        functools.partial(pack_kernel, line),
+        out_shape=[jax.ShapeDtypeStruct((2, 2, width, height), w_value.dtype)] * line,
+        in_specs=[SMEM, VMEM, VMEM],
+        out_specs=[VMEM] * line,
+        compiler_params=PARAMS,
+        cost_estimate=pl.CostEstimate(
+            flops=0, bytes_accessed=8 * height * columns, transcendentals=0
+        ),
+    )(place, w_value, w_gate)
+
+
+def project_kernel(pick_ref, weight_ref, inv_ref, gain_ref, *refs):
+    parts = len(refs) - 2
+    mine_ref, other_ref = refs[parts:]
+    x = pick_ref[parts]
+    inv_row = inv_ref[...]
+    rows = mine_ref.shape[0]
+    height = weight_ref.shape[-1]
+    mine = jnp.zeros(mine_ref.shape, jnp.float32)
+    other = jnp.zeros(mine_ref.shape, jnp.float32)
+    for part in range(parts):
+        pick = pick_ref[part]
+        scaled = refs[part][...].astype(jnp.float32) * inv_row * gain_ref[part]
+        scaled = scaled.astype(jnp.bfloat16)
+        near = weight_ref[pick, x].reshape(rows, height)
+        far = weight_ref[pick, 1 - x].reshape(rows, height)
+        mine += jnp.dot(near, scaled, preferred_element_type=jnp.float32)
+        other += jnp.dot(far, scaled, preferred_element_type=jnp.float32)
+    mine_ref[...] = mine
+    other_ref[...] = other.astype(jnp.bfloat16)
+
+
+def project(picks, weights, inv_row, gain_columns, blocks):
+    line, _, _, width, height = weights.shape
+    count = blocks[0].shape[1]
+    out = (2 * width, count)
+    return pl.pallas_call(
+        project_kernel,
+        out_shape=[
+            jax.ShapeDtypeStruct(out, jnp.float32),
+            jax.ShapeDtypeStruct(out, jnp.bfloat16),
+        ],
+        in_specs=[SMEM] + [VMEM] * (3 + len(blocks)),
+        out_specs=[VMEM, VMEM],
+        compiler_params=PARAMS,
+        cost_estimate=pl.CostEstimate(
+            flops=8 * width * height * count * len(blocks),
+            bytes_accessed=weights.size * 2 + 2 * height * count * len(blocks),
+            transcendentals=0,
+        ),
+    )(picks, weights, inv_row, gain_columns, *blocks)
+
+
+def mix_kernel(slots, taps_blocks, flag_ref, place_ref, taps_ref, skip_ref, *refs):
+    mine_refs, theirs_refs, token_refs = refs[:slots], refs[slots : 2 * slots], refs[2 * slots : 3 * slots]
+    out_ref = refs[3 * slots]
+    whole, band = refs[3 * slots + 1], refs[3 * slots + 2]
+    shifted = refs[3 * slots + 3 :]
+    chan = taps_ref.shape[0]
+    count = mine_refs[0].shape[1]
+    pieces = shifted[0].shape[0] // chan
+    total = pieces * LANES
+    for slot in range(slots):
+        summed = (mine_refs[slot][...] + theirs_refs[slot][...].astype(jnp.float32)).astype(jnp.bfloat16)
+        stacked = jnp.concatenate([summed, token_refs[slot][...]], axis=0)
+        spot = lax.broadcasted_iota(jnp.int32, (count, total), 1)
+        onehot = (place_ref[slot] == spot).astype(jnp.float32).astype(jnp.bfloat16)
+        moved = jnp.dot(stacked, onehot, preferred_element_type=jnp.float32)
+        if slot == 0:
+            whole[...] = moved
+        else:
+            whole[...] += moved
+    for piece in range(pieces):
+        for back in range(taps_blocks + 1):
+            rows = pl.ds(piece * chan, chan)
+            if back > piece:
+                shifted[back][rows, :] = jnp.zeros((chan, LANES), jnp.float32)
+                continue
+            first = (piece - back) * LANES
+            part = whole[0:chan, first : first + LANES]
+            if back > piece % taps_blocks:
+                part = part * flag_ref[piece // taps_blocks]
+            shifted[back][rows, :] = part
+    column = lax.broadcasted_iota(jnp.int32, (LANES, LANES), 1)
+    row = lax.broadcasted_iota(jnp.int32, (LANES, LANES), 0)
+    later = column >= row
+
+    zero = jnp.zeros((LANES, LANES), jnp.float32)
+
+    def one(group, carry):
+        base = pl.multiple_of(group * SUBLANES, SUBLANES)
+        group_taps = taps_ref[pl.ds(base, SUBLANES), :]
+        for member in range(SUBLANES):
+            turned = [zero]
+            for block in range(taps_blocks):
+                line_row = group_taps[member : member + 1, block * LANES : (block + 1) * LANES]
+                square = jnp.broadcast_to(line_row, (LANES, LANES))
+                turned.append(pltpu.roll(square, 0, 1, stride=1, stride_axis=0))
+            turned.append(zero)
+            rows = pl.ds(base + member, pieces, stride=chan)
+            tiles, inputs = [], []
+            for back in range(taps_blocks + 1):
+                tiles.append(jnp.where(later, turned[back + 1], turned[back]).astype(jnp.bfloat16))
+                inputs.append(shifted[back][rows, :].astype(jnp.bfloat16))
+            band[rows, :] = jnp.dot(
+                jnp.concatenate(inputs, axis=1),
+                jnp.concatenate(tiles, axis=0),
+                preferred_element_type=jnp.float32,
+            )
+        return carry
+
+    lax.fori_loop(0, chan // SUBLANES, one, 0)
+    skip = skip_ref[...]
+    wide = out_ref.shape[2] // LANES
+    for piece in range(pieces):
+        lanes = slice(piece * LANES, (piece + 1) * LANES)
+        rows = pl.ds(piece * chan, chan)
+        z = (band[rows, :] + skip * whole[0:chan, lanes]).astype(jnp.bfloat16).astype(jnp.float32)
+        mixed = whole[2 * chan : 3 * chan, lanes] + whole[chan : 2 * chan, lanes] * z
+        inner = (piece % wide) * LANES
+        out_ref[piece // wide, :, inner : inner + LANES] = mixed.astype(jnp.bfloat16)
+
+
+def mix(flags, places, taps, skip, mine, theirs, tokens, shards):
+    slots = len(mine)
+    chan, tap_count = taps.shape
+    total = slots * mine[0].shape[1]
+    taps_blocks = tap_count // LANES
+    return pl.pallas_call(
+        functools.partial(mix_kernel, slots, taps_blocks),
+        out_shape=jax.ShapeDtypeStruct((shards, chan, total // shards), jnp.bfloat16),
+        in_specs=[SMEM] + [VMEM] * (3 + 3 * slots),
+        out_specs=VMEM,
+        scratch_shapes=[
+            pltpu.VMEM((3 * chan, total), jnp.float32),
+            pltpu.VMEM((total // LANES * chan, LANES), jnp.float32),
+        ]
+        + [pltpu.VMEM((total // LANES * chan, LANES), jnp.float32)] * (taps_blocks + 1),
+        compiler_params=PARAMS,
+        cost_estimate=pl.CostEstimate(
+            flops=6 * chan * total * total, bytes_accessed=16 * chan * total, transcendentals=0
+        ),
+    )(flags, places, taps, skip, *mine, *theirs, *tokens)
+
+
+def on_device_line(tokens, packing, norm_gain, w_value, w_gate, filters, skip_gain, lengths):
+    shards, groups = lax.axis_size("seq"), lax.axis_size("mp")
+    line = shards // 2
+    s, m = lax.axis_index("seq"), lax.axis_index("mp")
+    z, x = s // 2, s % 2
+    features, row_count = tokens.shape
+    half = features // 2
+    total_rows = packing.shape[0]
+    pair_rows = 2 * row_count
+    width = features // shards
+
+    def send(array, target):
+        pairs = []
+        for zz in range(line):
+            for xx in range(2):
+                for mm in range(groups):
+                    to = target(zz, xx, mm)
+                    if to is not None:
+                        pairs.append(
+                            (
+                                (zz * 2 + xx) * groups + mm,
+                                (to[0] * 2 + to[1]) * groups + to[2],
+                            )
+                        )
+        return lax.ppermute(array, AXES, pairs)
+
+    def across(array):
+        return send(array, lambda zz, xx, mm: (zz, 1 - xx, mm))
+
+    keep = lax.dynamic_slice_in_dim(tokens, x * half, half, 0)
+    give = lax.dynamic_slice_in_dim(tokens, (1 - x) * half, half, 0)
+    got = across(give)
+    place = jnp.stack([z]).astype(jnp.int32)
+    packed_weights = pack_weights(place, w_value, w_gate, line)
+    weights = [packed_weights[0]]
+    for d in range(1, line):
+        weights.append(send(packed_weights[d], lambda zz, xx, mm, d=d: ((zz + d) % line, xx, mm)))
+    weights = jnp.stack(weights)
+
+    own = jnp.where(
+        x == 0, jnp.concatenate([keep, got], axis=1), jnp.concatenate([got, keep], axis=1)
+    )
+    up, down = [own], [own]
+    for step in range(1, line):
+        up.append(
+            send(
+                up[-1],
+                lambda zz, xx, mm: (zz + 1, xx, mm) if step - 1 <= zz < line - 1 else None,
+            )
+        )
+        down.append(
+            send(
+                down[-1],
+                lambda zz, xx, mm: (zz - 1, xx, mm) if 0 < zz <= line - step else None,
+            )
+        )
+    order = [sorted(range(line), key=lambda other: (abs(other - zz), other)) for zz in range(line)]
+    slots = []
+    for j in range(line):
+        chosen = None
+        for zz in range(line):
+            other = order[zz][j]
+            array = up[zz - other] if other <= zz else down[other - zz]
+            chosen = array if chosen is None or array is chosen else jnp.where(z == zz, array, chosen)
+        slots.append(chosen)
+    slot_pair = jnp.asarray(order, jnp.int32)[z]
+
+    widened = tokens.astype(jnp.float32)
+    squares = jnp.sum(widened * widened, axis=0)
+    spread = lax.dynamic_update_slice_in_dim(
+        jnp.zeros((total_rows,), jnp.float32), squares, s * row_count, 0
+    )
+    mean = lax.psum(spread, AXES) / (features * groups)
+    inv_scale = lax.rsqrt(mean + epsilon)
+
+    gain_blocks = norm_gain.reshape(groups, 2, half)[:, x]
+    offsets = range(groups)
+    owners = [m ^ o for o in offsets]
+    picks = jnp.stack([lax.rem(z - owner + line, line) for owner in owners] + [x]).astype(jnp.int32)
+    gains = jnp.stack([gain_blocks[owner] for owner in owners])[:, :, None]
+
+    def to_owner(array, o):
+        return send(array, lambda zz, xx, mm: (zz, xx, mm ^ o))
+
+    row_blocks = inv_scale.reshape(line, 1, pair_rows)
+    pack_blocks = packing.reshape(line, pair_rows, 1)
+    mine, theirs, kept, places = [], [], [], []
+    for j in range(line):
+        own_block = slots[j]
+        blocks = [own_block]
+        while len(blocks) < groups:
+            step = groups // 2 // len(blocks)
+            blocks = blocks + [to_owner(b, step) for b in blocks]
+        offset_order = [0]
+        while len(offset_order) < groups:
+            step = groups // 2 // len(offset_order)
+            offset_order = offset_order + [o ^ step for o in offset_order]
+        blocks = [blocks[offset_order.index(o)] for o in offsets]
+        near, far = project(picks, weights, row_blocks[slot_pair[j]], gains, blocks)
+        mine.append(near)
+        theirs.append(across(far))
+        kept.append(lax.dynamic_slice_in_dim(own_block, z * width, width, 0))
+        places.append(pack_blocks[slot_pair[j]])
+
+    first = x * half + z * width
+    taps = lax.dynamic_slice_in_dim(filters, first, width, 0).astype(jnp.float32)
+    skip = lax.dynamic_slice_in_dim(skip_gain, first, width, 0)[:, None]
+    flags = doc_flags(lengths, total_rows // filters.shape[1], jnp.float32)
+    mixed = mix(flags, jnp.stack(places), taps, skip, mine, theirs, kept, shards)
+    mixed = lax.all_to_all(mixed, "seq", split_axis=0, concat_axis=0, tiled=True)
+    mixed = mixed.reshape(line, 2, width, row_count).transpose(1, 0, 2, 3)
+    return mixed.reshape(features, row_count)
+
+
 def solution(mesh):
     placed = (P("mp", "seq"), P(), P(), P("seq", "mp"), P("seq", "mp"), P("mp", None), P("mp"), P())
-    return jax.shard_map(
-        on_device, mesh=mesh, in_specs=placed, out_specs=P("mp", "seq"), check_vma=False
-    )
+    shards, groups = mesh.shape["seq"], mesh.shape["mp"]
+
+    def whole(*args):
+        tokens, w_value, filters = args[0], args[3], args[5]
+        moves_tokens = (
+            tokens.shape[1] <= w_value.shape[1]
+            and shards == 2 * groups
+            and groups & (groups - 1) == 0
+            and tokens.shape[0] % (LANES * shards * groups) == 0
+            and filters.shape[1] % LANES == 0
+            and tokens.shape[1] // shards % filters.shape[1] == 0
+        )
+        body = on_device_line if moves_tokens else on_device
+        return jax.shard_map(
+            body, mesh=mesh, in_specs=placed, out_specs=P("mp", "seq"), check_vma=False
+        )(*args)
+
+    return whole

time: 502 us -> 228 us (0.45)
  local copies, waits for them, and re-layouts: 228 us -> 10.8 us
  waiting for transfers between devices: 204 us -> 77.6 us
  blocking collectives: 0 us -> 72 us
  matrix products: 32.6 us -> 0 us
  Pallas kernels: 0 us -> 22 us
  starting transfers between devices: 15.2 us -> 30.5 us
  between operations: 13.4 us -> 7.98 us
    all_gather x3 -> x0, waiting for transfers between devices: 145 us -> none  [the longest x1 125 us: on_device(): lax.all_gather(w_value, 'seq', axis=0, tiled=True)]
    reshape x3 -> x2, local copies, waits for them, and re-layouts: 124 us -> 0.02 us  [the longest x1 0.01 us: on_device_line(): gain_blocks = norm_gain.reshape(groups, 2, half)[:, x]]
    ppermute x0 -> x26, waiting for transfers between devices: none -> 77.6 us  [send(): return lax.ppermute(array, AXES, pairs)]
    all_to_all x3 -> x0, waiting for transfers between devices: 57.1 us -> none  [the longest x1 27.8 us: on_device(): lax.all_to_all(value_part, 'seq', split_axis=0, concat_axis=1, tiled=True)]
    psum x0 -> x1, blocking collectives: none -> 54.1 us  [on_device_line(): mean = lax.psum(spread, AXES) / (features * groups)]
    slice x3 -> x1, local copies, waits for them, and re-layouts: 41.3 us -> 0.65 us  [on_device_line(): places.append(pack_blocks[slot_pair[j]])]
    dot_general x4 -> x0, matrix products: 32.6 us -> none  [the longest x2 19.5 us: one_group(): jnp.einsum('cpq,cbq->cbp', toeplitz(part_taps), joined, preferred_element...]
    while x4 -> x0, local copies, waits for them, and re-layouts: 31.8 us -> none
  transfers between devices with their start and end apart: 6 -> 26, of which waited for: 5 -> 11; matrix products, arithmetic and copies ran while one was open for 50% -> 4% of each run, Pallas kernels for 0% -> 5%
where the time goes in v1:
time: 228 us; the launch traced here: 227 us
  waiting for transfers between devices  77.6 us (34%)
  blocking collectives  72 us (32%)
  starting transfers between devices  30.5 us (13%)
  Pallas kernels  22 us (10%)
  local copies, waits for them, and re-layouts  10.8 us (5%)
  between operations  7.98 us (4%)
  other arithmetic  6.23 us (3%)
    ppermute x26, waiting for transfers between devices, send(): return lax.ppermute(array, AXES, pairs)  77.6 us
    psum x1, blocking collectives, on_device_line(): mean = lax.psum(spread, AXES) / (features * groups)  54.1 us
    ppermute x26, starting transfers between devices, send(): return lax.ppermute(array, AXES, pairs)  30.5 us
    all_to_all x1, blocking collectives, on_device_line(): lax.all_to_all(mixed, 'seq', split_axis=0, concat_axis=0, tiled=True)  17.8 us
    pallas_call x4, Pallas kernels, project(): pl.pallas_call(project_kernel, out_shape=[jax.ShapeDtypeStruct(out, jnp.f...  10.3 us
    pallas_call x1, Pallas kernels, mix(): pl.pallas_call(functools.partial(mix_kernel, slots, taps_blocks), out_sha...  10.2 us
    unnamed x38, local copies, waits for them, and re-layouts  5.04 us
  transfers between devices with their start and end apart: 26, of which 11 were waited for; matrix products, arithmetic and copies ran while one was open for 4% of the time, Pallas kernels for 5%

profile of v1, /device:TPU:0, one launch (start us, length us, event | category | flops | bytes accessed | tf_op | source)
XLA Modules:
  0.0 227.1 jit_solution(10513960857041338204)
XLA Ops:
  0.0 1.2 constant_dynamic-slice_fusion.8
  1.3 3.0 %collective-permute-start.3 = (bf16[512,256]{1,0:T(8,128)(2,1)S(1)}, bf16[512,256]{1,0:T(8,128)(2,1)S(1)}, u32[]{:S(2)}, u32[]{:S(2)}) collective-permute-start(bf16[512,256]{1,0:T(8,128)(2,1)S(1)} %get-tuple-element.33), channel_id=1, source_target_pairs={{0,4},{1,5},{2,6},{3,7},{4,0},{5,1},{6,2},{7,3},{8,12},{9,13},{10,... | collective-permute-start | bytes 786440 | tf_op jit(solution)/shard_map/ppermute | solution.py:310
  4.3 6.3 %collective-permute-done.3 = bf16[512,256]{1,0:T(8,128)(2,1)S(1)} collective-permute-done((bf16[512,256]{1,0:T(8,128)(2,1)S(1)}, bf16[512,256]{1,0:T(8,128)(2,1)S(1)}, u32[]{:S(2)}, u32[]{:S(2)}) %collective-permute-start.3) | collective-permute-done | bytes 262176 | tf_op jit(solution)/shard_map/ppermute | solution.py:310
  10.7 4.5 %collective-permute-start.7 = (bf16[512,512]{1,0:T(8,128)(2,1)S(1)}, bf16[512,512]{1,0:T(8,128)(2,1)}, u32[]{:S(2)}, u32[]{:S(2)}) collective-permute-start(bf16[512,512]{1,0:T(8,128)(2,1)S(1)} %maximum_select_fusion.refs_0_), channel_id=1, source_target_pairs={{0,8},{1,9},{2,10},{3,11},{4,12},{5,13},{6,14},{7,15},{8,16},{9,17... | collective-permute-start | bytes 1572872 | tf_op jit(solution)/shard_map/ppermute | solution.py:310
  15.3 1.3 collective-permute-start.8
  16.5 8.2 %collective-permute-done.7 = bf16[512,512]{1,0:T(8,128)(2,1)} collective-permute-done((bf16[512,512]{1,0:T(8,128)(2,1)S(1)}, bf16[512,512]{1,0:T(8,128)(2,1)}, u32[]{:S(2)}, u32[]{:S(2)}) %collective-permute-start.7) | collective-permute-done | bytes 524320 | tf_op jit(solution)/shard_map/ppermute | solution.py:310
  24.8 1.5 collective-permute-start.12
  26.2 3.5 %collective-permute-done.8 = bf16[512,512]{1,0:T(8,128)(2,1)} collective-permute-done((bf16[512,512]{1,0:T(8,128)(2,1)S(1)}, bf16[512,512]{1,0:T(8,128)(2,1)}, u32[]{:S(2)}, u32[]{:S(2)}) %collective-permute-start.8) | collective-permute-done | bytes 524320 | tf_op jit(solution)/shard_map/ppermute | solution.py:310
  29.8 1.3 collective-permute-start.13
  31.1 1.5 shard_map.91
  32.6 0.8 copy-done.12
  33.4 2.6 %collective-permute-start = (bf16[2,2,128,512]{3,2,1,0:T(8,128)(2,1)}, bf16[2,2,128,512]{3,2,1,0:T(8,128)(2,1)}, u32[]{:S(2)}, u32[]{:S(2)}) collective-permute-start(bf16[2,2,128,512]{3,2,1,0:T(8,128)(2,1)} %get-tuple-element.18), channel_id=1, source_target_pairs={{0,8},{1,9},{2,10},{3,11},{4,12},{5,13},{6,14},{7,15},{8,16},{9,17... | collective-permute-start | bytes 1572872 | tf_op jit(solution)/shard_map/ppermute | solution.py:310
  36.1 2.1 collective-permute-start.1
  39.0 1.2 multiply_reduce_fusion
  40.2 0.7 collective-permute-start.17
  40.9 14.0 %collective-permute-done.13 = bf16[512,512]{1,0:T(8,128)(2,1)} collective-permute-done((bf16[512,512]{1,0:T(8,128)(2,1)}, bf16[512,512]{1,0:T(8,128)(2,1)}, u32[]{:S(2)}, u32[]{:S(2)}) %collective-permute-start.13) | collective-permute-done | bytes 524320 | tf_op jit(solution)/shard_map/ppermute | solution.py:310
  54.9 1.3 collective-permute-start.18
  64.8 54.1 %psum.7 = f32[2048]{0:T(1024)S(1)} all-reduce(f32[2048]{0:T(1024)S(1)} %dynamic_update_slice.3), channel_id=1, replica_groups=mesh['seq'=8,'mp'=4] {'seq','mp'}, use_global_device_ids=true, to_apply=%region_3.4 | all-reduce | flops 2048 | bytes 16384 | tf_op jit(solution)/shard_map/psum | solution.py:358
  119.0 0.9 dynamic-slice_convert_fusion.taps_ref
  119.8 2.4 %collective-permute-start.5 = (bf16[512,512]{1,0:T(8,128)(2,1)S(1)}, bf16[512,512]{1,0:T(8,128)(2,1)S(1)}, u32[]{:S(2)}, u32[]{:S(2)}) collective-permute-start(bf16[512,512]{1,0:T(8,128)(2,1)S(1)} %maximum_select_fusion.refs_0_), channel_id=1, source_target_pairs={{0,2},{1,3},{2,0},{3,1},{4,6},{5,7},{6,4},{7,5},{8,10},{9,11},{10,... | collective-permute-start | bytes 1572872 | tf_op jit(solution)/shard_map/ppermute | solution.py:310
  122.3 1.8 collective-permute-start.2
  124.1 0.8 copy-done.15
  124.9 1.8 select_select_fusion.2
  126.9 8.2 %collective-permute-done.5.refs_2_ = bf16[512,512]{1,0:T(8,128)(2,1)S(1)} collective-permute-done((bf16[512,512]{1,0:T(8,128)(2,1)S(1)}, bf16[512,512]{1,0:T(8,128)(2,1)S(1)}, u32[]{:S(2)}, u32[]{:S(2)}) %collective-permute-start.5) | collective-permute-done | bytes 524320 | tf_op jit(solution)/shard_map/ppermute | solution.py:310
  135.0 0.8 copy-done.4
  135.8 2.0 collective-permute-start.15
  138.2 0.8 copy-done.6
  139.3 7.0 %collective-permute-done.20.refs_2_ = bf16[512,512]{1,0:T(8,128)(2,1)} collective-permute-done((bf16[512,512]{1,0:T(8,128)(2,1)S(1)}, bf16[512,512]{1,0:T(8,128)(2,1)}, u32[]{:S(2)}, u32[]{:S(2)}) %collective-permute-start.20) | collective-permute-done | bytes 524320 | tf_op jit(solution)/shard_map/ppermute | solution.py:310
  146.4 0.8 copy-done.8
  147.7 9.9 %collective-permute-done.15.refs_2_ = bf16[512,512]{1,0:T(8,128)(2,1)} collective-permute-done((bf16[512,512]{1,0:T(8,128)(2,1)S(1)}, bf16[512,512]{1,0:T(8,128)(2,1)}, u32[]{:S(2)}, u32[]{:S(2)}) %collective-permute-start.15) | collective-permute-done | bytes 524320 | tf_op jit(solution)/shard_map/ppermute | solution.py:310
  157.6 0.8 copy-done.10
  159.0 7.6 %collective-permute-done.10.refs_2_ = bf16[512,512]{1,0:T(8,128)(2,1)} collective-permute-done((bf16[512,512]{1,0:T(8,128)(2,1)S(1)}, bf16[512,512]{1,0:T(8,128)(2,1)}, u32[]{:S(2)}, u32[]{:S(2)}) %collective-permute-start.10) | collective-permute-done | bytes 524320 | tf_op jit(solution)/shard_map/ppermute | solution.py:310
  167.0 1.4 copy.33.place_ref
  168.6 1.9 pad_maximum_fusion.weight_ref
  170.6 2.0 shard_map.92
  172.6 1.4 collective-permute-start.22
  174.0 2.6 %shard_map.95 = (f32[256,512]{1,0:T(8,128)S(1)}, bf16[256,512]{1,0:T(8,128)(2,1)S(1)}) custom-call(s32[5]{0:T(128)S(1)} %stack.48.pick_ref, bf16[4,2,2,128,512]{4,3,2,1,0:T(8,128)(2,1)S(1)} %pad_maximum_fusion.weight_ref, f32[1,512]{1,0:T(1,128)S(1)} %get-tuple-element.38.inv_ref, f32[4,512,1]{2,1,0:T(8,128)S(1)} %copy.29.gain_ref, ...), custom_call_target="tpu_custom_call" | custom-call | flops 1073741824 | bytes 4194304 | tf_op jit(solution)/shard_map/pallas_call | solution.py:177
  176.7 0.7 collective-permute-start.25
  177.4 2.8 %shard_map.94 = (f32[256,512]{1,0:T(8,128)S(1)}, bf16[256,512]{1,0:T(8,128)(2,1)S(1)}) custom-call(s32[5]{0:T(128)S(1)} %stack.48.pick_ref, bf16[4,2,2,128,512]{4,3,2,1,0:T(8,128)(2,1)S(1)} %pad_maximum_fusion.weight_ref, f32[1,512]{1,0:T(1,128)S(1)} %get-tuple-element.39.inv_ref, f32[4,512,1]{2,1,0:T(8,128)S(1)} %copy.29.gain_ref, ...), custom_call_target="tpu_custom_call" | custom-call | flops 1073741824 | bytes 4194304 | tf_op jit(solution)/shard_map/pallas_call | solution.py:177
  180.2 1.4 collective-permute-start.24
  181.6 2.9 %shard_map.93 = (f32[256,512]{1,0:T(8,128)S(1)}, bf16[256,512]{1,0:T(8,128)(2,1)S(1)}) custom-call(s32[5]{0:T(128)S(1)} %stack.48.pick_ref, bf16[4,2,2,128,512]{4,3,2,1,0:T(8,128)(2,1)S(1)} %pad_maximum_fusion.weight_ref, f32[1,512]{1,0:T(1,128)S(1)} %get-tuple-element.40.inv_ref, f32[4,512,1]{2,1,0:T(8,128)S(1)} %copy.29.gain_ref, ...), custom_call_target="tpu_custom_call" | custom-call | flops 1073741824 | bytes 4194304 | tf_op jit(solution)/shard_map/pallas_call | solution.py:177
  184.5 0.8 collective-permute-start.23
  185.4 2.0 collective-permute-done.25.refs_7_
  187.4 5.6 %collective-permute-done.24.refs_6_ = bf16[256,512]{1,0:T(8,128)(2,1)S(1)} collective-permute-done((bf16[256,512]{1,0:T(8,128)(2,1)S(1)}, bf16[256,512]{1,0:T(8,128)(2,1)S(1)}, u32[]{:S(2)}, u32[]{:S(2)}) %collective-permute-start.24) | collective-permute-done | bytes 262176 | tf_op jit(solution)/shard_map/ppermute | solution.py:310
  193.0 5.2 %collective-permute-done.23.refs_5_ = bf16[256,512]{1,0:T(8,128)(2,1)S(1)} collective-permute-done((bf16[256,512]{1,0:T(8,128)(2,1)S(1)}, bf16[256,512]{1,0:T(8,128)(2,1)S(1)}, u32[]{:S(2)}, u32[]{:S(2)}) %collective-permute-start.23) | collective-permute-done | bytes 262176 | tf_op jit(solution)/shard_map/ppermute | solution.py:310
  198.2 10.2 %shard_map.96 = bf16[8,128,256]{2,1,0:T(8,128)(2,1)S(1)} custom-call(f32[8]{0:T(128)S(1)} %broadcast_select_fusion.flag_ref, s32[4,512,1]{2,1,0:T(8,128)S(1)} %copy-done.3, f32[128,256]{1,0:T(8,128)S(1)} %dynamic-slice_convert_fusion.taps_ref, f32[128,1]{1,0:T(8,128)S(1)} %copy.34.skip_ref, f32[256,512]{1,0:T(8,128)S(1)} %get-tuple-element.21.refs_0_, ...), custom_call_target="tpu_custom_call" | custom-call | flops 3221225472 | bytes 4194304 | tf_op jit(solution)/shard_map/pallas_call | solution.py:269
  208.4 17.8 %all_to_all.5 = bf16[8,128,256]{2,1,0:T(8,128)(2,1)S(1)} all-to-all(bf16[8,128,256]{2,1,0:T(8,128)(2,1)S(1)} %shard_map.96), channel_id=1, replica_groups=mesh['seq'=8,'mp'=4] {'seq'}, dimensions={0} | all-to-all | bytes 1048576 | tf_op jit(solution)/shard_map/all_to_all | solution.py:395
  226.2 0.8 copy.35
  (81 shorter events, 4.7 us)
Async XLA Ops:
  0.0 166.6 %copy-start = (f32[1024]{0:T(1024)S(1)}, f32[1024]{0:T(1024)}, u32[]{:S(2)}) copy-start(f32[1024]{0:T(1024)} %param.15) | copy-start | bytes 12292
  0.0 31.1 %copy-start.1 = (bf16[512,1024]{1,0:T(8,128)(2,1)S(1)}, bf16[512,1024]{1,0:T(8,128)(2,1)}, u32[]{:S(2)}) copy-start(bf16[512,1024]{1,0:T(8,128)(2,1)} %value_ref.1) | copy-start | bytes 3145732
  0.0 31.1 %copy-start.2 = (bf16[512,1024]{1,0:T(8,128)(2,1)S(1)}, bf16[512,1024]{1,0:T(8,128)(2,1)}, u32[]{:S(2)}) copy-start(bf16[512,1024]{1,0:T(8,128)(2,1)} %gate_ref.1) | copy-start | bytes 3145732
  0.0 38.1 %copy-start.18 = (s32[4]{0:T(128)S(1)}, s32[4]{0:T(128)}, u32[]{:S(2)}) copy-start(s32[4]{0:T(128)} %param.16) | copy-start | bytes 52
  1.2 60.7 %copy-start.16 = (f32[4096]{0:T(1024)S(1)}, f32[4096]{0:T(1024)}, u32[]{:S(2)}) copy-start(f32[4096]{0:T(1024)} %param.11) | copy-start | bytes 49156
  1.2 60.7 %copy-start.17 = (s32[2048]{0:T(1024)S(1)}, s32[2048]{0:T(1024)}, u32[]{:S(2)}) copy-start(s32[2048]{0:T(1024)} %param.10) | copy-start | bytes 24580
  1.3 9.3 %collective-permute-start.3 = (bf16[512,256]{1,0:T(8,128)(2,1)S(1)}, bf16[512,256]{1,0:T(8,128)(2,1)S(1)}, u32[]{:S(2)}, u32[]{:S(2)}) collective-permute-start(bf16[512,256]{1,0:T(8,128)(2,1)S(1)} %get-tuple-element.33), channel_id=1, source_target_pairs={{0,4},{1,5},{2,6},{3,7},{4,0},{5,1},{6,2},{7,3},{8,12},{9,13},{10,... | collective-permute-start | bytes 786440 | tf_op jit(solution)/shard_map/ppermute | solution.py:310
  10.7 14.0 %collective-permute-start.7 = (bf16[512,512]{1,0:T(8,128)(2,1)S(1)}, bf16[512,512]{1,0:T(8,128)(2,1)}, u32[]{:S(2)}, u32[]{:S(2)}) collective-permute-start(bf16[512,512]{1,0:T(8,128)(2,1)S(1)} %maximum_select_fusion.refs_0_), channel_id=1, source_target_pairs={{0,8},{1,9},{2,10},{3,11},{4,12},{5,13},{6,14},{7,15},{8,16},{9,17... | collective-permute-start | bytes 1572872 | tf_op jit(solution)/shard_map/ppermute | solution.py:310
  15.3 14.5 %collective-permute-start.8 = (bf16[512,512]{1,0:T(8,128)(2,1)S(1)}, bf16[512,512]{1,0:T(8,128)(2,1)}, u32[]{:S(2)}, u32[]{:S(2)}) collective-permute-start(bf16[512,512]{1,0:T(8,128)(2,1)S(1)} %maximum_select_fusion.refs_0_), channel_id=1, source_target_pairs={{8,0},{9,1},{10,2},{11,3},{12,4},{13,5},{14,6},{15,7},{16,8},{17,9... | collective-permute-start | bytes 1572872 | tf_op jit(solution)/shard_map/ppermute | solution.py:310
  24.8 15.5 %collective-permute-start.12 = (bf16[512,512]{1,0:T(8,128)(2,1)}, bf16[512,512]{1,0:T(8,128)(2,1)}, u32[]{:S(2)}, u32[]{:S(2)}) collective-permute-start(bf16[512,512]{1,0:T(8,128)(2,1)} %collective-permute-done.7), channel_id=1, source_target_pairs={{8,16},{9,17},{10,18},{11,19},{12,20},{13,21},{14,22},{15,23},{16,... | collective-permute-start | bytes 1572872 | tf_op jit(solution)/shard_map/ppermute | solution.py:310
  29.8 25.2 %collective-permute-start.13 = (bf16[512,512]{1,0:T(8,128)(2,1)}, bf16[512,512]{1,0:T(8,128)(2,1)}, u32[]{:S(2)}, u32[]{:S(2)}) collective-permute-start(bf16[512,512]{1,0:T(8,128)(2,1)} %collective-permute-done.8), channel_id=1, source_target_pairs={{8,0},{9,1},{10,2},{11,3},{12,4},{13,5},{14,6},{15,7},{16,8},{17,9... | collective-permute-start | bytes 1572872 | tf_op jit(solution)/shard_map/ppermute | solution.py:310
  32.6 0.8 copy-start.12
  33.4 93.3 %collective-permute-start = (bf16[2,2,128,512]{3,2,1,0:T(8,128)(2,1)}, bf16[2,2,128,512]{3,2,1,0:T(8,128)(2,1)}, u32[]{:S(2)}, u32[]{:S(2)}) collective-permute-start(bf16[2,2,128,512]{3,2,1,0:T(8,128)(2,1)} %get-tuple-element.18), channel_id=1, source_target_pairs={{0,8},{1,9},{2,10},{3,11},{4,12},{5,13},{6,14},{7,15},{8,16},{9,17... | collective-permute-start | bytes 1572872 | tf_op jit(solution)/shard_map/ppermute | solution.py:310
  36.1 99.8 %collective-permute-start.1 = (bf16[2,2,128,512]{3,2,1,0:T(8,128)(2,1)}, bf16[2,2,128,512]{3,2,1,0:T(8,128)(2,1)}, u32[]{:S(2)}, u32[]{:S(2)}) collective-permute-start(bf16[2,2,128,512]{3,2,1,0:T(8,128)(2,1)} %get-tuple-element.19), channel_id=1, source_target_pairs={{0,16},{1,17},{2,18},{3,19},{4,20},{5,21},{6,22},{7,23},{8,24},{9,... | collective-permute-start | bytes 1572872 | tf_op jit(solution)/shard_map/ppermute | solution.py:310
  40.2 82.0 %collective-permute-start.17 = (bf16[512,512]{1,0:T(8,128)(2,1)}, bf16[512,512]{1,0:T(8,128)(2,1)S(1)}, u32[]{:S(2)}, u32[]{:S(2)}) collective-permute-start(bf16[512,512]{1,0:T(8,128)(2,1)} %collective-permute-done.12), channel_id=1, source_target_pairs={{16,24},{17,25},{18,26},{19,27},{20,28},{21,29},{22,30},{23,31}} | collective-permute-start | bytes 1572872 | tf_op jit(solution)/shard_map/ppermute | solution.py:310
  54.9 69.1 %collective-permute-start.18 = (bf16[512,512]{1,0:T(8,128)(2,1)}, bf16[512,512]{1,0:T(8,128)(2,1)S(1)}, u32[]{:S(2)}, u32[]{:S(2)}) collective-permute-start(bf16[512,512]{1,0:T(8,128)(2,1)} %collective-permute-done.13), channel_id=1, source_target_pairs={{8,0},{9,1},{10,2},{11,3},{12,4},{13,5},{14,6},{15,7}} | collective-permute-start | bytes 1572872 | tf_op jit(solution)/shard_map/ppermute | solution.py:310
  119.8 15.2 %collective-permute-start.5 = (bf16[512,512]{1,0:T(8,128)(2,1)S(1)}, bf16[512,512]{1,0:T(8,128)(2,1)S(1)}, u32[]{:S(2)}, u32[]{:S(2)}) collective-permute-start(bf16[512,512]{1,0:T(8,128)(2,1)S(1)} %maximum_select_fusion.refs_0_), channel_id=1, source_target_pairs={{0,2},{1,3},{2,0},{3,1},{4,6},{5,7},{6,4},{7,5},{8,10},{9,11},{10,... | collective-permute-start | bytes 1572872 | tf_op jit(solution)/shard_map/ppermute | solution.py:310
  122.3 1.8 copy-start.14
  122.3 15.6 %collective-permute-start.2 = (bf16[2,2,128,512]{3,2,1,0:T(8,128)(2,1)S(1)}, bf16[2,2,128,512]{3,2,1,0:T(8,128)(2,1)S(1)}, u32[]{:S(2)}, u32[]{:S(2)}) collective-permute-start(bf16[2,2,128,512]{3,2,1,0:T(8,128)(2,1)S(1)} %get-tuple-element.20), channel_id=1, source_target_pairs={{0,24},{1,25},{2,26},{3,27},{4,28},{5,29},{6,30},{7,31},{8,0},{9,1... | collective-permute-start | bytes 1572872 | tf_op jit(solution)/shard_map/ppermute | solution.py:310
  124.1 0.8 copy-start.15
  124.9 13.3 %collective-permute-start.4 = (bf16[512,512]{1,0:T(8,128)(2,1)S(1)}, bf16[512,512]{1,0:T(8,128)(2,1)S(1)}, u32[]{:S(2)}, u32[]{:S(2)}) collective-permute-start(bf16[512,512]{1,0:T(8,128)(2,1)S(1)} %maximum_select_fusion.refs_0_), channel_id=1, source_target_pairs={{0,1},{1,0},{2,3},{3,2},{4,5},{5,4},{6,7},{7,6},{8,9},{9,8},{10,11... | collective-permute-start | bytes 1572872 | tf_op jit(solution)/shard_map/ppermute | solution.py:310
  126.8 19.6 %collective-permute-start.20 = (bf16[512,512]{1,0:T(8,128)(2,1)S(1)}, bf16[512,512]{1,0:T(8,128)(2,1)}, u32[]{:S(2)}, u32[]{:S(2)}) collective-permute-start(bf16[512,512]{1,0:T(8,128)(2,1)S(1)} %get-tuple-element.29.refs_0_), channel_id=1, source_target_pairs={{0,2},{1,3},{2,0},{3,1},{4,6},{5,7},{6,4},{7,5},{8,10},{9,11},{10,... | collective-permute-start | bytes 1572872 | tf_op jit(solution)/shard_map/ppermute | solution.py:310
  135.0 11.4 %collective-permute-start.6 = (bf16[512,512]{1,0:T(8,128)(2,1)S(1)}, bf16[512,512]{1,0:T(8,128)(2,1)S(1)}, u32[]{:S(2)}, u32[]{:S(2)}) collective-permute-start(bf16[512,512]{1,0:T(8,128)(2,1)S(1)} %collective-permute-done.5.refs_2_), channel_id=1, source_target_pairs={{0,1},{1,0},{2,3},{3,2},{4,5},{5,4},{6,7},{7,6},{8,9},{9,8},{10,11... | collective-permute-start | bytes 1572872 | tf_op jit(solution)/shard_map/ppermute | solution.py:310
  135.0 0.8 copy-start.4
  135.8 21.8 %collective-permute-start.15 = (bf16[512,512]{1,0:T(8,128)(2,1)S(1)}, bf16[512,512]{1,0:T(8,128)(2,1)}, u32[]{:S(2)}, u32[]{:S(2)}) collective-permute-start(bf16[512,512]{1,0:T(8,128)(2,1)S(1)} %get-tuple-element.30.refs_0_), channel_id=1, source_target_pairs={{0,2},{1,3},{2,0},{3,1},{4,6},{5,7},{6,4},{7,5},{8,10},{9,11},{10,... | collective-permute-start | bytes 1572872 | tf_op jit(solution)/shard_map/ppermute | solution.py:310
  137.9 28.8 %copy-start.13 = (bf16[2,2,128,512]{3,2,1,0:T(8,128)(2,1)}, bf16[2,2,128,512]{3,2,1,0:T(8,128)(2,1)S(1)}, u32[]{:S(2)}) copy-start(bf16[2,2,128,512]{3,2,1,0:T(8,128)(2,1)S(1)} %collective-permute-done.2) | copy-start | bytes 1572868
  137.9 19.7 %collective-permute-start.19 = (bf16[512,512]{1,0:T(8,128)(2,1)S(1)}, bf16[512,512]{1,0:T(8,128)(2,1)S(1)}, u32[]{:S(2)}, u32[]{:S(2)}) collective-permute-start(bf16[512,512]{1,0:T(8,128)(2,1)S(1)} %get-tuple-element.29.refs_0_), channel_id=1, source_target_pairs={{0,1},{1,0},{2,3},{3,2},{4,5},{5,4},{6,7},{7,6},{8,9},{9,8},{10,11... | collective-permute-start | bytes 1572872 | tf_op jit(solution)/shard_map/ppermute | solution.py:310
  138.2 0.8 copy-start.6
  139.0 27.5 %collective-permute-start.10 = (bf16[512,512]{1,0:T(8,128)(2,1)S(1)}, bf16[512,512]{1,0:T(8,128)(2,1)}, u32[]{:S(2)}, u32[]{:S(2)}) collective-permute-start(bf16[512,512]{1,0:T(8,128)(2,1)S(1)} %get-tuple-element.31.refs_0_), channel_id=1, source_target_pairs={{0,2},{1,3},{2,0},{3,1},{4,6},{5,7},{6,4},{7,5},{8,10},{9,11},{10,... | collective-permute-start | bytes 1572872 | tf_op jit(solution)/shard_map/ppermute | solution.py:310
  146.4 26.2 %collective-permute-start.21 = (bf16[512,512]{1,0:T(8,128)(2,1)}, bf16[512,512]{1,0:T(8,128)(2,1)}, u32[]{:S(2)}, u32[]{:S(2)}) collective-permute-start(bf16[512,512]{1,0:T(8,128)(2,1)} %collective-permute-done.20.refs_2_), channel_id=1, source_target_pairs={{0,1},{1,0},{2,3},{3,2},{4,5},{5,4},{6,7},{7,6},{8,9},{9,8},{10,11... | collective-permute-start | bytes 1572872 | tf_op jit(solution)/shard_map/ppermute | solution.py:310
  146.4 0.8 copy-start.8
  147.2 29.4 %collective-permute-start.14 = (bf16[512,512]{1,0:T(8,128)(2,1)S(1)}, bf16[512,512]{1,0:T(8,128)(2,1)}, u32[]{:S(2)}, u32[]{:S(2)}) collective-permute-start(bf16[512,512]{1,0:T(8,128)(2,1)S(1)} %get-tuple-element.30.refs_0_), channel_id=1, source_target_pairs={{0,1},{1,0},{2,3},{3,2},{4,5},{5,4},{6,7},{7,6},{8,9},{9,8},{10,11... | collective-permute-start | bytes 1572872 | tf_op jit(solution)/shard_map/ppermute | solution.py:310
  157.6 19.8 %collective-permute-start.16 = (bf16[512,512]{1,0:T(8,128)(2,1)}, bf16[512,512]{1,0:T(8,128)(2,1)}, u32[]{:S(2)}, u32[]{:S(2)}) collective-permute-start(bf16[512,512]{1,0:T(8,128)(2,1)} %collective-permute-done.15.refs_2_), channel_id=1, source_target_pairs={{0,1},{1,0},{2,3},{3,2},{4,5},{5,4},{6,7},{7,6},{8,9},{9,8},{10,11... | collective-permute-start | bytes 1572872 | tf_op jit(solution)/shard_map/ppermute | solution.py:310
  157.6 0.8 copy-start.10
  158.5 23.2 %collective-permute-start.9 = (bf16[512,512]{1,0:T(8,128)(2,1)S(1)}, bf16[512,512]{1,0:T(8,128)(2,1)}, u32[]{:S(2)}, u32[]{:S(2)}) collective-permute-start(bf16[512,512]{1,0:T(8,128)(2,1)S(1)} %get-tuple-element.31.refs_0_), channel_id=1, source_target_pairs={{0,1},{1,0},{2,3},{3,2},{4,5},{5,4},{6,7},{7,6},{8,9},{9,8},{10,11... | collective-permute-start | bytes 1572872 | tf_op jit(solution)/shard_map/ppermute | solution.py:310
  166.6 15.1 %collective-permute-start.11 = (bf16[512,512]{1,0:T(8,128)(2,1)}, bf16[512,512]{1,0:T(8,128)(2,1)}, u32[]{:S(2)}, u32[]{:S(2)}) collective-permute-start(bf16[512,512]{1,0:T(8,128)(2,1)} %collective-permute-done.10.refs_2_), channel_id=1, source_target_pairs={{0,1},{1,0},{2,3},{3,2},{4,5},{5,4},{6,7},{7,6},{8,9},{9,8},{10,11... | collective-permute-start | bytes 1572872 | tf_op jit(solution)/shard_map/ppermute | solution.py:310
  168.6 1.9 copy-start.5
  168.6 1.9 copy-start.7
  168.6 2.0 copy-start.9
  170.6 3.4 %copy-start.11 = (bf16[512,512]{1,0:T(8,128)(2,1)S(1)}, bf16[512,512]{1,0:T(8,128)(2,1)}, u32[]{:S(2)}) copy-start(bf16[512,512]{1,0:T(8,128)(2,1)} %copy-done.10) | copy-start | bytes 1572868
  172.6 12.8 %collective-permute-start.22 = (bf16[256,512]{1,0:T(8,128)(2,1)S(1)}, bf16[256,512]{1,0:T(8,128)(2,1)S(1)}, u32[]{:S(2)}, u32[]{:S(2)}) collective-permute-start(bf16[256,512]{1,0:T(8,128)(2,1)S(1)} %get-tuple-element.25), channel_id=1, source_target_pairs={{0,4},{1,5},{2,6},{3,7},{4,0},{5,1},{6,2},{7,3},{8,12},{9,13},{10,... | collective-permute-start | bytes 786440 | tf_op jit(solution)/shard_map/ppermute | solution.py:310
  176.7 10.7 %collective-permute-start.25 = (bf16[256,512]{1,0:T(8,128)(2,1)S(1)}, bf16[256,512]{1,0:T(8,128)(2,1)S(1)}, u32[]{:S(2)}, u32[]{:S(2)}) collective-permute-start(bf16[256,512]{1,0:T(8,128)(2,1)S(1)} %get-tuple-element.28), channel_id=1, source_target_pairs={{0,4},{1,5},{2,6},{3,7},{4,0},{5,1},{6,2},{7,3},{8,12},{9,13},{10,... | collective-permute-start | bytes 786440 | tf_op jit(solution)/shard_map/ppermute | solution.py:310
  180.2 12.8 %collective-permute-start.24 = (bf16[256,512]{1,0:T(8,128)(2,1)S(1)}, bf16[256,512]{1,0:T(8,128)(2,1)S(1)}, u32[]{:S(2)}, u32[]{:S(2)}) collective-permute-start(bf16[256,512]{1,0:T(8,128)(2,1)S(1)} %get-tuple-element.27), channel_id=1, source_target_pairs={{0,4},{1,5},{2,6},{3,7},{4,0},{5,1},{6,2},{7,3},{8,12},{9,13},{10,... | collective-permute-start | bytes 786440 | tf_op jit(solution)/shard_map/ppermute | solution.py:310
  181.6 16.6 %copy-start.3 = (s32[4,512,1]{2,1,0:T(8,128)S(1)}, s32[4,512,1]{2,1,0:T(8,128)}, u32[]{:S(2)}) copy-start(s32[4,512,1]{2,1,0:T(8,128)} %copy.33.place_ref) | copy-start | bytes 24580
  184.5 13.7 %collective-permute-start.23 = (bf16[256,512]{1,0:T(8,128)(2,1)S(1)}, bf16[256,512]{1,0:T(8,128)(2,1)S(1)}, u32[]{:S(2)}, u32[]{:S(2)}) collective-permute-start(bf16[256,512]{1,0:T(8,128)(2,1)S(1)} %get-tuple-element.26), channel_id=1, source_target_pairs={{0,4},{1,5},{2,6},{3,7},{4,0},{5,1},{6,2},{7,3},{8,12},{9,13},{10,... | collective-permute-start | bytes 786440 | tf_op jit(solution)/shard_map/ppermute | solution.py:310

commit v2 on v0

--- a/solution.py
+++ b/solution.py
@@ -1,11 +1,22 @@
+import functools
 import math
 
 import jax
 import jax.numpy as jnp
 from jax import lax
+from jax.experimental import pallas as pl
+from jax.experimental.pallas import tpu as pltpu
 from jax.sharding import PartitionSpec as P
 
 epsilon = 1e-05
+AXES = ("seq", "mp")
+LANES = 128
+SUBLANES = 8
+EXTRA = 2 * SUBLANES
+VMEM = pl.BlockSpec(memory_space=pltpu.VMEM)
+ANY = pl.BlockSpec(memory_space=pl.ANY)
+SMEM = pl.BlockSpec(memory_space=pltpu.SMEM)
+PARAMS = pltpu.CompilerParams(vmem_limit_bytes=16 * 1024 * 1024)
 
 
 def toeplitz(filter_taps):
@@ -54,7 +65,7 @@
     return result.reshape(chan_count, seq_length)
 
 
-def project(all_features, norm_gain, weight_pair):
+def project_all(all_features, norm_gain, weight_pair):
     widened = all_features.astype(jnp.float32)
     inv_scale = lax.rsqrt(jnp.mean(widened * widened, axis=0, keepdims=True) + epsilon)
     normed = (widened * inv_scale * norm_gain[:, None]).astype(jnp.bfloat16)
@@ -99,7 +110,7 @@
     arrival_rank = (jnp.cumsum(to_me, axis=1, dtype=jnp.int32) - to_me).reshape(all_count)
     packed = received[:, my_sources // row_count * slot_cap + arrival_rank[my_sources]]
     all_features = lax.all_gather(packed, "mp", axis=0, tiled=True)
-    value_part, gate_part = project(all_features, norm_gain, weight_pair)
+    value_part, gate_part = project_all(all_features, norm_gain, weight_pair)
     value_chan = lax.all_to_all(value_part, "seq", split_axis=0, concat_axis=1, tiled=True)
     link_flags = doc_flags(lengths, all_count // tap_count, jnp.bfloat16)
     prior_rim = jnp.zeros((chan_count, tap_count), jnp.bfloat16)
@@ -113,8 +124,493 @@
     )
 
 
+def extend_kernel(token_ref, out_ref):
+    features, count = token_ref.shape
+    widened = token_ref[...].astype(jnp.float32)
+    rest = jnp.sum(widened * widened, axis=0, keepdims=True)
+    terms = []
+    for _ in range(3):
+        term = rest.astype(jnp.bfloat16).astype(jnp.float32)
+        terms.append(term)
+        rest = rest - term
+    row = lax.broadcasted_iota(jnp.int32, (EXTRA, count), 0)
+    extra = jnp.zeros(row.shape, jnp.float32)
+    for i, term in enumerate(terms):
+        extra = jnp.where(row == i, term, extra)
+    out_ref[0:features, :] = token_ref[...]
+    out_ref[features : features + EXTRA, :] = extra.astype(jnp.bfloat16)
+
+
+def extend(tokens):
+    features, count = tokens.shape
+    return pl.pallas_call(
+        extend_kernel,
+        out_shape=jax.ShapeDtypeStruct((features + EXTRA, count), tokens.dtype),
+        in_specs=[VMEM],
+        out_specs=VMEM,
+        compiler_params=PARAMS,
+        cost_estimate=pl.CostEstimate(
+            flops=2 * features * count, bytes_accessed=4 * features * count, transcendentals=0
+        ),
+    )(tokens)
+
+
+def halve_kernel(x_ref, *refs):
+    arrays, (keep_ref, give_ref) = refs[:-2], refs[-2:]
+    features = arrays[0].shape[0] - EXTRA
+    half = features // 2
+    x = x_ref[0]
+    for number, ref in enumerate(arrays):
+        first = number * (half + EXTRA)
+        for out_ref, which in ((keep_ref, x), (give_ref, 1 - x)):
+            rows = pl.ds(pl.multiple_of(which * half, half), half)
+            out_ref[first : first + half, :] = ref[rows, :]
+            out_ref[first + half : first + half + EXTRA, :] = ref[features : features + EXTRA, :]
+
+
+def halve(x, arrays):
+    tall, count = arrays[0].shape
+    half = (tall - EXTRA) // 2
+    out = jax.ShapeDtypeStruct(((half + EXTRA) * len(arrays), count), arrays[0].dtype)
+    return pl.pallas_call(
+        halve_kernel,
+        out_shape=[out, out],
+        in_specs=[SMEM] + [VMEM] * len(arrays),
+        out_specs=[VMEM, VMEM],
+        compiler_params=PARAMS,
+        cost_estimate=pl.CostEstimate(
+            flops=0, bytes_accessed=4 * tall * count * len(arrays), transcendentals=0
+        ),
+    )(x, *arrays)
+
+
+def pack_kernel(after_ref, *refs):
+    out_ref = refs[-1]
+    line, _, _, width, _ = out_ref.shape
+    for which, ref in enumerate(refs[:-1]):
+        for target in range(line):
+            for half in range(2):
+                first = (half * line + target) * width
+                out_ref[target, which, half] = ref[:, first : first + width].T
+
+
+def pack_weights(after, weights, line):
+    height, columns = weights[0].shape
+    out = (line, len(weights), 2, columns // (2 * line), height)
+    return pl.pallas_call(
+        pack_kernel,
+        out_shape=jax.ShapeDtypeStruct(out, weights[0].dtype),
+        in_specs=[ANY] + [VMEM] * len(weights),
+        out_specs=VMEM,
+        compiler_params=PARAMS,
+        cost_estimate=pl.CostEstimate(
+            flops=0, bytes_accessed=4 * height * columns * len(weights), transcendentals=0
+        ),
+    )(after, *weights)
+
+
+def scale_kernel(height, pick_ref, gain_ref, *refs):
+    arrays, out_ref = refs[:-1], refs[-1]
+    parts = out_ref.shape[0]
+    tall = height + EXTRA
+    blocks = [
+        ref.at[first : first + tall] for ref in arrays for first in range(0, ref.shape[0], tall)
+    ]
+    each = len(blocks) // parts
+    count = out_ref.shape[2] // each
+    slots = each // 2 if each > 1 else 1
+    features = 2 * height * parts
+    gain_columns = gain_ref[...].T
+    for number in range(each):
+        slot, half = number % slots, number // slots
+        first = (slot * (each // slots) + half) * count
+        squares = jnp.zeros((1, count), jnp.float32)
+        for block in blocks[number::each]:
+            terms = block[height:tall, :].astype(jnp.float32)
+            squares += jnp.sum(terms, axis=0, keepdims=True)
+        inv_row = lax.rsqrt(squares / features + epsilon)
+        for part in range(parts):
+            scaled = blocks[part * each + number][0:height, :].astype(jnp.float32) * inv_row
+            scaled = (scaled * gain_columns[:, part : part + 1]).astype(jnp.bfloat16)
+            out_ref[pick_ref[part], :, first : first + count] = scaled
+
+
+def scale(picks, gains, height, arrays):
+    parts = picks.shape[0]
+    count = arrays[0].shape[1]
+    each = sum(array.shape[0] for array in arrays) // (height + EXTRA) // parts
+    return pl.pallas_call(
+        functools.partial(scale_kernel, height),
+        out_shape=jax.ShapeDtypeStruct((parts, height, count * each), jnp.bfloat16),
+        in_specs=[SMEM] + [VMEM] * (1 + len(arrays)),
+        out_specs=VMEM,
+        compiler_params=PARAMS,
+        cost_estimate=pl.CostEstimate(
+            flops=2 * parts * height * count * each,
+            bytes_accessed=4 * parts * height * count * each,
+            transcendentals=0,
+        ),
+    )(picks, gains, *arrays)
+
+
+def project_kernel(number, starts, row_count, x_ref, weight_ref, *refs):
+    mine_ref, other_ref = refs[-2:]
+    x = x_ref[0]
+    first = 0
+    for ref, far in zip(refs[:-2], starts):
+        parts, _, count = ref.shape
+        for begin in range(0, count, 2 * row_count):
+            columns = slice(begin, min(begin + 2 * row_count, count))
+            wide = columns.stop - begin
+            mine = jnp.zeros((mine_ref.shape[0], wide), jnp.float32)
+            other = jnp.zeros((mine_ref.shape[0], wide), jnp.float32)
+            for part in range(parts):
+                block = ref[part, :, columns]
+                for which, is_mine in ((x, True), (1 - x, False)):
+                    result = jnp.dot(
+                        weight_ref[part, number, which], block, preferred_element_type=jnp.float32
+                    )
+                    mine, other = (mine + result, other) if is_mine else (mine, other + result)
+            mine_ref[:, first + begin : first + begin + wide] = mine
+            other = other.astype(jnp.bfloat16)
+            if wide > row_count:
+                other = jnp.concatenate([other[:, row_count:], other[:, :row_count]], axis=1)
+            other_ref[:, far + begin : far + begin + wide] = other
+        first += count
+
+
+def project(x, weights, number, normed, row_count, starts=None):
+    line, _, _, width, height = weights.shape
+    counts = [some.shape[2] for some in normed]
+    starts = starts or [sum(counts[:i]) for i in range(len(counts))]
+    out = (width, sum(counts))
+    return pl.pallas_call(
+        functools.partial(project_kernel, number, starts, row_count),
+        out_shape=[
+            jax.ShapeDtypeStruct(out, jnp.float32),
+            jax.ShapeDtypeStruct(out, jnp.bfloat16),
+        ],
+        in_specs=[SMEM] + [VMEM] * (1 + len(normed)),
+        out_specs=[VMEM] * 2,
+        compiler_params=PARAMS,
+        cost_estimate=pl.CostEstimate(
+            flops=4 * width * height * out[1] * line,
+            bytes_accessed=weights.size + 2 * height * out[1] * line,
+            transcendentals=0,
+        ),
+    )(x, weights, *normed)
+
+
+def column_of(row):
+    tall = jnp.broadcast_to(row.astype(jnp.float32), (SUBLANES, row.shape[1])).T
+    return tall[:, 0:1].astype(row.dtype)
+
+
+def at_places(array, place_row, total):
+    spot = lax.broadcasted_iota(jnp.int32, (array.shape[1], total), 1)
+    onehot = (column_of(place_row) == spot).astype(jnp.float32).astype(jnp.bfloat16)
+    return jnp.dot(array, onehot, preferred_element_type=jnp.float32)
+
+
+def with_tokens(first, tall, summed, token_refs):
+    chan = summed.shape[0]
+    first = pl.multiple_of(first, chan)
+    tokens = []
+    for kept_ref, got_ref in zip(token_refs[::2], token_refs[1::2]):
+        for start in range(0, kept_ref.shape[0], tall):
+            tokens += [ref[pl.ds(first + start, chan), :] for ref in (kept_ref, got_ref)]
+    return jnp.concatenate([summed, jnp.concatenate(tokens, axis=1)], axis=0)
+
+
+def place_kernel(tall, many, first_ref, mine_ref, theirs_ref, place_ref, *refs):
+    tokens, before, out_ref = refs[:many], refs[many:-1], refs[-1]
+    count = place_ref.shape[1]
+    summed = mine_ref[:, :count] + theirs_ref[:, :count].astype(jnp.float32)
+    summed = summed.astype(jnp.bfloat16)
+    if tokens:
+        summed = with_tokens(first_ref[0], tall, summed, tokens)
+    moved = at_places(summed, place_ref[...], out_ref.shape[1])
+    for ref in before:
+        moved += ref[...].astype(jnp.float32)
+    out_ref[...] = moved.astype(jnp.bfloat16)
+
+
+def place(first, total, mine, theirs, places, tall=0, tokens=(), before=()):
+    chan, count = mine.shape[0], places.shape[1]
+    return pl.pallas_call(
+        functools.partial(place_kernel, tall, len(tokens)),
+        out_shape=jax.ShapeDtypeStruct((2 * chan if tokens else chan, total), jnp.bfloat16),
+        in_specs=[SMEM] + [VMEM] * (3 + len(tokens) + len(before)),
+        out_specs=VMEM,
+        compiler_params=PARAMS,
+        cost_estimate=pl.CostEstimate(
+            flops=2 * chan * total * count, bytes_accessed=8 * chan * total, transcendentals=0
+        ),
+    )(first, mine, theirs, places, *tokens, *before)
+
+
+def band_kernel(
+    taps_blocks, tall, flag_ref, first_ref, taps_ref, skip_ref, early_ref, mine_ref, theirs_ref,
+    last_mine_ref, last_theirs_ref, place_ref, *refs
+):
+    shifted = refs[-taps_blocks - 1 :]
+    out_ref, packed_ref, whole, band = refs[-taps_blocks - 5 : -taps_blocks - 1]
+    chan = taps_ref.shape[0]
+    total = whole.shape[1]
+    pieces = total // LANES
+    cut = mine_ref.shape[1] - last_mine_ref.shape[1]
+    mine = jnp.concatenate([mine_ref[:, cut:], last_mine_ref[...]], axis=1)
+    theirs = jnp.concatenate([last_theirs_ref[...], theirs_ref[:, cut:]], axis=1)
+    summed = (mine + theirs.astype(jnp.float32)).astype(jnp.bfloat16)
+    summed = with_tokens(first_ref[0], tall, summed, refs[: -taps_blocks - 5])
+    moved = at_places(summed, place_ref[...], total) + early_ref[...].astype(jnp.float32)
+    whole[...] = moved[0:chan]
+    packed_ref[...] = moved[chan : 2 * chan].astype(jnp.bfloat16)
+    for piece in range(pieces):
+        for back in range(taps_blocks + 1):
+            rows = pl.ds(piece * chan, chan)
+            if back > piece:
+                shifted[back][rows, :] = jnp.zeros((chan, LANES), jnp.float32)
+                continue
+            first = (piece - back) * LANES
+            part = whole[:, first : first + LANES]
+            if back > piece % taps_blocks:
+                part = part * flag_ref[piece // taps_blocks]
+            shifted[back][rows, :] = part
+    column = lax.broadcasted_iota(jnp.int32, (LANES, LANES), 1)
+    row = lax.broadcasted_iota(jnp.int32, (LANES, LANES), 0)
+    later = column >= row
+    zero = jnp.zeros((LANES, LANES), jnp.float32)
+
+    def one(group, carry):
+        base = pl.multiple_of(group * SUBLANES, SUBLANES)
+        group_taps = taps_ref[pl.ds(base, SUBLANES), :]
+        for member in range(SUBLANES):
+            turned = [zero]
+            for block in range(taps_blocks):
+                line_row = group_taps[member : member + 1, block * LANES : (block + 1) * LANES]
+                square = jnp.broadcast_to(line_row, (LANES, LANES))
+                turned.append(pltpu.roll(square, 0, 1, stride=1, stride_axis=0))
+            turned.append(zero)
+            rows = pl.ds(base + member, pieces, stride=chan)
+            tiles, inputs = [], []
+            for back in range(taps_blocks + 1):
+                tiles.append(jnp.where(later, turned[back + 1], turned[back]).astype(jnp.bfloat16))
+                inputs.append(shifted[back][rows, :].astype(jnp.bfloat16))
+            band[rows, :] = jnp.dot(
+                jnp.concatenate(inputs, axis=1),
+                jnp.concatenate(tiles, axis=0),
+                preferred_element_type=jnp.float32,
+            )
+        return carry
+
+    lax.fori_loop(0, chan // SUBLANES, one, 0)
+    skip = column_of(skip_ref[...])
+    for piece in range(pieces):
+        lanes = slice(piece * LANES, (piece + 1) * LANES)
+        rows = pl.ds(piece * chan, chan)
+        out_ref[:, lanes] = (band[rows, :] + skip * whole[:, lanes]).astype(jnp.bfloat16)
+
+
+def band_of(flags, first, taps, skip, early, late, last, places, tall, tokens):
+    chan, tap_count = taps.shape
+    total = early.shape[1]
+    taps_blocks = tap_count // LANES
+    tower = (total // LANES * chan, LANES)
+    out = jax.ShapeDtypeStruct((chan, total), jnp.bfloat16)
+    return pl.pallas_call(
+        functools.partial(band_kernel, taps_blocks, tall),
+        out_shape=[out, out],
+        in_specs=[SMEM, SMEM] + [VMEM] * (8 + len(tokens)),
+        out_specs=[VMEM, VMEM],
+        scratch_shapes=[pltpu.VMEM((chan, total), jnp.float32)]
+        + [pltpu.VMEM(tower, jnp.float32)] * (taps_blocks + 2),
+        compiler_params=PARAMS,
+        cost_estimate=pl.CostEstimate(
+            flops=3 * chan * total * total, bytes_accessed=16 * chan * total, transcendentals=0
+        ),
+    )(flags, first, taps, skip, early, *late, *last, places, *tokens)
+
+
+def mix_kernel(z_ref, packed_ref, early_ref, mine_ref, theirs_ref, place_ref, out_ref):
+    summed = (mine_ref[...] + theirs_ref[...].astype(jnp.float32)).astype(jnp.bfloat16)
+    gate = at_places(summed, place_ref[...], z_ref.shape[1]) + early_ref[...].astype(jnp.float32)
+    mixed = packed_ref[...].astype(jnp.float32) + gate * z_ref[...].astype(jnp.float32)
+    mixed = mixed.astype(jnp.bfloat16)
+    wide = out_ref.shape[2]
+    for owner in range(out_ref.shape[0]):
+        out_ref[owner] = mixed[:, owner * wide : (owner + 1) * wide]
+
+
+def mix(z, packed, early, mine, theirs, places, shards):
+    chan, total = z.shape
+    return pl.pallas_call(
+        mix_kernel,
+        out_shape=jax.ShapeDtypeStruct((shards, chan, total // shards), jnp.bfloat16),
+        in_specs=[VMEM] * 6,
+        out_specs=VMEM,
+        compiler_params=PARAMS,
+        cost_estimate=pl.CostEstimate(
+            flops=chan * total * total, bytes_accessed=16 * chan * total, transcendentals=0
+        ),
+    )(z, packed, early, mine, theirs, places)
+
+
+def on_device_line(tokens, packing, norm_gain, w_value, w_gate, filters, skip_gain, lengths):
+    shards, groups = lax.axis_size("seq"), lax.axis_size("mp")
+    line = shards // 2
+    s, m = lax.axis_index("seq"), lax.axis_index("mp")
+    z, x = s // 2, s % 2
+    features, row_count = tokens.shape
+    half = features // 2
+    total_rows = packing.shape[0]
+    width = features // shards
+
+    def number(zz, xx, mm):
+        return (zz * 2 + xx) * groups + mm
+
+    def send(array, target):
+        pairs = []
+        for zz in range(line):
+            for xx in range(2):
+                for mm in range(groups):
+                    to = target(zz, xx, mm)
+                    if to is not None:
+                        pairs.append((number(zz, xx, mm), number(*to)))
+        return lax.ppermute(array, AXES, pairs)
+
+    def across(array):
+        return send(array, lambda zz, xx, mm: (zz, 1 - xx, mm))
+
+    def to_owner(array, o):
+        return send(array, lambda zz, xx, mm: (zz, xx, mm ^ o))
+
+    columns = [[number(zz, xx, mm) for zz in range(line)] for xx in range(2) for mm in range(groups)]
+
+    def along_line(array):
+        return lax.all_to_all(
+            array, AXES, split_axis=0, concat_axis=0, tiled=True, axis_index_groups=columns
+        )
+
+    def to_pair(array, o):
+        return send(array, lambda zz, xx, mm: (zz ^ o, xx, mm))
+
+    slot_pair = jnp.stack([z ^ o for o in range(line)])
+    far_owner, near_owner, far_pair, near_pair = groups // 2, groups // 4, line // 2, line // 4
+    owners = jnp.stack([m ^ o for o in (0, far_owner, near_owner, far_owner ^ near_owner)])
+    which = x[None].astype(jnp.int32)
+    picks = owners.astype(jnp.int32)
+    gains = norm_gain.reshape(groups, 2, half)[:, x][owners]
+    gains = jnp.pad(gains, ((0, -groups % SUBLANES), (0, 0)))
+    places = packing.reshape(line, 2, row_count)[slot_pair]
+    places = jnp.stack([places[:, x], places[:, 1 - x]], axis=1).reshape(1, total_rows)
+    first = x * half + z * width
+    taps = lax.dynamic_slice_in_dim(filters, first, width, 0).astype(jnp.float32)
+    skip = lax.dynamic_slice_in_dim(skip_gain, first, width, 0)[None]
+    flags = doc_flags(lengths, total_rows // filters.shape[1], jnp.float32)
+    row_first = (z * width)[None].astype(jnp.int32)
+    tall = half + EXTRA
+    wide = 2 * row_count
+
+    def projected(number, some, starts=None):
+        return project(which, weights, number, some, row_count, starts)
+
+    def scaled(arrays):
+        return scale(picks, gains, half, arrays)
+
+    def to_near(arrays):
+        stacked = jnp.concatenate(arrays, axis=0) if len(arrays) > 1 else arrays[0]
+        return to_owner(stacked, near_owner)
+
+    def tie(*arrays):
+        return lax.optimization_barrier(arrays)
+
+    extended = extend(tokens)
+    kept0, give0 = halve(which, [extended])
+    by_far, by_near = to_pair(extended, far_pair), to_pair(extended, near_pair)
+    got0, kept0_far = across(give0), to_owner(kept0, far_owner)
+    got0_far = to_owner(got0, far_owner)
+    packed_weights = pack_weights(give0, [w_value, w_gate], line)
+    small = picks, gains, taps, skip, flags, row_first, places, which
+    by_both = to_pair(by_far, near_pair)
+    by_far, by_near, got0, kept0_far, got0_far, small, packed_weights = tie(
+        by_far, by_near, got0, kept0_far, got0_far, small, packed_weights
+    )
+    picks, gains, taps, skip, flags, row_first, places, which = small
+
+    kept1, give1 = halve(which, [by_near, by_far])
+    got1, kept1_far = across(give1), to_owner(kept1, far_owner)
+    packed_weights, _ = tie(packed_weights, got1)
+    weights = along_line(packed_weights)
+    all0 = to_near([kept0, got0, kept0_far, got0_far])
+    by_both, got1, kept1_far, all0 = tie(by_both, got1, kept1_far, all0)
+
+    kept2, give2 = halve(which, [by_both])
+    got2, kept2_far = across(give2), to_owner(kept2, far_owner)
+    got1_far = to_owner(got1, far_owner)
+    some1 = to_near([kept1, got1, kept1_far])
+    normed0 = scaled([kept0, got0, kept0_far, got0_far, all0])
+    got2, kept2_far, got1_far, some1, normed0 = tie(got2, kept2_far, got1_far, some1, normed0)
+
+    got2_far = to_owner(got2, far_owner)
+    rest1 = to_near([got1_far])
+    near_kept2, near_kept2_far, near_got2 = [to_near([some]) for some in (kept2, kept2_far, got2)]
+    got2_far, rest1, near_kept2, near_kept2_far, near_got2 = tie(
+        got2_far, rest1, near_kept2, near_kept2_far, near_got2
+    )
+
+    near_got2_far = to_near([got2_far])
+    normed1 = scaled([kept1, got1, kept1_far, got1_far, some1, rest1])
+    normed2 = scaled([kept2, kept2_far, near_kept2, near_kept2_far])
+    near_got2_far, normed1, normed2, weights = tie(near_got2_far, normed1, normed2, weights)
+
+    near0, far0 = projected(0, [normed0])
+    theirs0 = across(far0)
+    near1, far1 = projected(0, [normed1, normed2])
+    theirs1 = across(far1)
+    normed3 = scaled([got2, got2_far, near_got2, near_got2_far])
+    near3, far3 = projected(0, [normed3])
+    theirs3 = across(far3)
+    normed0, normed1, near3 = tie(normed0, normed1, near3)
+    gate_near0, gate_far0 = projected(1, [normed0, normed1])
+    gate_near3, gate_far3 = projected(1, [normed2, normed3], [row_count, 0])
+    early = place(
+        row_first, total_rows, near0, theirs0, places[:, :wide], tall, [kept0, got0]
+    )
+    early = place(
+        row_first, total_rows, near1, theirs1, places[:, wide:-wide], tall, [kept1, got1], [early]
+    )
+    early, theirs3, gate_far0, gate_far3 = tie(early, theirs3, gate_far0, gate_far3)
+    gate_theirs0, gate_theirs3 = across(gate_far0), across(gate_far3)
+    banded, packed = band_of(
+        flags, row_first, taps, skip, early, (near1, theirs1), (near3, theirs3),
+        places[:, -wide:], tall, [kept2, got2],
+    )
+    early = place(row_first, total_rows, gate_near0, gate_theirs0, places[:, :-wide])
+    mixed = mix(banded, packed, early, gate_near3, gate_theirs3, places[:, -wide:], shards)
+    mixed = lax.all_to_all(mixed, "seq", split_axis=0, concat_axis=0, tiled=True)
+    mixed = mixed.reshape(line, 2, width, row_count).transpose(1, 0, 2, 3)
+    return mixed.reshape(features, row_count)
+
+
 def solution(mesh):
     placed = (P("mp", "seq"), P(), P(), P("seq", "mp"), P("seq", "mp"), P("mp", None), P("mp"), P())
-    return jax.shard_map(
-        on_device, mesh=mesh, in_specs=placed, out_specs=P("mp", "seq"), check_vma=False
-    )
+    shards, groups = mesh.shape["seq"], mesh.shape["mp"]
+
+    def whole(*args):
+        tokens, w_value, filters = args[0], args[3], args[5]
+        moves_tokens = (
+            tokens.shape[1] <= w_value.shape[1]
+            and shards == 2 * groups
+            and groups & (groups - 1) == 0
+            and (groups - 1).bit_count() == 2
+            and tokens.shape[0] % (LANES * shards * groups) == 0
+            and filters.shape[1] % LANES == 0
+            and tokens.shape[1] // shards % filters.shape[1] == 0
+        )
+        body = on_device_line if moves_tokens else on_device
+        return jax.shard_map(
+            body, mesh=mesh, in_specs=placed, out_specs=P("mp", "seq"), check_vma=False
+        )(*args)
+
+    return whole

time: 502 us -> 148 us (0.29)
  local copies, waits for them, and re-layouts: 228 us -> 15.5 us
  waiting for transfers between devices: 204 us -> 53.4 us
  matrix products: 32.6 us -> 0 us
  Pallas kernels: 0 us -> 27.5 us
  starting transfers between devices: 15.2 us -> 30 us
  blocking collectives: 0 us -> 14.4 us
  between operations: 13.4 us -> 0.59 us
    all_gather x3 -> x0, waiting for transfers between devices: 145 us -> none  [the longest x1 125 us: on_device(): lax.all_gather(w_value, 'seq', axis=0, tiled=True)]
    reshape x3, local copies, waits for them, and re-layouts: 124 us -> 1.46 us  [the longest x1 0.73 us: on_device_line(): gains = norm_gain.reshape(groups, 2, half)[:, x][owners]]
    all_to_all x3 -> x1, waiting for transfers between devices: 57.1 us -> 10.8 us  [along_line(): lax.all_to_all(array, AXES, split_axis=0, concat_axis=0, tiled=True, axis...]
    ppermute x0 -> x24, waiting for transfers between devices: none -> 42.6 us  [send(): return lax.ppermute(array, AXES, pairs)]
    slice x3, local copies, waits for them, and re-layouts: 41.3 us -> 0.01 us  [the longest x1 0.01 us: on_device_line(): places[:, -wide:]]
    dot_general x4 -> x0, matrix products: 32.6 us -> none  [the longest x2 19.5 us: one_group(): jnp.einsum('cpq,cbq->cbp', toeplitz(part_taps), joined, preferred_element...]
    while x4 -> x0, local copies, waits for them, and re-layouts: 31.8 us -> none
    pallas_call x0 -> x19, Pallas kernels: none -> 27.5 us  [the longest x1 7.43 us: band_of(): pl.pallas_call(functools.partial(band_kernel, taps_blocks, tall), out_sha...]
  transfers between devices with their start and end apart: 6 -> 25, of which waited for: 5 -> 9; matrix products, arithmetic and copies ran while one was open for 50% -> 5% of each run, Pallas kernels for 0% -> 17%
where the time goes in v2:
time: 148 us; the launch traced here: 147 us
  waiting for transfers between devices  53.4 us (36%)
  starting transfers between devices  30 us (20%)
  Pallas kernels  27.5 us (19%)
  local copies, waits for them, and re-layouts  15.5 us (10%)
  blocking collectives  14.4 us (10%)
  other arithmetic  5.56 us (4%)
    ppermute x24, waiting for transfers between devices, send(): return lax.ppermute(array, AXES, pairs)  42.6 us
    ppermute x24, starting transfers between devices, send(): return lax.ppermute(array, AXES, pairs)  25.5 us
    all_to_all x1, blocking collectives, on_device_line(): lax.all_to_all(mixed, 'seq', split_axis=0, concat_axis=0, tiled=True)  14.4 us
    unnamed x75, local copies, waits for them, and re-layouts  12 us
    all_to_all x1, waiting for transfers between devices, along_line(): lax.all_to_all(array, AXES, split_axis=0, concat_axis=0, tiled=True, axis...  10.8 us
    pallas_call x1, Pallas kernels, band_of(): pl.pallas_call(functools.partial(band_kernel, taps_blocks, tall), out_sha...  7.43 us
    pallas_call x4, Pallas kernels, scale(): pl.pallas_call(functools.partial(scale_kernel, height), out_shape=jax.Sha...  6.54 us
    pallas_call x5, Pallas kernels, project(): pl.pallas_call(functools.partial(project_kernel, number, starts, row_coun...  5.22 us
  transfers between devices with their start and end apart: 25, of which 9 were waited for; matrix products, arithmetic and copies ran while one was open for 5% of the time, Pallas kernels for 17%

profile of v2, /device:TPU:0, one launch (start us, length us, event | category | flops | bytes accessed | tf_op | source)
XLA Modules:
  0.0 147.0 jit_solution(8769808474498811120)
XLA Ops:
  0.0 1.1 copy-done.23
  1.2 4.1 %collective-permute-start = (bf16[1040,256]{1,0:T(8,128)(2,1)S(1)}, bf16[1040,256]{1,0:T(8,128)(2,1)S(1)}, u32[]{:S(2)}, u32[]{:S(2)}) collective-permute-start(bf16[1040,256]{1,0:T(8,128)(2,1)S(1)} %shard_map.82.refs_0_), channel_id=1, source_target_pairs={{0,16},{1,17},{2,18},{3,19},{4,20},{5,21},{6,22},{7,23},{8,24},{9,... | collective-permute-start | bytes 1597448 | tf_op jit(solution)/shard_map/ppermute | solution.py:480
  5.3 1.6 %collective-permute-start.1 = (bf16[1040,256]{1,0:T(8,128)(2,1)S(1)}, bf16[1040,256]{1,0:T(8,128)(2,1)}, u32[]{:S(2)}, u32[]{:S(2)}) collective-permute-start(bf16[1040,256]{1,0:T(8,128)(2,1)S(1)} %shard_map.82.refs_0_), channel_id=1, source_target_pairs={{0,8},{1,9},{2,10},{3,11},{4,12},{5,13},{6,14},{7,15},{8,0},{9,1},... | collective-permute-start | bytes 1597448 | tf_op jit(solution)/shard_map/ppermute | solution.py:480
  7.0 1.6 %collective-permute-start.3 = (bf16[528,256]{1,0:T(8,128)(2,1)S(1)}, bf16[528,256]{1,0:T(8,128)(2,1)S(1)}, u32[]{:S(2)}, u32[]{:S(2)}) collective-permute-start(bf16[528,256]{1,0:T(8,128)(2,1)S(1)} %get-tuple-element.64.refs_0_), channel_id=1, source_target_pairs={{0,2},{1,3},{2,0},{3,1},{4,6},{5,7},{6,4},{7,5},{8,10},{9,11},{10,... | collective-permute-start | bytes 811016 | tf_op jit(solution)/shard_map/ppermute | solution.py:480
  8.5 1.5 %collective-permute-start.2 = (bf16[528,256]{1,0:T(8,128)(2,1)S(1)}, bf16[528,256]{1,0:T(8,128)(2,1)S(1)}, u32[]{:S(2)}, u32[]{:S(2)}) collective-permute-start(bf16[528,256]{1,0:T(8,128)(2,1)S(1)} %get-tuple-element.63.after_ref), channel_id=1, source_target_pairs={{0,4},{1,5},{2,6},{3,7},{4,0},{5,1},{6,2},{7,3},{8,12},{9,13},{10,... | collective-permute-start | bytes 811016 | tf_op jit(solution)/shard_map/ppermute | solution.py:480
  10.8 0.7 reshape.364
  11.6 0.8 reduce-window.9
  13.9 1.5 %dynamic-slice_convert_fusion.taps_ref = f32[128,256]{1,0:T(8,128)} fusion(bf16[1024,256]{1,0:T(8,128)(2,1)} %param.13, s32[]{:T(128)S(6)} %select_n.50), kind=kLoop, calls=%fused_computation.4 | loop fusion | flops 32768 | bytes 196612 | tf_op jit(solution)/shard_map/convert_element_type | solution.py:508
  17.1 1.2 copy-done.21
  18.4 1.0 copy-done.29
  19.9 1.4 copy-done.6
  21.3 7.7 %collective-permute-done.refs_1_ = bf16[1040,256]{1,0:T(8,128)(2,1)S(1)} collective-permute-done((bf16[1040,256]{1,0:T(8,128)(2,1)S(1)}, bf16[1040,256]{1,0:T(8,128)(2,1)S(1)}, u32[]{:S(2)}, u32[]{:S(2)}) %collective-permute-start) | collective-permute-done | bytes 532512 | tf_op jit(solution)/shard_map/ppermute | solution.py:480
  29.3 1.1 pad_maximum_fusion.1
  30.3 1.1 shard_map.85
  31.5 1.6 %collective-permute-start.6 = (bf16[1056,256]{1,0:T(8,128)(2,1)S(1)}, bf16[1056,256]{1,0:T(8,128)(2,1)S(1)}, u32[]{:S(2)}, u32[]{:S(2)}) collective-permute-start(bf16[1056,256]{1,0:T(8,128)(2,1)S(1)} %get-tuple-element.72), channel_id=1, source_target_pairs={{0,4},{1,5},{2,6},{3,7},{4,0},{5,1},{6,2},{7,3},{8,12},{9,13},{10,... | collective-permute-start | bytes 1622024 | tf_op jit(solution)/shard_map/ppermute | solution.py:480
  33.1 1.5 %collective-permute-start.7 = (bf16[1056,256]{1,0:T(8,128)(2,1)S(1)}, bf16[1056,256]{1,0:T(8,128)(2,1)}, u32[]{:S(2)}, u32[]{:S(2)}) collective-permute-start(bf16[1056,256]{1,0:T(8,128)(2,1)S(1)} %get-tuple-element.73.refs_0_), channel_id=1, source_target_pairs={{0,2},{1,3},{2,0},{3,1},{4,6},{5,7},{6,4},{7,5},{8,10},{9,11},{10,... | collective-permute-start | bytes 1622024 | tf_op jit(solution)/shard_map/ppermute | solution.py:480
  34.6 1.4 collective-permute-start.5
  36.0 10.2 %collective-permute-done.6.refs_1_ = bf16[1056,256]{1,0:T(8,128)(2,1)S(1)} collective-permute-done((bf16[1056,256]{1,0:T(8,128)(2,1)S(1)}, bf16[1056,256]{1,0:T(8,128)(2,1)S(1)}, u32[]{:S(2)}, u32[]{:S(2)}) %collective-permute-start.6) | collective-permute-done | bytes 540704 | tf_op jit(solution)/shard_map/ppermute | solution.py:480
  46.2 4.5 %all-to-all-start = ((bf16[4,2,2,128,512]{4,3,2,1,0:T(8,128)(2,1)}), bf16[4,2,2,128,512]{4,3,2,1,0:T(8,128)(2,1)S(1)}, u32[]{:S(2)}, u32[]{:S(2)}) async-start(bf16[4,2,2,128,512]{4,3,2,1,0:T(8,128)(2,1)} %copy-done.6), calls=%async_computation | async-start | bytes 4194304 | tf_op jit(solution)/shard_map/all_to_all | solution.py:491
  50.8 1.2 pad_maximum_fusion
  52.1 1.6 %collective-permute-start.11 = (bf16[1056,256]{1,0:T(8,128)(2,1)S(1)}, bf16[1056,256]{1,0:T(8,128)(2,1)S(1)}, u32[]{:S(2)}, u32[]{:S(2)}) collective-permute-start(bf16[1056,256]{1,0:T(8,128)(2,1)S(1)} %collective-permute-done.6.refs_1_), channel_id=1, source_target_pairs={{0,2},{1,3},{2,0},{3,1},{4,6},{5,7},{6,4},{7,5},{8,10},{9,11},{10,... | collective-permute-start | bytes 1622024 | tf_op jit(solution)/shard_map/ppermute | solution.py:480
  53.7 1.1 shard_map.86
  55.4 1.5 %collective-permute-start.9 = (bf16[528,256]{1,0:T(8,128)(2,1)S(1)}, bf16[528,256]{1,0:T(8,128)(2,1)S(1)}, u32[]{:S(2)}, u32[]{:S(2)}) collective-permute-start(bf16[528,256]{1,0:T(8,128)(2,1)S(1)} %get-tuple-element.78), channel_id=1, source_target_pairs={{0,4},{1,5},{2,6},{3,7},{4,0},{5,1},{6,2},{7,3},{8,12},{9,13},{10,... | collective-permute-start | bytes 811016 | tf_op jit(solution)/shard_map/ppermute | solution.py:480
  56.9 1.9 %shard_map.87.refs_0_ = bf16[4,512,512]{2,1,0:T(8,128)(2,1)S(1)} custom-call(s32[4]{0:T(128)S(1)} %pad_add_fusion.1.pick_ref, f32[8,512]{1,0:T(8,128)S(1)} %pad.4.gain_ref, bf16[528,256]{1,0:T(8,128)(2,1)S(1)} %get-tuple-element.64.refs_0_, bf16[528,256]{1,0:T(8,128)(2,1)S(1)} %copy-done.14, bf16[528,256]{1,0:T(8,128)(2,1)S(1)} %copy-done.17, ...), custom_call_target="tpu_custom_call" | custom-call | flops 2097152 | bytes 4194304 | tf_op jit(solution)/shard_map/pallas_call | solution.py:242
  58.8 1.4 copy-done.4
  60.2 12.4 %collective-permute-done.10.refs_1_ = bf16[528,256]{1,0:T(8,128)(2,1)S(1)} collective-permute-done((bf16[528,256]{1,0:T(8,128)(2,1)S(1)}, bf16[528,256]{1,0:T(8,128)(2,1)S(1)}, u32[]{:S(2)}, u32[]{:S(2)}) %collective-permute-start.10) | collective-permute-done | bytes 270368 | tf_op jit(solution)/shard_map/ppermute | solution.py:480
  73.2 1.5 %collective-permute-start.13 = (bf16[528,256]{1,0:T(8,128)(2,1)S(1)}, bf16[528,256]{1,0:T(8,128)(2,1)S(1)}, u32[]{:S(2)}, u32[]{:S(2)}) collective-permute-start(bf16[528,256]{1,0:T(8,128)(2,1)S(1)} %collective-permute-done.9.refs_0_.refs_1_), channel_id=1, source_target_pairs={{0,2},{1,3},{2,0},{3,1},{4,6},{5,7},{6,4},{7,5},{8,10},{9,11},{10,... | collective-permute-start | bytes 811016 | tf_op jit(solution)/shard_map/ppermute | solution.py:480
  75.2 6.4 %collective-permute-done.13.refs_1_ = bf16[528,256]{1,0:T(8,128)(2,1)S(1)} collective-permute-done((bf16[528,256]{1,0:T(8,128)(2,1)S(1)}, bf16[528,256]{1,0:T(8,128)(2,1)S(1)}, u32[]{:S(2)}, u32[]{:S(2)}) %collective-permute-start.13) | collective-permute-done | bytes 270368 | tf_op jit(solution)/shard_map/ppermute | solution.py:480
  81.8 1.0 shard_map.89.refs_1_.refs_0_
  82.8 2.6 %shard_map.88.refs_0_.refs_1_ = bf16[4,512,1024]{2,1,0:T(8,128)(2,1)S(1)} custom-call(s32[4]{0:T(128)S(1)} %pad_add_fusion.1.pick_ref, f32[8,512]{1,0:T(8,128)S(1)} %pad.4.gain_ref, bf16[1056,256]{1,0:T(8,128)(2,1)S(1)} %copy-done.8, bf16[1056,256]{1,0:T(8,128)(2,1)S(1)} %copy-done.11, bf16[1056,256]{1,0:T(8,128)(2,1)} %collective-permute-done.7.refs_2_, ...), custom_call_target="tpu_custom_call" | custom-call | flops 4194304 | bytes 8388608 | tf_op jit(solution)/shard_map/pallas_call | solution.py:242
  85.4 2.0 %copy-done.1 = bf16[4,512,1024]{2,1,0:T(8,128)(2,1)} copy-done((bf16[4,512,1024]{2,1,0:T(8,128)(2,1)}, bf16[4,512,1024]{2,1,0:T(8,128)(2,1)S(1)}, u32[]{:S(2)}) %copy-start.1) | copy-done | bytes 4194328
  88.1 10.8 %all-to-all-done.weight_ref = bf16[4,2,2,128,512]{4,3,2,1,0:T(8,128)(2,1)S(1)} async-done(((bf16[4,2,2,128,512]{4,3,2,1,0:T(8,128)(2,1)}), bf16[4,2,2,128,512]{4,3,2,1,0:T(8,128)(2,1)S(1)}, u32[]{:S(2)}, u32[]{:S(2)}) %all-to-all-start) | async-done | bytes 2097184 | tf_op jit(solution)/shard_map/all_to_all | solution.py:491
  98.9 2.2 %copy-done.2 = bf16[4,512,1024]{2,1,0:T(8,128)(2,1)S(1)} copy-done((bf16[4,512,1024]{2,1,0:T(8,128)(2,1)S(1)}, bf16[4,512,1024]{2,1,0:T(8,128)(2,1)}, u32[]{:S(2)}) %copy-start.2) | copy-done | bytes 4194328
  101.1 1.5 %shard_map.90 = (f32[128,1280]{1,0:T(8,128)S(1)}, bf16[128,1280]{1,0:T(8,128)(2,1)S(1)}) custom-call(s32[1]{0:T(128)} %bitcast.x_ref, bf16[4,2,2,128,512]{4,3,2,1,0:T(8,128)(2,1)S(1)} %all-to-all-done.weight_ref, bf16[4,512,1024]{2,1,0:T(8,128)(2,1)S(1)} %copy-done.2, bf16[4,512,256]{2,1,0:T(8,128)(2,1)S(1)} %shard_map.89.refs_1_.refs_0_), custom_call_target="tpu_custom_call" | custom-call | flops 1342177280 | bytes 6291456 | tf_op jit(solution)/shard_map/pallas_call | solution.py:287
  102.7 1.6 %collective-permute-start.19 = (bf16[128,1280]{1,0:T(8,128)(2,1)S(1)}, bf16[128,1280]{1,0:T(8,128)(2,1)S(1)}, u32[]{:S(2)}, u32[]{:S(2)}) collective-permute-start(bf16[128,1280]{1,0:T(8,128)(2,1)S(1)} %get-tuple-element.99), channel_id=1, source_target_pairs={{0,4},{1,5},{2,6},{3,7},{4,0},{5,1},{6,2},{7,3},{8,12},{9,13},{10,... | collective-permute-start | bytes 983048 | tf_op jit(solution)/shard_map/ppermute | solution.py:480
  104.3 1.0 shard_map.94.refs_0_.refs_1_
  107.6 1.0 collective-permute-start.20
  109.8 1.8 %shard_map.96 = (f32[128,1536]{1,0:T(8,128)S(1)}, bf16[128,1536]{1,0:T(8,128)(2,1)S(1)}) custom-call(s32[1]{0:T(128)} %bitcast.x_ref, bf16[4,2,2,128,512]{4,3,2,1,0:T(8,128)(2,1)S(1)} %all-to-all-done.weight_ref, bf16[4,512,512]{2,1,0:T(8,128)(2,1)S(1)} %copy-done.5, bf16[4,512,1024]{2,1,0:T(8,128)(2,1)S(1)} %copy-done.3), custom_call_target="tpu_custom_call" | custom-call | flops 1610612736 | bytes 7340032 | tf_op jit(solution)/shard_map/pallas_call | solution.py:287
  111.6 4.0 %collective-permute-done.20.theirs_ref = bf16[128,512]{1,0:T(8,128)(2,1)S(1)} collective-permute-done((bf16[128,512]{1,0:T(8,128)(2,1)S(1)}, bf16[128,512]{1,0:T(8,128)(2,1)S(1)}, u32[]{:S(2)}, u32[]{:S(2)}) %collective-permute-start.20) | collective-permute-done | bytes 131104 | tf_op jit(solution)/shard_map/ppermute | solution.py:480
  115.6 1.1 shard_map.92.refs_2_
  116.7 1.9 %shard_map.93.early_ref = bf16[256,2048]{1,0:T(8,128)(2,1)S(1)} custom-call(s32[1]{0:T(128)} %bitcast.13.first_ref, f32[128,1280]{1,0:T(8,128)S(1)} %get-tuple-element.98.mine_ref, bf16[128,1280]{1,0:T(8,128)(2,1)S(1)} %collective-permute-done.19.theirs_ref, s32[1,1024]{1,0:T(1,128)S(1)} %slice.13.place_ref, bf16[1056,256]{1,0:T(8,128)(2,1)S(1)} %copy-done.9, ...), custom_call_target="tpu_custom_call" | custom-call | flops 536870912 | bytes 2097152 | tf_op jit(solution)/shard_map/pallas_call | solution.py:340
  118.6 1.6 %collective-permute-start.22 = (bf16[128,1536]{1,0:T(8,128)(2,1)S(1)}, bf16[128,1536]{1,0:T(8,128)(2,1)S(1)}, u32[]{:S(2)}, u32[]{:S(2)}) collective-permute-start(bf16[128,1536]{1,0:T(8,128)(2,1)S(1)} %get-tuple-element.118), channel_id=1, source_target_pairs={{0,4},{1,5},{2,6},{3,7},{4,0},{5,1},{6,2},{7,3},{8,12},{9,13},{10,... | collective-permute-start | bytes 1179656 | tf_op jit(solution)/shard_map/ppermute | solution.py:480
  120.7 7.4 %shard_map.98 = (bf16[128,2048]{1,0:T(8,128)(2,1)S(1)}, bf16[128,2048]{1,0:T(8,128)(2,1)S(1)}) custom-call(f32[8]{0:T(128)S(1)} %broadcast_select_fusion.flag_ref, s32[1]{0:T(128)} %bitcast.13.first_ref, f32[128,256]{1,0:T(8,128)S(1)} %copy-done.36, f32[1,128]{1,0:T(1,128)S(1)} %dynamic-slice_bitcast_fusion.skip_ref, ...), custom_call_target="tpu_custom_call" | custom-call | flops 1610612736 | bytes 4194304 | tf_op jit(solution)/shard_map/pallas_call | solution.py:421
  128.1 1.1 collective-permute-done.22.theirs_ref
  129.2 1.5 %shard_map.99.early_ref = bf16[128,2048]{1,0:T(8,128)(2,1)S(1)} custom-call(s32[1]{0:T(128)} %bitcast.13.first_ref, f32[128,1536]{1,0:T(8,128)S(1)} %get-tuple-element.117.mine_ref, bf16[128,1536]{1,0:T(8,128)(2,1)S(1)} %collective-permute-done.22.theirs_ref, s32[1,1536]{1,0:T(1,128)S(1)} %slice.16.place_ref), custom_call_target="tpu_custom_call" | custom-call | flops 805306368 | bytes 2097152 | tf_op jit(solution)/shard_map/pallas_call | solution.py:340
  130.8 1.0 shard_map.100
  131.8 14.4 %all_to_all.10 = bf16[8,128,256]{2,1,0:T(8,128)(2,1)S(1)} all-to-all(bf16[8,128,256]{2,1,0:T(8,128)(2,1)S(1)} %shard_map.100), channel_id=1, replica_groups=mesh['seq'=8,'mp'=4] {'seq'}, dimensions={0} | all-to-all | bytes 1048576 | tf_op jit(solution)/shard_map/all_to_all | solution.py:591
  146.2 0.8 copy.11
  (122 shorter events, 11.6 us)
Async XLA Ops:
  0.0 13.8 %copy-start = (f32[1024]{0:T(1024)S(1)}, f32[1024]{0:T(1024)}, u32[]{:S(2)}) copy-start(f32[1024]{0:T(1024)} %param.14) | copy-start | bytes 12292
  0.0 17.1 %copy-start.20 = (bf16[512,1024]{1,0:T(8,128)(2,1)S(1)}, bf16[512,1024]{1,0:T(8,128)(2,1)}, u32[]{:S(2)}) copy-start(bf16[512,1024]{1,0:T(8,128)(2,1)} %refs_0_.1) | copy-start | bytes 3145732
  1.2 27.7 %collective-permute-start = (bf16[1040,256]{1,0:T(8,128)(2,1)S(1)}, bf16[1040,256]{1,0:T(8,128)(2,1)S(1)}, u32[]{:S(2)}, u32[]{:S(2)}) collective-permute-start(bf16[1040,256]{1,0:T(8,128)(2,1)S(1)} %shard_map.82.refs_0_), channel_id=1, source_target_pairs={{0,16},{1,17},{2,18},{3,19},{4,20},{5,21},{6,22},{7,23},{8,24},{9,... | collective-permute-start | bytes 1597448 | tf_op jit(solution)/shard_map/ppermute | solution.py:480
  5.3 23.9 %collective-permute-start.1 = (bf16[1040,256]{1,0:T(8,128)(2,1)S(1)}, bf16[1040,256]{1,0:T(8,128)(2,1)}, u32[]{:S(2)}, u32[]{:S(2)}) collective-permute-start(bf16[1040,256]{1,0:T(8,128)(2,1)S(1)} %shard_map.82.refs_0_), channel_id=1, source_target_pairs={{0,8},{1,9},{2,10},{3,11},{4,12},{5,13},{6,14},{7,15},{8,0},{9,1},... | collective-permute-start | bytes 1597448 | tf_op jit(solution)/shard_map/ppermute | solution.py:480
  6.9 8.4 %copy-start.28 = (bf16[528,256]{1,0:T(8,128)(2,1)}, bf16[528,256]{1,0:T(8,128)(2,1)S(1)}, u32[]{:S(2)}) copy-start(bf16[528,256]{1,0:T(8,128)(2,1)S(1)} %get-tuple-element.63.after_ref) | copy-start | bytes 811012
  7.0 14.3 %collective-permute-start.3 = (bf16[528,256]{1,0:T(8,128)(2,1)S(1)}, bf16[528,256]{1,0:T(8,128)(2,1)S(1)}, u32[]{:S(2)}, u32[]{:S(2)}) collective-permute-start(bf16[528,256]{1,0:T(8,128)(2,1)S(1)} %get-tuple-element.64.refs_0_), channel_id=1, source_target_pairs={{0,2},{1,3},{2,0},{3,1},{4,6},{5,7},{6,4},{7,5},{8,10},{9,11},{10,... | collective-permute-start | bytes 811016 | tf_op jit(solution)/shard_map/ppermute | solution.py:480
  8.5 7.4 %collective-permute-start.2 = (bf16[528,256]{1,0:T(8,128)(2,1)S(1)}, bf16[528,256]{1,0:T(8,128)(2,1)S(1)}, u32[]{:S(2)}, u32[]{:S(2)}) collective-permute-start(bf16[528,256]{1,0:T(8,128)(2,1)S(1)} %get-tuple-element.63.after_ref), channel_id=1, source_target_pairs={{0,4},{1,5},{2,6},{3,7},{4,0},{5,1},{6,2},{7,3},{8,12},{9,13},{10,... | collective-permute-start | bytes 811016 | tf_op jit(solution)/shard_map/ppermute | solution.py:480
  15.9 13.3 %copy-start.13 = (bf16[528,256]{1,0:T(8,128)(2,1)}, bf16[528,256]{1,0:T(8,128)(2,1)S(1)}, u32[]{:S(2)}) copy-start(bf16[528,256]{1,0:T(8,128)(2,1)S(1)} %collective-permute-done.2.refs_1_) | copy-start | bytes 811012
  15.9 13.3 %collective-permute-start.4 = (bf16[528,256]{1,0:T(8,128)(2,1)S(1)}, bf16[528,256]{1,0:T(8,128)(2,1)S(1)}, u32[]{:S(2)}, u32[]{:S(2)}) collective-permute-start(bf16[528,256]{1,0:T(8,128)(2,1)S(1)} %collective-permute-done.2.refs_1_), channel_id=1, source_target_pairs={{0,2},{1,3},{2,0},{3,1},{4,6},{5,7},{6,4},{7,5},{8,10},{9,11},{10,... | collective-permute-start | bytes 811016 | tf_op jit(solution)/shard_map/ppermute | solution.py:480
  21.3 24.9 %copy-start.16 = (bf16[528,256]{1,0:T(8,128)(2,1)}, bf16[528,256]{1,0:T(8,128)(2,1)S(1)}, u32[]{:S(2)}) copy-start(bf16[528,256]{1,0:T(8,128)(2,1)S(1)} %collective-permute-done.3.refs_2_) | copy-start | bytes 811012
  29.2 17.0 %copy-start.18 = (bf16[528,256]{1,0:T(8,128)(2,1)}, bf16[528,256]{1,0:T(8,128)(2,1)S(1)}, u32[]{:S(2)}) copy-start(bf16[528,256]{1,0:T(8,128)(2,1)S(1)} %collective-permute-done.4.refs_3_) | copy-start | bytes 811012
  30.3 20.4 %collective-permute-start.8 = (bf16[2112,256]{1,0:T(8,128)(2,1)}, bf16[2112,256]{1,0:T(8,128)(2,1)}, u32[]{:S(2)}, u32[]{:S(2)}) collective-permute-start(bf16[2112,256]{1,0:T(8,128)(2,1)} %pad_maximum_fusion.1), channel_id=1, source_target_pairs={{0,1},{1,0},{2,3},{3,2},{4,5},{5,4},{6,7},{7,6},{8,9},{9,8},{10,11... | collective-permute-start | bytes 3244040 | tf_op jit(solution)/shard_map/ppermute | solution.py:480
  31.5 19.3 %copy-start.7 = (bf16[1056,256]{1,0:T(8,128)(2,1)}, bf16[1056,256]{1,0:T(8,128)(2,1)S(1)}, u32[]{:S(2)}) copy-start(bf16[1056,256]{1,0:T(8,128)(2,1)S(1)} %get-tuple-element.73.refs_0_) | copy-start | bytes 1622020
  31.5 14.8 %collective-permute-start.6 = (bf16[1056,256]{1,0:T(8,128)(2,1)S(1)}, bf16[1056,256]{1,0:T(8,128)(2,1)S(1)}, u32[]{:S(2)}, u32[]{:S(2)}) collective-permute-start(bf16[1056,256]{1,0:T(8,128)(2,1)S(1)} %get-tuple-element.72), channel_id=1, source_target_pairs={{0,4},{1,5},{2,6},{3,7},{4,0},{5,1},{6,2},{7,3},{8,12},{9,13},{10,... | collective-permute-start | bytes 1622024 | tf_op jit(solution)/shard_map/ppermute | solution.py:480
  33.1 17.7 %collective-permute-start.7 = (bf16[1056,256]{1,0:T(8,128)(2,1)S(1)}, bf16[1056,256]{1,0:T(8,128)(2,1)}, u32[]{:S(2)}, u32[]{:S(2)}) collective-permute-start(bf16[1056,256]{1,0:T(8,128)(2,1)S(1)} %get-tuple-element.73.refs_0_), channel_id=1, source_target_pairs={{0,2},{1,3},{2,0},{3,1},{4,6},{5,7},{6,4},{7,5},{8,10},{9,11},{10,... | collective-permute-start | bytes 1622024 | tf_op jit(solution)/shard_map/ppermute | solution.py:480
  34.6 16.2 %collective-permute-start.5 = (bf16[1040,256]{1,0:T(8,128)(2,1)}, bf16[1040,256]{1,0:T(8,128)(2,1)}, u32[]{:S(2)}, u32[]{:S(2)}) collective-permute-start(bf16[1040,256]{1,0:T(8,128)(2,1)} %copy-done.22), channel_id=1, source_target_pairs={{0,8},{1,9},{2,10},{3,11},{4,12},{5,13},{6,14},{7,15},{8,0},{9,1},... | collective-permute-start | bytes 1597448 | tf_op jit(solution)/shard_map/ppermute | solution.py:480
  46.2 5.9 %copy-start.10 = (bf16[1056,256]{1,0:T(8,128)(2,1)}, bf16[1056,256]{1,0:T(8,128)(2,1)S(1)}, u32[]{:S(2)}) copy-start(bf16[1056,256]{1,0:T(8,128)(2,1)S(1)} %collective-permute-done.6.refs_1_) | copy-start | bytes 1622020
  46.2 52.7 %all-to-all-start = ((bf16[4,2,2,128,512]{4,3,2,1,0:T(8,128)(2,1)}), bf16[4,2,2,128,512]{4,3,2,1,0:T(8,128)(2,1)S(1)}, u32[]{:S(2)}, u32[]{:S(2)}) async-start(bf16[4,2,2,128,512]{4,3,2,1,0:T(8,128)(2,1)} %copy-done.6), calls=%async_computation | async-start | bytes 4194304 | tf_op jit(solution)/shard_map/all_to_all | solution.py:491
  50.7 6.1 %copy-start.14 = (bf16[528,256]{1,0:T(8,128)(2,1)S(1)}, bf16[528,256]{1,0:T(8,128)(2,1)}, u32[]{:S(2)}) copy-start(bf16[528,256]{1,0:T(8,128)(2,1)} %copy-done.13) | copy-start | bytes 811012
  50.8 6.1 %copy-start.17 = (bf16[528,256]{1,0:T(8,128)(2,1)S(1)}, bf16[528,256]{1,0:T(8,128)(2,1)}, u32[]{:S(2)}) copy-start(bf16[528,256]{1,0:T(8,128)(2,1)} %copy-done.16) | copy-start | bytes 811012
  50.8 6.1 %copy-start.19 = (bf16[528,256]{1,0:T(8,128)(2,1)S(1)}, bf16[528,256]{1,0:T(8,128)(2,1)}, u32[]{:S(2)}) copy-start(bf16[528,256]{1,0:T(8,128)(2,1)} %copy-done.18) | copy-start | bytes 811012
  52.0 20.6 %collective-permute-start.12 = (bf16[3168,256]{1,0:T(8,128)(2,1)S(1)}, bf16[3168,256]{1,0:T(8,128)(2,1)S(1)}, u32[]{:S(2)}, u32[]{:S(2)}) collective-permute-start(bf16[3168,256]{1,0:T(8,128)(2,1)S(1)} %pad_maximum_fusion), channel_id=1, source_target_pairs={{0,1},{1,0},{2,3},{3,2},{4,5},{5,4},{6,7},{7,6},{8,9},{9,8},{10,11... | collective-permute-start | bytes 4866056 | tf_op jit(solution)/shard_map/ppermute | solution.py:480
  52.1 20.5 %collective-permute-start.11 = (bf16[1056,256]{1,0:T(8,128)(2,1)S(1)}, bf16[1056,256]{1,0:T(8,128)(2,1)S(1)}, u32[]{:S(2)}, u32[]{:S(2)}) collective-permute-start(bf16[1056,256]{1,0:T(8,128)(2,1)S(1)} %collective-permute-done.6.refs_1_), channel_id=1, source_target_pairs={{0,2},{1,3},{2,0},{3,1},{4,6},{5,7},{6,4},{7,5},{8,10},{9,11},{10,... | collective-permute-start | bytes 1622024 | tf_op jit(solution)/shard_map/ppermute | solution.py:480
  54.8 27.0 %copy-start.24 = (bf16[528,256]{1,0:T(8,128)(2,1)}, bf16[528,256]{1,0:T(8,128)(2,1)S(1)}, u32[]{:S(2)}) copy-start(bf16[528,256]{1,0:T(8,128)(2,1)S(1)} %get-tuple-element.79.refs_0_) | copy-start | bytes 811012
  54.8 17.8 %collective-permute-start.10 = (bf16[528,256]{1,0:T(8,128)(2,1)S(1)}, bf16[528,256]{1,0:T(8,128)(2,1)S(1)}, u32[]{:S(2)}, u32[]{:S(2)}) collective-permute-start(bf16[528,256]{1,0:T(8,128)(2,1)S(1)} %get-tuple-element.79.refs_0_), channel_id=1, source_target_pairs={{0,2},{1,3},{2,0},{3,1},{4,6},{5,7},{6,4},{7,5},{8,10},{9,11},{10,... | collective-permute-start | bytes 811016 | tf_op jit(solution)/shard_map/ppermute | solution.py:480
  55.4 17.2 %collective-permute-start.9 = (bf16[528,256]{1,0:T(8,128)(2,1)S(1)}, bf16[528,256]{1,0:T(8,128)(2,1)S(1)}, u32[]{:S(2)}, u32[]{:S(2)}) collective-permute-start(bf16[528,256]{1,0:T(8,128)(2,1)S(1)} %get-tuple-element.78), channel_id=1, source_target_pairs={{0,4},{1,5},{2,6},{3,7},{4,0},{5,1},{6,2},{7,3},{8,12},{9,13},{10,... | collective-permute-start | bytes 811016 | tf_op jit(solution)/shard_map/ppermute | solution.py:480
  60.2 22.6 %copy-start.8 = (bf16[1056,256]{1,0:T(8,128)(2,1)S(1)}, bf16[1056,256]{1,0:T(8,128)(2,1)}, u32[]{:S(2)}) copy-start(bf16[1056,256]{1,0:T(8,128)(2,1)} %copy-done.7) | copy-start | bytes 1622020
  60.2 22.6 %copy-start.11 = (bf16[1056,256]{1,0:T(8,128)(2,1)S(1)}, bf16[1056,256]{1,0:T(8,128)(2,1)}, u32[]{:S(2)}) copy-start(bf16[1056,256]{1,0:T(8,128)(2,1)} %copy-done.10) | copy-start | bytes 1622020
  72.6 12.8 %copy-start.26 = (bf16[528,256]{1,0:T(8,128)(2,1)}, bf16[528,256]{1,0:T(8,128)(2,1)S(1)}, u32[]{:S(2)}) copy-start(bf16[528,256]{1,0:T(8,128)(2,1)S(1)} %collective-permute-done.9.refs_0_.refs_1_) | copy-start | bytes 811012
  72.6 9.1 %collective-permute-start.14 = (bf16[1056,256]{1,0:T(8,128)(2,1)S(1)}, bf16[1056,256]{1,0:T(8,128)(2,1)S(1)}, u32[]{:S(2)}, u32[]{:S(2)}) collective-permute-start(bf16[1056,256]{1,0:T(8,128)(2,1)S(1)} %collective-permute-done.11.refs_3_), channel_id=1, source_target_pairs={{0,1},{1,0},{2,3},{3,2},{4,5},{5,4},{6,7},{7,6},{8,9},{9,8},{10,11... | collective-permute-start | bytes 1622024 | tf_op jit(solution)/shard_map/ppermute | solution.py:480
  72.7 2.5 %collective-permute-start.15 = (bf16[528,256]{1,0:T(8,128)(2,1)S(1)}, bf16[528,256]{1,0:T(8,128)(2,1)S(1)}, u32[]{:S(2)}, u32[]{:S(2)}) collective-permute-start(bf16[528,256]{1,0:T(8,128)(2,1)S(1)} %get-tuple-element.79.refs_0_), channel_id=1, source_target_pairs={{0,1},{1,0},{2,3},{3,2},{4,5},{5,4},{6,7},{7,6},{8,9},{9,8},{10,11... | collective-permute-start | bytes 811016 | tf_op jit(solution)/shard_map/ppermute | solution.py:480
  73.2 8.5 %collective-permute-start.13 = (bf16[528,256]{1,0:T(8,128)(2,1)S(1)}, bf16[528,256]{1,0:T(8,128)(2,1)S(1)}, u32[]{:S(2)}, u32[]{:S(2)}) collective-permute-start(bf16[528,256]{1,0:T(8,128)(2,1)S(1)} %collective-permute-done.9.refs_0_.refs_1_), channel_id=1, source_target_pairs={{0,2},{1,3},{2,0},{3,1},{4,6},{5,7},{6,4},{7,5},{8,10},{9,11},{10,... | collective-permute-start | bytes 811016 | tf_op jit(solution)/shard_map/ppermute | solution.py:480
  74.7 7.0 %collective-permute-start.16 = (bf16[528,256]{1,0:T(8,128)(2,1)S(1)}, bf16[528,256]{1,0:T(8,128)(2,1)S(1)}, u32[]{:S(2)}, u32[]{:S(2)}) collective-permute-start(bf16[528,256]{1,0:T(8,128)(2,1)S(1)} %collective-permute-done.10.refs_1_), channel_id=1, source_target_pairs={{0,1},{1,0},{2,3},{3,2},{4,5},{5,4},{6,7},{7,6},{8,9},{9,8},{10,11... | collective-permute-start | bytes 811016 | tf_op jit(solution)/shard_map/ppermute | solution.py:480
  74.7 7.0 %collective-permute-start.17 = (bf16[528,256]{1,0:T(8,128)(2,1)S(1)}, bf16[528,256]{1,0:T(8,128)(2,1)S(1)}, u32[]{:S(2)}, u32[]{:S(2)}) collective-permute-start(bf16[528,256]{1,0:T(8,128)(2,1)S(1)} %collective-permute-done.9.refs_0_.refs_1_), channel_id=1, source_target_pairs={{0,1},{1,0},{2,3},{3,2},{4,5},{5,4},{6,7},{7,6},{8,9},{9,8},{10,11... | collective-permute-start | bytes 811016 | tf_op jit(solution)/shard_map/ppermute | solution.py:480
  81.7 3.8 %copy-start.30 = (bf16[528,256]{1,0:T(8,128)(2,1)}, bf16[528,256]{1,0:T(8,128)(2,1)S(1)}, u32[]{:S(2)}) copy-start(bf16[528,256]{1,0:T(8,128)(2,1)S(1)} %collective-permute-done.13.refs_1_) | copy-start | bytes 811012
  81.7 3.8 %copy-start.32 = (bf16[528,256]{1,0:T(8,128)(2,1)}, bf16[528,256]{1,0:T(8,128)(2,1)S(1)}, u32[]{:S(2)}) copy-start(bf16[528,256]{1,0:T(8,128)(2,1)S(1)} %collective-permute-done.17.refs_2_) | copy-start | bytes 811012
  81.7 5.7 %collective-permute-start.18 = (bf16[528,256]{1,0:T(8,128)(2,1)S(1)}, bf16[528,256]{1,0:T(8,128)(2,1)S(1)}, u32[]{:S(2)}, u32[]{:S(2)}) collective-permute-start(bf16[528,256]{1,0:T(8,128)(2,1)S(1)} %collective-permute-done.13.refs_1_), channel_id=1, source_target_pairs={{0,1},{1,0},{2,3},{3,2},{4,5},{5,4},{6,7},{7,6},{8,9},{9,8},{10,11... | collective-permute-start | bytes 811016 | tf_op jit(solution)/shard_map/ppermute | solution.py:480
  101.1 3.1 %copy-start.35 = (bf16[528,256]{1,0:T(8,128)(2,1)S(1)}, bf16[528,256]{1,0:T(8,128)(2,1)}, u32[]{:S(2)}) copy-start(bf16[528,256]{1,0:T(8,128)(2,1)} %copy-done.34) | copy-start | bytes 811012
  102.7 14.0 %collective-permute-start.19 = (bf16[128,1280]{1,0:T(8,128)(2,1)S(1)}, bf16[128,1280]{1,0:T(8,128)(2,1)S(1)}, u32[]{:S(2)}, u32[]{:S(2)}) collective-permute-start(bf16[128,1280]{1,0:T(8,128)(2,1)S(1)} %get-tuple-element.99), channel_id=1, source_target_pairs={{0,4},{1,5},{2,6},{3,7},{4,0},{5,1},{6,2},{7,3},{8,12},{9,13},{10,... | collective-permute-start | bytes 983048 | tf_op jit(solution)/shard_map/ppermute | solution.py:480
  105.7 12.9 %collective-permute-start.21 = (bf16[128,256]{1,0:T(8,128)(2,1)S(1)}, bf16[128,256]{1,0:T(8,128)(2,1)S(1)}, u32[]{:S(2)}, u32[]{:S(2)}) collective-permute-start(bf16[128,256]{1,0:T(8,128)(2,1)S(1)} %get-tuple-element.106), channel_id=1, source_target_pairs={{0,4},{1,5},{2,6},{3,7},{4,0},{5,1},{6,2},{7,3},{8,12},{9,13},{10,... | collective-permute-start | bytes 196616 | tf_op jit(solution)/shard_map/ppermute | solution.py:480
  107.6 8.0 %collective-permute-start.20 = (bf16[128,512]{1,0:T(8,128)(2,1)S(1)}, bf16[128,512]{1,0:T(8,128)(2,1)S(1)}, u32[]{:S(2)}, u32[]{:S(2)}) collective-permute-start(bf16[128,512]{1,0:T(8,128)(2,1)S(1)} %get-tuple-element.103), channel_id=1, source_target_pairs={{0,4},{1,5},{2,6},{3,7},{4,0},{5,1},{6,2},{7,3},{8,12},{9,13},{10,... | collective-permute-start | bytes 393224 | tf_op jit(solution)/shard_map/ppermute | solution.py:480
  109.8 5.9 %copy-start.15 = (bf16[528,256]{1,0:T(8,128)(2,1)S(1)}, bf16[528,256]{1,0:T(8,128)(2,1)}, u32[]{:S(2)}) copy-start(bf16[528,256]{1,0:T(8,128)(2,1)} %copy-done.13) | copy-start | bytes 811012
  111.6 5.1 %copy-start.9 = (bf16[1056,256]{1,0:T(8,128)(2,1)S(1)}, bf16[1056,256]{1,0:T(8,128)(2,1)}, u32[]{:S(2)}) copy-start(bf16[1056,256]{1,0:T(8,128)(2,1)} %copy-done.7) | copy-start | bytes 1622020
  111.6 5.1 %copy-start.12 = (bf16[1056,256]{1,0:T(8,128)(2,1)S(1)}, bf16[1056,256]{1,0:T(8,128)(2,1)}, u32[]{:S(2)}) copy-start(bf16[1056,256]{1,0:T(8,128)(2,1)} %copy-done.10) | copy-start | bytes 1622020
  116.7 4.0 %copy-start.25 = (bf16[528,256]{1,0:T(8,128)(2,1)S(1)}, bf16[528,256]{1,0:T(8,128)(2,1)}, u32[]{:S(2)}) copy-start(bf16[528,256]{1,0:T(8,128)(2,1)} %copy-done.24) | copy-start | bytes 811012
  116.7 4.0 %copy-start.36 = (f32[128,256]{1,0:T(8,128)S(1)}, f32[128,256]{1,0:T(8,128)}, u32[]{:S(2)}) copy-start(f32[128,256]{1,0:T(8,128)} %dynamic-slice_convert_fusion.taps_ref) | copy-start | bytes 393220
  118.6 10.6 %collective-permute-start.22 = (bf16[128,1536]{1,0:T(8,128)(2,1)S(1)}, bf16[128,1536]{1,0:T(8,128)(2,1)S(1)}, u32[]{:S(2)}, u32[]{:S(2)}) collective-permute-start(bf16[128,1536]{1,0:T(8,128)(2,1)S(1)} %get-tuple-element.118), channel_id=1, source_target_pairs={{0,4},{1,5},{2,6},{3,7},{4,0},{5,1},{6,2},{7,3},{8,12},{9,13},{10,... | collective-permute-start | bytes 1179656 | tf_op jit(solution)/shard_map/ppermute | solution.py:480
  120.2 10.6 %collective-permute-start.23 = (bf16[128,512]{1,0:T(8,128)(2,1)S(1)}, bf16[128,512]{1,0:T(8,128)(2,1)S(1)}, u32[]{:S(2)}, u32[]{:S(2)}) collective-permute-start(bf16[128,512]{1,0:T(8,128)(2,1)S(1)} %get-tuple-element.120), channel_id=1, source_target_pairs={{0,4},{1,5},{2,6},{3,7},{4,0},{5,1},{6,2},{7,3},{8,12},{9,13},{10,... | collective-permute-start | bytes 393224 | tf_op jit(solution)/shard_map/ppermute | solution.py:480
  (14 other events, 26.6 us)

commit v3 on v2

--- a/solution.py
+++ b/solution.py
@@ -124,8 +124,10 @@
     )
 
 
-def extend_kernel(token_ref, out_ref):
+def halve_kernel(x_ref, token_ref, keep_ref, give_ref):
     features, count = token_ref.shape
+    half = features // 2
+    x = x_ref[0]
     widened = token_ref[...].astype(jnp.float32)
     rest = jnp.sum(widened * widened, axis=0, keepdims=True)
     terms = []
@@ -137,51 +139,25 @@
     extra = jnp.zeros(row.shape, jnp.float32)
     for i, term in enumerate(terms):
         extra = jnp.where(row == i, term, extra)
-    out_ref[0:features, :] = token_ref[...]
-    out_ref[features : features + EXTRA, :] = extra.astype(jnp.bfloat16)
-
-
-def extend(tokens):
+    extra = extra.astype(jnp.bfloat16)
+    for out_ref, which in ((keep_ref, x), (give_ref, 1 - x)):
+        out_ref[0:half, :] = token_ref[pl.ds(pl.multiple_of(which * half, half), half), :]
+        out_ref[half : half + EXTRA, :] = extra
+
+
+def halve(x, tokens):
     features, count = tokens.shape
+    out = jax.ShapeDtypeStruct((features // 2 + EXTRA, count), tokens.dtype)
     return pl.pallas_call(
-        extend_kernel,
-        out_shape=jax.ShapeDtypeStruct((features + EXTRA, count), tokens.dtype),
-        in_specs=[VMEM],
-        out_specs=VMEM,
+        halve_kernel,
+        out_shape=[out, out],
+        in_specs=[SMEM, VMEM],
+        out_specs=[VMEM, VMEM],
         compiler_params=PARAMS,
         cost_estimate=pl.CostEstimate(
             flops=2 * features * count, bytes_accessed=4 * features * count, transcendentals=0
         ),
-    )(tokens)
-
-
-def halve_kernel(x_ref, *refs):
-    arrays, (keep_ref, give_ref) = refs[:-2], refs[-2:]
-    features = arrays[0].shape[0] - EXTRA
-    half = features // 2
-    x = x_ref[0]
-    for number, ref in enumerate(arrays):
-        first = number * (half + EXTRA)
-        for out_ref, which in ((keep_ref, x), (give_ref, 1 - x)):
-            rows = pl.ds(pl.multiple_of(which * half, half), half)
-            out_ref[first : first + half, :] = ref[rows, :]
-            out_ref[first + half : first + half + EXTRA, :] = ref[features : features + EXTRA, :]
-
-
-def halve(x, arrays):
-    tall, count = arrays[0].shape
-    half = (tall - EXTRA) // 2
-    out = jax.ShapeDtypeStruct(((half + EXTRA) * len(arrays), count), arrays[0].dtype)
-    return pl.pallas_call(
-        halve_kernel,
-        out_shape=[out, out],
-        in_specs=[SMEM] + [VMEM] * len(arrays),
-        out_specs=[VMEM, VMEM],
-        compiler_params=PARAMS,
-        cost_estimate=pl.CostEstimate(
-            flops=0, bytes_accessed=4 * tall * count * len(arrays), transcendentals=0
-        ),
-    )(x, *arrays)
+    )(x, tokens)
 
 
 def pack_kernel(after_ref, *refs):
@@ -253,45 +229,51 @@
     )(picks, gains, *arrays)
 
 
-def project_kernel(number, starts, row_count, x_ref, weight_ref, *refs):
-    mine_ref, other_ref = refs[-2:]
+def project_kernel(number, row_count, x_ref, weight_ref, *refs):
+    mine_ref, other_ref, mine, other = refs[-4:]
     x = x_ref[0]
+    part = pl.program_id(0)
+
+    @pl.when(part == 0)
+    def _():
+        mine[...] = jnp.zeros(mine.shape, jnp.float32)
+        other[...] = jnp.zeros(mine.shape, jnp.float32)
+
     first = 0
-    for ref, far in zip(refs[:-2], starts):
-        parts, _, count = ref.shape
-        for begin in range(0, count, 2 * row_count):
-            columns = slice(begin, min(begin + 2 * row_count, count))
-            wide = columns.stop - begin
-            mine = jnp.zeros((mine_ref.shape[0], wide), jnp.float32)
-            other = jnp.zeros((mine_ref.shape[0], wide), jnp.float32)
-            for part in range(parts):
-                block = ref[part, :, columns]
-                for which, is_mine in ((x, True), (1 - x, False)):
-                    result = jnp.dot(
-                        weight_ref[part, number, which], block, preferred_element_type=jnp.float32
-                    )
-                    mine, other = (mine + result, other) if is_mine else (mine, other + result)
-            mine_ref[:, first + begin : first + begin + wide] = mine
-            other = other.astype(jnp.bfloat16)
-            if wide > row_count:
-                other = jnp.concatenate([other[:, row_count:], other[:, :row_count]], axis=1)
-            other_ref[:, far + begin : far + begin + wide] = other
-        first += count
-
-
-def project(x, weights, number, normed, row_count, starts=None):
-    line, _, _, width, height = weights.shape
-    counts = [some.shape[2] for some in normed]
-    starts = starts or [sum(counts[:i]) for i in range(len(counts))]
-    out = (width, sum(counts))
+    for ref in refs[:-4]:
+        columns = slice(first, first + ref.shape[2])
+        first = columns.stop
+        block = ref[0]
+        for which, total in ((x, mine), (1 - x, other)):
+            total[:, columns] += jnp.dot(
+                weight_ref[0, number, which], block, preferred_element_type=jnp.float32
+            )
+
+    @pl.when(part == pl.num_programs(0) - 1)
+    def _():
+        mine_ref[...] = mine[...]
+        for begin in range(0, mine.shape[1], row_count):
+            swapped = begin + row_count if begin // row_count % 2 == 0 else begin - row_count
+            other_ref[:, begin : begin + row_count] = other[
+                :, swapped : swapped + row_count
+            ].astype(jnp.bfloat16)
+
+
+def project(x, weights, number, normed, row_count):
+    line, kinds, _, width, height = weights.shape
+    out = (width, sum(some.shape[2] for some in normed))
+    whole = pl.BlockSpec(out, lambda part: (0, 0))
     return pl.pallas_call(
-        functools.partial(project_kernel, number, starts, row_count),
+        functools.partial(project_kernel, number, row_count),
+        grid=(line,),
         out_shape=[
             jax.ShapeDtypeStruct(out, jnp.float32),
             jax.ShapeDtypeStruct(out, jnp.bfloat16),
         ],
-        in_specs=[SMEM] + [VMEM] * (1 + len(normed)),
-        out_specs=[VMEM] * 2,
+        in_specs=[SMEM, pl.BlockSpec((1, kinds, 2, width, height), lambda part: (part, 0, 0, 0, 0))]
+        + [pl.BlockSpec((1, *some.shape[1:]), lambda part: (part, 0, 0)) for some in normed],
+        out_specs=[whole, whole],
+        scratch_shapes=[pltpu.VMEM(out, jnp.float32)] * 2,
         compiler_params=PARAMS,
         cost_estimate=pl.CostEstimate(
             flops=4 * width * height * out[1] * line,
@@ -351,17 +333,14 @@
 
 def band_kernel(
     taps_blocks, tall, flag_ref, first_ref, taps_ref, skip_ref, early_ref, mine_ref, theirs_ref,
-    last_mine_ref, last_theirs_ref, place_ref, *refs
+    place_ref, *refs
 ):
     shifted = refs[-taps_blocks - 1 :]
     out_ref, packed_ref, whole, band = refs[-taps_blocks - 5 : -taps_blocks - 1]
     chan = taps_ref.shape[0]
     total = whole.shape[1]
     pieces = total // LANES
-    cut = mine_ref.shape[1] - last_mine_ref.shape[1]
-    mine = jnp.concatenate([mine_ref[:, cut:], last_mine_ref[...]], axis=1)
-    theirs = jnp.concatenate([last_theirs_ref[...], theirs_ref[:, cut:]], axis=1)
-    summed = (mine + theirs.astype(jnp.float32)).astype(jnp.bfloat16)
+    summed = (mine_ref[...] + theirs_ref[...].astype(jnp.float32)).astype(jnp.bfloat16)
     summed = with_tokens(first_ref[0], tall, summed, refs[: -taps_blocks - 5])
     moved = at_places(summed, place_ref[...], total) + early_ref[...].astype(jnp.float32)
     whole[...] = moved[0:chan]
@@ -412,7 +391,7 @@
         out_ref[:, lanes] = (band[rows, :] + skip * whole[:, lanes]).astype(jnp.bfloat16)
 
 
-def band_of(flags, first, taps, skip, early, late, last, places, tall, tokens):
+def band_of(flags, first, taps, skip, early, mine, theirs, places, tall, tokens):
     chan, tap_count = taps.shape
     total = early.shape[1]
     taps_blocks = tap_count // LANES
@@ -421,7 +400,7 @@
     return pl.pallas_call(
         functools.partial(band_kernel, taps_blocks, tall),
         out_shape=[out, out],
-        in_specs=[SMEM, SMEM] + [VMEM] * (8 + len(tokens)),
+        in_specs=[SMEM, SMEM] + [VMEM] * (6 + len(tokens)),
         out_specs=[VMEM, VMEM],
         scratch_shapes=[pltpu.VMEM((chan, total), jnp.float32)]
         + [pltpu.VMEM(tower, jnp.float32)] * (taps_blocks + 2),
@@ -429,7 +408,7 @@
         cost_estimate=pl.CostEstimate(
             flops=3 * chan * total * total, bytes_accessed=16 * chan * total, transcendentals=0
         ),
-    )(flags, first, taps, skip, early, *late, *last, places, *tokens)
+    )(flags, first, taps, skip, early, mine, theirs, places, *tokens)
 
 
 def mix_kernel(z_ref, packed_ref, early_ref, mine_ref, theirs_ref, place_ref, out_ref):
@@ -438,8 +417,10 @@
     mixed = packed_ref[...].astype(jnp.float32) + gate * z_ref[...].astype(jnp.float32)
     mixed = mixed.astype(jnp.bfloat16)
     wide = out_ref.shape[2]
-    for owner in range(out_ref.shape[0]):
-        out_ref[owner] = mixed[:, owner * wide : (owner + 1) * wide]
+    pairs = out_ref.shape[0] // 2
+    for place in range(2 * pairs):
+        owner = place % pairs * 2 + place // pairs
+        out_ref[place] = mixed[:, owner * wide : (owner + 1) * wide]
 
 
 def mix(z, packed, early, mine, theirs, places, shards):
@@ -512,8 +493,8 @@
     tall = half + EXTRA
     wide = 2 * row_count
 
-    def projected(number, some, starts=None):
-        return project(which, weights, number, some, row_count, starts)
+    def projected(number, some):
+        return project(which, weights, number, some, row_count)
 
     def scaled(arrays):
         return scale(picks, gains, half, arrays)
@@ -525,71 +506,77 @@
     def tie(*arrays):
         return lax.optimization_barrier(arrays)
 
-    extended = extend(tokens)
-    kept0, give0 = halve(which, [extended])
-    by_far, by_near = to_pair(extended, far_pair), to_pair(extended, near_pair)
+    by_far, by_near = to_pair(tokens, far_pair), to_pair(tokens, near_pair)
+    kept0, give0 = halve(which, tokens)
     got0, kept0_far = across(give0), to_owner(kept0, far_owner)
     got0_far = to_owner(got0, far_owner)
     packed_weights = pack_weights(give0, [w_value, w_gate], line)
+    packed_weights, by_near = tie(packed_weights, by_near)
+    kept1, give1 = halve(which, by_near)
     small = picks, gains, taps, skip, flags, row_first, places, which
     by_both = to_pair(by_far, near_pair)
-    by_far, by_near, got0, kept0_far, got0_far, small, packed_weights = tie(
-        by_far, by_near, got0, kept0_far, got0_far, small, packed_weights
+    by_far, got0, kept0_far, got0_far, kept1, give1, small, packed_weights = tie(
+        by_far, got0, kept0_far, got0_far, kept1, give1, small, packed_weights
     )
     picks, gains, taps, skip, flags, row_first, places, which = small
 
-    kept1, give1 = halve(which, [by_near, by_far])
+    kept2, give2 = halve(which, by_far)
     got1, kept1_far = across(give1), to_owner(kept1, far_owner)
-    packed_weights, _ = tie(packed_weights, got1)
+    got2, kept2_far = across(give2), to_owner(kept2, far_owner)
+    got1_far = to_owner(got1, far_owner)
     weights = along_line(packed_weights)
     all0 = to_near([kept0, got0, kept0_far, got0_far])
-    by_both, got1, kept1_far, all0 = tie(by_both, got1, kept1_far, all0)
-
-    kept2, give2 = halve(which, [by_both])
-    got2, kept2_far = across(give2), to_owner(kept2, far_owner)
-    got1_far = to_owner(got1, far_owner)
-    some1 = to_near([kept1, got1, kept1_far])
+    by_both, got1, kept1_far, got1_far, got2, kept2_far, all0 = tie(
+        by_both, got1, kept1_far, got1_far, got2, kept2_far, all0
+    )
+
+    kept3, give3 = halve(which, by_both)
+    got3, kept3_far = across(give3), to_owner(kept3, far_owner)
+    got2_far = to_owner(got2, far_owner)
+    all1 = to_near([kept1, got1, kept1_far, got1_far])
     normed0 = scaled([kept0, got0, kept0_far, got0_far, all0])
-    got2, kept2_far, got1_far, some1, normed0 = tie(got2, kept2_far, got1_far, some1, normed0)
-
-    got2_far = to_owner(got2, far_owner)
-    rest1 = to_near([got1_far])
-    near_kept2, near_kept2_far, near_got2 = [to_near([some]) for some in (kept2, kept2_far, got2)]
-    got2_far, rest1, near_kept2, near_kept2_far, near_got2 = tie(
-        got2_far, rest1, near_kept2, near_kept2_far, near_got2
-    )
-
-    near_got2_far = to_near([got2_far])
-    normed1 = scaled([kept1, got1, kept1_far, got1_far, some1, rest1])
-    normed2 = scaled([kept2, kept2_far, near_kept2, near_kept2_far])
-    near_got2_far, normed1, normed2, weights = tie(near_got2_far, normed1, normed2, weights)
-
-    near0, far0 = projected(0, [normed0])
+    got3, kept3_far, got2_far, all1, normed0 = tie(got3, kept3_far, got2_far, all1, normed0)
+
+    got3_far = to_owner(got3, far_owner)
+    all2 = to_near([kept2, got2, kept2_far, got2_far])
+    near_kept3, near_kept3_far, near_got3 = [to_near([some]) for some in (kept3, kept3_far, got3)]
+    normed1 = scaled([kept1, got1, kept1_far, got1_far, all1])
+    got3_far, all2, near_kept3, near_kept3_far, near_got3, normed1 = tie(
+        got3_far, all2, near_kept3, near_kept3_far, near_got3, normed1
+    )
+
+    near_got3_far = to_near([got3_far])
+    normed2 = scaled([kept2, got2, kept2_far, got2_far, all2])
+    near_got3_far, normed2 = tie(near_got3_far, normed2)
+    normed3 = scaled(
+        [kept3, got3, kept3_far, got3_far, near_kept3, near_got3, near_kept3_far, near_got3_far]
+    )
+    normed3, weights = tie(normed3, weights)
+
+    cut = 2 * wide
+    value0, far0 = projected(0, [normed0, normed1])
     theirs0 = across(far0)
-    near1, far1 = projected(0, [normed1, normed2])
-    theirs1 = across(far1)
-    normed3 = scaled([got2, got2_far, near_got2, near_got2_far])
-    near3, far3 = projected(0, [normed3])
-    theirs3 = across(far3)
-    normed0, normed1, near3 = tie(normed0, normed1, near3)
-    gate_near0, gate_far0 = projected(1, [normed0, normed1])
-    gate_near3, gate_far3 = projected(1, [normed2, normed3], [row_count, 0])
+    value0, normed2 = tie(value0, normed2)
+    value2, far2 = projected(0, [normed2, normed3])
+    theirs2 = across(far2)
+    normed0, value2 = tie(normed0, value2)
+    gate0, gate_far0 = projected(1, [normed0, normed1])
+    gate2, gate_far2 = projected(1, [normed2, normed3])
     early = place(
-        row_first, total_rows, near0, theirs0, places[:, :wide], tall, [kept0, got0]
-    )
-    early = place(
-        row_first, total_rows, near1, theirs1, places[:, wide:-wide], tall, [kept1, got1], [early]
-    )
-    early, theirs3, gate_far0, gate_far3 = tie(early, theirs3, gate_far0, gate_far3)
-    gate_theirs0, gate_theirs3 = across(gate_far0), across(gate_far3)
+        row_first, total_rows, value0, theirs0, places[:, :cut], tall, [kept0, got0, kept1, got1]
+    )
+    early, theirs2, gate_far0, gate_far2 = tie(early, theirs2, gate_far0, gate_far2)
+    gate_theirs0, gate_theirs2 = across(gate_far0), across(gate_far2)
     banded, packed = band_of(
-        flags, row_first, taps, skip, early, (near1, theirs1), (near3, theirs3),
-        places[:, -wide:], tall, [kept2, got2],
-    )
-    early = place(row_first, total_rows, gate_near0, gate_theirs0, places[:, :-wide])
-    mixed = mix(banded, packed, early, gate_near3, gate_theirs3, places[:, -wide:], shards)
-    mixed = lax.all_to_all(mixed, "seq", split_axis=0, concat_axis=0, tiled=True)
-    mixed = mixed.reshape(line, 2, width, row_count).transpose(1, 0, 2, 3)
+        flags, row_first, taps, skip, early, value2, theirs2, places[:, cut:], tall,
+        [kept2, got2, kept3, got3],
+    )
+    early = place(row_first, total_rows, gate0, gate_theirs0, places[:, :cut])
+    mixed = mix(banded, packed, early, gate2, gate_theirs2, places[:, cut:], shards)
+    owners = [[number(zz, xx, mm) for xx in range(2) for zz in range(line)] for mm in range(groups)]
+    mixed = lax.all_to_all(
+        mixed, AXES, split_axis=0, concat_axis=0, tiled=True, axis_index_groups=owners
+    )
     return mixed.reshape(features, row_count)
 
 

time: 148 us -> 142 us (0.959)
  waiting for transfers between devices: 53.4 us -> 37.1 us
  Pallas kernels: 27.5 us -> 31.7 us
  starting transfers between devices: 30 us -> 32.2 us
  local copies, waits for them, and re-layouts: 15.5 us -> 17.7 us
    ppermute x24 -> x26, waiting for transfers between devices: 42.6 us -> 30.9 us  [send(): return lax.ppermute(array, AXES, pairs)]
    all_to_all x1, waiting for transfers between devices: 10.8 us -> 6.29 us  [along_line(): lax.all_to_all(array, AXES, split_axis=0, concat_axis=0, tiled=True, axis...]
    pallas_call x9 -> x8, Pallas kernels: 7.54 us -> 11.3 us  [the longest x4 7.99 us: project(): pl.pallas_call(functools.partial(project_kernel, number, row_count), grid...]
    unnamed x75 -> x48, local copies, waits for them, and re-layouts: 12 us -> 15 us
    ppermute x24 -> x26, starting transfers between devices: 25.5 us -> 27.8 us  [send(): return lax.ppermute(array, AXES, pairs)]
    pallas_call x3 -> x2, Pallas kernels: 4.41 us -> 2.84 us  [place(): pl.pallas_call(functools.partial(place_kernel, tall, len(tokens)), out_sh...]
    concatenate x2 -> x3, other arithmetic: 2.3 us -> 3.35 us  [to_near(): stacked = jnp.concatenate(arrays, axis=0) if len(arrays) > 1 else arrays[0]]
  transfers between devices with their start and end apart: 25 -> 27, of which waited for: 9 -> 12; matrix products, arithmetic and copies ran while one was open for 5% -> 6% of each run, Pallas kernels for 17% -> 20%
where the time goes in v3:
time: 142 us
  waiting for transfers between devices  37.1 us (26%)
  starting transfers between devices  32.2 us (23%)
  Pallas kernels  31.7 us (22%)
  local copies, waits for them, and re-layouts  17.7 us (12%)
  blocking collectives  15.7 us (11%)
  other arithmetic  6.61 us (5%)
    ppermute x26, waiting for transfers between devices, send(): return lax.ppermute(array, AXES, pairs)  30.9 us
    ppermute x26, starting transfers between devices, send(): return lax.ppermute(array, AXES, pairs)  27.8 us
    all_to_all x1, blocking collectives, on_device_line(): lax.all_to_all(mixed, AXES, split_axis=0, concat_axis=0, tiled=True, axis...  15.7 us
    unnamed x48, local copies, waits for them, and re-layouts  15 us
    pallas_call x1, Pallas kernels, band_of(): pl.pallas_call(functools.partial(band_kernel, taps_blocks, tall), out_sha...  8.68 us
    pallas_call x4, Pallas kernels, project(): pl.pallas_call(functools.partial(project_kernel, number, row_count), grid...  7.99 us
    pallas_call x4, Pallas kernels, scale(): pl.pallas_call(functools.partial(scale_kernel, height), out_shape=jax.Sha...  6.71 us
    all_to_all x1, waiting for transfers between devices, along_line(): lax.all_to_all(array, AXES, split_axis=0, concat_axis=0, tiled=True, axis...  6.29 us
  transfers between devices with their start and end apart: 27, of which 12 were waited for; matrix products, arithmetic and copies ran while one was open for 6% of the time, Pallas kernels for 20%

profile of v3, /device:TPU:0, one launch (start us, length us, event | category | flops | bytes accessed | tf_op | source)
XLA Modules:
  0.0 141.5 jit_solution(6509904419162717516)
XLA Ops:
  0.0 4.0 %collective-permute-start = (bf16[1024,256]{1,0:T(8,128)(2,1)}, bf16[1024,256]{1,0:T(8,128)(2,1)}, u32[]{:S(2)}, u32[]{:S(2)}) collective-permute-start(bf16[1024,256]{1,0:T(8,128)(2,1)} %token_ref.1), channel_id=1, source_target_pairs={{0,16},{1,17},{2,18},{3,19},{4,20},{5,21},{6,22},{7,23},{8,24},{9,... | collective-permute-start | bytes 1572872 | tf_op jit(solution)/shard_map/ppermute | solution.py:461
  4.0 1.6 %collective-permute-start.4 = (bf16[1024,256]{1,0:T(8,128)(2,1)}, bf16[1024,256]{1,0:T(8,128)(2,1)S(1)}, u32[]{:S(2)}, u32[]{:S(2)}) collective-permute-start(bf16[1024,256]{1,0:T(8,128)(2,1)} %token_ref.1), channel_id=1, source_target_pairs={{0,8},{1,9},{2,10},{3,11},{4,12},{5,13},{6,14},{7,15},{8,0},{9,1},... | collective-permute-start | bytes 1572872 | tf_op jit(solution)/shard_map/ppermute | solution.py:461
  6.8 1.6 %collective-permute-start.1 = (bf16[528,256]{1,0:T(8,128)(2,1)S(1)}, bf16[528,256]{1,0:T(8,128)(2,1)S(1)}, u32[]{:S(2)}, u32[]{:S(2)}) collective-permute-start(bf16[528,256]{1,0:T(8,128)(2,1)S(1)} %get-tuple-element.70.after_ref), channel_id=1, source_target_pairs={{0,4},{1,5},{2,6},{3,7},{4,0},{5,1},{6,2},{7,3},{8,12},{9,13},{10,... | collective-permute-start | bytes 811016 | tf_op jit(solution)/shard_map/ppermute | solution.py:461
  8.3 1.5 %collective-permute-start.2 = (bf16[528,256]{1,0:T(8,128)(2,1)S(1)}, bf16[528,256]{1,0:T(8,128)(2,1)S(1)}, u32[]{:S(2)}, u32[]{:S(2)}) collective-permute-start(bf16[528,256]{1,0:T(8,128)(2,1)S(1)} %get-tuple-element.71.refs_0_), channel_id=1, source_target_pairs={{0,2},{1,3},{2,0},{3,1},{4,6},{5,7},{6,4},{7,5},{8,10},{9,11},{10,... | collective-permute-start | bytes 811016 | tf_op jit(solution)/shard_map/ppermute | solution.py:461
  13.7 1.5 %dynamic-slice_convert_fusion.taps_ref = f32[128,256]{1,0:T(8,128)} fusion(bf16[1024,256]{1,0:T(8,128)(2,1)} %param.13, s32[]{:T(128)S(6)} %select_n.50), kind=kLoop, calls=%fused_computation.5 | loop fusion | flops 32768 | bytes 196612 | tf_op jit(solution)/shard_map/convert_element_type | solution.py:489
  16.7 1.2 copy-done.15
  17.9 1.2 copy-done.16
  19.8 1.3 copy-done.10
  21.1 6.6 %collective-permute-done.4.token_ref = bf16[1024,256]{1,0:T(8,128)(2,1)S(1)} collective-permute-done((bf16[1024,256]{1,0:T(8,128)(2,1)}, bf16[1024,256]{1,0:T(8,128)(2,1)S(1)}, u32[]{:S(2)}, u32[]{:S(2)}) %collective-permute-start.4) | collective-permute-done | bytes 524320 | tf_op jit(solution)/shard_map/ppermute | solution.py:461
  28.9 1.5 %collective-permute-start.6 = (bf16[528,256]{1,0:T(8,128)(2,1)S(1)}, bf16[528,256]{1,0:T(8,128)(2,1)S(1)}, u32[]{:S(2)}, u32[]{:S(2)}) collective-permute-start(bf16[528,256]{1,0:T(8,128)(2,1)S(1)} %get-tuple-element.83), channel_id=1, source_target_pairs={{0,4},{1,5},{2,6},{3,7},{4,0},{5,1},{6,2},{7,3},{8,12},{9,13},{10,... | collective-permute-start | bytes 811016 | tf_op jit(solution)/shard_map/ppermute | solution.py:461
  30.4 1.5 %collective-permute-start.7 = (bf16[528,256]{1,0:T(8,128)(2,1)S(1)}, bf16[528,256]{1,0:T(8,128)(2,1)S(1)}, u32[]{:S(2)}, u32[]{:S(2)}) collective-permute-start(bf16[528,256]{1,0:T(8,128)(2,1)S(1)} %get-tuple-element.84.refs_0_.refs_2_), channel_id=1, source_target_pairs={{0,2},{1,3},{2,0},{3,1},{4,6},{5,7},{6,4},{7,5},{8,10},{9,11},{10,... | collective-permute-start | bytes 811016 | tf_op jit(solution)/shard_map/ppermute | solution.py:461
  32.0 1.4 %collective-permute-start.5 = (bf16[1024,256]{1,0:T(8,128)(2,1)}, bf16[1024,256]{1,0:T(8,128)(2,1)}, u32[]{:S(2)}, u32[]{:S(2)}) collective-permute-start(bf16[1024,256]{1,0:T(8,128)(2,1)} %collective-permute-done.token_ref), channel_id=1, source_target_pairs={{0,8},{1,9},{2,10},{3,11},{4,12},{5,13},{6,14},{7,15},{8,0},{9,1},... | collective-permute-start | bytes 1572872 | tf_op jit(solution)/shard_map/ppermute | solution.py:461
  33.4 2.0 %shard_map.85 = (bf16[528,256]{1,0:T(8,128)(2,1)}, bf16[528,256]{1,0:T(8,128)(2,1)}) custom-call(s32[1]{0:T(128)} %bitcast.x_ref, bf16[1024,256]{1,0:T(8,128)(2,1)} %collective-permute-done.token_ref), custom_call_target="tpu_custom_call" | custom-call | flops 524288 | bytes 1048576 | tf_op jit(solution)/shard_map/pallas_call | solution.py:151
  35.9 1.9 %collective-permute-done.6.refs_1_.refs_3_ = bf16[528,256]{1,0:T(8,128)(2,1)S(1)} collective-permute-done((bf16[528,256]{1,0:T(8,128)(2,1)S(1)}, bf16[528,256]{1,0:T(8,128)(2,1)S(1)}, u32[]{:S(2)}, u32[]{:S(2)}) %collective-permute-start.6) | collective-permute-done | bytes 270368 | tf_op jit(solution)/shard_map/ppermute | solution.py:461
  37.8 2.0 %collective-permute-start.10 = (bf16[528,256]{1,0:T(8,128)(2,1)}, bf16[528,256]{1,0:T(8,128)(2,1)}, u32[]{:S(2)}, u32[]{:S(2)}) collective-permute-start(bf16[528,256]{1,0:T(8,128)(2,1)} %get-tuple-element.87.refs_0_), channel_id=1, source_target_pairs={{0,2},{1,3},{2,0},{3,1},{4,6},{5,7},{6,4},{7,5},{8,10},{9,11},{10,... | collective-permute-start | bytes 811016 | tf_op jit(solution)/shard_map/ppermute | solution.py:461
  41.3 4.5 %all-to-all-start = ((bf16[4,2,2,128,512]{4,3,2,1,0:T(8,128)(2,1)}), bf16[4,2,2,128,512]{4,3,2,1,0:T(8,128)(2,1)S(1)}, u32[]{:S(2)}, u32[]{:S(2)}) async-start(bf16[4,2,2,128,512]{4,3,2,1,0:T(8,128)(2,1)} %copy-done.10), calls=%async_computation | async-start | bytes 4194304 | tf_op jit(solution)/shard_map/all_to_all | solution.py:472
  45.7 1.7 %collective-permute-done.10.refs_2_ = bf16[528,256]{1,0:T(8,128)(2,1)} collective-permute-done((bf16[528,256]{1,0:T(8,128)(2,1)}, bf16[528,256]{1,0:T(8,128)(2,1)}, u32[]{:S(2)}, u32[]{:S(2)}) %collective-permute-start.10) | collective-permute-done | bytes 270368 | tf_op jit(solution)/shard_map/ppermute | solution.py:461
  47.5 4.6 %collective-permute-done.8.refs_3_ = bf16[528,256]{1,0:T(8,128)(2,1)} collective-permute-done((bf16[528,256]{1,0:T(8,128)(2,1)S(1)}, bf16[528,256]{1,0:T(8,128)(2,1)}, u32[]{:S(2)}, u32[]{:S(2)}) %collective-permute-start.8) | collective-permute-done | bytes 270368 | tf_op jit(solution)/shard_map/ppermute | solution.py:461
  54.5 1.6 %collective-permute-start.12 = (bf16[528,256]{1,0:T(8,128)(2,1)S(1)}, bf16[528,256]{1,0:T(8,128)(2,1)S(1)}, u32[]{:S(2)}, u32[]{:S(2)}) collective-permute-start(bf16[528,256]{1,0:T(8,128)(2,1)S(1)} %get-tuple-element.93), channel_id=1, source_target_pairs={{0,4},{1,5},{2,6},{3,7},{4,0},{5,1},{6,2},{7,3},{8,12},{9,13},{10,... | collective-permute-start | bytes 811016 | tf_op jit(solution)/shard_map/ppermute | solution.py:461
  56.1 1.5 %collective-permute-start.13 = (bf16[528,256]{1,0:T(8,128)(2,1)S(1)}, bf16[528,256]{1,0:T(8,128)(2,1)S(1)}, u32[]{:S(2)}, u32[]{:S(2)}) collective-permute-start(bf16[528,256]{1,0:T(8,128)(2,1)S(1)} %get-tuple-element.92.refs_0_.refs_2_), channel_id=1, source_target_pairs={{0,2},{1,3},{2,0},{3,1},{4,6},{5,7},{6,4},{7,5},{8,10},{9,11},{10,... | collective-permute-start | bytes 811016 | tf_op jit(solution)/shard_map/ppermute | solution.py:461
  58.1 2.0 %shard_map.87.refs_0_ = bf16[4,512,512]{2,1,0:T(8,128)(2,1)S(1)} custom-call(s32[4]{0:T(128)S(1)} %pad_add_fusion.1.pick_ref, f32[8,512]{1,0:T(8,128)S(1)} %pad.4.gain_ref, bf16[528,256]{1,0:T(8,128)(2,1)S(1)} %get-tuple-element.71.refs_0_, bf16[528,256]{1,0:T(8,128)(2,1)S(1)} %collective-permute-done.1.refs_1_, ...), custom_call_target="tpu_custom_call" | custom-call | flops 2097152 | bytes 4194304 | tf_op jit(solution)/shard_map/pallas_call | solution.py:218
  60.1 1.4 copy-done.1
  61.5 2.0 %collective-permute-done.12.refs_1_.refs_3_ = bf16[528,256]{1,0:T(8,128)(2,1)S(1)} collective-permute-done((bf16[528,256]{1,0:T(8,128)(2,1)S(1)}, bf16[528,256]{1,0:T(8,128)(2,1)S(1)}, u32[]{:S(2)}, u32[]{:S(2)}) %collective-permute-start.12) | collective-permute-done | bytes 270368 | tf_op jit(solution)/shard_map/ppermute | solution.py:461
  63.4 2.0 %collective-permute-done.13.refs_2_ = bf16[528,256]{1,0:T(8,128)(2,1)S(1)} collective-permute-done((bf16[528,256]{1,0:T(8,128)(2,1)S(1)}, bf16[528,256]{1,0:T(8,128)(2,1)S(1)}, u32[]{:S(2)}, u32[]{:S(2)}) %collective-permute-start.13) | collective-permute-done | bytes 270368 | tf_op jit(solution)/shard_map/ppermute | solution.py:461
  65.4 5.1 %collective-permute-done.14.refs_3_ = bf16[528,256]{1,0:T(8,128)(2,1)S(1)} collective-permute-done((bf16[528,256]{1,0:T(8,128)(2,1)}, bf16[528,256]{1,0:T(8,128)(2,1)S(1)}, u32[]{:S(2)}, u32[]{:S(2)}) %collective-permute-start.14) | collective-permute-done | bytes 270368 | tf_op jit(solution)/shard_map/ppermute | solution.py:461
  70.5 1.2 pad_maximum_fusion.2
  72.8 1.5 %collective-permute-start.16 = (bf16[528,256]{1,0:T(8,128)(2,1)S(1)}, bf16[528,256]{1,0:T(8,128)(2,1)S(1)}, u32[]{:S(2)}, u32[]{:S(2)}) collective-permute-start(bf16[528,256]{1,0:T(8,128)(2,1)S(1)} %collective-permute-done.12.refs_1_.refs_3_), channel_id=1, source_target_pairs={{0,2},{1,3},{2,0},{3,1},{4,6},{5,7},{6,4},{7,5},{8,10},{9,11},{10,... | collective-permute-start | bytes 811016 | tf_op jit(solution)/shard_map/ppermute | solution.py:461
  74.3 1.7 %shard_map.88.refs_1_ = bf16[4,512,512]{2,1,0:T(8,128)(2,1)S(1)} custom-call(s32[4]{0:T(128)S(1)} %pad_add_fusion.1.pick_ref, f32[8,512]{1,0:T(8,128)S(1)} %pad.4.gain_ref, bf16[528,256]{1,0:T(8,128)(2,1)S(1)} %get-tuple-element.84.refs_0_.refs_2_, bf16[528,256]{1,0:T(8,128)(2,1)S(1)} %collective-permute-done.6.refs_1_.refs_3_, ...), custom_call_target="tpu_custom_call" | custom-call | flops 2097152 | bytes 4194304 | tf_op jit(solution)/shard_map/pallas_call | solution.py:218
  76.0 1.3 copy-done.3
  77.3 3.9 %collective-permute-done.16.refs_3_ = bf16[528,256]{1,0:T(8,128)(2,1)S(1)} collective-permute-done((bf16[528,256]{1,0:T(8,128)(2,1)S(1)}, bf16[528,256]{1,0:T(8,128)(2,1)S(1)}, u32[]{:S(2)}, u32[]{:S(2)}) %collective-permute-start.16) | collective-permute-done | bytes 270368 | tf_op jit(solution)/shard_map/ppermute | solution.py:461
  81.2 1.8 %shard_map.89.refs_0_ = bf16[4,512,512]{2,1,0:T(8,128)(2,1)S(1)} custom-call(s32[4]{0:T(128)S(1)} %pad_add_fusion.1.pick_ref, f32[8,512]{1,0:T(8,128)S(1)} %pad.4.gain_ref, bf16[528,256]{1,0:T(8,128)(2,1)} %get-tuple-element.87.refs_0_, bf16[528,256]{1,0:T(8,128)(2,1)} %collective-permute-done.9.refs_1_, bf16[528,256]{1,0:T(8,128)(2,1)} %collective-permute-done.10.refs_2_, ...), custom_call_target="tpu_custom_call" | custom-call | flops 2097152 | bytes 4194304 | tf_op jit(solution)/shard_map/pallas_call | solution.py:218
  83.1 1.4 copy-done.6
  84.5 1.3 shard_map.90.refs_1_
  85.7 1.3 copy-done.8
  87.0 6.3 %all-to-all-done.weight_ref = bf16[4,2,2,128,512]{4,3,2,1,0:T(8,128)(2,1)S(1)} async-done(((bf16[4,2,2,128,512]{4,3,2,1,0:T(8,128)(2,1)}), bf16[4,2,2,128,512]{4,3,2,1,0:T(8,128)(2,1)S(1)}, u32[]{:S(2)}, u32[]{:S(2)}) %all-to-all-start) | async-done | bytes 2097184 | tf_op jit(solution)/shard_map/all_to_all | solution.py:472
  93.3 1.6 %copy-done.2 = bf16[4,512,512]{2,1,0:T(8,128)(2,1)S(1)} copy-done((bf16[4,512,512]{2,1,0:T(8,128)(2,1)S(1)}, bf16[4,512,512]{2,1,0:T(8,128)(2,1)}, u32[]{:S(2)}) %copy-start.2) | copy-done | bytes 2097176
  94.9 1.6 %copy-done.4 = bf16[4,512,512]{2,1,0:T(8,128)(2,1)S(1)} copy-done((bf16[4,512,512]{2,1,0:T(8,128)(2,1)S(1)}, bf16[4,512,512]{2,1,0:T(8,128)(2,1)}, u32[]{:S(2)}) %copy-start.4) | copy-done | bytes 2097176
  96.5 2.0 %shard_map.91 = (f32[128,1024]{1,0:T(8,128)S(1)}, bf16[128,1024]{1,0:T(8,128)(2,1)S(1)}) custom-call(s32[1]{0:T(128)} %bitcast.x_ref, bf16[4,2,2,128,512]{4,3,2,1,0:T(8,128)(2,1)S(1)} %all-to-all-done.weight_ref, bf16[4,512,512]{2,1,0:T(8,128)(2,1)S(1)} %copy-done.2, bf16[4,512,512]{2,1,0:T(8,128)(2,1)S(1)} %copy-done.4), custom_call_target="tpu_custom_call" | custom-call | flops 1073741824 | bytes 5242880 | tf_op jit(solution)/shard_map/pallas_call | solution.py:266
  99.4 2.0 %shard_map.93 = (f32[128,1024]{1,0:T(8,128)S(1)}, bf16[128,1024]{1,0:T(8,128)(2,1)S(1)}) custom-call(s32[1]{0:T(128)} %bitcast.x_ref, bf16[4,2,2,128,512]{4,3,2,1,0:T(8,128)(2,1)S(1)} %all-to-all-done.weight_ref, bf16[4,512,512]{2,1,0:T(8,128)(2,1)S(1)} %copy-done.7, bf16[4,512,512]{2,1,0:T(8,128)(2,1)S(1)} %copy-done.9), custom_call_target="tpu_custom_call" | custom-call | flops 1073741824 | bytes 5242880 | tf_op jit(solution)/shard_map/pallas_call | solution.py:266
  101.4 1.3 collective-permute-start.23
  102.7 2.0 %shard_map.95 = (f32[128,1024]{1,0:T(8,128)S(1)}, bf16[128,1024]{1,0:T(8,128)(2,1)S(1)}) custom-call(s32[1]{0:T(128)} %bitcast.x_ref, bf16[4,2,2,128,512]{4,3,2,1,0:T(8,128)(2,1)S(1)} %all-to-all-done.weight_ref, bf16[4,512,512]{2,1,0:T(8,128)(2,1)S(1)} %copy-done.7, bf16[4,512,512]{2,1,0:T(8,128)(2,1)S(1)} %copy-done.9), custom_call_target="tpu_custom_call" | custom-call | flops 1073741824 | bytes 5242880 | tf_op jit(solution)/shard_map/pallas_call | solution.py:266
  104.7 2.0 %shard_map.94 = (f32[128,1024]{1,0:T(8,128)S(1)}, bf16[128,1024]{1,0:T(8,128)(2,1)S(1)}) custom-call(s32[1]{0:T(128)} %bitcast.x_ref, bf16[4,2,2,128,512]{4,3,2,1,0:T(8,128)(2,1)S(1)} %all-to-all-done.weight_ref, bf16[4,512,512]{2,1,0:T(8,128)(2,1)S(1)} %copy-done.2, bf16[4,512,512]{2,1,0:T(8,128)(2,1)S(1)} %copy-done.5), custom_call_target="tpu_custom_call" | custom-call | flops 1073741824 | bytes 5242880 | tf_op jit(solution)/shard_map/pallas_call | solution.py:266
  107.8 1.7 %shard_map.92.early_ref = bf16[256,2048]{1,0:T(8,128)(2,1)S(1)} custom-call(s32[1]{0:T(128)} %bitcast.13.first_ref, f32[128,1024]{1,0:T(8,128)S(1)} %get-tuple-element.116.mine_ref, bf16[128,1024]{1,0:T(8,128)(2,1)S(1)} %collective-permute-done.22.theirs_ref, s32[1,1024]{1,0:T(1,128)S(1)} %get-tuple-element.136.place_ref, ...), custom_call_target="tpu_custom_call" | custom-call | flops 536870912 | bytes 2097152 | tf_op jit(solution)/shard_map/pallas_call | solution.py:322
  109.5 1.9 %collective-permute-done.23.theirs_ref = bf16[128,1024]{1,0:T(8,128)(2,1)S(1)} collective-permute-done((bf16[128,1024]{1,0:T(8,128)(2,1)S(1)}, bf16[128,1024]{1,0:T(8,128)(2,1)S(1)}, u32[]{:S(2)}, u32[]{:S(2)}) %collective-permute-start.23) | collective-permute-done | bytes 262176 | tf_op jit(solution)/shard_map/ppermute | solution.py:461
  112.3 1.2 collective-permute-start.25
  113.5 8.7 %shard_map.96 = (bf16[128,2048]{1,0:T(8,128)(2,1)S(1)}, bf16[128,2048]{1,0:T(8,128)(2,1)S(1)}) custom-call(f32[8]{0:T(128)S(1)} %broadcast_select_fusion.flag_ref, s32[1]{0:T(128)} %bitcast.13.first_ref, f32[128,256]{1,0:T(8,128)S(1)} %copy-done.22, f32[1,128]{1,0:T(1,128)S(1)} %dynamic-slice_bitcast_fusion.skip_ref, ...), custom_call_target="tpu_custom_call" | custom-call | flops 1610612736 | bytes 4194304 | tf_op jit(solution)/shard_map/pallas_call | solution.py:400
  123.4 1.6 %shard_map.98 = bf16[8,128,256]{2,1,0:T(8,128)(2,1)S(1)} custom-call(bf16[128,2048]{1,0:T(8,128)(2,1)S(1)} %get-tuple-element.129.z_ref, bf16[128,2048]{1,0:T(8,128)(2,1)S(1)} %get-tuple-element.130.packed_ref, bf16[128,2048]{1,0:T(8,128)(2,1)S(1)} %shard_map.97.early_ref, f32[128,1024]{1,0:T(8,128)S(1)} %get-tuple-element.133.mine_ref, ...), custom_call_target="tpu_custom_call" | custom-call | flops 536870912 | bytes 4194304 | tf_op jit(solution)/shard_map/pallas_call | solution.py:428
  125.0 15.7 %all_to_all.10 = bf16[8,128,256]{2,1,0:T(8,128)(2,1)S(1)} all-to-all(bf16[8,128,256]{2,1,0:T(8,128)(2,1)S(1)} %shard_map.98), channel_id=1, replica_groups={{0,8,16,24,4,12,20,28},{1,9,17,25,5,13,21,29},{2,10,18,26,6,14,22,30},{..., dimensions={0} | all-to-all | bytes 1048576 | tf_op jit(solution)/shard_map/all_to_all | solution.py:577
  (95 shorter events, 19.1 us)
Async XLA Ops:
  0.0 13.6 %copy-start = (f32[1024]{0:T(1024)S(1)}, f32[1024]{0:T(1024)}, u32[]{:S(2)}) copy-start(f32[1024]{0:T(1024)} %param.14) | copy-start | bytes 12292
  0.0 27.8 %collective-permute-start = (bf16[1024,256]{1,0:T(8,128)(2,1)}, bf16[1024,256]{1,0:T(8,128)(2,1)}, u32[]{:S(2)}, u32[]{:S(2)}) collective-permute-start(bf16[1024,256]{1,0:T(8,128)(2,1)} %token_ref.1), channel_id=1, source_target_pairs={{0,16},{1,17},{2,18},{3,19},{4,20},{5,21},{6,22},{7,23},{8,24},{9,... | collective-permute-start | bytes 1572872 | tf_op jit(solution)/shard_map/ppermute | solution.py:461
  4.0 23.7 %collective-permute-start.4 = (bf16[1024,256]{1,0:T(8,128)(2,1)}, bf16[1024,256]{1,0:T(8,128)(2,1)S(1)}, u32[]{:S(2)}, u32[]{:S(2)}) collective-permute-start(bf16[1024,256]{1,0:T(8,128)(2,1)} %token_ref.1), channel_id=1, source_target_pairs={{0,8},{1,9},{2,10},{3,11},{4,12},{5,13},{6,14},{7,15},{8,0},{9,1},... | collective-permute-start | bytes 1572872 | tf_op jit(solution)/shard_map/ppermute | solution.py:461
  5.6 1.1 copy-start.17
  6.8 8.4 %collective-permute-start.1 = (bf16[528,256]{1,0:T(8,128)(2,1)S(1)}, bf16[528,256]{1,0:T(8,128)(2,1)S(1)}, u32[]{:S(2)}, u32[]{:S(2)}) collective-permute-start(bf16[528,256]{1,0:T(8,128)(2,1)S(1)} %get-tuple-element.70.after_ref), channel_id=1, source_target_pairs={{0,4},{1,5},{2,6},{3,7},{4,0},{5,1},{6,2},{7,3},{8,12},{9,13},{10,... | collective-permute-start | bytes 811016 | tf_op jit(solution)/shard_map/ppermute | solution.py:461
  8.3 19.5 %collective-permute-start.2 = (bf16[528,256]{1,0:T(8,128)(2,1)S(1)}, bf16[528,256]{1,0:T(8,128)(2,1)S(1)}, u32[]{:S(2)}, u32[]{:S(2)}) collective-permute-start(bf16[528,256]{1,0:T(8,128)(2,1)S(1)} %get-tuple-element.71.refs_0_), channel_id=1, source_target_pairs={{0,2},{1,3},{2,0},{3,1},{4,6},{5,7},{6,4},{7,5},{8,10},{9,11},{10,... | collective-permute-start | bytes 811016 | tf_op jit(solution)/shard_map/ppermute | solution.py:461
  15.2 12.6 %collective-permute-start.3 = (bf16[528,256]{1,0:T(8,128)(2,1)S(1)}, bf16[528,256]{1,0:T(8,128)(2,1)S(1)}, u32[]{:S(2)}, u32[]{:S(2)}) collective-permute-start(bf16[528,256]{1,0:T(8,128)(2,1)S(1)} %collective-permute-done.1.refs_1_), channel_id=1, source_target_pairs={{0,2},{1,3},{2,0},{3,1},{4,6},{5,7},{6,4},{7,5},{8,10},{9,11},{10,... | collective-permute-start | bytes 811016 | tf_op jit(solution)/shard_map/ppermute | solution.py:461
  16.7 1.2 copy-start.15
  17.9 1.2 copy-start.16
  19.8 1.3 copy-start.10
  28.9 23.2 %collective-permute-start.11 = (bf16[2112,256]{1,0:T(8,128)(2,1)}, bf16[2112,256]{1,0:T(8,128)(2,1)}, u32[]{:S(2)}, u32[]{:S(2)}) collective-permute-start(bf16[2112,256]{1,0:T(8,128)(2,1)} %pad_maximum_fusion), channel_id=1, source_target_pairs={{0,1},{1,0},{2,3},{3,2},{4,5},{5,4},{6,7},{7,6},{8,9},{9,8},{10,11... | collective-permute-start | bytes 3244040 | tf_op jit(solution)/shard_map/ppermute | solution.py:461
  28.9 8.9 %collective-permute-start.6 = (bf16[528,256]{1,0:T(8,128)(2,1)S(1)}, bf16[528,256]{1,0:T(8,128)(2,1)S(1)}, u32[]{:S(2)}, u32[]{:S(2)}) collective-permute-start(bf16[528,256]{1,0:T(8,128)(2,1)S(1)} %get-tuple-element.83), channel_id=1, source_target_pairs={{0,4},{1,5},{2,6},{3,7},{4,0},{5,1},{6,2},{7,3},{8,12},{9,13},{10,... | collective-permute-start | bytes 811016 | tf_op jit(solution)/shard_map/ppermute | solution.py:461
  30.4 9.3 %collective-permute-start.7 = (bf16[528,256]{1,0:T(8,128)(2,1)S(1)}, bf16[528,256]{1,0:T(8,128)(2,1)S(1)}, u32[]{:S(2)}, u32[]{:S(2)}) collective-permute-start(bf16[528,256]{1,0:T(8,128)(2,1)S(1)} %get-tuple-element.84.refs_0_.refs_2_), channel_id=1, source_target_pairs={{0,2},{1,3},{2,0},{3,1},{4,6},{5,7},{6,4},{7,5},{8,10},{9,11},{10,... | collective-permute-start | bytes 811016 | tf_op jit(solution)/shard_map/ppermute | solution.py:461
  32.0 15.5 %collective-permute-start.5 = (bf16[1024,256]{1,0:T(8,128)(2,1)}, bf16[1024,256]{1,0:T(8,128)(2,1)}, u32[]{:S(2)}, u32[]{:S(2)}) collective-permute-start(bf16[1024,256]{1,0:T(8,128)(2,1)} %collective-permute-done.token_ref), channel_id=1, source_target_pairs={{0,8},{1,9},{2,10},{3,11},{4,12},{5,13},{6,14},{7,15},{8,0},{9,1},... | collective-permute-start | bytes 1572872 | tf_op jit(solution)/shard_map/ppermute | solution.py:461
  35.4 10.4 %collective-permute-start.9 = (bf16[528,256]{1,0:T(8,128)(2,1)}, bf16[528,256]{1,0:T(8,128)(2,1)}, u32[]{:S(2)}, u32[]{:S(2)}) collective-permute-start(bf16[528,256]{1,0:T(8,128)(2,1)} %get-tuple-element.86), channel_id=1, source_target_pairs={{0,4},{1,5},{2,6},{3,7},{4,0},{5,1},{6,2},{7,3},{8,12},{9,13},{10,... | collective-permute-start | bytes 811016 | tf_op jit(solution)/shard_map/ppermute | solution.py:461
  37.8 9.7 %collective-permute-start.10 = (bf16[528,256]{1,0:T(8,128)(2,1)}, bf16[528,256]{1,0:T(8,128)(2,1)}, u32[]{:S(2)}, u32[]{:S(2)}) collective-permute-start(bf16[528,256]{1,0:T(8,128)(2,1)} %get-tuple-element.87.refs_0_), channel_id=1, source_target_pairs={{0,2},{1,3},{2,0},{3,1},{4,6},{5,7},{6,4},{7,5},{8,10},{9,11},{10,... | collective-permute-start | bytes 811016 | tf_op jit(solution)/shard_map/ppermute | solution.py:461
  40.5 11.7 %collective-permute-start.8 = (bf16[528,256]{1,0:T(8,128)(2,1)S(1)}, bf16[528,256]{1,0:T(8,128)(2,1)}, u32[]{:S(2)}, u32[]{:S(2)}) collective-permute-start(bf16[528,256]{1,0:T(8,128)(2,1)S(1)} %collective-permute-done.6.refs_1_.refs_3_), channel_id=1, source_target_pairs={{0,2},{1,3},{2,0},{3,1},{4,6},{5,7},{6,4},{7,5},{8,10},{9,11},{10,... | collective-permute-start | bytes 811016 | tf_op jit(solution)/shard_map/ppermute | solution.py:461
  41.3 52.0 %all-to-all-start = ((bf16[4,2,2,128,512]{4,3,2,1,0:T(8,128)(2,1)}), bf16[4,2,2,128,512]{4,3,2,1,0:T(8,128)(2,1)S(1)}, u32[]{:S(2)}, u32[]{:S(2)}) async-start(bf16[4,2,2,128,512]{4,3,2,1,0:T(8,128)(2,1)} %copy-done.10), calls=%async_computation | async-start | bytes 4194304 | tf_op jit(solution)/shard_map/all_to_all | solution.py:472
  45.7 12.4 %copy-start.12 = (bf16[528,256]{1,0:T(8,128)(2,1)S(1)}, bf16[528,256]{1,0:T(8,128)(2,1)}, u32[]{:S(2)}) copy-start(bf16[528,256]{1,0:T(8,128)(2,1)} %copy-done.11) | copy-start | bytes 811012
  53.2 17.3 %collective-permute-start.15 = (bf16[2112,256]{1,0:T(8,128)(2,1)S(1)}, bf16[2112,256]{1,0:T(8,128)(2,1)S(1)}, u32[]{:S(2)}, u32[]{:S(2)}) collective-permute-start(bf16[2112,256]{1,0:T(8,128)(2,1)S(1)} %pad_maximum_fusion.1), channel_id=1, source_target_pairs={{0,1},{1,0},{2,3},{3,2},{4,5},{5,4},{6,7},{7,6},{8,9},{9,8},{10,11... | collective-permute-start | bytes 3244040 | tf_op jit(solution)/shard_map/ppermute | solution.py:461
  54.5 30.0 %copy-start.18 = (bf16[528,256]{1,0:T(8,128)(2,1)}, bf16[528,256]{1,0:T(8,128)(2,1)S(1)}, u32[]{:S(2)}) copy-start(bf16[528,256]{1,0:T(8,128)(2,1)S(1)} %get-tuple-element.92.refs_0_.refs_2_) | copy-start | bytes 811012
  54.5 8.9 %collective-permute-start.12 = (bf16[528,256]{1,0:T(8,128)(2,1)S(1)}, bf16[528,256]{1,0:T(8,128)(2,1)S(1)}, u32[]{:S(2)}, u32[]{:S(2)}) collective-permute-start(bf16[528,256]{1,0:T(8,128)(2,1)S(1)} %get-tuple-element.93), channel_id=1, source_target_pairs={{0,4},{1,5},{2,6},{3,7},{4,0},{5,1},{6,2},{7,3},{8,12},{9,13},{10,... | collective-permute-start | bytes 811016 | tf_op jit(solution)/shard_map/ppermute | solution.py:461
  56.1 9.3 %collective-permute-start.13 = (bf16[528,256]{1,0:T(8,128)(2,1)S(1)}, bf16[528,256]{1,0:T(8,128)(2,1)S(1)}, u32[]{:S(2)}, u32[]{:S(2)}) collective-permute-start(bf16[528,256]{1,0:T(8,128)(2,1)S(1)} %get-tuple-element.92.refs_0_.refs_2_), channel_id=1, source_target_pairs={{0,2},{1,3},{2,0},{3,1},{4,6},{5,7},{6,4},{7,5},{8,10},{9,11},{10,... | collective-permute-start | bytes 811016 | tf_op jit(solution)/shard_map/ppermute | solution.py:461
  57.6 12.9 %collective-permute-start.14 = (bf16[528,256]{1,0:T(8,128)(2,1)}, bf16[528,256]{1,0:T(8,128)(2,1)S(1)}, u32[]{:S(2)}, u32[]{:S(2)}) collective-permute-start(bf16[528,256]{1,0:T(8,128)(2,1)} %collective-permute-done.9.refs_1_), channel_id=1, source_target_pairs={{0,2},{1,3},{2,0},{3,1},{4,6},{5,7},{6,4},{7,5},{8,10},{9,11},{10,... | collective-permute-start | bytes 811016 | tf_op jit(solution)/shard_map/ppermute | solution.py:461
  60.1 1.4 copy-start.1
  61.5 12.8 %copy-start.14 = (bf16[528,256]{1,0:T(8,128)(2,1)S(1)}, bf16[528,256]{1,0:T(8,128)(2,1)}, u32[]{:S(2)}) copy-start(bf16[528,256]{1,0:T(8,128)(2,1)} %copy-done.13) | copy-start | bytes 811012
  63.4 21.0 %copy-start.20 = (bf16[528,256]{1,0:T(8,128)(2,1)}, bf16[528,256]{1,0:T(8,128)(2,1)S(1)}, u32[]{:S(2)}) copy-start(bf16[528,256]{1,0:T(8,128)(2,1)S(1)} %collective-permute-done.12.refs_1_.refs_3_) | copy-start | bytes 811012
  71.7 9.6 %collective-permute-start.17 = (bf16[2112,256]{1,0:T(8,128)(2,1)S(1)}, bf16[2112,256]{1,0:T(8,128)(2,1)S(1)}, u32[]{:S(2)}, u32[]{:S(2)}) collective-permute-start(bf16[2112,256]{1,0:T(8,128)(2,1)S(1)} %pad_maximum_fusion.2), channel_id=1, source_target_pairs={{0,1},{1,0},{2,3},{3,2},{4,5},{5,4},{6,7},{7,6},{8,9},{9,8},{10,11... | collective-permute-start | bytes 3244040 | tf_op jit(solution)/shard_map/ppermute | solution.py:461
  71.8 5.6 %collective-permute-start.18 = (bf16[528,256]{1,0:T(8,128)(2,1)S(1)}, bf16[528,256]{1,0:T(8,128)(2,1)S(1)}, u32[]{:S(2)}, u32[]{:S(2)}) collective-permute-start(bf16[528,256]{1,0:T(8,128)(2,1)S(1)} %get-tuple-element.92.refs_0_.refs_2_), channel_id=1, source_target_pairs={{0,1},{1,0},{2,3},{3,2},{4,5},{5,4},{6,7},{7,6},{8,9},{9,8},{10,11... | collective-permute-start | bytes 811016 | tf_op jit(solution)/shard_map/ppermute | solution.py:461
  72.3 5.1 %collective-permute-start.19 = (bf16[528,256]{1,0:T(8,128)(2,1)S(1)}, bf16[528,256]{1,0:T(8,128)(2,1)S(1)}, u32[]{:S(2)}, u32[]{:S(2)}) collective-permute-start(bf16[528,256]{1,0:T(8,128)(2,1)S(1)} %collective-permute-done.13.refs_2_), channel_id=1, source_target_pairs={{0,1},{1,0},{2,3},{3,2},{4,5},{5,4},{6,7},{7,6},{8,9},{9,8},{10,11... | collective-permute-start | bytes 811016 | tf_op jit(solution)/shard_map/ppermute | solution.py:461
  72.3 5.0 %collective-permute-start.20 = (bf16[528,256]{1,0:T(8,128)(2,1)S(1)}, bf16[528,256]{1,0:T(8,128)(2,1)S(1)}, u32[]{:S(2)}, u32[]{:S(2)}) collective-permute-start(bf16[528,256]{1,0:T(8,128)(2,1)S(1)} %collective-permute-done.12.refs_1_.refs_3_), channel_id=1, source_target_pairs={{0,1},{1,0},{2,3},{3,2},{4,5},{5,4},{6,7},{7,6},{8,9},{9,8},{10,11... | collective-permute-start | bytes 811016 | tf_op jit(solution)/shard_map/ppermute | solution.py:461
  72.8 8.5 %collective-permute-start.16 = (bf16[528,256]{1,0:T(8,128)(2,1)S(1)}, bf16[528,256]{1,0:T(8,128)(2,1)S(1)}, u32[]{:S(2)}, u32[]{:S(2)}) collective-permute-start(bf16[528,256]{1,0:T(8,128)(2,1)S(1)} %collective-permute-done.12.refs_1_.refs_3_), channel_id=1, source_target_pairs={{0,2},{1,3},{2,0},{3,1},{4,6},{5,7},{6,4},{7,5},{8,10},{9,11},{10,... | collective-permute-start | bytes 811016 | tf_op jit(solution)/shard_map/ppermute | solution.py:461
  76.0 1.4 copy-start.3
  81.2 3.2 %collective-permute-start.21 = (bf16[528,256]{1,0:T(8,128)(2,1)S(1)}, bf16[528,256]{1,0:T(8,128)(2,1)S(1)}, u32[]{:S(2)}, u32[]{:S(2)}) collective-permute-start(bf16[528,256]{1,0:T(8,128)(2,1)S(1)} %collective-permute-done.16.refs_3_), channel_id=1, source_target_pairs={{0,1},{1,0},{2,3},{3,2},{4,5},{5,4},{6,7},{7,6},{8,9},{9,8},{10,11... | collective-permute-start | bytes 811016 | tf_op jit(solution)/shard_map/ppermute | solution.py:461
  83.1 1.4 copy-start.6
  85.7 1.3 copy-start.8
  93.3 1.6 %copy-start.2 = (bf16[4,512,512]{2,1,0:T(8,128)(2,1)S(1)}, bf16[4,512,512]{2,1,0:T(8,128)(2,1)}, u32[]{:S(2)}) copy-start(bf16[4,512,512]{2,1,0:T(8,128)(2,1)} %copy-done.1) | copy-start | bytes 6291460
  94.9 1.6 %copy-start.4 = (bf16[4,512,512]{2,1,0:T(8,128)(2,1)S(1)}, bf16[4,512,512]{2,1,0:T(8,128)(2,1)}, u32[]{:S(2)}) copy-start(bf16[4,512,512]{2,1,0:T(8,128)(2,1)} %copy-done.3) | copy-start | bytes 6291460
  96.5 2.9 %copy-start.7 = (bf16[4,512,512]{2,1,0:T(8,128)(2,1)S(1)}, bf16[4,512,512]{2,1,0:T(8,128)(2,1)}, u32[]{:S(2)}) copy-start(bf16[4,512,512]{2,1,0:T(8,128)(2,1)} %copy-done.6) | copy-start | bytes 6291460
  96.5 2.9 %copy-start.9 = (bf16[4,512,512]{2,1,0:T(8,128)(2,1)S(1)}, bf16[4,512,512]{2,1,0:T(8,128)(2,1)}, u32[]{:S(2)}) copy-start(bf16[4,512,512]{2,1,0:T(8,128)(2,1)} %copy-done.8) | copy-start | bytes 6291460
  98.5 9.3 %collective-permute-start.22 = (bf16[128,1024]{1,0:T(8,128)(2,1)S(1)}, bf16[128,1024]{1,0:T(8,128)(2,1)S(1)}, u32[]{:S(2)}, u32[]{:S(2)}) collective-permute-start(bf16[128,1024]{1,0:T(8,128)(2,1)S(1)} %get-tuple-element.117), channel_id=1, source_target_pairs={{0,4},{1,5},{2,6},{3,7},{4,0},{5,1},{6,2},{7,3},{8,12},{9,13},{10,... | collective-permute-start | bytes 786440 | tf_op jit(solution)/shard_map/ppermute | solution.py:461
  101.4 10.1 %collective-permute-start.23 = (bf16[128,1024]{1,0:T(8,128)(2,1)S(1)}, bf16[128,1024]{1,0:T(8,128)(2,1)S(1)}, u32[]{:S(2)}, u32[]{:S(2)}) collective-permute-start(bf16[128,1024]{1,0:T(8,128)(2,1)S(1)} %get-tuple-element.121), channel_id=1, source_target_pairs={{0,4},{1,5},{2,6},{3,7},{4,0},{5,1},{6,2},{7,3},{8,12},{9,13},{10,... | collective-permute-start | bytes 786440 | tf_op jit(solution)/shard_map/ppermute | solution.py:461
  102.7 2.0 %copy-start.5 = (bf16[4,512,512]{2,1,0:T(8,128)(2,1)S(1)}, bf16[4,512,512]{2,1,0:T(8,128)(2,1)}, u32[]{:S(2)}) copy-start(bf16[4,512,512]{2,1,0:T(8,128)(2,1)} %copy-done.3) | copy-start | bytes 6291460
  106.7 6.8 %copy-start.19 = (bf16[528,256]{1,0:T(8,128)(2,1)S(1)}, bf16[528,256]{1,0:T(8,128)(2,1)}, u32[]{:S(2)}) copy-start(bf16[528,256]{1,0:T(8,128)(2,1)} %copy-done.18) | copy-start | bytes 811012
  106.7 6.8 %copy-start.21 = (bf16[528,256]{1,0:T(8,128)(2,1)S(1)}, bf16[528,256]{1,0:T(8,128)(2,1)}, u32[]{:S(2)}) copy-start(bf16[528,256]{1,0:T(8,128)(2,1)} %copy-done.20) | copy-start | bytes 811012
  106.7 6.8 %copy-start.22 = (f32[128,256]{1,0:T(8,128)S(1)}, f32[128,256]{1,0:T(8,128)}, u32[]{:S(2)}) copy-start(f32[128,256]{1,0:T(8,128)} %dynamic-slice_convert_fusion.taps_ref) | copy-start | bytes 393220
  111.5 10.7 %collective-permute-start.24 = (bf16[128,1024]{1,0:T(8,128)(2,1)S(1)}, bf16[128,1024]{1,0:T(8,128)(2,1)S(1)}, u32[]{:S(2)}, u32[]{:S(2)}) collective-permute-start(bf16[128,1024]{1,0:T(8,128)(2,1)S(1)} %get-tuple-element.132), channel_id=1, source_target_pairs={{0,4},{1,5},{2,6},{3,7},{4,0},{5,1},{6,2},{7,3},{8,12},{9,13},{10,... | collective-permute-start | bytes 786440 | tf_op jit(solution)/shard_map/ppermute | solution.py:461
  112.3 11.1 %collective-permute-start.25 = (bf16[128,1024]{1,0:T(8,128)(2,1)S(1)}, bf16[128,1024]{1,0:T(8,128)(2,1)S(1)}, u32[]{:S(2)}, u32[]{:S(2)}) collective-permute-start(bf16[128,1024]{1,0:T(8,128)(2,1)S(1)} %get-tuple-element.134), channel_id=1, source_target_pairs={{0,4},{1,5},{2,6},{3,7},{4,0},{5,1},{6,2},{7,3},{8,12},{9,13},{10,... | collective-permute-start | bytes 786440 | tf_op jit(solution)/shard_map/ppermute | solution.py:461
  (2 other events, 1.8 us)

commit v4 on v3

--- a/solution.py
+++ b/solution.py
@@ -230,50 +230,39 @@
 
 
 def project_kernel(number, row_count, x_ref, weight_ref, *refs):
-    mine_ref, other_ref, mine, other = refs[-4:]
+    mine_ref, other_ref = refs[-2:]
     x = x_ref[0]
-    part = pl.program_id(0)
-
-    @pl.when(part == 0)
-    def _():
-        mine[...] = jnp.zeros(mine.shape, jnp.float32)
-        other[...] = jnp.zeros(mine.shape, jnp.float32)
-
     first = 0
-    for ref in refs[:-4]:
-        columns = slice(first, first + ref.shape[2])
-        first = columns.stop
-        block = ref[0]
-        for which, total in ((x, mine), (1 - x, other)):
-            total[:, columns] += jnp.dot(
-                weight_ref[0, number, which], block, preferred_element_type=jnp.float32
+    for ref in refs[:-2]:
+        parts, _, count = ref.shape
+        mine = jnp.zeros((mine_ref.shape[0], count), jnp.float32)
+        other = jnp.zeros((mine_ref.shape[0], count), jnp.float32)
+        for part in range(parts):
+            block = ref[part]
+            mine += jnp.dot(
+                weight_ref[part, number, x], block, preferred_element_type=jnp.float32
             )
-
-    @pl.when(part == pl.num_programs(0) - 1)
-    def _():
-        mine_ref[...] = mine[...]
-        for begin in range(0, mine.shape[1], row_count):
-            swapped = begin + row_count if begin // row_count % 2 == 0 else begin - row_count
-            other_ref[:, begin : begin + row_count] = other[
-                :, swapped : swapped + row_count
-            ].astype(jnp.bfloat16)
+            other += jnp.dot(
+                weight_ref[part, number, 1 - x], block, preferred_element_type=jnp.float32
+            )
+        mine_ref[:, first : first + count] = mine
+        other = other.astype(jnp.bfloat16)
+        other_ref[:, first : first + row_count] = other[:, row_count:]
+        other_ref[:, first + row_count : first + count] = other[:, :row_count]
+        first += count
 
 
 def project(x, weights, number, normed, row_count):
-    line, kinds, _, width, height = weights.shape
+    line, _, _, width, height = weights.shape
     out = (width, sum(some.shape[2] for some in normed))
-    whole = pl.BlockSpec(out, lambda part: (0, 0))
     return pl.pallas_call(
         functools.partial(project_kernel, number, row_count),
-        grid=(line,),
         out_shape=[
             jax.ShapeDtypeStruct(out, jnp.float32),
             jax.ShapeDtypeStruct(out, jnp.bfloat16),
         ],
-        in_specs=[SMEM, pl.BlockSpec((1, kinds, 2, width, height), lambda part: (part, 0, 0, 0, 0))]
-        + [pl.BlockSpec((1, *some.shape[1:]), lambda part: (part, 0, 0)) for some in normed],
-        out_specs=[whole, whole],
-        scratch_shapes=[pltpu.VMEM(out, jnp.float32)] * 2,
+        in_specs=[SMEM] + [VMEM] * (1 + len(normed)),
+        out_specs=[VMEM, VMEM],
         compiler_params=PARAMS,
         cost_estimate=pl.CostEstimate(
             flops=4 * width * height * out[1] * line,
@@ -356,10 +345,10 @@
             if back > piece % taps_blocks:
                 part = part * flag_ref[piece // taps_blocks]
             shifted[back][rows, :] = part
-    column = lax.broadcasted_iota(jnp.int32, (LANES, LANES), 1)
-    row = lax.broadcasted_iota(jnp.int32, (LANES, LANES), 0)
+    column = lax.broadcasted_iota(jnp.int32, (LANES, LANES), 1).astype(jnp.bfloat16)
+    row = lax.broadcasted_iota(jnp.int32, (LANES, LANES), 0).astype(jnp.bfloat16)
     later = column >= row
-    zero = jnp.zeros((LANES, LANES), jnp.float32)
+    zero = jnp.zeros((LANES, LANES), jnp.bfloat16)
 
     def one(group, carry):
         base = pl.multiple_of(group * SUBLANES, SUBLANES)
@@ -369,12 +358,13 @@
             for block in range(taps_blocks):
                 line_row = group_taps[member : member + 1, block * LANES : (block + 1) * LANES]
                 square = jnp.broadcast_to(line_row, (LANES, LANES))
-                turned.append(pltpu.roll(square, 0, 1, stride=1, stride_axis=0))
+                square = pltpu.roll(square, 0, 1, stride=1, stride_axis=0)
+                turned.append(square.astype(jnp.bfloat16))
             turned.append(zero)
             rows = pl.ds(base + member, pieces, stride=chan)
             tiles, inputs = [], []
             for back in range(taps_blocks + 1):
-                tiles.append(jnp.where(later, turned[back + 1], turned[back]).astype(jnp.bfloat16))
+                tiles.append(jnp.where(later, turned[back + 1], turned[back]))
                 inputs.append(shifted[back][rows, :].astype(jnp.bfloat16))
             band[rows, :] = jnp.dot(
                 jnp.concatenate(inputs, axis=1),
@@ -383,7 +373,7 @@
             )
         return carry
 
-    lax.fori_loop(0, chan // SUBLANES, one, 0)
+    lax.fori_loop(0, chan // SUBLANES, one, 0, unroll=4)
     skip = column_of(skip_ref[...])
     for piece in range(pieces):
         lanes = slice(piece * LANES, (piece + 1) * LANES)
@@ -510,13 +500,14 @@
     kept0, give0 = halve(which, tokens)
     got0, kept0_far = across(give0), to_owner(kept0, far_owner)
     got0_far = to_owner(got0, far_owner)
+    most0 = jnp.concatenate([kept0, got0, kept0_far, got0_far], axis=0)
     packed_weights = pack_weights(give0, [w_value, w_gate], line)
     packed_weights, by_near = tie(packed_weights, by_near)
     kept1, give1 = halve(which, by_near)
     small = picks, gains, taps, skip, flags, row_first, places, which
     by_both = to_pair(by_far, near_pair)
-    by_far, got0, kept0_far, got0_far, kept1, give1, small, packed_weights = tie(
-        by_far, got0, kept0_far, got0_far, kept1, give1, small, packed_weights
+    by_far, got0, kept0_far, got0_far, most0, kept1, give1, small, packed_weights = tie(
+        by_far, got0, kept0_far, got0_far, most0, kept1, give1, small, packed_weights
     )
     picks, gains, taps, skip, flags, row_first, places, which = small
 
@@ -525,24 +516,24 @@
     got2, kept2_far = across(give2), to_owner(kept2, far_owner)
     got1_far = to_owner(got1, far_owner)
     weights = along_line(packed_weights)
-    all0 = to_near([kept0, got0, kept0_far, got0_far])
-    by_both, got1, kept1_far, got1_far, got2, kept2_far, all0 = tie(
-        by_both, got1, kept1_far, got1_far, got2, kept2_far, all0
+    by_both, got1, kept1_far, got1_far, got2, kept2_far = tie(
+        by_both, got1, kept1_far, got1_far, got2, kept2_far
     )
 
     kept3, give3 = halve(which, by_both)
     got3, kept3_far = across(give3), to_owner(kept3, far_owner)
     got2_far = to_owner(got2, far_owner)
     all1 = to_near([kept1, got1, kept1_far, got1_far])
-    normed0 = scaled([kept0, got0, kept0_far, got0_far, all0])
-    got3, kept3_far, got2_far, all1, normed0 = tie(got3, kept3_far, got2_far, all1, normed0)
+    all0 = to_near([most0])
+    got3, kept3_far, got2_far, all0, all1 = tie(got3, kept3_far, got2_far, all0, all1)
 
     got3_far = to_owner(got3, far_owner)
     all2 = to_near([kept2, got2, kept2_far, got2_far])
     near_kept3, near_kept3_far, near_got3 = [to_near([some]) for some in (kept3, kept3_far, got3)]
+    normed0 = scaled([kept0, got0, kept0_far, got0_far, all0])
     normed1 = scaled([kept1, got1, kept1_far, got1_far, all1])
-    got3_far, all2, near_kept3, near_kept3_far, near_got3, normed1 = tie(
-        got3_far, all2, near_kept3, near_kept3_far, near_got3, normed1
+    got3_far, all2, near_kept3, near_kept3_far, near_got3, normed0, normed1 = tie(
+        got3_far, all2, near_kept3, near_kept3_far, near_got3, normed0, normed1
     )
 
     near_got3_far = to_near([got3_far])

time: 142 us -> 138 us (0.972)
  Pallas kernels: 31.7 us -> 26.5 us
    pallas_call x4, Pallas kernels: 7.99 us -> 5.02 us  [project(): pl.pallas_call(functools.partial(project_kernel, number, row_count), out_...]
    ppermute x26, waiting for transfers between devices: 30.9 us -> 32.9 us  [send(): return lax.ppermute(array, AXES, pairs)]
    pallas_call x1, Pallas kernels: 8.68 us -> 7.11 us  [band_of(): pl.pallas_call(functools.partial(band_kernel, taps_blocks, tall), out_sha...]
    concatenate x3 -> x2, other arithmetic: 3.35 us -> 2.29 us  [to_near(): stacked = jnp.concatenate(arrays, axis=0) if len(arrays) > 1 else arrays[0]]
    unnamed x48 -> x44, local copies, waits for them, and re-layouts: 15 us -> 14.6 us
  transfers between devices with their start and end apart: 27 -> 27, of which waited for: 12 -> 12; matrix products, arithmetic and copies ran while one was open for 6% -> 7% of each run, Pallas kernels for 20% -> 17%
where the time goes in v4:
time: 138 us; the launch traced here: 137 us
  waiting for transfers between devices  38.2 us (28%)
  starting transfers between devices  32.3 us (23%)
  Pallas kernels  26.5 us (19%)
  local copies, waits for them, and re-layouts  17.3 us (13%)
  blocking collectives  15.5 us (11%)
  other arithmetic  6.61 us (5%)
    ppermute x26, waiting for transfers between devices, send(): return lax.ppermute(array, AXES, pairs)  32.9 us
    ppermute x26, starting transfers between devices, send(): return lax.ppermute(array, AXES, pairs)  27.1 us
    all_to_all x1, blocking collectives, on_device_line(): lax.all_to_all(mixed, AXES, split_axis=0, concat_axis=0, tiled=True, axis...  15.5 us
    unnamed x44, local copies, waits for them, and re-layouts  14.6 us
    pallas_call x1, Pallas kernels, band_of(): pl.pallas_call(functools.partial(band_kernel, taps_blocks, tall), out_sha...  7.11 us
    pallas_call x4, Pallas kernels, scale(): pl.pallas_call(functools.partial(scale_kernel, height), out_shape=jax.Sha...  6.06 us
    all_to_all x1, waiting for transfers between devices, along_line(): lax.all_to_all(array, AXES, split_axis=0, concat_axis=0, tiled=True, axis...  5.33 us
    all_to_all x1, starting transfers between devices, along_line(): lax.all_to_all(array, AXES, split_axis=0, concat_axis=0, tiled=True, axis...  5.25 us
  transfers between devices with their start and end apart: 27, of which 12 were waited for; matrix products, arithmetic and copies ran while one was open for 7% of the time, Pallas kernels for 17%

profile of v4, /device:TPU:0, one launch (start us, length us, event | category | flops | bytes accessed | tf_op | source)
XLA Modules:
  0.0 136.8 jit_solution(587975912111837765)
XLA Ops:
  0.0 4.0 %collective-permute-start = (bf16[1024,256]{1,0:T(8,128)(2,1)}, bf16[1024,256]{1,0:T(8,128)(2,1)}, u32[]{:S(2)}, u32[]{:S(2)}) collective-permute-start(bf16[1024,256]{1,0:T(8,128)(2,1)} %token_ref.1), channel_id=1, source_target_pairs={{0,16},{1,17},{2,18},{3,19},{4,20},{5,21},{6,22},{7,23},{8,24},{9,... | collective-permute-start | bytes 1572872 | tf_op jit(solution)/shard_map/ppermute | solution.py:451
  4.0 1.6 %collective-permute-start.4 = (bf16[1024,256]{1,0:T(8,128)(2,1)}, bf16[1024,256]{1,0:T(8,128)(2,1)S(1)}, u32[]{:S(2)}, u32[]{:S(2)}) collective-permute-start(bf16[1024,256]{1,0:T(8,128)(2,1)} %token_ref.1), channel_id=1, source_target_pairs={{0,8},{1,9},{2,10},{3,11},{4,12},{5,13},{6,14},{7,15},{8,0},{9,1},... | collective-permute-start | bytes 1572872 | tf_op jit(solution)/shard_map/ppermute | solution.py:451
  6.8 1.6 %collective-permute-start.1 = (bf16[528,256]{1,0:T(8,128)(2,1)S(1)}, bf16[528,256]{1,0:T(8,128)(2,1)S(1)}, u32[]{:S(2)}, u32[]{:S(2)}) collective-permute-start(bf16[528,256]{1,0:T(8,128)(2,1)S(1)} %get-tuple-element.71.after_ref), channel_id=1, source_target_pairs={{0,4},{1,5},{2,6},{3,7},{4,0},{5,1},{6,2},{7,3},{8,12},{9,13},{10,... | collective-permute-start | bytes 811016 | tf_op jit(solution)/shard_map/ppermute | solution.py:451
  8.3 1.5 %collective-permute-start.2 = (bf16[528,256]{1,0:T(8,128)(2,1)S(1)}, bf16[528,256]{1,0:T(8,128)(2,1)S(1)}, u32[]{:S(2)}, u32[]{:S(2)}) collective-permute-start(bf16[528,256]{1,0:T(8,128)(2,1)S(1)} %get-tuple-element.72.refs_0_), channel_id=1, source_target_pairs={{0,2},{1,3},{2,0},{3,1},{4,6},{5,7},{6,4},{7,5},{8,10},{9,11},{10,... | collective-permute-start | bytes 811016 | tf_op jit(solution)/shard_map/ppermute | solution.py:451
  14.5 1.5 %collective-permute-start.3 = (bf16[528,256]{1,0:T(8,128)(2,1)S(1)}, bf16[528,256]{1,0:T(8,128)(2,1)S(1)}, u32[]{:S(2)}, u32[]{:S(2)}) collective-permute-start(bf16[528,256]{1,0:T(8,128)(2,1)S(1)} %collective-permute-done.1.refs_1_), channel_id=1, source_target_pairs={{0,2},{1,3},{2,0},{3,1},{4,6},{5,7},{6,4},{7,5},{8,10},{9,11},{10,... | collective-permute-start | bytes 811016 | tf_op jit(solution)/shard_map/ppermute | solution.py:451
  16.8 1.2 copy-done.13
  18.0 1.2 copy-done.14
  19.8 1.3 copy-done.10
  21.2 1.5 %dynamic-slice_convert_fusion.taps_ref = f32[128,256]{1,0:T(8,128)} fusion(bf16[1024,256]{1,0:T(8,128)(2,1)} %param.13, s32[]{:T(128)S(6)} %select_n.50), kind=kLoop, calls=%fused_computation.5 | loop fusion | flops 32768 | bytes 196612 | tf_op jit(solution)/shard_map/convert_element_type | solution.py:479
  22.7 5.0 %collective-permute-done.4.token_ref = bf16[1024,256]{1,0:T(8,128)(2,1)S(1)} collective-permute-done((bf16[1024,256]{1,0:T(8,128)(2,1)}, bf16[1024,256]{1,0:T(8,128)(2,1)S(1)}, u32[]{:S(2)}, u32[]{:S(2)}) %collective-permute-start.4) | collective-permute-done | bytes 524320 | tf_op jit(solution)/shard_map/ppermute | solution.py:451
  28.9 1.5 %collective-permute-start.6 = (bf16[528,256]{1,0:T(8,128)(2,1)S(1)}, bf16[528,256]{1,0:T(8,128)(2,1)S(1)}, u32[]{:S(2)}, u32[]{:S(2)}) collective-permute-start(bf16[528,256]{1,0:T(8,128)(2,1)S(1)} %get-tuple-element.84), channel_id=1, source_target_pairs={{0,4},{1,5},{2,6},{3,7},{4,0},{5,1},{6,2},{7,3},{8,12},{9,13},{10,... | collective-permute-start | bytes 811016 | tf_op jit(solution)/shard_map/ppermute | solution.py:451
  30.4 1.4 %collective-permute-start.5 = (bf16[1024,256]{1,0:T(8,128)(2,1)}, bf16[1024,256]{1,0:T(8,128)(2,1)}, u32[]{:S(2)}, u32[]{:S(2)}) collective-permute-start(bf16[1024,256]{1,0:T(8,128)(2,1)} %collective-permute-done.token_ref), channel_id=1, source_target_pairs={{0,8},{1,9},{2,10},{3,11},{4,12},{5,13},{6,14},{7,15},{8,0},{9,1},... | collective-permute-start | bytes 1572872 | tf_op jit(solution)/shard_map/ppermute | solution.py:451
  31.9 1.5 %collective-permute-start.7 = (bf16[528,256]{1,0:T(8,128)(2,1)S(1)}, bf16[528,256]{1,0:T(8,128)(2,1)}, u32[]{:S(2)}, u32[]{:S(2)}) collective-permute-start(bf16[528,256]{1,0:T(8,128)(2,1)S(1)} %get-tuple-element.85.refs_0_.refs_2_), channel_id=1, source_target_pairs={{0,2},{1,3},{2,0},{3,1},{4,6},{5,7},{6,4},{7,5},{8,10},{9,11},{10,... | collective-permute-start | bytes 811016 | tf_op jit(solution)/shard_map/ppermute | solution.py:451
  33.4 2.0 %shard_map.85 = (bf16[528,256]{1,0:T(8,128)(2,1)}, bf16[528,256]{1,0:T(8,128)(2,1)}) custom-call(s32[1]{0:T(128)} %bitcast.x_ref, bf16[1024,256]{1,0:T(8,128)(2,1)} %collective-permute-done.token_ref), custom_call_target="tpu_custom_call" | custom-call | flops 524288 | bytes 1048576 | tf_op jit(solution)/shard_map/pallas_call | solution.py:151
  36.4 1.5 %collective-permute-start.8 = (bf16[528,256]{1,0:T(8,128)(2,1)S(1)}, bf16[528,256]{1,0:T(8,128)(2,1)}, u32[]{:S(2)}, u32[]{:S(2)}) collective-permute-start(bf16[528,256]{1,0:T(8,128)(2,1)S(1)} %collective-permute-done.6.refs_1_.refs_3_), channel_id=1, source_target_pairs={{0,2},{1,3},{2,0},{3,1},{4,6},{5,7},{6,4},{7,5},{8,10},{9,11},{10,... | collective-permute-start | bytes 811016 | tf_op jit(solution)/shard_map/ppermute | solution.py:451
  37.9 5.2 %all-to-all-start = ((bf16[4,2,2,128,512]{4,3,2,1,0:T(8,128)(2,1)}), bf16[4,2,2,128,512]{4,3,2,1,0:T(8,128)(2,1)S(1)}, u32[]{:S(2)}, u32[]{:S(2)}) async-start(bf16[4,2,2,128,512]{4,3,2,1,0:T(8,128)(2,1)} %copy-done.10), calls=%async_computation | async-start | bytes 4194304 | tf_op jit(solution)/shard_map/all_to_all | solution.py:462
  43.2 3.5 %collective-permute-done.10.refs_2_ = bf16[528,256]{1,0:T(8,128)(2,1)} collective-permute-done((bf16[528,256]{1,0:T(8,128)(2,1)}, bf16[528,256]{1,0:T(8,128)(2,1)}, u32[]{:S(2)}, u32[]{:S(2)}) %collective-permute-start.10) | collective-permute-done | bytes 270368 | tf_op jit(solution)/shard_map/ppermute | solution.py:451
  46.7 3.7 %collective-permute-done.8.refs_3_ = bf16[528,256]{1,0:T(8,128)(2,1)} collective-permute-done((bf16[528,256]{1,0:T(8,128)(2,1)S(1)}, bf16[528,256]{1,0:T(8,128)(2,1)}, u32[]{:S(2)}, u32[]{:S(2)}) %collective-permute-start.8) | collective-permute-done | bytes 270368 | tf_op jit(solution)/shard_map/ppermute | solution.py:451
  53.3 1.5 %collective-permute-start.12 = (bf16[528,256]{1,0:T(8,128)(2,1)S(1)}, bf16[528,256]{1,0:T(8,128)(2,1)S(1)}, u32[]{:S(2)}, u32[]{:S(2)}) collective-permute-start(bf16[528,256]{1,0:T(8,128)(2,1)S(1)} %get-tuple-element.90.refs_0_.refs_2_), channel_id=1, source_target_pairs={{0,2},{1,3},{2,0},{3,1},{4,6},{5,7},{6,4},{7,5},{8,10},{9,11},{10,... | collective-permute-start | bytes 811016 | tf_op jit(solution)/shard_map/ppermute | solution.py:451
  55.3 6.3 %collective-permute-done.11.refs_1_.refs_3_ = bf16[528,256]{1,0:T(8,128)(2,1)S(1)} collective-permute-done((bf16[528,256]{1,0:T(8,128)(2,1)S(1)}, bf16[528,256]{1,0:T(8,128)(2,1)S(1)}, u32[]{:S(2)}, u32[]{:S(2)}) %collective-permute-start.11) | collective-permute-done | bytes 270368 | tf_op jit(solution)/shard_map/ppermute | solution.py:451
  62.6 5.1 %collective-permute-done.13.refs_3_ = bf16[528,256]{1,0:T(8,128)(2,1)S(1)} collective-permute-done((bf16[528,256]{1,0:T(8,128)(2,1)}, bf16[528,256]{1,0:T(8,128)(2,1)S(1)}, u32[]{:S(2)}, u32[]{:S(2)}) %collective-permute-start.13) | collective-permute-done | bytes 270368 | tf_op jit(solution)/shard_map/ppermute | solution.py:451
  67.7 1.2 pad_maximum_fusion.2
  70.0 1.5 %collective-permute-start.16 = (bf16[528,256]{1,0:T(8,128)(2,1)S(1)}, bf16[528,256]{1,0:T(8,128)(2,1)S(1)}, u32[]{:S(2)}, u32[]{:S(2)}) collective-permute-start(bf16[528,256]{1,0:T(8,128)(2,1)S(1)} %collective-permute-done.11.refs_1_.refs_3_), channel_id=1, source_target_pairs={{0,2},{1,3},{2,0},{3,1},{4,6},{5,7},{6,4},{7,5},{8,10},{9,11},{10,... | collective-permute-start | bytes 811016 | tf_op jit(solution)/shard_map/ppermute | solution.py:451
  71.5 1.7 %shard_map.88.refs_1_ = bf16[4,512,512]{2,1,0:T(8,128)(2,1)S(1)} custom-call(s32[4]{0:T(128)S(1)} %pad_add_fusion.1.pick_ref, f32[8,512]{1,0:T(8,128)S(1)} %pad.4.gain_ref, bf16[528,256]{1,0:T(8,128)(2,1)S(1)} %get-tuple-element.85.refs_0_.refs_2_, bf16[528,256]{1,0:T(8,128)(2,1)S(1)} %collective-permute-done.6.refs_1_.refs_3_, ...), custom_call_target="tpu_custom_call" | custom-call | flops 2097152 | bytes 4194304 | tf_op jit(solution)/shard_map/pallas_call | solution.py:218
  73.3 1.3 copy-done.1
  74.6 1.3 shard_map.87.refs_0_
  75.9 1.4 copy-done.4
  77.3 1.2 collective-permute-done.16.refs_3_
  78.5 1.8 %shard_map.89.refs_0_ = bf16[4,512,512]{2,1,0:T(8,128)(2,1)S(1)} custom-call(s32[4]{0:T(128)S(1)} %pad_add_fusion.1.pick_ref, f32[8,512]{1,0:T(8,128)S(1)} %pad.4.gain_ref, bf16[528,256]{1,0:T(8,128)(2,1)} %get-tuple-element.88.refs_0_, bf16[528,256]{1,0:T(8,128)(2,1)} %collective-permute-done.9.refs_1_, bf16[528,256]{1,0:T(8,128)(2,1)} %collective-permute-done.10.refs_2_, ...), custom_call_target="tpu_custom_call" | custom-call | flops 2097152 | bytes 4194304 | tf_op jit(solution)/shard_map/pallas_call | solution.py:218
  80.3 1.4 %copy-done.6 = bf16[4,512,512]{2,1,0:T(8,128)(2,1)} copy-done((bf16[4,512,512]{2,1,0:T(8,128)(2,1)}, bf16[4,512,512]{2,1,0:T(8,128)(2,1)S(1)}, u32[]{:S(2)}) %copy-start.6) | copy-done | bytes 2097176
  81.7 1.2 shard_map.90.refs_1_
  83.0 1.3 copy-done.8
  84.3 5.3 %all-to-all-done.weight_ref = bf16[4,2,2,128,512]{4,3,2,1,0:T(8,128)(2,1)S(1)} async-done(((bf16[4,2,2,128,512]{4,3,2,1,0:T(8,128)(2,1)}), bf16[4,2,2,128,512]{4,3,2,1,0:T(8,128)(2,1)S(1)}, u32[]{:S(2)}, u32[]{:S(2)}) %all-to-all-start) | async-done | bytes 2097184 | tf_op jit(solution)/shard_map/all_to_all | solution.py:462
  89.6 1.6 %copy-done.2 = bf16[4,512,512]{2,1,0:T(8,128)(2,1)S(1)} copy-done((bf16[4,512,512]{2,1,0:T(8,128)(2,1)S(1)}, bf16[4,512,512]{2,1,0:T(8,128)(2,1)}, u32[]{:S(2)}) %copy-start.2) | copy-done | bytes 2097176
  91.2 1.6 %copy-done.5 = bf16[4,512,512]{2,1,0:T(8,128)(2,1)S(1)} copy-done((bf16[4,512,512]{2,1,0:T(8,128)(2,1)S(1)}, bf16[4,512,512]{2,1,0:T(8,128)(2,1)}, u32[]{:S(2)}) %copy-start.5) | copy-done | bytes 2097176
  92.8 1.3 shard_map.91
  94.1 1.6 %collective-permute-start.22 = (bf16[128,1024]{1,0:T(8,128)(2,1)S(1)}, bf16[128,1024]{1,0:T(8,128)(2,1)S(1)}, u32[]{:S(2)}, u32[]{:S(2)}) collective-permute-start(bf16[128,1024]{1,0:T(8,128)(2,1)S(1)} %get-tuple-element.119), channel_id=1, source_target_pairs={{0,4},{1,5},{2,6},{3,7},{4,0},{5,1},{6,2},{7,3},{8,12},{9,13},{10,... | collective-permute-start | bytes 786440 | tf_op jit(solution)/shard_map/ppermute | solution.py:451
  95.6 1.3 shard_map.93
  97.8 1.3 shard_map.95
  99.4 1.3 shard_map.94
  100.7 2.6 %collective-permute-done.22.theirs_ref = bf16[128,1024]{1,0:T(8,128)(2,1)S(1)} collective-permute-done((bf16[128,1024]{1,0:T(8,128)(2,1)S(1)}, bf16[128,1024]{1,0:T(8,128)(2,1)S(1)}, u32[]{:S(2)}, u32[]{:S(2)}) %collective-permute-start.22) | collective-permute-done | bytes 262176 | tf_op jit(solution)/shard_map/ppermute | solution.py:451
  103.4 1.7 %shard_map.92.early_ref = bf16[256,2048]{1,0:T(8,128)(2,1)S(1)} custom-call(s32[1]{0:T(128)} %bitcast.13.first_ref, f32[128,1024]{1,0:T(8,128)S(1)} %get-tuple-element.118.mine_ref, bf16[128,1024]{1,0:T(8,128)(2,1)S(1)} %collective-permute-done.22.theirs_ref, s32[1,1024]{1,0:T(1,128)S(1)} %get-tuple-element.138.place_ref, ...), custom_call_target="tpu_custom_call" | custom-call | flops 536870912 | bytes 2097152 | tf_op jit(solution)/shard_map/pallas_call | solution.py:311
  105.1 1.9 %collective-permute-done.23.theirs_ref = bf16[128,1024]{1,0:T(8,128)(2,1)S(1)} collective-permute-done((bf16[128,1024]{1,0:T(8,128)(2,1)S(1)}, bf16[128,1024]{1,0:T(8,128)(2,1)S(1)}, u32[]{:S(2)}, u32[]{:S(2)}) %collective-permute-start.23) | collective-permute-done | bytes 262176 | tf_op jit(solution)/shard_map/ppermute | solution.py:451
  107.0 1.5 %collective-permute-start.24 = (bf16[128,1024]{1,0:T(8,128)(2,1)S(1)}, bf16[128,1024]{1,0:T(8,128)(2,1)S(1)}, u32[]{:S(2)}, u32[]{:S(2)}) collective-permute-start(bf16[128,1024]{1,0:T(8,128)(2,1)S(1)} %get-tuple-element.134), channel_id=1, source_target_pairs={{0,4},{1,5},{2,6},{3,7},{4,0},{5,1},{6,2},{7,3},{8,12},{9,13},{10,... | collective-permute-start | bytes 786440 | tf_op jit(solution)/shard_map/ppermute | solution.py:451
  109.0 7.1 %shard_map.96 = (bf16[128,2048]{1,0:T(8,128)(2,1)S(1)}, bf16[128,2048]{1,0:T(8,128)(2,1)S(1)}) custom-call(f32[8]{0:T(128)S(1)} %broadcast_select_fusion.flag_ref, s32[1]{0:T(128)} %bitcast.13.first_ref, f32[128,256]{1,0:T(8,128)S(1)} %copy-done.20, f32[1,128]{1,0:T(1,128)S(1)} %dynamic-slice_bitcast_fusion.skip_ref, ...), custom_call_target="tpu_custom_call" | custom-call | flops 1610612736 | bytes 4194304 | tf_op jit(solution)/shard_map/pallas_call | solution.py:390
  117.3 1.7 %collective-permute-done.25.theirs_ref = bf16[128,1024]{1,0:T(8,128)(2,1)S(1)} collective-permute-done((bf16[128,1024]{1,0:T(8,128)(2,1)S(1)}, bf16[128,1024]{1,0:T(8,128)(2,1)S(1)}, u32[]{:S(2)}, u32[]{:S(2)}) %collective-permute-start.25) | collective-permute-done | bytes 262176 | tf_op jit(solution)/shard_map/ppermute | solution.py:451
  119.0 1.6 %shard_map.98 = bf16[8,128,256]{2,1,0:T(8,128)(2,1)S(1)} custom-call(bf16[128,2048]{1,0:T(8,128)(2,1)S(1)} %get-tuple-element.131.z_ref, bf16[128,2048]{1,0:T(8,128)(2,1)S(1)} %get-tuple-element.132.packed_ref, bf16[128,2048]{1,0:T(8,128)(2,1)S(1)} %shard_map.97.early_ref, f32[128,1024]{1,0:T(8,128)S(1)} %get-tuple-element.135.mine_ref, ...), custom_call_target="tpu_custom_call" | custom-call | flops 536870912 | bytes 4194304 | tf_op jit(solution)/shard_map/pallas_call | solution.py:418
  120.6 15.5 %all_to_all.10 = bf16[8,128,256]{2,1,0:T(8,128)(2,1)S(1)} all-to-all(bf16[8,128,256]{2,1,0:T(8,128)(2,1)S(1)} %shard_map.98), channel_id=1, replica_groups={{0,8,16,24,4,12,20,28},{1,9,17,25,5,13,21,29},{2,10,18,26,6,14,22,30},{..., dimensions={0} | all-to-all | bytes 1048576 | tf_op jit(solution)/shard_map/all_to_all | solution.py:568
  (91 shorter events, 18.6 us)
Async XLA Ops:
  0.0 16.0 %copy-start = (f32[1024]{0:T(1024)S(1)}, f32[1024]{0:T(1024)}, u32[]{:S(2)}) copy-start(f32[1024]{0:T(1024)} %param.14) | copy-start | bytes 12292
  0.0 28.9 %collective-permute-start = (bf16[1024,256]{1,0:T(8,128)(2,1)}, bf16[1024,256]{1,0:T(8,128)(2,1)}, u32[]{:S(2)}, u32[]{:S(2)}) collective-permute-start(bf16[1024,256]{1,0:T(8,128)(2,1)} %token_ref.1), channel_id=1, source_target_pairs={{0,16},{1,17},{2,18},{3,19},{4,20},{5,21},{6,22},{7,23},{8,24},{9,... | collective-permute-start | bytes 1572872 | tf_op jit(solution)/shard_map/ppermute | solution.py:451
  4.0 23.7 %collective-permute-start.4 = (bf16[1024,256]{1,0:T(8,128)(2,1)}, bf16[1024,256]{1,0:T(8,128)(2,1)S(1)}, u32[]{:S(2)}, u32[]{:S(2)}) collective-permute-start(bf16[1024,256]{1,0:T(8,128)(2,1)} %token_ref.1), channel_id=1, source_target_pairs={{0,8},{1,9},{2,10},{3,11},{4,12},{5,13},{6,14},{7,15},{8,0},{9,1},... | collective-permute-start | bytes 1572872 | tf_op jit(solution)/shard_map/ppermute | solution.py:451
  5.6 1.1 copy-start.15
  6.8 7.7 %collective-permute-start.1 = (bf16[528,256]{1,0:T(8,128)(2,1)S(1)}, bf16[528,256]{1,0:T(8,128)(2,1)S(1)}, u32[]{:S(2)}, u32[]{:S(2)}) collective-permute-start(bf16[528,256]{1,0:T(8,128)(2,1)S(1)} %get-tuple-element.71.after_ref), channel_id=1, source_target_pairs={{0,4},{1,5},{2,6},{3,7},{4,0},{5,1},{6,2},{7,3},{8,12},{9,13},{10,... | collective-permute-start | bytes 811016 | tf_op jit(solution)/shard_map/ppermute | solution.py:451
  8.3 19.5 %collective-permute-start.2 = (bf16[528,256]{1,0:T(8,128)(2,1)S(1)}, bf16[528,256]{1,0:T(8,128)(2,1)S(1)}, u32[]{:S(2)}, u32[]{:S(2)}) collective-permute-start(bf16[528,256]{1,0:T(8,128)(2,1)S(1)} %get-tuple-element.72.refs_0_), channel_id=1, source_target_pairs={{0,2},{1,3},{2,0},{3,1},{4,6},{5,7},{6,4},{7,5},{8,10},{9,11},{10,... | collective-permute-start | bytes 811016 | tf_op jit(solution)/shard_map/ppermute | solution.py:451
  14.5 13.3 %collective-permute-start.3 = (bf16[528,256]{1,0:T(8,128)(2,1)S(1)}, bf16[528,256]{1,0:T(8,128)(2,1)S(1)}, u32[]{:S(2)}, u32[]{:S(2)}) collective-permute-start(bf16[528,256]{1,0:T(8,128)(2,1)S(1)} %collective-permute-done.1.refs_1_), channel_id=1, source_target_pairs={{0,2},{1,3},{2,0},{3,1},{4,6},{5,7},{6,4},{7,5},{8,10},{9,11},{10,... | collective-permute-start | bytes 811016 | tf_op jit(solution)/shard_map/ppermute | solution.py:451
  16.8 1.2 copy-start.13
  18.0 1.2 copy-start.14
  19.8 1.3 copy-start.10
  27.8 1.1 copy-start.11
  28.9 7.5 %collective-permute-start.6 = (bf16[528,256]{1,0:T(8,128)(2,1)S(1)}, bf16[528,256]{1,0:T(8,128)(2,1)S(1)}, u32[]{:S(2)}, u32[]{:S(2)}) collective-permute-start(bf16[528,256]{1,0:T(8,128)(2,1)S(1)} %get-tuple-element.84), channel_id=1, source_target_pairs={{0,4},{1,5},{2,6},{3,7},{4,0},{5,1},{6,2},{7,3},{8,12},{9,13},{10,... | collective-permute-start | bytes 811016 | tf_op jit(solution)/shard_map/ppermute | solution.py:451
  30.4 16.2 %collective-permute-start.5 = (bf16[1024,256]{1,0:T(8,128)(2,1)}, bf16[1024,256]{1,0:T(8,128)(2,1)}, u32[]{:S(2)}, u32[]{:S(2)}) collective-permute-start(bf16[1024,256]{1,0:T(8,128)(2,1)} %collective-permute-done.token_ref), channel_id=1, source_target_pairs={{0,8},{1,9},{2,10},{3,11},{4,12},{5,13},{6,14},{7,15},{8,0},{9,1},... | collective-permute-start | bytes 1572872 | tf_op jit(solution)/shard_map/ppermute | solution.py:451
  31.9 11.3 %collective-permute-start.7 = (bf16[528,256]{1,0:T(8,128)(2,1)S(1)}, bf16[528,256]{1,0:T(8,128)(2,1)}, u32[]{:S(2)}, u32[]{:S(2)}) collective-permute-start(bf16[528,256]{1,0:T(8,128)(2,1)S(1)} %get-tuple-element.85.refs_0_.refs_2_), channel_id=1, source_target_pairs={{0,2},{1,3},{2,0},{3,1},{4,6},{5,7},{6,4},{7,5},{8,10},{9,11},{10,... | collective-permute-start | bytes 811016 | tf_op jit(solution)/shard_map/ppermute | solution.py:451
  35.4 7.8 %collective-permute-start.9 = (bf16[528,256]{1,0:T(8,128)(2,1)}, bf16[528,256]{1,0:T(8,128)(2,1)}, u32[]{:S(2)}, u32[]{:S(2)}) collective-permute-start(bf16[528,256]{1,0:T(8,128)(2,1)} %get-tuple-element.87), channel_id=1, source_target_pairs={{0,4},{1,5},{2,6},{3,7},{4,0},{5,1},{6,2},{7,3},{8,12},{9,13},{10,... | collective-permute-start | bytes 811016 | tf_op jit(solution)/shard_map/ppermute | solution.py:451
  35.9 10.8 %collective-permute-start.10 = (bf16[528,256]{1,0:T(8,128)(2,1)}, bf16[528,256]{1,0:T(8,128)(2,1)}, u32[]{:S(2)}, u32[]{:S(2)}) collective-permute-start(bf16[528,256]{1,0:T(8,128)(2,1)} %get-tuple-element.88.refs_0_), channel_id=1, source_target_pairs={{0,2},{1,3},{2,0},{3,1},{4,6},{5,7},{6,4},{7,5},{8,10},{9,11},{10,... | collective-permute-start | bytes 811016 | tf_op jit(solution)/shard_map/ppermute | solution.py:451
  36.4 13.9 %collective-permute-start.8 = (bf16[528,256]{1,0:T(8,128)(2,1)S(1)}, bf16[528,256]{1,0:T(8,128)(2,1)}, u32[]{:S(2)}, u32[]{:S(2)}) collective-permute-start(bf16[528,256]{1,0:T(8,128)(2,1)S(1)} %collective-permute-done.6.refs_1_.refs_3_), channel_id=1, source_target_pairs={{0,2},{1,3},{2,0},{3,1},{4,6},{5,7},{6,4},{7,5},{8,10},{9,11},{10,... | collective-permute-start | bytes 811016 | tf_op jit(solution)/shard_map/ppermute | solution.py:451
  37.9 51.7 %all-to-all-start = ((bf16[4,2,2,128,512]{4,3,2,1,0:T(8,128)(2,1)}), bf16[4,2,2,128,512]{4,3,2,1,0:T(8,128)(2,1)S(1)}, u32[]{:S(2)}, u32[]{:S(2)}) async-start(bf16[4,2,2,128,512]{4,3,2,1,0:T(8,128)(2,1)} %copy-done.10), calls=%async_computation | async-start | bytes 4194304 | tf_op jit(solution)/shard_map/all_to_all | solution.py:462
  43.2 24.5 %collective-permute-start.14 = (bf16[2112,256]{1,0:T(8,128)(2,1)}, bf16[2112,256]{1,0:T(8,128)(2,1)S(1)}, u32[]{:S(2)}, u32[]{:S(2)}) collective-permute-start(bf16[2112,256]{1,0:T(8,128)(2,1)} %pad_maximum_fusion), channel_id=1, source_target_pairs={{0,1},{1,0},{2,3},{3,2},{4,5},{5,4},{6,7},{7,6},{8,9},{9,8},{10,11... | collective-permute-start | bytes 3244040 | tf_op jit(solution)/shard_map/ppermute | solution.py:451
  51.5 16.2 %collective-permute-start.15 = (bf16[2112,256]{1,0:T(8,128)(2,1)S(1)}, bf16[2112,256]{1,0:T(8,128)(2,1)S(1)}, u32[]{:S(2)}, u32[]{:S(2)}) collective-permute-start(bf16[2112,256]{1,0:T(8,128)(2,1)S(1)} %pad_maximum_fusion.1), channel_id=1, source_target_pairs={{0,1},{1,0},{2,3},{3,2},{4,5},{5,4},{6,7},{7,6},{8,9},{9,8},{10,11... | collective-permute-start | bytes 3244040 | tf_op jit(solution)/shard_map/ppermute | solution.py:451
  52.7 29.0 %copy-start.16 = (bf16[528,256]{1,0:T(8,128)(2,1)}, bf16[528,256]{1,0:T(8,128)(2,1)S(1)}, u32[]{:S(2)}) copy-start(bf16[528,256]{1,0:T(8,128)(2,1)S(1)} %get-tuple-element.90.refs_0_.refs_2_) | copy-start | bytes 811012
  52.7 8.9 %collective-permute-start.11 = (bf16[528,256]{1,0:T(8,128)(2,1)S(1)}, bf16[528,256]{1,0:T(8,128)(2,1)S(1)}, u32[]{:S(2)}, u32[]{:S(2)}) collective-permute-start(bf16[528,256]{1,0:T(8,128)(2,1)S(1)} %get-tuple-element.91), channel_id=1, source_target_pairs={{0,4},{1,5},{2,6},{3,7},{4,0},{5,1},{6,2},{7,3},{8,12},{9,13},{10,... | collective-permute-start | bytes 811016 | tf_op jit(solution)/shard_map/ppermute | solution.py:451
  53.3 9.3 %collective-permute-start.12 = (bf16[528,256]{1,0:T(8,128)(2,1)S(1)}, bf16[528,256]{1,0:T(8,128)(2,1)S(1)}, u32[]{:S(2)}, u32[]{:S(2)}) collective-permute-start(bf16[528,256]{1,0:T(8,128)(2,1)S(1)} %get-tuple-element.90.refs_0_.refs_2_), channel_id=1, source_target_pairs={{0,2},{1,3},{2,0},{3,1},{4,6},{5,7},{6,4},{7,5},{8,10},{9,11},{10,... | collective-permute-start | bytes 811016 | tf_op jit(solution)/shard_map/ppermute | solution.py:451
  54.8 12.9 %collective-permute-start.13 = (bf16[528,256]{1,0:T(8,128)(2,1)}, bf16[528,256]{1,0:T(8,128)(2,1)S(1)}, u32[]{:S(2)}, u32[]{:S(2)}) collective-permute-start(bf16[528,256]{1,0:T(8,128)(2,1)} %collective-permute-done.9.refs_1_), channel_id=1, source_target_pairs={{0,2},{1,3},{2,0},{3,1},{4,6},{5,7},{6,4},{7,5},{8,10},{9,11},{10,... | collective-permute-start | bytes 811016 | tf_op jit(solution)/shard_map/ppermute | solution.py:451
  61.7 20.0 %copy-start.18 = (bf16[528,256]{1,0:T(8,128)(2,1)}, bf16[528,256]{1,0:T(8,128)(2,1)S(1)}, u32[]{:S(2)}) copy-start(bf16[528,256]{1,0:T(8,128)(2,1)S(1)} %collective-permute-done.11.refs_1_.refs_3_) | copy-start | bytes 811012
  68.9 5.7 %copy-start.12 = (bf16[528,256]{1,0:T(8,128)(2,1)S(1)}, bf16[528,256]{1,0:T(8,128)(2,1)}, u32[]{:S(2)}) copy-start(bf16[528,256]{1,0:T(8,128)(2,1)} %copy-done.11) | copy-start | bytes 811012
  68.9 9.6 %collective-permute-start.17 = (bf16[2112,256]{1,0:T(8,128)(2,1)S(1)}, bf16[2112,256]{1,0:T(8,128)(2,1)S(1)}, u32[]{:S(2)}, u32[]{:S(2)}) collective-permute-start(bf16[2112,256]{1,0:T(8,128)(2,1)S(1)} %pad_maximum_fusion.2), channel_id=1, source_target_pairs={{0,1},{1,0},{2,3},{3,2},{4,5},{5,4},{6,7},{7,6},{8,9},{9,8},{10,11... | collective-permute-start | bytes 3244040 | tf_op jit(solution)/shard_map/ppermute | solution.py:451
  69.0 8.3 %collective-permute-start.18 = (bf16[528,256]{1,0:T(8,128)(2,1)S(1)}, bf16[528,256]{1,0:T(8,128)(2,1)S(1)}, u32[]{:S(2)}, u32[]{:S(2)}) collective-permute-start(bf16[528,256]{1,0:T(8,128)(2,1)S(1)} %get-tuple-element.90.refs_0_.refs_2_), channel_id=1, source_target_pairs={{0,1},{1,0},{2,3},{3,2},{4,5},{5,4},{6,7},{7,6},{8,9},{9,8},{10,11... | collective-permute-start | bytes 811016 | tf_op jit(solution)/shard_map/ppermute | solution.py:451
  69.5 7.8 %collective-permute-start.19 = (bf16[528,256]{1,0:T(8,128)(2,1)S(1)}, bf16[528,256]{1,0:T(8,128)(2,1)S(1)}, u32[]{:S(2)}, u32[]{:S(2)}) collective-permute-start(bf16[528,256]{1,0:T(8,128)(2,1)S(1)} %collective-permute-done.12.refs_2_), channel_id=1, source_target_pairs={{0,1},{1,0},{2,3},{3,2},{4,5},{5,4},{6,7},{7,6},{8,9},{9,8},{10,11... | collective-permute-start | bytes 811016 | tf_op jit(solution)/shard_map/ppermute | solution.py:451
  69.6 7.7 %collective-permute-start.20 = (bf16[528,256]{1,0:T(8,128)(2,1)S(1)}, bf16[528,256]{1,0:T(8,128)(2,1)S(1)}, u32[]{:S(2)}, u32[]{:S(2)}) collective-permute-start(bf16[528,256]{1,0:T(8,128)(2,1)S(1)} %collective-permute-done.11.refs_1_.refs_3_), channel_id=1, source_target_pairs={{0,1},{1,0},{2,3},{3,2},{4,5},{5,4},{6,7},{7,6},{8,9},{9,8},{10,11... | collective-permute-start | bytes 811016 | tf_op jit(solution)/shard_map/ppermute | solution.py:451
  70.0 8.5 %collective-permute-start.16 = (bf16[528,256]{1,0:T(8,128)(2,1)S(1)}, bf16[528,256]{1,0:T(8,128)(2,1)S(1)}, u32[]{:S(2)}, u32[]{:S(2)}) collective-permute-start(bf16[528,256]{1,0:T(8,128)(2,1)S(1)} %collective-permute-done.11.refs_1_.refs_3_), channel_id=1, source_target_pairs={{0,2},{1,3},{2,0},{3,1},{4,6},{5,7},{6,4},{7,5},{8,10},{9,11},{10,... | collective-permute-start | bytes 811016 | tf_op jit(solution)/shard_map/ppermute | solution.py:451
  73.3 1.4 copy-start.1
  75.9 1.4 copy-start.4
  78.5 3.2 %collective-permute-start.21 = (bf16[528,256]{1,0:T(8,128)(2,1)S(1)}, bf16[528,256]{1,0:T(8,128)(2,1)S(1)}, u32[]{:S(2)}, u32[]{:S(2)}) collective-permute-start(bf16[528,256]{1,0:T(8,128)(2,1)S(1)} %collective-permute-done.16.refs_3_), channel_id=1, source_target_pairs={{0,1},{1,0},{2,3},{3,2},{4,5},{5,4},{6,7},{7,6},{8,9},{9,8},{10,11... | collective-permute-start | bytes 811016 | tf_op jit(solution)/shard_map/ppermute | solution.py:451
  80.3 1.4 %copy-start.6 = (bf16[4,512,512]{2,1,0:T(8,128)(2,1)}, bf16[4,512,512]{2,1,0:T(8,128)(2,1)S(1)}, u32[]{:S(2)}) copy-start(bf16[4,512,512]{2,1,0:T(8,128)(2,1)S(1)} %shard_map.89.refs_0_) | copy-start | bytes 6291460
  83.0 1.3 copy-start.8
  89.6 1.6 %copy-start.2 = (bf16[4,512,512]{2,1,0:T(8,128)(2,1)S(1)}, bf16[4,512,512]{2,1,0:T(8,128)(2,1)}, u32[]{:S(2)}) copy-start(bf16[4,512,512]{2,1,0:T(8,128)(2,1)} %copy-done.1) | copy-start | bytes 6291460
  91.2 1.6 %copy-start.5 = (bf16[4,512,512]{2,1,0:T(8,128)(2,1)S(1)}, bf16[4,512,512]{2,1,0:T(8,128)(2,1)}, u32[]{:S(2)}) copy-start(bf16[4,512,512]{2,1,0:T(8,128)(2,1)} %copy-done.4) | copy-start | bytes 6291460
  92.8 2.8 %copy-start.7 = (bf16[4,512,512]{2,1,0:T(8,128)(2,1)S(1)}, bf16[4,512,512]{2,1,0:T(8,128)(2,1)}, u32[]{:S(2)}) copy-start(bf16[4,512,512]{2,1,0:T(8,128)(2,1)} %copy-done.6) | copy-start | bytes 6291460
  92.8 2.8 %copy-start.9 = (bf16[4,512,512]{2,1,0:T(8,128)(2,1)S(1)}, bf16[4,512,512]{2,1,0:T(8,128)(2,1)}, u32[]{:S(2)}) copy-start(bf16[4,512,512]{2,1,0:T(8,128)(2,1)} %copy-done.8) | copy-start | bytes 6291460
  94.1 9.3 %collective-permute-start.22 = (bf16[128,1024]{1,0:T(8,128)(2,1)S(1)}, bf16[128,1024]{1,0:T(8,128)(2,1)S(1)}, u32[]{:S(2)}, u32[]{:S(2)}) collective-permute-start(bf16[128,1024]{1,0:T(8,128)(2,1)S(1)} %get-tuple-element.119), channel_id=1, source_target_pairs={{0,4},{1,5},{2,6},{3,7},{4,0},{5,1},{6,2},{7,3},{8,12},{9,13},{10,... | collective-permute-start | bytes 786440 | tf_op jit(solution)/shard_map/ppermute | solution.py:451
  96.9 10.1 %collective-permute-start.23 = (bf16[128,1024]{1,0:T(8,128)(2,1)S(1)}, bf16[128,1024]{1,0:T(8,128)(2,1)S(1)}, u32[]{:S(2)}, u32[]{:S(2)}) collective-permute-start(bf16[128,1024]{1,0:T(8,128)(2,1)S(1)} %get-tuple-element.123), channel_id=1, source_target_pairs={{0,4},{1,5},{2,6},{3,7},{4,0},{5,1},{6,2},{7,3},{8,12},{9,13},{10,... | collective-permute-start | bytes 786440 | tf_op jit(solution)/shard_map/ppermute | solution.py:451
  97.8 1.6 %copy-start.3 = (bf16[4,512,512]{2,1,0:T(8,128)(2,1)S(1)}, bf16[4,512,512]{2,1,0:T(8,128)(2,1)}, u32[]{:S(2)}) copy-start(bf16[4,512,512]{2,1,0:T(8,128)(2,1)} %copy-done.1) | copy-start | bytes 6291460
  100.7 8.3 %copy-start.17 = (bf16[528,256]{1,0:T(8,128)(2,1)S(1)}, bf16[528,256]{1,0:T(8,128)(2,1)}, u32[]{:S(2)}) copy-start(bf16[528,256]{1,0:T(8,128)(2,1)} %copy-done.16) | copy-start | bytes 811012
  100.7 8.3 %copy-start.19 = (bf16[528,256]{1,0:T(8,128)(2,1)S(1)}, bf16[528,256]{1,0:T(8,128)(2,1)}, u32[]{:S(2)}) copy-start(bf16[528,256]{1,0:T(8,128)(2,1)} %copy-done.18) | copy-start | bytes 811012
  100.7 8.3 %copy-start.20 = (f32[128,256]{1,0:T(8,128)S(1)}, f32[128,256]{1,0:T(8,128)}, u32[]{:S(2)}) copy-start(f32[128,256]{1,0:T(8,128)} %dynamic-slice_convert_fusion.taps_ref) | copy-start | bytes 393220
  107.0 9.2 %collective-permute-start.24 = (bf16[128,1024]{1,0:T(8,128)(2,1)S(1)}, bf16[128,1024]{1,0:T(8,128)(2,1)S(1)}, u32[]{:S(2)}, u32[]{:S(2)}) collective-permute-start(bf16[128,1024]{1,0:T(8,128)(2,1)S(1)} %get-tuple-element.134), channel_id=1, source_target_pairs={{0,4},{1,5},{2,6},{3,7},{4,0},{5,1},{6,2},{7,3},{8,12},{9,13},{10,... | collective-permute-start | bytes 786440 | tf_op jit(solution)/shard_map/ppermute | solution.py:451
  108.5 10.5 %collective-permute-start.25 = (bf16[128,1024]{1,0:T(8,128)(2,1)S(1)}, bf16[128,1024]{1,0:T(8,128)(2,1)S(1)}, u32[]{:S(2)}, u32[]{:S(2)}) collective-permute-start(bf16[128,1024]{1,0:T(8,128)(2,1)S(1)} %get-tuple-element.136), channel_id=1, source_target_pairs={{0,4},{1,5},{2,6},{3,7},{4,0},{5,1},{6,2},{7,3},{8,12},{9,13},{10,... | collective-permute-start | bytes 786440 | tf_op jit(solution)/shard_map/ppermute | solution.py:451

commit v5 on v4

--- a/solution.py
+++ b/solution.py
@@ -322,14 +322,20 @@
 
 def band_kernel(
     taps_blocks, tall, flag_ref, first_ref, taps_ref, skip_ref, early_ref, mine_ref, theirs_ref,
-    place_ref, *refs
+    last_mine_ref, last_theirs_ref, place_ref, *refs
 ):
     shifted = refs[-taps_blocks - 1 :]
     out_ref, packed_ref, whole, band = refs[-taps_blocks - 5 : -taps_blocks - 1]
     chan = taps_ref.shape[0]
     total = whole.shape[1]
     pieces = total // LANES
-    summed = (mine_ref[...] + theirs_ref[...].astype(jnp.float32)).astype(jnp.bfloat16)
+    summed = jnp.concatenate(
+        [
+            (mine[...] + theirs[...].astype(jnp.float32)).astype(jnp.bfloat16)
+            for mine, theirs in ((mine_ref, theirs_ref), (last_mine_ref, last_theirs_ref))
+        ],
+        axis=1,
+    )
     summed = with_tokens(first_ref[0], tall, summed, refs[: -taps_blocks - 5])
     moved = at_places(summed, place_ref[...], total) + early_ref[...].astype(jnp.float32)
     whole[...] = moved[0:chan]
@@ -381,7 +387,7 @@
         out_ref[:, lanes] = (band[rows, :] + skip * whole[:, lanes]).astype(jnp.bfloat16)
 
 
-def band_of(flags, first, taps, skip, early, mine, theirs, places, tall, tokens):
+def band_of(flags, first, taps, skip, early, late, last, places, tall, tokens):
     chan, tap_count = taps.shape
     total = early.shape[1]
     taps_blocks = tap_count // LANES
@@ -390,7 +396,7 @@
     return pl.pallas_call(
         functools.partial(band_kernel, taps_blocks, tall),
         out_shape=[out, out],
-        in_specs=[SMEM, SMEM] + [VMEM] * (6 + len(tokens)),
+        in_specs=[SMEM, SMEM] + [VMEM] * (8 + len(tokens)),
         out_specs=[VMEM, VMEM],
         scratch_shapes=[pltpu.VMEM((chan, total), jnp.float32)]
         + [pltpu.VMEM(tower, jnp.float32)] * (taps_blocks + 2),
@@ -398,7 +404,7 @@
         cost_estimate=pl.CostEstimate(
             flops=3 * chan * total * total, bytes_accessed=16 * chan * total, transcendentals=0
         ),
-    )(flags, first, taps, skip, early, mine, theirs, places, *tokens)
+    )(flags, first, taps, skip, early, *late, *last, places, *tokens)
 
 
 def mix_kernel(z_ref, packed_ref, early_ref, mine_ref, theirs_ref, place_ref, out_ref):
@@ -502,7 +508,7 @@
     got0_far = to_owner(got0, far_owner)
     most0 = jnp.concatenate([kept0, got0, kept0_far, got0_far], axis=0)
     packed_weights = pack_weights(give0, [w_value, w_gate], line)
-    packed_weights, by_near = tie(packed_weights, by_near)
+    packed_weights, by_near, most0 = tie(packed_weights, by_near, most0)
     kept1, give1 = halve(which, by_near)
     small = picks, gains, taps, skip, flags, row_first, places, which
     by_both = to_pair(by_far, near_pair)
@@ -544,24 +550,27 @@
     )
     normed3, weights = tie(normed3, weights)
 
-    cut = 2 * wide
-    value0, far0 = projected(0, [normed0, normed1])
+    value0, far0 = projected(0, [normed0])
     theirs0 = across(far0)
-    value0, normed2 = tie(value0, normed2)
-    value2, far2 = projected(0, [normed2, normed3])
-    theirs2 = across(far2)
-    normed0, value2 = tie(normed0, value2)
+    value0, normed1 = tie(value0, normed1)
+    value1, far1 = projected(0, [normed1, normed2])
+    theirs1 = across(far1)
+    value1, normed3, theirs0 = tie(value1, normed3, theirs0)
+    value3, far3 = projected(0, [normed3])
+    theirs3 = across(far3)
+    normed0, normed3, value3 = tie(normed0, normed3, value3)
     gate0, gate_far0 = projected(1, [normed0, normed1])
     gate2, gate_far2 = projected(1, [normed2, normed3])
     early = place(
-        row_first, total_rows, value0, theirs0, places[:, :cut], tall, [kept0, got0, kept1, got1]
-    )
-    early, theirs2, gate_far0, gate_far2 = tie(early, theirs2, gate_far0, gate_far2)
+        row_first, total_rows, value0, theirs0, places[:, :wide], tall, [kept0, got0]
+    )
+    theirs1, gate_far0, gate_far2 = tie(theirs1, gate_far0, gate_far2)
     gate_theirs0, gate_theirs2 = across(gate_far0), across(gate_far2)
     banded, packed = band_of(
-        flags, row_first, taps, skip, early, value2, theirs2, places[:, cut:], tall,
-        [kept2, got2, kept3, got3],
-    )
+        flags, row_first, taps, skip, early, (value1, theirs1), (value3, theirs3),
+        places[:, wide:], tall, [kept1, got1, kept2, got2, kept3, got3],
+    )
+    cut = 2 * wide
     early = place(row_first, total_rows, gate0, gate_theirs0, places[:, :cut])
     mixed = mix(banded, packed, early, gate2, gate_theirs2, places[:, cut:], shards)
     owners = [[number(zz, xx, mm) for xx in range(2) for zz in range(line)] for mm in range(groups)]

time: 138 us -> 134 us (0.971)
  waiting for transfers between devices: 38.2 us -> 32.6 us
  starting transfers between devices: 32.3 us -> 34.2 us
  local copies, waits for them, and re-layouts: 17.3 us -> 15.4 us
  blocking collectives: 15.5 us -> 17.2 us
    all_to_all x1, waiting for transfers between devices: 5.33 us -> 1.41 us  [along_line(): lax.all_to_all(array, AXES, split_axis=0, concat_axis=0, tiled=True, axis...]
    ppermute x26 -> x27, starting transfers between devices: 27.1 us -> 29.3 us  [send(): return lax.ppermute(array, AXES, pairs)]
    unnamed x44, local copies, waits for them, and re-layouts: 14.6 us -> 12.7 us
    all_to_all x1, blocking collectives: 15.5 us -> 17.2 us  [on_device_line(): lax.all_to_all(mixed, AXES, split_axis=0, concat_axis=0, tiled=True, axis...]
    ppermute x26 -> x27, waiting for transfers between devices: 32.9 us -> 31.2 us  [send(): return lax.ppermute(array, AXES, pairs)]
    pallas_call x4 -> x5, Pallas kernels: 5.02 us -> 5.2 us  [project(): pl.pallas_call(functools.partial(project_kernel, number, row_count), out_...]
  transfers between devices with their start and end apart: 27 -> 28, of which waited for: 12 -> 14; matrix products, arithmetic and copies ran while one was open for 7% -> 7% of each run, Pallas kernels for 17% -> 18%
where the time goes in v5:
time: 134 us; the launch traced here: 133 us
  starting transfers between devices  34.2 us (26%)
  waiting for transfers between devices  32.6 us (24%)
  Pallas kernels  26.5 us (20%)
  blocking collectives  17.2 us (13%)
  local copies, waits for them, and re-layouts  15.4 us (11%)
  other arithmetic  6.62 us (5%)
    ppermute x27, waiting for transfers between devices, send(): return lax.ppermute(array, AXES, pairs)  31.2 us
    ppermute x27, starting transfers between devices, send(): return lax.ppermute(array, AXES, pairs)  29.3 us
    all_to_all x1, blocking collectives, on_device_line(): lax.all_to_all(mixed, AXES, split_axis=0, concat_axis=0, tiled=True, axis...  17.2 us
    unnamed x44, local copies, waits for them, and re-layouts  12.7 us
    pallas_call x1, Pallas kernels, band_of(): pl.pallas_call(functools.partial(band_kernel, taps_blocks, tall), out_sha...  7.59 us
    pallas_call x4, Pallas kernels, scale(): pl.pallas_call(functools.partial(scale_kernel, height), out_shape=jax.Sha...  6.07 us
    pallas_call x5, Pallas kernels, project(): pl.pallas_call(functools.partial(project_kernel, number, row_count), out_...  5.2 us
    all_to_all x1, starting transfers between devices, along_line(): lax.all_to_all(array, AXES, split_axis=0, concat_axis=0, tiled=True, axis...  4.88 us
  transfers between devices with their start and end apart: 28, of which 14 were waited for; matrix products, arithmetic and copies ran while one was open for 7% of the time, Pallas kernels for 18%

profile of v5, /device:TPU:0, one launch (start us, length us, event | category | flops | bytes accessed | tf_op | source)
XLA Modules:
  0.0 132.9 jit_solution(10794012914498633339)
XLA Ops:
  0.0 3.0 %collective-permute-start.4 = (bf16[1024,256]{1,0:T(8,128)(2,1)}, bf16[1024,256]{1,0:T(8,128)(2,1)S(1)}, u32[]{:S(2)}, u32[]{:S(2)}) collective-permute-start(bf16[1024,256]{1,0:T(8,128)(2,1)} %token_ref.1), channel_id=1, source_target_pairs={{0,8},{1,9},{2,10},{3,11},{4,12},{5,13},{6,14},{7,15},{8,0},{9,1},... | collective-permute-start | bytes 1572872 | tf_op jit(solution)/shard_map/ppermute | solution.py:457
  3.0 2.6 %collective-permute-start = (bf16[1024,256]{1,0:T(8,128)(2,1)}, bf16[1024,256]{1,0:T(8,128)(2,1)}, u32[]{:S(2)}, u32[]{:S(2)}) collective-permute-start(bf16[1024,256]{1,0:T(8,128)(2,1)} %token_ref.1), channel_id=1, source_target_pairs={{0,16},{1,17},{2,18},{3,19},{4,20},{5,21},{6,22},{7,23},{8,24},{9,... | collective-permute-start | bytes 1572872 | tf_op jit(solution)/shard_map/ppermute | solution.py:457
  6.8 1.6 %collective-permute-start.1 = (bf16[528,256]{1,0:T(8,128)(2,1)S(1)}, bf16[528,256]{1,0:T(8,128)(2,1)S(1)}, u32[]{:S(2)}, u32[]{:S(2)}) collective-permute-start(bf16[528,256]{1,0:T(8,128)(2,1)S(1)} %get-tuple-element.77.after_ref), channel_id=1, source_target_pairs={{0,4},{1,5},{2,6},{3,7},{4,0},{5,1},{6,2},{7,3},{8,12},{9,13},{10,... | collective-permute-start | bytes 811016 | tf_op jit(solution)/shard_map/ppermute | solution.py:457
  8.3 1.5 %collective-permute-start.2 = (bf16[528,256]{1,0:T(8,128)(2,1)S(1)}, bf16[528,256]{1,0:T(8,128)(2,1)S(1)}, u32[]{:S(2)}, u32[]{:S(2)}) collective-permute-start(bf16[528,256]{1,0:T(8,128)(2,1)S(1)} %get-tuple-element.78.refs_0_), channel_id=1, source_target_pairs={{0,2},{1,3},{2,0},{3,1},{4,6},{5,7},{6,4},{7,5},{8,10},{9,11},{10,... | collective-permute-start | bytes 811016 | tf_op jit(solution)/shard_map/ppermute | solution.py:457
  14.5 1.5 %collective-permute-start.3 = (bf16[528,256]{1,0:T(8,128)(2,1)S(1)}, bf16[528,256]{1,0:T(8,128)(2,1)S(1)}, u32[]{:S(2)}, u32[]{:S(2)}) collective-permute-start(bf16[528,256]{1,0:T(8,128)(2,1)S(1)} %collective-permute-done.1.refs_1_), channel_id=1, source_target_pairs={{0,2},{1,3},{2,0},{3,1},{4,6},{5,7},{6,4},{7,5},{8,10},{9,11},{10,... | collective-permute-start | bytes 811016 | tf_op jit(solution)/shard_map/ppermute | solution.py:457
  16.2 1.2 copy-done.13
  17.4 1.2 copy-done.14
  19.3 1.3 %copy-done.10 = bf16[4,2,2,128,512]{4,3,2,1,0:T(8,128)(2,1)} copy-done((bf16[4,2,2,128,512]{4,3,2,1,0:T(8,128)(2,1)}, bf16[4,2,2,128,512]{4,3,2,1,0:T(8,128)(2,1)S(1)}, u32[]{:S(2)}) %copy-start.10) | copy-done | bytes 2097176
  21.2 1.5 %dynamic-slice_convert_fusion.taps_ref = f32[128,256]{1,0:T(8,128)} fusion(bf16[1024,256]{1,0:T(8,128)(2,1)} %param.13, s32[]{:T(128)S(6)} %select_n.50), kind=kLoop, calls=%fused_computation.5 | loop fusion | flops 32768 | bytes 196612 | tf_op jit(solution)/shard_map/convert_element_type | solution.py:485
  23.8 2.5 %collective-permute-done.4.token_ref = bf16[1024,256]{1,0:T(8,128)(2,1)S(1)} collective-permute-done((bf16[1024,256]{1,0:T(8,128)(2,1)}, bf16[1024,256]{1,0:T(8,128)(2,1)S(1)}, u32[]{:S(2)}, u32[]{:S(2)}) %collective-permute-start.4) | collective-permute-done | bytes 524320 | tf_op jit(solution)/shard_map/ppermute | solution.py:457
  26.4 2.6 %collective-permute-done.token_ref = bf16[1024,256]{1,0:T(8,128)(2,1)} collective-permute-done((bf16[1024,256]{1,0:T(8,128)(2,1)}, bf16[1024,256]{1,0:T(8,128)(2,1)}, u32[]{:S(2)}, u32[]{:S(2)}) %collective-permute-start) | collective-permute-done | bytes 524320 | tf_op jit(solution)/shard_map/ppermute | solution.py:457
  28.9 1.5 %collective-permute-start.6 = (bf16[528,256]{1,0:T(8,128)(2,1)S(1)}, bf16[528,256]{1,0:T(8,128)(2,1)S(1)}, u32[]{:S(2)}, u32[]{:S(2)}) collective-permute-start(bf16[528,256]{1,0:T(8,128)(2,1)S(1)} %get-tuple-element.91), channel_id=1, source_target_pairs={{0,4},{1,5},{2,6},{3,7},{4,0},{5,1},{6,2},{7,3},{8,12},{9,13},{10,... | collective-permute-start | bytes 811016 | tf_op jit(solution)/shard_map/ppermute | solution.py:457
  30.8 2.0 %shard_map.85 = (bf16[528,256]{1,0:T(8,128)(2,1)}, bf16[528,256]{1,0:T(8,128)(2,1)}) custom-call(s32[1]{0:T(128)} %bitcast.x_ref, bf16[1024,256]{1,0:T(8,128)(2,1)} %collective-permute-done.token_ref), custom_call_target="tpu_custom_call" | custom-call | flops 524288 | bytes 1048576 | tf_op jit(solution)/shard_map/pallas_call | solution.py:151
  32.8 1.5 %collective-permute-start.10 = (bf16[528,256]{1,0:T(8,128)(2,1)}, bf16[528,256]{1,0:T(8,128)(2,1)}, u32[]{:S(2)}, u32[]{:S(2)}) collective-permute-start(bf16[528,256]{1,0:T(8,128)(2,1)} %get-tuple-element.95.refs_0_.refs_2_), channel_id=1, source_target_pairs={{0,2},{1,3},{2,0},{3,1},{4,6},{5,7},{6,4},{7,5},{8,10},{9,11},{10,... | collective-permute-start | bytes 811016 | tf_op jit(solution)/shard_map/ppermute | solution.py:457
  35.5 2.6 %collective-permute-start.8 = (bf16[528,256]{1,0:T(8,128)(2,1)S(1)}, bf16[528,256]{1,0:T(8,128)(2,1)}, u32[]{:S(2)}, u32[]{:S(2)}) collective-permute-start(bf16[528,256]{1,0:T(8,128)(2,1)S(1)} %collective-permute-done.6.refs_1_), channel_id=1, source_target_pairs={{0,2},{1,3},{2,0},{3,1},{4,6},{5,7},{6,4},{7,5},{8,10},{9,11},{10,... | collective-permute-start | bytes 811016 | tf_op jit(solution)/shard_map/ppermute | solution.py:457
  38.1 4.9 %all-to-all-start = ((bf16[4,2,2,128,512]{4,3,2,1,0:T(8,128)(2,1)}), bf16[4,2,2,128,512]{4,3,2,1,0:T(8,128)(2,1)S(1)}, u32[]{:S(2)}, u32[]{:S(2)}) async-start(bf16[4,2,2,128,512]{4,3,2,1,0:T(8,128)(2,1)} %copy-done.10), calls=%async_computation | async-start | bytes 4194304 | tf_op jit(solution)/shard_map/all_to_all | solution.py:468
  43.0 5.4 %collective-permute-done.7.refs_2_ = bf16[528,256]{1,0:T(8,128)(2,1)} collective-permute-done((bf16[528,256]{1,0:T(8,128)(2,1)S(1)}, bf16[528,256]{1,0:T(8,128)(2,1)}, u32[]{:S(2)}, u32[]{:S(2)}) %collective-permute-start.7) | collective-permute-done | bytes 270368 | tf_op jit(solution)/shard_map/ppermute | solution.py:457
  48.4 3.1 %collective-permute-done.8.refs_3_ = bf16[528,256]{1,0:T(8,128)(2,1)} collective-permute-done((bf16[528,256]{1,0:T(8,128)(2,1)S(1)}, bf16[528,256]{1,0:T(8,128)(2,1)}, u32[]{:S(2)}, u32[]{:S(2)}) %collective-permute-start.8) | collective-permute-done | bytes 270368 | tf_op jit(solution)/shard_map/ppermute | solution.py:457
  51.5 1.1 pad_maximum_fusion.1
  52.7 1.2 shard_map.86
  54.4 1.5 %collective-permute-start.12 = (bf16[528,256]{1,0:T(8,128)(2,1)S(1)}, bf16[528,256]{1,0:T(8,128)(2,1)S(1)}, u32[]{:S(2)}, u32[]{:S(2)}) collective-permute-start(bf16[528,256]{1,0:T(8,128)(2,1)S(1)} %get-tuple-element.97.refs_0_.refs_4_), channel_id=1, source_target_pairs={{0,2},{1,3},{2,0},{3,1},{4,6},{5,7},{6,4},{7,5},{8,10},{9,11},{10,... | collective-permute-start | bytes 811016 | tf_op jit(solution)/shard_map/ppermute | solution.py:457
  56.4 6.3 %collective-permute-done.11.refs_1_.refs_5_ = bf16[528,256]{1,0:T(8,128)(2,1)S(1)} collective-permute-done((bf16[528,256]{1,0:T(8,128)(2,1)S(1)}, bf16[528,256]{1,0:T(8,128)(2,1)S(1)}, u32[]{:S(2)}, u32[]{:S(2)}) %collective-permute-start.11) | collective-permute-done | bytes 270368 | tf_op jit(solution)/shard_map/ppermute | solution.py:457
  63.7 5.1 %collective-permute-done.13.refs_3_ = bf16[528,256]{1,0:T(8,128)(2,1)S(1)} collective-permute-done((bf16[528,256]{1,0:T(8,128)(2,1)}, bf16[528,256]{1,0:T(8,128)(2,1)S(1)}, u32[]{:S(2)}, u32[]{:S(2)}) %collective-permute-start.13) | collective-permute-done | bytes 270368 | tf_op jit(solution)/shard_map/ppermute | solution.py:457
  68.8 1.2 pad_maximum_fusion.2
  70.6 1.7 %collective-permute-start.16 = (bf16[528,256]{1,0:T(8,128)(2,1)S(1)}, bf16[528,256]{1,0:T(8,128)(2,1)S(1)}, u32[]{:S(2)}, u32[]{:S(2)}) collective-permute-start(bf16[528,256]{1,0:T(8,128)(2,1)S(1)} %collective-permute-done.11.refs_1_.refs_5_), channel_id=1, source_target_pairs={{0,2},{1,3},{2,0},{3,1},{4,6},{5,7},{6,4},{7,5},{8,10},{9,11},{10,... | collective-permute-start | bytes 811016 | tf_op jit(solution)/shard_map/ppermute | solution.py:457
  72.8 1.7 %shard_map.88.refs_0_.refs_1_ = bf16[4,512,512]{2,1,0:T(8,128)(2,1)S(1)} custom-call(s32[4]{0:T(128)S(1)} %pad_add_fusion.1.pick_ref, f32[8,512]{1,0:T(8,128)S(1)} %pad.4.gain_ref, bf16[528,256]{1,0:T(8,128)(2,1)S(1)} %get-tuple-element.92.refs_0_, bf16[528,256]{1,0:T(8,128)(2,1)S(1)} %collective-permute-done.6.refs_1_, ...), custom_call_target="tpu_custom_call" | custom-call | flops 2097152 | bytes 4194304 | tf_op jit(solution)/shard_map/pallas_call | solution.py:218
  74.6 1.3 %copy-done.1 = bf16[4,512,512]{2,1,0:T(8,128)(2,1)} copy-done((bf16[4,512,512]{2,1,0:T(8,128)(2,1)}, bf16[4,512,512]{2,1,0:T(8,128)(2,1)S(1)}, u32[]{:S(2)}) %copy-start.1) | copy-done | bytes 2097176
  75.9 1.3 shard_map.87.refs_0_
  77.2 1.4 %copy-done.5 = bf16[4,512,512]{2,1,0:T(8,128)(2,1)} copy-done((bf16[4,512,512]{2,1,0:T(8,128)(2,1)}, bf16[4,512,512]{2,1,0:T(8,128)(2,1)S(1)}, u32[]{:S(2)}) %copy-start.5) | copy-done | bytes 2097176
  79.2 1.8 %shard_map.89.refs_1_.refs_0_ = bf16[4,512,512]{2,1,0:T(8,128)(2,1)S(1)} custom-call(s32[4]{0:T(128)S(1)} %pad_add_fusion.1.pick_ref, f32[8,512]{1,0:T(8,128)S(1)} %pad.4.gain_ref, bf16[528,256]{1,0:T(8,128)(2,1)} %get-tuple-element.95.refs_0_.refs_2_, bf16[528,256]{1,0:T(8,128)(2,1)} %collective-permute-done.9.refs_1_.refs_3_, ...), custom_call_target="tpu_custom_call" | custom-call | flops 2097152 | bytes 4194304 | tf_op jit(solution)/shard_map/pallas_call | solution.py:218
  81.0 1.4 %copy-done.3 = bf16[4,512,512]{2,1,0:T(8,128)(2,1)} copy-done((bf16[4,512,512]{2,1,0:T(8,128)(2,1)}, bf16[4,512,512]{2,1,0:T(8,128)(2,1)S(1)}, u32[]{:S(2)}) %copy-start.3) | copy-done | bytes 2097176
  82.4 1.3 shard_map.90.refs_0_.refs_1_
  83.6 1.3 copy-done.8
  85.0 1.4 %all-to-all-done.weight_ref = bf16[4,2,2,128,512]{4,3,2,1,0:T(8,128)(2,1)S(1)} async-done(((bf16[4,2,2,128,512]{4,3,2,1,0:T(8,128)(2,1)}), bf16[4,2,2,128,512]{4,3,2,1,0:T(8,128)(2,1)S(1)}, u32[]{:S(2)}, u32[]{:S(2)}) %all-to-all-start) | async-done | bytes 2097184 | tf_op jit(solution)/shard_map/all_to_all | solution.py:468
  86.4 1.6 %copy-done.6 = bf16[4,512,512]{2,1,0:T(8,128)(2,1)S(1)} copy-done((bf16[4,512,512]{2,1,0:T(8,128)(2,1)S(1)}, bf16[4,512,512]{2,1,0:T(8,128)(2,1)}, u32[]{:S(2)}) %copy-start.6) | copy-done | bytes 2097176
  88.7 1.6 %collective-permute-start.22 = (bf16[128,512]{1,0:T(8,128)(2,1)S(1)}, bf16[128,512]{1,0:T(8,128)(2,1)S(1)}, u32[]{:S(2)}, u32[]{:S(2)}) collective-permute-start(bf16[128,512]{1,0:T(8,128)(2,1)S(1)} %get-tuple-element.129), channel_id=1, source_target_pairs={{0,4},{1,5},{2,6},{3,7},{4,0},{5,1},{6,2},{7,3},{8,12},{9,13},{10,... | collective-permute-start | bytes 393224 | tf_op jit(solution)/shard_map/ppermute | solution.py:457
  90.2 1.3 shard_map.92
  91.5 1.5 %collective-permute-start.23 = (bf16[128,1024]{1,0:T(8,128)(2,1)S(1)}, bf16[128,1024]{1,0:T(8,128)(2,1)S(1)}, u32[]{:S(2)}, u32[]{:S(2)}) collective-permute-start(bf16[128,1024]{1,0:T(8,128)(2,1)S(1)} %get-tuple-element.133), channel_id=1, source_target_pairs={{0,4},{1,5},{2,6},{3,7},{4,0},{5,1},{6,2},{7,3},{8,12},{9,13},{10,... | collective-permute-start | bytes 786440 | tf_op jit(solution)/shard_map/ppermute | solution.py:457
  93.0 1.2 collective-permute-done.22.theirs_ref
  95.0 1.4 %collective-permute-start.24 = (bf16[128,512]{1,0:T(8,128)(2,1)S(1)}, bf16[128,512]{1,0:T(8,128)(2,1)S(1)}, u32[]{:S(2)}, u32[]{:S(2)}) collective-permute-start(bf16[128,512]{1,0:T(8,128)(2,1)S(1)} %get-tuple-element.142), channel_id=1, source_target_pairs={{0,4},{1,5},{2,6},{3,7},{4,0},{5,1},{6,2},{7,3},{8,12},{9,13},{10,... | collective-permute-start | bytes 393224 | tf_op jit(solution)/shard_map/ppermute | solution.py:457
  96.4 1.3 shard_map.96
  97.7 1.3 shard_map.95
  99.0 1.8 %collective-permute-done.23.theirs_ref = bf16[128,1024]{1,0:T(8,128)(2,1)S(1)} collective-permute-done((bf16[128,1024]{1,0:T(8,128)(2,1)S(1)}, bf16[128,1024]{1,0:T(8,128)(2,1)S(1)}, u32[]{:S(2)}, u32[]{:S(2)}) %collective-permute-start.23) | collective-permute-done | bytes 262176 | tf_op jit(solution)/shard_map/ppermute | solution.py:457
  100.8 1.4 %collective-permute-start.25 = (bf16[128,1024]{1,0:T(8,128)(2,1)S(1)}, bf16[128,1024]{1,0:T(8,128)(2,1)S(1)}, u32[]{:S(2)}, u32[]{:S(2)}) collective-permute-start(bf16[128,1024]{1,0:T(8,128)(2,1)S(1)} %get-tuple-element.146), channel_id=1, source_target_pairs={{0,4},{1,5},{2,6},{3,7},{4,0},{5,1},{6,2},{7,3},{8,12},{9,13},{10,... | collective-permute-start | bytes 786440 | tf_op jit(solution)/shard_map/ppermute | solution.py:457
  104.0 7.6 %shard_map.97 = (bf16[128,2048]{1,0:T(8,128)(2,1)S(1)}, bf16[128,2048]{1,0:T(8,128)(2,1)S(1)}) custom-call(f32[8]{0:T(128)S(1)} %broadcast_select_fusion.flag_ref, s32[1]{0:T(128)} %bitcast.13.first_ref, f32[128,256]{1,0:T(8,128)S(1)} %copy-done.20, f32[1,128]{1,0:T(1,128)S(1)} %dynamic-slice_bitcast_fusion.skip_ref, ...), custom_call_target="tpu_custom_call" | custom-call | flops 1610612736 | bytes 4194304 | tf_op jit(solution)/shard_map/pallas_call | solution.py:396
  111.6 1.1 shard_map.98.early_ref
  113.4 1.6 %shard_map.99 = bf16[8,128,256]{2,1,0:T(8,128)(2,1)S(1)} custom-call(bf16[128,2048]{1,0:T(8,128)(2,1)S(1)} %get-tuple-element.143.z_ref, bf16[128,2048]{1,0:T(8,128)(2,1)S(1)} %get-tuple-element.144.packed_ref, bf16[128,2048]{1,0:T(8,128)(2,1)S(1)} %shard_map.98.early_ref, f32[128,1024]{1,0:T(8,128)S(1)} %get-tuple-element.147.mine_ref, ...), custom_call_target="tpu_custom_call" | custom-call | flops 536870912 | bytes 4194304 | tf_op jit(solution)/shard_map/pallas_call | solution.py:424
  115.0 17.2 %all_to_all.10 = bf16[8,128,256]{2,1,0:T(8,128)(2,1)S(1)} all-to-all(bf16[8,128,256]{2,1,0:T(8,128)(2,1)S(1)} %shard_map.99), channel_id=1, replica_groups={{0,8,16,24,4,12,20,28},{1,9,17,25,5,13,21,29},{2,10,18,26,6,14,22,30},{..., dimensions={0} | all-to-all | bytes 1048576 | tf_op jit(solution)/shard_map/all_to_all | solution.py:577
  (96 shorter events, 18.2 us)
Async XLA Ops:
  0.0 16.0 %copy-start = (f32[1024]{0:T(1024)S(1)}, f32[1024]{0:T(1024)}, u32[]{:S(2)}) copy-start(f32[1024]{0:T(1024)} %param.14) | copy-start | bytes 12292
  0.0 26.3 %collective-permute-start.4 = (bf16[1024,256]{1,0:T(8,128)(2,1)}, bf16[1024,256]{1,0:T(8,128)(2,1)S(1)}, u32[]{:S(2)}, u32[]{:S(2)}) collective-permute-start(bf16[1024,256]{1,0:T(8,128)(2,1)} %token_ref.1), channel_id=1, source_target_pairs={{0,8},{1,9},{2,10},{3,11},{4,12},{5,13},{6,14},{7,15},{8,0},{9,1},... | collective-permute-start | bytes 1572872 | tf_op jit(solution)/shard_map/ppermute | solution.py:457
  3.0 25.9 %collective-permute-start = (bf16[1024,256]{1,0:T(8,128)(2,1)}, bf16[1024,256]{1,0:T(8,128)(2,1)}, u32[]{:S(2)}, u32[]{:S(2)}) collective-permute-start(bf16[1024,256]{1,0:T(8,128)(2,1)} %token_ref.1), channel_id=1, source_target_pairs={{0,16},{1,17},{2,18},{3,19},{4,20},{5,21},{6,22},{7,23},{8,24},{9,... | collective-permute-start | bytes 1572872 | tf_op jit(solution)/shard_map/ppermute | solution.py:457
  6.8 7.7 %collective-permute-start.1 = (bf16[528,256]{1,0:T(8,128)(2,1)S(1)}, bf16[528,256]{1,0:T(8,128)(2,1)S(1)}, u32[]{:S(2)}, u32[]{:S(2)}) collective-permute-start(bf16[528,256]{1,0:T(8,128)(2,1)S(1)} %get-tuple-element.77.after_ref), channel_id=1, source_target_pairs={{0,4},{1,5},{2,6},{3,7},{4,0},{5,1},{6,2},{7,3},{8,12},{9,13},{10,... | collective-permute-start | bytes 811016 | tf_op jit(solution)/shard_map/ppermute | solution.py:457
  8.3 14.4 %collective-permute-start.2 = (bf16[528,256]{1,0:T(8,128)(2,1)S(1)}, bf16[528,256]{1,0:T(8,128)(2,1)S(1)}, u32[]{:S(2)}, u32[]{:S(2)}) collective-permute-start(bf16[528,256]{1,0:T(8,128)(2,1)S(1)} %get-tuple-element.78.refs_0_), channel_id=1, source_target_pairs={{0,2},{1,3},{2,0},{3,1},{4,6},{5,7},{6,4},{7,5},{8,10},{9,11},{10,... | collective-permute-start | bytes 811016 | tf_op jit(solution)/shard_map/ppermute | solution.py:457
  14.5 8.2 %collective-permute-start.3 = (bf16[528,256]{1,0:T(8,128)(2,1)S(1)}, bf16[528,256]{1,0:T(8,128)(2,1)S(1)}, u32[]{:S(2)}, u32[]{:S(2)}) collective-permute-start(bf16[528,256]{1,0:T(8,128)(2,1)S(1)} %collective-permute-done.1.refs_1_), channel_id=1, source_target_pairs={{0,2},{1,3},{2,0},{3,1},{4,6},{5,7},{6,4},{7,5},{8,10},{9,11},{10,... | collective-permute-start | bytes 811016 | tf_op jit(solution)/shard_map/ppermute | solution.py:457
  16.2 1.2 copy-start.13
  17.4 1.2 copy-start.14
  19.3 1.3 %copy-start.10 = (bf16[4,2,2,128,512]{4,3,2,1,0:T(8,128)(2,1)}, bf16[4,2,2,128,512]{4,3,2,1,0:T(8,128)(2,1)S(1)}, u32[]{:S(2)}) copy-start(bf16[4,2,2,128,512]{4,3,2,1,0:T(8,128)(2,1)S(1)} %shard_map.83) | copy-start | bytes 6291460
  22.7 15.4 %copy-start.11 = (bf16[528,256]{1,0:T(8,128)(2,1)}, bf16[528,256]{1,0:T(8,128)(2,1)S(1)}, u32[]{:S(2)}) copy-start(bf16[528,256]{1,0:T(8,128)(2,1)S(1)} %collective-permute-done.3.refs_3_) | copy-start | bytes 811012
  28.9 6.6 %collective-permute-start.6 = (bf16[528,256]{1,0:T(8,128)(2,1)S(1)}, bf16[528,256]{1,0:T(8,128)(2,1)S(1)}, u32[]{:S(2)}, u32[]{:S(2)}) collective-permute-start(bf16[528,256]{1,0:T(8,128)(2,1)S(1)} %get-tuple-element.91), channel_id=1, source_target_pairs={{0,4},{1,5},{2,6},{3,7},{4,0},{5,1},{6,2},{7,3},{8,12},{9,13},{10,... | collective-permute-start | bytes 811016 | tf_op jit(solution)/shard_map/ppermute | solution.py:457
  30.4 17.9 %collective-permute-start.5 = (bf16[1024,256]{1,0:T(8,128)(2,1)}, bf16[1024,256]{1,0:T(8,128)(2,1)}, u32[]{:S(2)}, u32[]{:S(2)}) collective-permute-start(bf16[1024,256]{1,0:T(8,128)(2,1)} %collective-permute-done.token_ref), channel_id=1, source_target_pairs={{0,8},{1,9},{2,10},{3,11},{4,12},{5,13},{6,14},{7,15},{8,0},{9,1},... | collective-permute-start | bytes 1572872 | tf_op jit(solution)/shard_map/ppermute | solution.py:457
  32.8 10.2 %collective-permute-start.10 = (bf16[528,256]{1,0:T(8,128)(2,1)}, bf16[528,256]{1,0:T(8,128)(2,1)}, u32[]{:S(2)}, u32[]{:S(2)}) collective-permute-start(bf16[528,256]{1,0:T(8,128)(2,1)} %get-tuple-element.95.refs_0_.refs_2_), channel_id=1, source_target_pairs={{0,2},{1,3},{2,0},{3,1},{4,6},{5,7},{6,4},{7,5},{8,10},{9,11},{10,... | collective-permute-start | bytes 811016 | tf_op jit(solution)/shard_map/ppermute | solution.py:457
  34.3 8.6 %collective-permute-start.9 = (bf16[528,256]{1,0:T(8,128)(2,1)}, bf16[528,256]{1,0:T(8,128)(2,1)}, u32[]{:S(2)}, u32[]{:S(2)}) collective-permute-start(bf16[528,256]{1,0:T(8,128)(2,1)} %get-tuple-element.94), channel_id=1, source_target_pairs={{0,4},{1,5},{2,6},{3,7},{4,0},{5,1},{6,2},{7,3},{8,12},{9,13},{10,... | collective-permute-start | bytes 811016 | tf_op jit(solution)/shard_map/ppermute | solution.py:457
  34.9 13.5 %collective-permute-start.7 = (bf16[528,256]{1,0:T(8,128)(2,1)S(1)}, bf16[528,256]{1,0:T(8,128)(2,1)}, u32[]{:S(2)}, u32[]{:S(2)}) collective-permute-start(bf16[528,256]{1,0:T(8,128)(2,1)S(1)} %get-tuple-element.92.refs_0_), channel_id=1, source_target_pairs={{0,2},{1,3},{2,0},{3,1},{4,6},{5,7},{6,4},{7,5},{8,10},{9,11},{10,... | collective-permute-start | bytes 811016 | tf_op jit(solution)/shard_map/ppermute | solution.py:457
  35.5 16.0 %collective-permute-start.8 = (bf16[528,256]{1,0:T(8,128)(2,1)S(1)}, bf16[528,256]{1,0:T(8,128)(2,1)}, u32[]{:S(2)}, u32[]{:S(2)}) collective-permute-start(bf16[528,256]{1,0:T(8,128)(2,1)S(1)} %collective-permute-done.6.refs_1_), channel_id=1, source_target_pairs={{0,2},{1,3},{2,0},{3,1},{4,6},{5,7},{6,4},{7,5},{8,10},{9,11},{10,... | collective-permute-start | bytes 811016 | tf_op jit(solution)/shard_map/ppermute | solution.py:457
  38.1 48.3 %all-to-all-start = ((bf16[4,2,2,128,512]{4,3,2,1,0:T(8,128)(2,1)}), bf16[4,2,2,128,512]{4,3,2,1,0:T(8,128)(2,1)S(1)}, u32[]{:S(2)}, u32[]{:S(2)}) async-start(bf16[4,2,2,128,512]{4,3,2,1,0:T(8,128)(2,1)} %copy-done.10), calls=%async_computation | async-start | bytes 4194304 | tf_op jit(solution)/shard_map/all_to_all | solution.py:468
  43.0 25.8 %collective-permute-start.14 = (bf16[2112,256]{1,0:T(8,128)(2,1)}, bf16[2112,256]{1,0:T(8,128)(2,1)S(1)}, u32[]{:S(2)}, u32[]{:S(2)}) collective-permute-start(bf16[2112,256]{1,0:T(8,128)(2,1)} %pad_maximum_fusion), channel_id=1, source_target_pairs={{0,1},{1,0},{2,3},{3,2},{4,5},{5,4},{6,7},{7,6},{8,9},{9,8},{10,11... | collective-permute-start | bytes 3244040 | tf_op jit(solution)/shard_map/ppermute | solution.py:457
  52.6 16.2 %collective-permute-start.15 = (bf16[2112,256]{1,0:T(8,128)(2,1)S(1)}, bf16[2112,256]{1,0:T(8,128)(2,1)S(1)}, u32[]{:S(2)}, u32[]{:S(2)}) collective-permute-start(bf16[2112,256]{1,0:T(8,128)(2,1)S(1)} %pad_maximum_fusion.1), channel_id=1, source_target_pairs={{0,1},{1,0},{2,3},{3,2},{4,5},{5,4},{6,7},{7,6},{8,9},{9,8},{10,11... | collective-permute-start | bytes 3244040 | tf_op jit(solution)/shard_map/ppermute | solution.py:457
  53.8 28.6 %copy-start.16 = (bf16[528,256]{1,0:T(8,128)(2,1)}, bf16[528,256]{1,0:T(8,128)(2,1)S(1)}, u32[]{:S(2)}) copy-start(bf16[528,256]{1,0:T(8,128)(2,1)S(1)} %get-tuple-element.97.refs_0_.refs_4_) | copy-start | bytes 811012
  53.8 8.9 %collective-permute-start.11 = (bf16[528,256]{1,0:T(8,128)(2,1)S(1)}, bf16[528,256]{1,0:T(8,128)(2,1)S(1)}, u32[]{:S(2)}, u32[]{:S(2)}) collective-permute-start(bf16[528,256]{1,0:T(8,128)(2,1)S(1)} %get-tuple-element.98), channel_id=1, source_target_pairs={{0,4},{1,5},{2,6},{3,7},{4,0},{5,1},{6,2},{7,3},{8,12},{9,13},{10,... | collective-permute-start | bytes 811016 | tf_op jit(solution)/shard_map/ppermute | solution.py:457
  54.4 9.3 %collective-permute-start.12 = (bf16[528,256]{1,0:T(8,128)(2,1)S(1)}, bf16[528,256]{1,0:T(8,128)(2,1)S(1)}, u32[]{:S(2)}, u32[]{:S(2)}) collective-permute-start(bf16[528,256]{1,0:T(8,128)(2,1)S(1)} %get-tuple-element.97.refs_0_.refs_4_), channel_id=1, source_target_pairs={{0,2},{1,3},{2,0},{3,1},{4,6},{5,7},{6,4},{7,5},{8,10},{9,11},{10,... | collective-permute-start | bytes 811016 | tf_op jit(solution)/shard_map/ppermute | solution.py:457
  56.0 12.8 %collective-permute-start.13 = (bf16[528,256]{1,0:T(8,128)(2,1)}, bf16[528,256]{1,0:T(8,128)(2,1)S(1)}, u32[]{:S(2)}, u32[]{:S(2)}) collective-permute-start(bf16[528,256]{1,0:T(8,128)(2,1)} %collective-permute-done.9.refs_1_.refs_3_), channel_id=1, source_target_pairs={{0,2},{1,3},{2,0},{3,1},{4,6},{5,7},{6,4},{7,5},{8,10},{9,11},{10,... | collective-permute-start | bytes 811016 | tf_op jit(solution)/shard_map/ppermute | solution.py:457
  62.8 19.6 %copy-start.18 = (bf16[528,256]{1,0:T(8,128)(2,1)}, bf16[528,256]{1,0:T(8,128)(2,1)S(1)}, u32[]{:S(2)}) copy-start(bf16[528,256]{1,0:T(8,128)(2,1)S(1)} %collective-permute-done.11.refs_1_.refs_5_) | copy-start | bytes 811012
  70.0 5.9 %copy-start.12 = (bf16[528,256]{1,0:T(8,128)(2,1)S(1)}, bf16[528,256]{1,0:T(8,128)(2,1)}, u32[]{:S(2)}) copy-start(bf16[528,256]{1,0:T(8,128)(2,1)} %copy-done.11) | copy-start | bytes 811012
  70.0 9.1 %collective-permute-start.17 = (bf16[2112,256]{1,0:T(8,128)(2,1)S(1)}, bf16[2112,256]{1,0:T(8,128)(2,1)S(1)}, u32[]{:S(2)}, u32[]{:S(2)}) collective-permute-start(bf16[2112,256]{1,0:T(8,128)(2,1)S(1)} %pad_maximum_fusion.2), channel_id=1, source_target_pairs={{0,1},{1,0},{2,3},{3,2},{4,5},{5,4},{6,7},{7,6},{8,9},{9,8},{10,11... | collective-permute-start | bytes 3244040 | tf_op jit(solution)/shard_map/ppermute | solution.py:457
  70.1 8.4 %collective-permute-start.18 = (bf16[528,256]{1,0:T(8,128)(2,1)S(1)}, bf16[528,256]{1,0:T(8,128)(2,1)S(1)}, u32[]{:S(2)}, u32[]{:S(2)}) collective-permute-start(bf16[528,256]{1,0:T(8,128)(2,1)S(1)} %get-tuple-element.97.refs_0_.refs_4_), channel_id=1, source_target_pairs={{0,1},{1,0},{2,3},{3,2},{4,5},{5,4},{6,7},{7,6},{8,9},{9,8},{10,11... | collective-permute-start | bytes 811016 | tf_op jit(solution)/shard_map/ppermute | solution.py:457
  70.6 8.5 %collective-permute-start.16 = (bf16[528,256]{1,0:T(8,128)(2,1)S(1)}, bf16[528,256]{1,0:T(8,128)(2,1)S(1)}, u32[]{:S(2)}, u32[]{:S(2)}) collective-permute-start(bf16[528,256]{1,0:T(8,128)(2,1)S(1)} %collective-permute-done.11.refs_1_.refs_5_), channel_id=1, source_target_pairs={{0,2},{1,3},{2,0},{3,1},{4,6},{5,7},{6,4},{7,5},{8,10},{9,11},{10,... | collective-permute-start | bytes 811016 | tf_op jit(solution)/shard_map/ppermute | solution.py:457
  72.3 6.8 %collective-permute-start.19 = (bf16[528,256]{1,0:T(8,128)(2,1)S(1)}, bf16[528,256]{1,0:T(8,128)(2,1)S(1)}, u32[]{:S(2)}, u32[]{:S(2)}) collective-permute-start(bf16[528,256]{1,0:T(8,128)(2,1)S(1)} %collective-permute-done.12.refs_2_), channel_id=1, source_target_pairs={{0,1},{1,0},{2,3},{3,2},{4,5},{5,4},{6,7},{7,6},{8,9},{9,8},{10,11... | collective-permute-start | bytes 811016 | tf_op jit(solution)/shard_map/ppermute | solution.py:457
  72.3 6.8 %collective-permute-start.20 = (bf16[528,256]{1,0:T(8,128)(2,1)S(1)}, bf16[528,256]{1,0:T(8,128)(2,1)S(1)}, u32[]{:S(2)}, u32[]{:S(2)}) collective-permute-start(bf16[528,256]{1,0:T(8,128)(2,1)S(1)} %collective-permute-done.11.refs_1_.refs_5_), channel_id=1, source_target_pairs={{0,1},{1,0},{2,3},{3,2},{4,5},{5,4},{6,7},{7,6},{8,9},{9,8},{10,11... | collective-permute-start | bytes 811016 | tf_op jit(solution)/shard_map/ppermute | solution.py:457
  74.6 1.4 %copy-start.1 = (bf16[4,512,512]{2,1,0:T(8,128)(2,1)}, bf16[4,512,512]{2,1,0:T(8,128)(2,1)S(1)}, u32[]{:S(2)}) copy-start(bf16[4,512,512]{2,1,0:T(8,128)(2,1)S(1)} %shard_map.88.refs_0_.refs_1_) | copy-start | bytes 6291460
  77.2 1.4 %copy-start.5 = (bf16[4,512,512]{2,1,0:T(8,128)(2,1)}, bf16[4,512,512]{2,1,0:T(8,128)(2,1)S(1)}, u32[]{:S(2)}) copy-start(bf16[4,512,512]{2,1,0:T(8,128)(2,1)S(1)} %shard_map.87.refs_0_) | copy-start | bytes 6291460
  79.1 3.3 %collective-permute-start.21 = (bf16[528,256]{1,0:T(8,128)(2,1)S(1)}, bf16[528,256]{1,0:T(8,128)(2,1)S(1)}, u32[]{:S(2)}, u32[]{:S(2)}) collective-permute-start(bf16[528,256]{1,0:T(8,128)(2,1)S(1)} %collective-permute-done.16.refs_3_), channel_id=1, source_target_pairs={{0,1},{1,0},{2,3},{3,2},{4,5},{5,4},{6,7},{7,6},{8,9},{9,8},{10,11... | collective-permute-start | bytes 811016 | tf_op jit(solution)/shard_map/ppermute | solution.py:457
  81.0 1.4 %copy-start.3 = (bf16[4,512,512]{2,1,0:T(8,128)(2,1)}, bf16[4,512,512]{2,1,0:T(8,128)(2,1)S(1)}, u32[]{:S(2)}) copy-start(bf16[4,512,512]{2,1,0:T(8,128)(2,1)S(1)} %shard_map.89.refs_1_.refs_0_) | copy-start | bytes 6291460
  83.6 1.3 copy-start.8
  86.4 1.6 %copy-start.6 = (bf16[4,512,512]{2,1,0:T(8,128)(2,1)S(1)}, bf16[4,512,512]{2,1,0:T(8,128)(2,1)}, u32[]{:S(2)}) copy-start(bf16[4,512,512]{2,1,0:T(8,128)(2,1)} %copy-done.5) | copy-start | bytes 6291460
  88.0 2.3 %copy-start.2 = (bf16[4,512,512]{2,1,0:T(8,128)(2,1)S(1)}, bf16[4,512,512]{2,1,0:T(8,128)(2,1)}, u32[]{:S(2)}) copy-start(bf16[4,512,512]{2,1,0:T(8,128)(2,1)} %copy-done.1) | copy-start | bytes 6291460
  88.0 2.3 %copy-start.4 = (bf16[4,512,512]{2,1,0:T(8,128)(2,1)S(1)}, bf16[4,512,512]{2,1,0:T(8,128)(2,1)}, u32[]{:S(2)}) copy-start(bf16[4,512,512]{2,1,0:T(8,128)(2,1)} %copy-done.3) | copy-start | bytes 6291460
  88.7 5.6 %collective-permute-start.22 = (bf16[128,512]{1,0:T(8,128)(2,1)S(1)}, bf16[128,512]{1,0:T(8,128)(2,1)S(1)}, u32[]{:S(2)}, u32[]{:S(2)}) collective-permute-start(bf16[128,512]{1,0:T(8,128)(2,1)S(1)} %get-tuple-element.129), channel_id=1, source_target_pairs={{0,4},{1,5},{2,6},{3,7},{4,0},{5,1},{6,2},{7,3},{8,12},{9,13},{10,... | collective-permute-start | bytes 393224 | tf_op jit(solution)/shard_map/ppermute | solution.py:457
  90.2 4.0 %copy-start.9 = (bf16[4,512,512]{2,1,0:T(8,128)(2,1)S(1)}, bf16[4,512,512]{2,1,0:T(8,128)(2,1)}, u32[]{:S(2)}) copy-start(bf16[4,512,512]{2,1,0:T(8,128)(2,1)} %copy-done.8) | copy-start | bytes 6291460
  91.5 9.3 %collective-permute-start.23 = (bf16[128,1024]{1,0:T(8,128)(2,1)S(1)}, bf16[128,1024]{1,0:T(8,128)(2,1)S(1)}, u32[]{:S(2)}, u32[]{:S(2)}) collective-permute-start(bf16[128,1024]{1,0:T(8,128)(2,1)S(1)} %get-tuple-element.133), channel_id=1, source_target_pairs={{0,4},{1,5},{2,6},{3,7},{4,0},{5,1},{6,2},{7,3},{8,12},{9,13},{10,... | collective-permute-start | bytes 786440 | tf_op jit(solution)/shard_map/ppermute | solution.py:457
  95.0 2.7 %copy-start.7 = (bf16[4,512,512]{2,1,0:T(8,128)(2,1)S(1)}, bf16[4,512,512]{2,1,0:T(8,128)(2,1)}, u32[]{:S(2)}) copy-start(bf16[4,512,512]{2,1,0:T(8,128)(2,1)} %copy-done.5) | copy-start | bytes 6291460
  95.0 8.9 %collective-permute-start.24 = (bf16[128,512]{1,0:T(8,128)(2,1)S(1)}, bf16[128,512]{1,0:T(8,128)(2,1)S(1)}, u32[]{:S(2)}, u32[]{:S(2)}) collective-permute-start(bf16[128,512]{1,0:T(8,128)(2,1)S(1)} %get-tuple-element.142), channel_id=1, source_target_pairs={{0,4},{1,5},{2,6},{3,7},{4,0},{5,1},{6,2},{7,3},{8,12},{9,13},{10,... | collective-permute-start | bytes 393224 | tf_op jit(solution)/shard_map/ppermute | solution.py:457
  97.7 6.3 %copy-start.17 = (bf16[528,256]{1,0:T(8,128)(2,1)S(1)}, bf16[528,256]{1,0:T(8,128)(2,1)}, u32[]{:S(2)}) copy-start(bf16[528,256]{1,0:T(8,128)(2,1)} %copy-done.16) | copy-start | bytes 811012
  97.7 6.3 %copy-start.19 = (bf16[528,256]{1,0:T(8,128)(2,1)S(1)}, bf16[528,256]{1,0:T(8,128)(2,1)}, u32[]{:S(2)}) copy-start(bf16[528,256]{1,0:T(8,128)(2,1)} %copy-done.18) | copy-start | bytes 811012
  97.7 6.3 %copy-start.20 = (f32[128,256]{1,0:T(8,128)S(1)}, f32[128,256]{1,0:T(8,128)}, u32[]{:S(2)}) copy-start(f32[128,256]{1,0:T(8,128)} %dynamic-slice_convert_fusion.taps_ref) | copy-start | bytes 393220
  100.8 10.7 %collective-permute-start.25 = (bf16[128,1024]{1,0:T(8,128)(2,1)S(1)}, bf16[128,1024]{1,0:T(8,128)(2,1)S(1)}, u32[]{:S(2)}, u32[]{:S(2)}) collective-permute-start(bf16[128,1024]{1,0:T(8,128)(2,1)S(1)} %get-tuple-element.146), channel_id=1, source_target_pairs={{0,4},{1,5},{2,6},{3,7},{4,0},{5,1},{6,2},{7,3},{8,12},{9,13},{10,... | collective-permute-start | bytes 786440 | tf_op jit(solution)/shard_map/ppermute | solution.py:457
  102.2 11.1 %collective-permute-start.26 = (bf16[128,1024]{1,0:T(8,128)(2,1)S(1)}, bf16[128,1024]{1,0:T(8,128)(2,1)S(1)}, u32[]{:S(2)}, u32[]{:S(2)}) collective-permute-start(bf16[128,1024]{1,0:T(8,128)(2,1)S(1)} %get-tuple-element.148), channel_id=1, source_target_pairs={{0,4},{1,5},{2,6},{3,7},{4,0},{5,1},{6,2},{7,3},{8,12},{9,13},{10,... | collective-permute-start | bytes 786440 | tf_op jit(solution)/shard_map/ppermute | solution.py:457
  (1 other events, 1.1 us)

commit v6 on v5

--- a/solution.py
+++ b/solution.py
@@ -522,13 +522,13 @@
     got2, kept2_far = across(give2), to_owner(kept2, far_owner)
     got1_far = to_owner(got1, far_owner)
     weights = along_line(packed_weights)
+    got2_far = to_owner(got2, far_owner)
     by_both, got1, kept1_far, got1_far, got2, kept2_far = tie(
         by_both, got1, kept1_far, got1_far, got2, kept2_far
     )
 
     kept3, give3 = halve(which, by_both)
     got3, kept3_far = across(give3), to_owner(kept3, far_owner)
-    got2_far = to_owner(got2, far_owner)
     all1 = to_near([kept1, got1, kept1_far, got1_far])
     all0 = to_near([most0])
     got3, kept3_far, got2_far, all0, all1 = tie(got3, kept3_far, got2_far, all0, all1)

time: 134 us -> 133 us (level)
  no operation moved by 1% of the time
where the time goes in v6:
time: 133 us; the launch traced here: 132 us
  starting transfers between devices  34.2 us (26%)
  waiting for transfers between devices  32.6 us (25%)
  Pallas kernels  26.5 us (20%)
  blocking collectives  16 us (12%)
  local copies, waits for them, and re-layouts  15.4 us (12%)
  other arithmetic  6.62 us (5%)
    ppermute x27, waiting for transfers between devices, send(): return lax.ppermute(array, AXES, pairs)  30 us
    ppermute x27, starting transfers between devices, send(): return lax.ppermute(array, AXES, pairs)  29.4 us
    all_to_all x1, blocking collectives, on_device_line(): lax.all_to_all(mixed, AXES, split_axis=0, concat_axis=0, tiled=True, axis...  16 us
    unnamed x44, local copies, waits for them, and re-layouts  12.7 us
    pallas_call x1, Pallas kernels, band_of(): pl.pallas_call(functools.partial(band_kernel, taps_blocks, tall), out_sha...  7.59 us
    pallas_call x4, Pallas kernels, scale(): pl.pallas_call(functools.partial(scale_kernel, height), out_shape=jax.Sha...  6.07 us
    pallas_call x5, Pallas kernels, project(): pl.pallas_call(functools.partial(project_kernel, number, row_count), out_...  5.19 us
    all_to_all x1, starting transfers between devices, along_line(): lax.all_to_all(array, AXES, split_axis=0, concat_axis=0, tiled=True, axis...  4.88 us
  transfers between devices with their start and end apart: 28, of which 14 were waited for; matrix products, arithmetic and copies ran while one was open for 7% of the time, Pallas kernels for 18%

profile of v6, /device:TPU:0, one launch (start us, length us, event | category | flops | bytes accessed | tf_op | source)
XLA Modules:
  0.0 131.8 jit_solution(6576725538462312497)
XLA Ops:
  0.0 3.0 %collective-permute-start.4 = (bf16[1024,256]{1,0:T(8,128)(2,1)}, bf16[1024,256]{1,0:T(8,128)(2,1)S(1)}, u32[]{:S(2)}, u32[]{:S(2)}) collective-permute-start(bf16[1024,256]{1,0:T(8,128)(2,1)} %token_ref.1), channel_id=1, source_target_pairs={{0,8},{1,9},{2,10},{3,11},{4,12},{5,13},{6,14},{7,15},{8,0},{9,1},... | collective-permute-start | bytes 1572872 | tf_op jit(solution)/shard_map/ppermute | solution.py:457
  3.0 2.6 %collective-permute-start = (bf16[1024,256]{1,0:T(8,128)(2,1)}, bf16[1024,256]{1,0:T(8,128)(2,1)}, u32[]{:S(2)}, u32[]{:S(2)}) collective-permute-start(bf16[1024,256]{1,0:T(8,128)(2,1)} %token_ref.1), channel_id=1, source_target_pairs={{0,16},{1,17},{2,18},{3,19},{4,20},{5,21},{6,22},{7,23},{8,24},{9,... | collective-permute-start | bytes 1572872 | tf_op jit(solution)/shard_map/ppermute | solution.py:457
  6.8 1.6 %collective-permute-start.1 = (bf16[528,256]{1,0:T(8,128)(2,1)S(1)}, bf16[528,256]{1,0:T(8,128)(2,1)S(1)}, u32[]{:S(2)}, u32[]{:S(2)}) collective-permute-start(bf16[528,256]{1,0:T(8,128)(2,1)S(1)} %get-tuple-element.77.after_ref), channel_id=1, source_target_pairs={{0,4},{1,5},{2,6},{3,7},{4,0},{5,1},{6,2},{7,3},{8,12},{9,13},{10,... | collective-permute-start | bytes 811016 | tf_op jit(solution)/shard_map/ppermute | solution.py:457
  8.3 1.5 %collective-permute-start.2 = (bf16[528,256]{1,0:T(8,128)(2,1)S(1)}, bf16[528,256]{1,0:T(8,128)(2,1)S(1)}, u32[]{:S(2)}, u32[]{:S(2)}) collective-permute-start(bf16[528,256]{1,0:T(8,128)(2,1)S(1)} %get-tuple-element.78.refs_0_), channel_id=1, source_target_pairs={{0,2},{1,3},{2,0},{3,1},{4,6},{5,7},{6,4},{7,5},{8,10},{9,11},{10,... | collective-permute-start | bytes 811016 | tf_op jit(solution)/shard_map/ppermute | solution.py:457
  14.5 1.5 %collective-permute-start.3 = (bf16[528,256]{1,0:T(8,128)(2,1)S(1)}, bf16[528,256]{1,0:T(8,128)(2,1)S(1)}, u32[]{:S(2)}, u32[]{:S(2)}) collective-permute-start(bf16[528,256]{1,0:T(8,128)(2,1)S(1)} %collective-permute-done.1.refs_1_), channel_id=1, source_target_pairs={{0,2},{1,3},{2,0},{3,1},{4,6},{5,7},{6,4},{7,5},{8,10},{9,11},{10,... | collective-permute-start | bytes 811016 | tf_op jit(solution)/shard_map/ppermute | solution.py:457
  16.2 1.2 copy-done.13
  17.4 1.2 copy-done.14
  19.3 1.3 %copy-done.10 = bf16[4,2,2,128,512]{4,3,2,1,0:T(8,128)(2,1)} copy-done((bf16[4,2,2,128,512]{4,3,2,1,0:T(8,128)(2,1)}, bf16[4,2,2,128,512]{4,3,2,1,0:T(8,128)(2,1)S(1)}, u32[]{:S(2)}) %copy-start.10) | copy-done | bytes 2097176
  21.2 1.5 %dynamic-slice_convert_fusion.taps_ref = f32[128,256]{1,0:T(8,128)} fusion(bf16[1024,256]{1,0:T(8,128)(2,1)} %param.13, s32[]{:T(128)S(6)} %select_n.50), kind=kLoop, calls=%fused_computation.5 | loop fusion | flops 32768 | bytes 196612 | tf_op jit(solution)/shard_map/convert_element_type | solution.py:485
  23.8 2.5 %collective-permute-done.4.token_ref = bf16[1024,256]{1,0:T(8,128)(2,1)S(1)} collective-permute-done((bf16[1024,256]{1,0:T(8,128)(2,1)}, bf16[1024,256]{1,0:T(8,128)(2,1)S(1)}, u32[]{:S(2)}, u32[]{:S(2)}) %collective-permute-start.4) | collective-permute-done | bytes 524320 | tf_op jit(solution)/shard_map/ppermute | solution.py:457
  26.4 2.6 %collective-permute-done.token_ref = bf16[1024,256]{1,0:T(8,128)(2,1)} collective-permute-done((bf16[1024,256]{1,0:T(8,128)(2,1)}, bf16[1024,256]{1,0:T(8,128)(2,1)}, u32[]{:S(2)}, u32[]{:S(2)}) %collective-permute-start) | collective-permute-done | bytes 524320 | tf_op jit(solution)/shard_map/ppermute | solution.py:457
  28.9 1.5 %collective-permute-start.6 = (bf16[528,256]{1,0:T(8,128)(2,1)S(1)}, bf16[528,256]{1,0:T(8,128)(2,1)S(1)}, u32[]{:S(2)}, u32[]{:S(2)}) collective-permute-start(bf16[528,256]{1,0:T(8,128)(2,1)S(1)} %get-tuple-element.91), channel_id=1, source_target_pairs={{0,4},{1,5},{2,6},{3,7},{4,0},{5,1},{6,2},{7,3},{8,12},{9,13},{10,... | collective-permute-start | bytes 811016 | tf_op jit(solution)/shard_map/ppermute | solution.py:457
  30.8 2.0 %shard_map.85 = (bf16[528,256]{1,0:T(8,128)(2,1)}, bf16[528,256]{1,0:T(8,128)(2,1)}) custom-call(s32[1]{0:T(128)} %bitcast.x_ref, bf16[1024,256]{1,0:T(8,128)(2,1)} %collective-permute-done.token_ref), custom_call_target="tpu_custom_call" | custom-call | flops 524288 | bytes 1048576 | tf_op jit(solution)/shard_map/pallas_call | solution.py:151
  32.8 1.5 %collective-permute-start.10 = (bf16[528,256]{1,0:T(8,128)(2,1)}, bf16[528,256]{1,0:T(8,128)(2,1)}, u32[]{:S(2)}, u32[]{:S(2)}) collective-permute-start(bf16[528,256]{1,0:T(8,128)(2,1)} %get-tuple-element.95.refs_0_.refs_2_), channel_id=1, source_target_pairs={{0,2},{1,3},{2,0},{3,1},{4,6},{5,7},{6,4},{7,5},{8,10},{9,11},{10,... | collective-permute-start | bytes 811016 | tf_op jit(solution)/shard_map/ppermute | solution.py:457
  35.5 2.6 %collective-permute-start.8 = (bf16[528,256]{1,0:T(8,128)(2,1)S(1)}, bf16[528,256]{1,0:T(8,128)(2,1)}, u32[]{:S(2)}, u32[]{:S(2)}) collective-permute-start(bf16[528,256]{1,0:T(8,128)(2,1)S(1)} %collective-permute-done.6.refs_1_), channel_id=1, source_target_pairs={{0,2},{1,3},{2,0},{3,1},{4,6},{5,7},{6,4},{7,5},{8,10},{9,11},{10,... | collective-permute-start | bytes 811016 | tf_op jit(solution)/shard_map/ppermute | solution.py:457
  38.1 4.9 %all-to-all-start = ((bf16[4,2,2,128,512]{4,3,2,1,0:T(8,128)(2,1)}), bf16[4,2,2,128,512]{4,3,2,1,0:T(8,128)(2,1)S(1)}, u32[]{:S(2)}, u32[]{:S(2)}) async-start(bf16[4,2,2,128,512]{4,3,2,1,0:T(8,128)(2,1)} %copy-done.10), calls=%async_computation | async-start | bytes 4194304 | tf_op jit(solution)/shard_map/all_to_all | solution.py:468
  43.0 5.4 %collective-permute-done.7.refs_2_ = bf16[528,256]{1,0:T(8,128)(2,1)} collective-permute-done((bf16[528,256]{1,0:T(8,128)(2,1)S(1)}, bf16[528,256]{1,0:T(8,128)(2,1)}, u32[]{:S(2)}, u32[]{:S(2)}) %collective-permute-start.7) | collective-permute-done | bytes 270368 | tf_op jit(solution)/shard_map/ppermute | solution.py:457
  48.4 3.1 %collective-permute-done.8.refs_3_ = bf16[528,256]{1,0:T(8,128)(2,1)} collective-permute-done((bf16[528,256]{1,0:T(8,128)(2,1)S(1)}, bf16[528,256]{1,0:T(8,128)(2,1)}, u32[]{:S(2)}, u32[]{:S(2)}) %collective-permute-start.8) | collective-permute-done | bytes 270368 | tf_op jit(solution)/shard_map/ppermute | solution.py:457
  52.7 1.9 %collective-permute-start.13 = (bf16[528,256]{1,0:T(8,128)(2,1)}, bf16[528,256]{1,0:T(8,128)(2,1)S(1)}, u32[]{:S(2)}, u32[]{:S(2)}) collective-permute-start(bf16[528,256]{1,0:T(8,128)(2,1)} %collective-permute-done.9.refs_1_.refs_3_), channel_id=1, source_target_pairs={{0,2},{1,3},{2,0},{3,1},{4,6},{5,7},{6,4},{7,5},{8,10},{9,11},{10,... | collective-permute-start | bytes 811016 | tf_op jit(solution)/shard_map/ppermute | solution.py:457
  54.6 1.2 shard_map.86
  56.5 5.7 %collective-permute-done.13.refs_3_ = bf16[528,256]{1,0:T(8,128)(2,1)S(1)} collective-permute-done((bf16[528,256]{1,0:T(8,128)(2,1)}, bf16[528,256]{1,0:T(8,128)(2,1)S(1)}, u32[]{:S(2)}, u32[]{:S(2)}) %collective-permute-start.13) | collective-permute-done | bytes 270368 | tf_op jit(solution)/shard_map/ppermute | solution.py:457
  62.2 2.2 %collective-permute-done.11.refs_1_.refs_5_ = bf16[528,256]{1,0:T(8,128)(2,1)S(1)} collective-permute-done((bf16[528,256]{1,0:T(8,128)(2,1)S(1)}, bf16[528,256]{1,0:T(8,128)(2,1)S(1)}, u32[]{:S(2)}, u32[]{:S(2)}) %collective-permute-start.11) | collective-permute-done | bytes 270368 | tf_op jit(solution)/shard_map/ppermute | solution.py:457
  64.4 3.3 %collective-permute-done.12.refs_2_ = bf16[528,256]{1,0:T(8,128)(2,1)S(1)} collective-permute-done((bf16[528,256]{1,0:T(8,128)(2,1)S(1)}, bf16[528,256]{1,0:T(8,128)(2,1)S(1)}, u32[]{:S(2)}, u32[]{:S(2)}) %collective-permute-start.12) | collective-permute-done | bytes 270368 | tf_op jit(solution)/shard_map/ppermute | solution.py:457
  67.7 1.2 pad_maximum_fusion.2
  69.5 1.8 %collective-permute-start.16 = (bf16[528,256]{1,0:T(8,128)(2,1)S(1)}, bf16[528,256]{1,0:T(8,128)(2,1)S(1)}, u32[]{:S(2)}, u32[]{:S(2)}) collective-permute-start(bf16[528,256]{1,0:T(8,128)(2,1)S(1)} %collective-permute-done.11.refs_1_.refs_5_), channel_id=1, source_target_pairs={{0,2},{1,3},{2,0},{3,1},{4,6},{5,7},{6,4},{7,5},{8,10},{9,11},{10,... | collective-permute-start | bytes 811016 | tf_op jit(solution)/shard_map/ppermute | solution.py:457
  71.7 1.7 %shard_map.88.refs_0_.refs_1_ = bf16[4,512,512]{2,1,0:T(8,128)(2,1)S(1)} custom-call(s32[4]{0:T(128)S(1)} %pad_add_fusion.1.pick_ref, f32[8,512]{1,0:T(8,128)S(1)} %pad.4.gain_ref, bf16[528,256]{1,0:T(8,128)(2,1)S(1)} %get-tuple-element.92.refs_0_, bf16[528,256]{1,0:T(8,128)(2,1)S(1)} %collective-permute-done.6.refs_1_, ...), custom_call_target="tpu_custom_call" | custom-call | flops 2097152 | bytes 4194304 | tf_op jit(solution)/shard_map/pallas_call | solution.py:218
  73.5 1.3 %copy-done.1 = bf16[4,512,512]{2,1,0:T(8,128)(2,1)} copy-done((bf16[4,512,512]{2,1,0:T(8,128)(2,1)}, bf16[4,512,512]{2,1,0:T(8,128)(2,1)S(1)}, u32[]{:S(2)}) %copy-start.1) | copy-done | bytes 2097176
  74.8 1.3 shard_map.87.refs_0_
  76.1 1.4 %copy-done.5 = bf16[4,512,512]{2,1,0:T(8,128)(2,1)} copy-done((bf16[4,512,512]{2,1,0:T(8,128)(2,1)}, bf16[4,512,512]{2,1,0:T(8,128)(2,1)S(1)}, u32[]{:S(2)}) %copy-start.5) | copy-done | bytes 2097176
  78.0 1.8 %shard_map.89.refs_1_.refs_0_ = bf16[4,512,512]{2,1,0:T(8,128)(2,1)S(1)} custom-call(s32[4]{0:T(128)S(1)} %pad_add_fusion.1.pick_ref, f32[8,512]{1,0:T(8,128)S(1)} %pad.4.gain_ref, bf16[528,256]{1,0:T(8,128)(2,1)} %get-tuple-element.95.refs_0_.refs_2_, bf16[528,256]{1,0:T(8,128)(2,1)} %collective-permute-done.9.refs_1_.refs_3_, ...), custom_call_target="tpu_custom_call" | custom-call | flops 2097152 | bytes 4194304 | tf_op jit(solution)/shard_map/pallas_call | solution.py:218
  79.9 1.4 %copy-done.3 = bf16[4,512,512]{2,1,0:T(8,128)(2,1)} copy-done((bf16[4,512,512]{2,1,0:T(8,128)(2,1)}, bf16[4,512,512]{2,1,0:T(8,128)(2,1)S(1)}, u32[]{:S(2)}) %copy-start.3) | copy-done | bytes 2097176
  81.2 1.3 shard_map.90.refs_0_.refs_1_
  82.5 1.3 copy-done.8
  83.8 2.5 %all-to-all-done.weight_ref = bf16[4,2,2,128,512]{4,3,2,1,0:T(8,128)(2,1)S(1)} async-done(((bf16[4,2,2,128,512]{4,3,2,1,0:T(8,128)(2,1)}), bf16[4,2,2,128,512]{4,3,2,1,0:T(8,128)(2,1)S(1)}, u32[]{:S(2)}, u32[]{:S(2)}) %all-to-all-start) | async-done | bytes 2097184 | tf_op jit(solution)/shard_map/all_to_all | solution.py:468
  86.4 1.6 %copy-done.6 = bf16[4,512,512]{2,1,0:T(8,128)(2,1)S(1)} copy-done((bf16[4,512,512]{2,1,0:T(8,128)(2,1)S(1)}, bf16[4,512,512]{2,1,0:T(8,128)(2,1)}, u32[]{:S(2)}) %copy-start.6) | copy-done | bytes 2097176
  88.7 1.6 %collective-permute-start.22 = (bf16[128,512]{1,0:T(8,128)(2,1)S(1)}, bf16[128,512]{1,0:T(8,128)(2,1)S(1)}, u32[]{:S(2)}, u32[]{:S(2)}) collective-permute-start(bf16[128,512]{1,0:T(8,128)(2,1)S(1)} %get-tuple-element.129), channel_id=1, source_target_pairs={{0,4},{1,5},{2,6},{3,7},{4,0},{5,1},{6,2},{7,3},{8,12},{9,13},{10,... | collective-permute-start | bytes 393224 | tf_op jit(solution)/shard_map/ppermute | solution.py:457
  90.2 1.3 shard_map.92
  91.5 1.5 %collective-permute-start.23 = (bf16[128,1024]{1,0:T(8,128)(2,1)S(1)}, bf16[128,1024]{1,0:T(8,128)(2,1)S(1)}, u32[]{:S(2)}, u32[]{:S(2)}) collective-permute-start(bf16[128,1024]{1,0:T(8,128)(2,1)S(1)} %get-tuple-element.133), channel_id=1, source_target_pairs={{0,4},{1,5},{2,6},{3,7},{4,0},{5,1},{6,2},{7,3},{8,12},{9,13},{10,... | collective-permute-start | bytes 786440 | tf_op jit(solution)/shard_map/ppermute | solution.py:457
  93.0 1.5 %collective-permute-done.22.theirs_ref = bf16[128,512]{1,0:T(8,128)(2,1)S(1)} collective-permute-done((bf16[128,512]{1,0:T(8,128)(2,1)S(1)}, bf16[128,512]{1,0:T(8,128)(2,1)S(1)}, u32[]{:S(2)}, u32[]{:S(2)}) %collective-permute-start.22) | collective-permute-done | bytes 131104 | tf_op jit(solution)/shard_map/ppermute | solution.py:457
  95.3 1.3 collective-permute-start.24
  96.6 1.3 shard_map.96
  97.9 1.3 shard_map.95
  99.1 1.7 %collective-permute-done.23.theirs_ref = bf16[128,1024]{1,0:T(8,128)(2,1)S(1)} collective-permute-done((bf16[128,1024]{1,0:T(8,128)(2,1)S(1)}, bf16[128,1024]{1,0:T(8,128)(2,1)S(1)}, u32[]{:S(2)}, u32[]{:S(2)}) %collective-permute-start.23) | collective-permute-done | bytes 262176 | tf_op jit(solution)/shard_map/ppermute | solution.py:457
  100.8 1.4 %collective-permute-start.25 = (bf16[128,1024]{1,0:T(8,128)(2,1)S(1)}, bf16[128,1024]{1,0:T(8,128)(2,1)S(1)}, u32[]{:S(2)}, u32[]{:S(2)}) collective-permute-start(bf16[128,1024]{1,0:T(8,128)(2,1)S(1)} %get-tuple-element.146), channel_id=1, source_target_pairs={{0,4},{1,5},{2,6},{3,7},{4,0},{5,1},{6,2},{7,3},{8,12},{9,13},{10,... | collective-permute-start | bytes 786440 | tf_op jit(solution)/shard_map/ppermute | solution.py:457
  104.0 7.6 %shard_map.97 = (bf16[128,2048]{1,0:T(8,128)(2,1)S(1)}, bf16[128,2048]{1,0:T(8,128)(2,1)S(1)}) custom-call(f32[8]{0:T(128)S(1)} %broadcast_select_fusion.flag_ref, s32[1]{0:T(128)} %bitcast.13.first_ref, f32[128,256]{1,0:T(8,128)S(1)} %copy-done.20, f32[1,128]{1,0:T(1,128)S(1)} %dynamic-slice_bitcast_fusion.skip_ref, ...), custom_call_target="tpu_custom_call" | custom-call | flops 1610612736 | bytes 4194304 | tf_op jit(solution)/shard_map/pallas_call | solution.py:396
  111.6 1.1 shard_map.98.early_ref
  113.4 1.6 %shard_map.99 = bf16[8,128,256]{2,1,0:T(8,128)(2,1)S(1)} custom-call(bf16[128,2048]{1,0:T(8,128)(2,1)S(1)} %get-tuple-element.143.z_ref, bf16[128,2048]{1,0:T(8,128)(2,1)S(1)} %get-tuple-element.144.packed_ref, bf16[128,2048]{1,0:T(8,128)(2,1)S(1)} %shard_map.98.early_ref, f32[128,1024]{1,0:T(8,128)S(1)} %get-tuple-element.147.mine_ref, ...), custom_call_target="tpu_custom_call" | custom-call | flops 536870912 | bytes 4194304 | tf_op jit(solution)/shard_map/pallas_call | solution.py:424
  115.0 16.0 %all_to_all.10 = bf16[8,128,256]{2,1,0:T(8,128)(2,1)S(1)} all-to-all(bf16[8,128,256]{2,1,0:T(8,128)(2,1)S(1)} %shard_map.99), channel_id=1, replica_groups={{0,8,16,24,4,12,20,28},{1,9,17,25,5,13,21,29},{2,10,18,26,6,14,22,30},{..., dimensions={0} | all-to-all | bytes 1048576 | tf_op jit(solution)/shard_map/all_to_all | solution.py:577
  (96 shorter events, 18.0 us)
Async XLA Ops:
  0.0 16.0 %copy-start = (f32[1024]{0:T(1024)S(1)}, f32[1024]{0:T(1024)}, u32[]{:S(2)}) copy-start(f32[1024]{0:T(1024)} %param.14) | copy-start | bytes 12292
  0.0 26.3 %collective-permute-start.4 = (bf16[1024,256]{1,0:T(8,128)(2,1)}, bf16[1024,256]{1,0:T(8,128)(2,1)S(1)}, u32[]{:S(2)}, u32[]{:S(2)}) collective-permute-start(bf16[1024,256]{1,0:T(8,128)(2,1)} %token_ref.1), channel_id=1, source_target_pairs={{0,8},{1,9},{2,10},{3,11},{4,12},{5,13},{6,14},{7,15},{8,0},{9,1},... | collective-permute-start | bytes 1572872 | tf_op jit(solution)/shard_map/ppermute | solution.py:457
  3.0 25.9 %collective-permute-start = (bf16[1024,256]{1,0:T(8,128)(2,1)}, bf16[1024,256]{1,0:T(8,128)(2,1)}, u32[]{:S(2)}, u32[]{:S(2)}) collective-permute-start(bf16[1024,256]{1,0:T(8,128)(2,1)} %token_ref.1), channel_id=1, source_target_pairs={{0,16},{1,17},{2,18},{3,19},{4,20},{5,21},{6,22},{7,23},{8,24},{9,... | collective-permute-start | bytes 1572872 | tf_op jit(solution)/shard_map/ppermute | solution.py:457
  6.8 7.7 %collective-permute-start.1 = (bf16[528,256]{1,0:T(8,128)(2,1)S(1)}, bf16[528,256]{1,0:T(8,128)(2,1)S(1)}, u32[]{:S(2)}, u32[]{:S(2)}) collective-permute-start(bf16[528,256]{1,0:T(8,128)(2,1)S(1)} %get-tuple-element.77.after_ref), channel_id=1, source_target_pairs={{0,4},{1,5},{2,6},{3,7},{4,0},{5,1},{6,2},{7,3},{8,12},{9,13},{10,... | collective-permute-start | bytes 811016 | tf_op jit(solution)/shard_map/ppermute | solution.py:457
  8.3 14.4 %collective-permute-start.2 = (bf16[528,256]{1,0:T(8,128)(2,1)S(1)}, bf16[528,256]{1,0:T(8,128)(2,1)S(1)}, u32[]{:S(2)}, u32[]{:S(2)}) collective-permute-start(bf16[528,256]{1,0:T(8,128)(2,1)S(1)} %get-tuple-element.78.refs_0_), channel_id=1, source_target_pairs={{0,2},{1,3},{2,0},{3,1},{4,6},{5,7},{6,4},{7,5},{8,10},{9,11},{10,... | collective-permute-start | bytes 811016 | tf_op jit(solution)/shard_map/ppermute | solution.py:457
  14.5 8.2 %collective-permute-start.3 = (bf16[528,256]{1,0:T(8,128)(2,1)S(1)}, bf16[528,256]{1,0:T(8,128)(2,1)S(1)}, u32[]{:S(2)}, u32[]{:S(2)}) collective-permute-start(bf16[528,256]{1,0:T(8,128)(2,1)S(1)} %collective-permute-done.1.refs_1_), channel_id=1, source_target_pairs={{0,2},{1,3},{2,0},{3,1},{4,6},{5,7},{6,4},{7,5},{8,10},{9,11},{10,... | collective-permute-start | bytes 811016 | tf_op jit(solution)/shard_map/ppermute | solution.py:457
  16.2 1.2 copy-start.13
  17.4 1.2 copy-start.14
  19.3 1.3 %copy-start.10 = (bf16[4,2,2,128,512]{4,3,2,1,0:T(8,128)(2,1)}, bf16[4,2,2,128,512]{4,3,2,1,0:T(8,128)(2,1)S(1)}, u32[]{:S(2)}) copy-start(bf16[4,2,2,128,512]{4,3,2,1,0:T(8,128)(2,1)S(1)} %shard_map.83) | copy-start | bytes 6291460
  22.7 15.4 %copy-start.11 = (bf16[528,256]{1,0:T(8,128)(2,1)}, bf16[528,256]{1,0:T(8,128)(2,1)S(1)}, u32[]{:S(2)}) copy-start(bf16[528,256]{1,0:T(8,128)(2,1)S(1)} %collective-permute-done.3.refs_3_) | copy-start | bytes 811012
  28.9 6.6 %collective-permute-start.6 = (bf16[528,256]{1,0:T(8,128)(2,1)S(1)}, bf16[528,256]{1,0:T(8,128)(2,1)S(1)}, u32[]{:S(2)}, u32[]{:S(2)}) collective-permute-start(bf16[528,256]{1,0:T(8,128)(2,1)S(1)} %get-tuple-element.91), channel_id=1, source_target_pairs={{0,4},{1,5},{2,6},{3,7},{4,0},{5,1},{6,2},{7,3},{8,12},{9,13},{10,... | collective-permute-start | bytes 811016 | tf_op jit(solution)/shard_map/ppermute | solution.py:457
  30.4 17.9 %collective-permute-start.5 = (bf16[1024,256]{1,0:T(8,128)(2,1)}, bf16[1024,256]{1,0:T(8,128)(2,1)}, u32[]{:S(2)}, u32[]{:S(2)}) collective-permute-start(bf16[1024,256]{1,0:T(8,128)(2,1)} %collective-permute-done.token_ref), channel_id=1, source_target_pairs={{0,8},{1,9},{2,10},{3,11},{4,12},{5,13},{6,14},{7,15},{8,0},{9,1},... | collective-permute-start | bytes 1572872 | tf_op jit(solution)/shard_map/ppermute | solution.py:457
  32.8 10.2 %collective-permute-start.10 = (bf16[528,256]{1,0:T(8,128)(2,1)}, bf16[528,256]{1,0:T(8,128)(2,1)}, u32[]{:S(2)}, u32[]{:S(2)}) collective-permute-start(bf16[528,256]{1,0:T(8,128)(2,1)} %get-tuple-element.95.refs_0_.refs_2_), channel_id=1, source_target_pairs={{0,2},{1,3},{2,0},{3,1},{4,6},{5,7},{6,4},{7,5},{8,10},{9,11},{10,... | collective-permute-start | bytes 811016 | tf_op jit(solution)/shard_map/ppermute | solution.py:457
  34.3 8.6 %collective-permute-start.9 = (bf16[528,256]{1,0:T(8,128)(2,1)}, bf16[528,256]{1,0:T(8,128)(2,1)}, u32[]{:S(2)}, u32[]{:S(2)}) collective-permute-start(bf16[528,256]{1,0:T(8,128)(2,1)} %get-tuple-element.94), channel_id=1, source_target_pairs={{0,4},{1,5},{2,6},{3,7},{4,0},{5,1},{6,2},{7,3},{8,12},{9,13},{10,... | collective-permute-start | bytes 811016 | tf_op jit(solution)/shard_map/ppermute | solution.py:457
  34.9 13.5 %collective-permute-start.7 = (bf16[528,256]{1,0:T(8,128)(2,1)S(1)}, bf16[528,256]{1,0:T(8,128)(2,1)}, u32[]{:S(2)}, u32[]{:S(2)}) collective-permute-start(bf16[528,256]{1,0:T(8,128)(2,1)S(1)} %get-tuple-element.92.refs_0_), channel_id=1, source_target_pairs={{0,2},{1,3},{2,0},{3,1},{4,6},{5,7},{6,4},{7,5},{8,10},{9,11},{10,... | collective-permute-start | bytes 811016 | tf_op jit(solution)/shard_map/ppermute | solution.py:457
  35.5 16.0 %collective-permute-start.8 = (bf16[528,256]{1,0:T(8,128)(2,1)S(1)}, bf16[528,256]{1,0:T(8,128)(2,1)}, u32[]{:S(2)}, u32[]{:S(2)}) collective-permute-start(bf16[528,256]{1,0:T(8,128)(2,1)S(1)} %collective-permute-done.6.refs_1_), channel_id=1, source_target_pairs={{0,2},{1,3},{2,0},{3,1},{4,6},{5,7},{6,4},{7,5},{8,10},{9,11},{10,... | collective-permute-start | bytes 811016 | tf_op jit(solution)/shard_map/ppermute | solution.py:457
  38.1 48.3 %all-to-all-start = ((bf16[4,2,2,128,512]{4,3,2,1,0:T(8,128)(2,1)}), bf16[4,2,2,128,512]{4,3,2,1,0:T(8,128)(2,1)S(1)}, u32[]{:S(2)}, u32[]{:S(2)}) async-start(bf16[4,2,2,128,512]{4,3,2,1,0:T(8,128)(2,1)} %copy-done.10), calls=%async_computation | async-start | bytes 4194304 | tf_op jit(solution)/shard_map/all_to_all | solution.py:468
  43.0 24.7 %collective-permute-start.14 = (bf16[2112,256]{1,0:T(8,128)(2,1)}, bf16[2112,256]{1,0:T(8,128)(2,1)S(1)}, u32[]{:S(2)}, u32[]{:S(2)}) collective-permute-start(bf16[2112,256]{1,0:T(8,128)(2,1)} %pad_maximum_fusion), channel_id=1, source_target_pairs={{0,1},{1,0},{2,3},{3,2},{4,5},{5,4},{6,7},{7,6},{8,9},{9,8},{10,11... | collective-permute-start | bytes 3244040 | tf_op jit(solution)/shard_map/ppermute | solution.py:457
  52.6 15.1 %collective-permute-start.15 = (bf16[2112,256]{1,0:T(8,128)(2,1)S(1)}, bf16[2112,256]{1,0:T(8,128)(2,1)S(1)}, u32[]{:S(2)}, u32[]{:S(2)}) collective-permute-start(bf16[2112,256]{1,0:T(8,128)(2,1)S(1)} %pad_maximum_fusion.1), channel_id=1, source_target_pairs={{0,1},{1,0},{2,3},{3,2},{4,5},{5,4},{6,7},{7,6},{8,9},{9,8},{10,11... | collective-permute-start | bytes 3244040 | tf_op jit(solution)/shard_map/ppermute | solution.py:457
  52.7 9.5 %collective-permute-start.13 = (bf16[528,256]{1,0:T(8,128)(2,1)}, bf16[528,256]{1,0:T(8,128)(2,1)S(1)}, u32[]{:S(2)}, u32[]{:S(2)}) collective-permute-start(bf16[528,256]{1,0:T(8,128)(2,1)} %collective-permute-done.9.refs_1_.refs_3_), channel_id=1, source_target_pairs={{0,2},{1,3},{2,0},{3,1},{4,6},{5,7},{6,4},{7,5},{8,10},{9,11},{10,... | collective-permute-start | bytes 811016 | tf_op jit(solution)/shard_map/ppermute | solution.py:457
  55.7 25.5 %copy-start.16 = (bf16[528,256]{1,0:T(8,128)(2,1)}, bf16[528,256]{1,0:T(8,128)(2,1)S(1)}, u32[]{:S(2)}) copy-start(bf16[528,256]{1,0:T(8,128)(2,1)S(1)} %get-tuple-element.97.refs_0_.refs_4_) | copy-start | bytes 811012
  55.8 8.6 %collective-permute-start.11 = (bf16[528,256]{1,0:T(8,128)(2,1)S(1)}, bf16[528,256]{1,0:T(8,128)(2,1)S(1)}, u32[]{:S(2)}, u32[]{:S(2)}) collective-permute-start(bf16[528,256]{1,0:T(8,128)(2,1)S(1)} %get-tuple-element.98), channel_id=1, source_target_pairs={{0,4},{1,5},{2,6},{3,7},{4,0},{5,1},{6,2},{7,3},{8,12},{9,13},{10,... | collective-permute-start | bytes 811016 | tf_op jit(solution)/shard_map/ppermute | solution.py:457
  56.0 11.7 %collective-permute-start.12 = (bf16[528,256]{1,0:T(8,128)(2,1)S(1)}, bf16[528,256]{1,0:T(8,128)(2,1)S(1)}, u32[]{:S(2)}, u32[]{:S(2)}) collective-permute-start(bf16[528,256]{1,0:T(8,128)(2,1)S(1)} %get-tuple-element.97.refs_0_.refs_4_), channel_id=1, source_target_pairs={{0,2},{1,3},{2,0},{3,1},{4,6},{5,7},{6,4},{7,5},{8,10},{9,11},{10,... | collective-permute-start | bytes 811016 | tf_op jit(solution)/shard_map/ppermute | solution.py:457
  64.4 16.9 %copy-start.18 = (bf16[528,256]{1,0:T(8,128)(2,1)}, bf16[528,256]{1,0:T(8,128)(2,1)S(1)}, u32[]{:S(2)}) copy-start(bf16[528,256]{1,0:T(8,128)(2,1)S(1)} %collective-permute-done.11.refs_1_.refs_5_) | copy-start | bytes 811012
  68.9 6.0 %copy-start.12 = (bf16[528,256]{1,0:T(8,128)(2,1)S(1)}, bf16[528,256]{1,0:T(8,128)(2,1)}, u32[]{:S(2)}) copy-start(bf16[528,256]{1,0:T(8,128)(2,1)} %copy-done.11) | copy-start | bytes 811012
  68.9 9.1 %collective-permute-start.17 = (bf16[2112,256]{1,0:T(8,128)(2,1)S(1)}, bf16[2112,256]{1,0:T(8,128)(2,1)S(1)}, u32[]{:S(2)}, u32[]{:S(2)}) collective-permute-start(bf16[2112,256]{1,0:T(8,128)(2,1)S(1)} %pad_maximum_fusion.2), channel_id=1, source_target_pairs={{0,1},{1,0},{2,3},{3,2},{4,5},{5,4},{6,7},{7,6},{8,9},{9,8},{10,11... | collective-permute-start | bytes 3244040 | tf_op jit(solution)/shard_map/ppermute | solution.py:457
  69.0 8.5 %collective-permute-start.18 = (bf16[528,256]{1,0:T(8,128)(2,1)S(1)}, bf16[528,256]{1,0:T(8,128)(2,1)S(1)}, u32[]{:S(2)}, u32[]{:S(2)}) collective-permute-start(bf16[528,256]{1,0:T(8,128)(2,1)S(1)} %get-tuple-element.97.refs_0_.refs_4_), channel_id=1, source_target_pairs={{0,1},{1,0},{2,3},{3,2},{4,5},{5,4},{6,7},{7,6},{8,9},{9,8},{10,11... | collective-permute-start | bytes 811016 | tf_op jit(solution)/shard_map/ppermute | solution.py:457
  69.5 8.5 %collective-permute-start.16 = (bf16[528,256]{1,0:T(8,128)(2,1)S(1)}, bf16[528,256]{1,0:T(8,128)(2,1)S(1)}, u32[]{:S(2)}, u32[]{:S(2)}) collective-permute-start(bf16[528,256]{1,0:T(8,128)(2,1)S(1)} %collective-permute-done.11.refs_1_.refs_5_), channel_id=1, source_target_pairs={{0,2},{1,3},{2,0},{3,1},{4,6},{5,7},{6,4},{7,5},{8,10},{9,11},{10,... | collective-permute-start | bytes 811016 | tf_op jit(solution)/shard_map/ppermute | solution.py:457
  71.2 6.7 %collective-permute-start.19 = (bf16[528,256]{1,0:T(8,128)(2,1)S(1)}, bf16[528,256]{1,0:T(8,128)(2,1)S(1)}, u32[]{:S(2)}, u32[]{:S(2)}) collective-permute-start(bf16[528,256]{1,0:T(8,128)(2,1)S(1)} %collective-permute-done.12.refs_2_), channel_id=1, source_target_pairs={{0,1},{1,0},{2,3},{3,2},{4,5},{5,4},{6,7},{7,6},{8,9},{9,8},{10,11... | collective-permute-start | bytes 811016 | tf_op jit(solution)/shard_map/ppermute | solution.py:457
  71.2 6.7 %collective-permute-start.20 = (bf16[528,256]{1,0:T(8,128)(2,1)S(1)}, bf16[528,256]{1,0:T(8,128)(2,1)S(1)}, u32[]{:S(2)}, u32[]{:S(2)}) collective-permute-start(bf16[528,256]{1,0:T(8,128)(2,1)S(1)} %collective-permute-done.11.refs_1_.refs_5_), channel_id=1, source_target_pairs={{0,1},{1,0},{2,3},{3,2},{4,5},{5,4},{6,7},{7,6},{8,9},{9,8},{10,11... | collective-permute-start | bytes 811016 | tf_op jit(solution)/shard_map/ppermute | solution.py:457
  73.5 1.4 %copy-start.1 = (bf16[4,512,512]{2,1,0:T(8,128)(2,1)}, bf16[4,512,512]{2,1,0:T(8,128)(2,1)S(1)}, u32[]{:S(2)}) copy-start(bf16[4,512,512]{2,1,0:T(8,128)(2,1)S(1)} %shard_map.88.refs_0_.refs_1_) | copy-start | bytes 6291460
  76.1 1.4 %copy-start.5 = (bf16[4,512,512]{2,1,0:T(8,128)(2,1)}, bf16[4,512,512]{2,1,0:T(8,128)(2,1)S(1)}, u32[]{:S(2)}) copy-start(bf16[4,512,512]{2,1,0:T(8,128)(2,1)S(1)} %shard_map.87.refs_0_) | copy-start | bytes 6291460
  77.9 3.3 %collective-permute-start.21 = (bf16[528,256]{1,0:T(8,128)(2,1)S(1)}, bf16[528,256]{1,0:T(8,128)(2,1)S(1)}, u32[]{:S(2)}, u32[]{:S(2)}) collective-permute-start(bf16[528,256]{1,0:T(8,128)(2,1)S(1)} %collective-permute-done.16.refs_3_), channel_id=1, source_target_pairs={{0,1},{1,0},{2,3},{3,2},{4,5},{5,4},{6,7},{7,6},{8,9},{9,8},{10,11... | collective-permute-start | bytes 811016 | tf_op jit(solution)/shard_map/ppermute | solution.py:457
  79.9 1.4 %copy-start.3 = (bf16[4,512,512]{2,1,0:T(8,128)(2,1)}, bf16[4,512,512]{2,1,0:T(8,128)(2,1)S(1)}, u32[]{:S(2)}) copy-start(bf16[4,512,512]{2,1,0:T(8,128)(2,1)S(1)} %shard_map.89.refs_1_.refs_0_) | copy-start | bytes 6291460
  82.5 1.3 %copy-start.8 = (bf16[4,512,512]{2,1,0:T(8,128)(2,1)}, bf16[4,512,512]{2,1,0:T(8,128)(2,1)S(1)}, u32[]{:S(2)}) copy-start(bf16[4,512,512]{2,1,0:T(8,128)(2,1)S(1)} %shard_map.90.refs_0_.refs_1_) | copy-start | bytes 6291460
  86.4 1.6 %copy-start.6 = (bf16[4,512,512]{2,1,0:T(8,128)(2,1)S(1)}, bf16[4,512,512]{2,1,0:T(8,128)(2,1)}, u32[]{:S(2)}) copy-start(bf16[4,512,512]{2,1,0:T(8,128)(2,1)} %copy-done.5) | copy-start | bytes 6291460
  88.0 2.3 %copy-start.2 = (bf16[4,512,512]{2,1,0:T(8,128)(2,1)S(1)}, bf16[4,512,512]{2,1,0:T(8,128)(2,1)}, u32[]{:S(2)}) copy-start(bf16[4,512,512]{2,1,0:T(8,128)(2,1)} %copy-done.1) | copy-start | bytes 6291460
  88.0 2.3 %copy-start.4 = (bf16[4,512,512]{2,1,0:T(8,128)(2,1)S(1)}, bf16[4,512,512]{2,1,0:T(8,128)(2,1)}, u32[]{:S(2)}) copy-start(bf16[4,512,512]{2,1,0:T(8,128)(2,1)} %copy-done.3) | copy-start | bytes 6291460
  88.7 5.9 %collective-permute-start.22 = (bf16[128,512]{1,0:T(8,128)(2,1)S(1)}, bf16[128,512]{1,0:T(8,128)(2,1)S(1)}, u32[]{:S(2)}, u32[]{:S(2)}) collective-permute-start(bf16[128,512]{1,0:T(8,128)(2,1)S(1)} %get-tuple-element.129), channel_id=1, source_target_pairs={{0,4},{1,5},{2,6},{3,7},{4,0},{5,1},{6,2},{7,3},{8,12},{9,13},{10,... | collective-permute-start | bytes 393224 | tf_op jit(solution)/shard_map/ppermute | solution.py:457
  90.2 4.3 %copy-start.9 = (bf16[4,512,512]{2,1,0:T(8,128)(2,1)S(1)}, bf16[4,512,512]{2,1,0:T(8,128)(2,1)}, u32[]{:S(2)}) copy-start(bf16[4,512,512]{2,1,0:T(8,128)(2,1)} %copy-done.8) | copy-start | bytes 6291460
  91.5 9.3 %collective-permute-start.23 = (bf16[128,1024]{1,0:T(8,128)(2,1)S(1)}, bf16[128,1024]{1,0:T(8,128)(2,1)S(1)}, u32[]{:S(2)}, u32[]{:S(2)}) collective-permute-start(bf16[128,1024]{1,0:T(8,128)(2,1)S(1)} %get-tuple-element.133), channel_id=1, source_target_pairs={{0,4},{1,5},{2,6},{3,7},{4,0},{5,1},{6,2},{7,3},{8,12},{9,13},{10,... | collective-permute-start | bytes 786440 | tf_op jit(solution)/shard_map/ppermute | solution.py:457
  95.3 2.6 %copy-start.7 = (bf16[4,512,512]{2,1,0:T(8,128)(2,1)S(1)}, bf16[4,512,512]{2,1,0:T(8,128)(2,1)}, u32[]{:S(2)}) copy-start(bf16[4,512,512]{2,1,0:T(8,128)(2,1)} %copy-done.5) | copy-start | bytes 6291460
  95.3 8.7 %collective-permute-start.24 = (bf16[128,512]{1,0:T(8,128)(2,1)S(1)}, bf16[128,512]{1,0:T(8,128)(2,1)S(1)}, u32[]{:S(2)}, u32[]{:S(2)}) collective-permute-start(bf16[128,512]{1,0:T(8,128)(2,1)S(1)} %get-tuple-element.142), channel_id=1, source_target_pairs={{0,4},{1,5},{2,6},{3,7},{4,0},{5,1},{6,2},{7,3},{8,12},{9,13},{10,... | collective-permute-start | bytes 393224 | tf_op jit(solution)/shard_map/ppermute | solution.py:457
  97.9 6.1 %copy-start.17 = (bf16[528,256]{1,0:T(8,128)(2,1)S(1)}, bf16[528,256]{1,0:T(8,128)(2,1)}, u32[]{:S(2)}) copy-start(bf16[528,256]{1,0:T(8,128)(2,1)} %copy-done.16) | copy-start | bytes 811012
  97.9 6.1 %copy-start.19 = (bf16[528,256]{1,0:T(8,128)(2,1)S(1)}, bf16[528,256]{1,0:T(8,128)(2,1)}, u32[]{:S(2)}) copy-start(bf16[528,256]{1,0:T(8,128)(2,1)} %copy-done.18) | copy-start | bytes 811012
  97.9 6.1 %copy-start.20 = (f32[128,256]{1,0:T(8,128)S(1)}, f32[128,256]{1,0:T(8,128)}, u32[]{:S(2)}) copy-start(f32[128,256]{1,0:T(8,128)} %dynamic-slice_convert_fusion.taps_ref) | copy-start | bytes 393220
  100.8 10.7 %collective-permute-start.25 = (bf16[128,1024]{1,0:T(8,128)(2,1)S(1)}, bf16[128,1024]{1,0:T(8,128)(2,1)S(1)}, u32[]{:S(2)}, u32[]{:S(2)}) collective-permute-start(bf16[128,1024]{1,0:T(8,128)(2,1)S(1)} %get-tuple-element.146), channel_id=1, source_target_pairs={{0,4},{1,5},{2,6},{3,7},{4,0},{5,1},{6,2},{7,3},{8,12},{9,13},{10,... | collective-permute-start | bytes 786440 | tf_op jit(solution)/shard_map/ppermute | solution.py:457
  102.2 11.1 %collective-permute-start.26 = (bf16[128,1024]{1,0:T(8,128)(2,1)S(1)}, bf16[128,1024]{1,0:T(8,128)(2,1)S(1)}, u32[]{:S(2)}, u32[]{:S(2)}) collective-permute-start(bf16[128,1024]{1,0:T(8,128)(2,1)S(1)} %get-tuple-element.148), channel_id=1, source_target_pairs={{0,4},{1,5},{2,6},{3,7},{4,0},{5,1},{6,2},{7,3},{8,12},{9,13},{10,... | collective-permute-start | bytes 786440 | tf_op jit(solution)/shard_map/ppermute | solution.py:457
  (1 other events, 1.1 us)

commit v7 on v6

--- a/solution.py
+++ b/solution.py
@@ -531,9 +531,9 @@
     got3, kept3_far = across(give3), to_owner(kept3, far_owner)
     all1 = to_near([kept1, got1, kept1_far, got1_far])
     all0 = to_near([most0])
+    got3_far = to_owner(got3, far_owner)
     got3, kept3_far, got2_far, all0, all1 = tie(got3, kept3_far, got2_far, all0, all1)
 
-    got3_far = to_owner(got3, far_owner)
     all2 = to_near([kept2, got2, kept2_far, got2_far])
     near_kept3, near_kept3_far, near_got3 = [to_near([some]) for some in (kept3, kept3_far, got3)]
     normed0 = scaled([kept0, got0, kept0_far, got0_far, all0])
@@ -564,7 +564,7 @@
     early = place(
         row_first, total_rows, value0, theirs0, places[:, :wide], tall, [kept0, got0]
     )
-    theirs1, gate_far0, gate_far2 = tie(theirs1, gate_far0, gate_far2)
+    theirs1, early, gate_far0, gate_far2 = tie(theirs1, early, gate_far0, gate_far2)
     gate_theirs0, gate_theirs2 = across(gate_far0), across(gate_far2)
     banded, packed = band_of(
         flags, row_first, taps, skip, early, (value1, theirs1), (value3, theirs3),

time: 133 us -> 133 us (level)
  transfers between devices with their start and end apart: 28 -> 28, of which waited for: 14 -> 15; matrix products, arithmetic and copies ran while one was open for 7% -> 7% of each run, Pallas kernels for 18% -> 18%
where the time goes in v7:
time: 133 us; the launch traced here: 132 us
  starting transfers between devices  34.2 us (26%)
  waiting for transfers between devices  32.3 us (24%)
  Pallas kernels  26.5 us (20%)
  blocking collectives  16 us (12%)
  local copies, waits for them, and re-layouts  15.7 us (12%)
  other arithmetic  6.62 us (5%)
    ppermute x27, waiting for transfers between devices, send(): return lax.ppermute(array, AXES, pairs)  29.8 us
    ppermute x27, starting transfers between devices, send(): return lax.ppermute(array, AXES, pairs)  29.4 us
    all_to_all x1, blocking collectives, on_device_line(): lax.all_to_all(mixed, AXES, split_axis=0, concat_axis=0, tiled=True, axis...  16 us
    unnamed x44, local copies, waits for them, and re-layouts  13 us
    pallas_call x1, Pallas kernels, band_of(): pl.pallas_call(functools.partial(band_kernel, taps_blocks, tall), out_sha...  7.59 us
    pallas_call x4, Pallas kernels, scale(): pl.pallas_call(functools.partial(scale_kernel, height), out_shape=jax.Sha...  6.07 us
    pallas_call x5, Pallas kernels, project(): pl.pallas_call(functools.partial(project_kernel, number, row_count), out_...  5.19 us
    all_to_all x1, starting transfers between devices, along_line(): lax.all_to_all(array, AXES, split_axis=0, concat_axis=0, tiled=True, axis...  4.88 us
  transfers between devices with their start and end apart: 28, of which 15 were waited for; matrix products, arithmetic and copies ran while one was open for 7% of the time, Pallas kernels for 18%

profile of v7, /device:TPU:0, one launch (start us, length us, event | category | flops | bytes accessed | tf_op | source)
XLA Modules:
  0.0 131.8 jit_solution(13291300347204719046)
XLA Ops:
  0.0 3.0 %collective-permute-start.4 = (bf16[1024,256]{1,0:T(8,128)(2,1)}, bf16[1024,256]{1,0:T(8,128)(2,1)S(1)}, u32[]{:S(2)}, u32[]{:S(2)}) collective-permute-start(bf16[1024,256]{1,0:T(8,128)(2,1)} %token_ref.1), channel_id=1, source_target_pairs={{0,8},{1,9},{2,10},{3,11},{4,12},{5,13},{6,14},{7,15},{8,0},{9,1},... | collective-permute-start | bytes 1572872 | tf_op jit(solution)/shard_map/ppermute | solution.py:457
  3.0 2.6 %collective-permute-start = (bf16[1024,256]{1,0:T(8,128)(2,1)}, bf16[1024,256]{1,0:T(8,128)(2,1)}, u32[]{:S(2)}, u32[]{:S(2)}) collective-permute-start(bf16[1024,256]{1,0:T(8,128)(2,1)} %token_ref.1), channel_id=1, source_target_pairs={{0,16},{1,17},{2,18},{3,19},{4,20},{5,21},{6,22},{7,23},{8,24},{9,... | collective-permute-start | bytes 1572872 | tf_op jit(solution)/shard_map/ppermute | solution.py:457
  6.8 1.6 %collective-permute-start.1 = (bf16[528,256]{1,0:T(8,128)(2,1)S(1)}, bf16[528,256]{1,0:T(8,128)(2,1)S(1)}, u32[]{:S(2)}, u32[]{:S(2)}) collective-permute-start(bf16[528,256]{1,0:T(8,128)(2,1)S(1)} %get-tuple-element.78.after_ref), channel_id=1, source_target_pairs={{0,4},{1,5},{2,6},{3,7},{4,0},{5,1},{6,2},{7,3},{8,12},{9,13},{10,... | collective-permute-start | bytes 811016 | tf_op jit(solution)/shard_map/ppermute | solution.py:457
  8.3 1.5 %collective-permute-start.2 = (bf16[528,256]{1,0:T(8,128)(2,1)S(1)}, bf16[528,256]{1,0:T(8,128)(2,1)S(1)}, u32[]{:S(2)}, u32[]{:S(2)}) collective-permute-start(bf16[528,256]{1,0:T(8,128)(2,1)S(1)} %get-tuple-element.79.refs_0_), channel_id=1, source_target_pairs={{0,2},{1,3},{2,0},{3,1},{4,6},{5,7},{6,4},{7,5},{8,10},{9,11},{10,... | collective-permute-start | bytes 811016 | tf_op jit(solution)/shard_map/ppermute | solution.py:457
  14.5 1.5 %collective-permute-start.3 = (bf16[528,256]{1,0:T(8,128)(2,1)S(1)}, bf16[528,256]{1,0:T(8,128)(2,1)S(1)}, u32[]{:S(2)}, u32[]{:S(2)}) collective-permute-start(bf16[528,256]{1,0:T(8,128)(2,1)S(1)} %collective-permute-done.1.refs_1_), channel_id=1, source_target_pairs={{0,2},{1,3},{2,0},{3,1},{4,6},{5,7},{6,4},{7,5},{8,10},{9,11},{10,... | collective-permute-start | bytes 811016 | tf_op jit(solution)/shard_map/ppermute | solution.py:457
  16.2 1.2 copy-done.13
  17.4 1.2 copy-done.14
  19.3 1.3 %copy-done.10 = bf16[4,2,2,128,512]{4,3,2,1,0:T(8,128)(2,1)} copy-done((bf16[4,2,2,128,512]{4,3,2,1,0:T(8,128)(2,1)}, bf16[4,2,2,128,512]{4,3,2,1,0:T(8,128)(2,1)S(1)}, u32[]{:S(2)}) %copy-start.10) | copy-done | bytes 2097176
  21.2 1.5 %dynamic-slice_convert_fusion.taps_ref = f32[128,256]{1,0:T(8,128)} fusion(bf16[1024,256]{1,0:T(8,128)(2,1)} %param.13, s32[]{:T(128)S(6)} %select_n.50), kind=kLoop, calls=%fused_computation.5 | loop fusion | flops 32768 | bytes 196612 | tf_op jit(solution)/shard_map/convert_element_type | solution.py:485
  23.8 2.5 %collective-permute-done.4.token_ref = bf16[1024,256]{1,0:T(8,128)(2,1)S(1)} collective-permute-done((bf16[1024,256]{1,0:T(8,128)(2,1)}, bf16[1024,256]{1,0:T(8,128)(2,1)S(1)}, u32[]{:S(2)}, u32[]{:S(2)}) %collective-permute-start.4) | collective-permute-done | bytes 524320 | tf_op jit(solution)/shard_map/ppermute | solution.py:457
  26.4 2.6 %collective-permute-done.token_ref = bf16[1024,256]{1,0:T(8,128)(2,1)} collective-permute-done((bf16[1024,256]{1,0:T(8,128)(2,1)}, bf16[1024,256]{1,0:T(8,128)(2,1)}, u32[]{:S(2)}, u32[]{:S(2)}) %collective-permute-start) | collective-permute-done | bytes 524320 | tf_op jit(solution)/shard_map/ppermute | solution.py:457
  28.9 1.5 %collective-permute-start.6 = (bf16[528,256]{1,0:T(8,128)(2,1)S(1)}, bf16[528,256]{1,0:T(8,128)(2,1)S(1)}, u32[]{:S(2)}, u32[]{:S(2)}) collective-permute-start(bf16[528,256]{1,0:T(8,128)(2,1)S(1)} %get-tuple-element.92), channel_id=1, source_target_pairs={{0,4},{1,5},{2,6},{3,7},{4,0},{5,1},{6,2},{7,3},{8,12},{9,13},{10,... | collective-permute-start | bytes 811016 | tf_op jit(solution)/shard_map/ppermute | solution.py:457
  30.8 2.0 %shard_map.85 = (bf16[528,256]{1,0:T(8,128)(2,1)}, bf16[528,256]{1,0:T(8,128)(2,1)}) custom-call(s32[1]{0:T(128)} %bitcast.x_ref, bf16[1024,256]{1,0:T(8,128)(2,1)} %collective-permute-done.token_ref), custom_call_target="tpu_custom_call" | custom-call | flops 524288 | bytes 1048576 | tf_op jit(solution)/shard_map/pallas_call | solution.py:151
  32.8 1.5 %collective-permute-start.10 = (bf16[528,256]{1,0:T(8,128)(2,1)}, bf16[528,256]{1,0:T(8,128)(2,1)}, u32[]{:S(2)}, u32[]{:S(2)}) collective-permute-start(bf16[528,256]{1,0:T(8,128)(2,1)} %get-tuple-element.96.refs_0_.refs_2_), channel_id=1, source_target_pairs={{0,2},{1,3},{2,0},{3,1},{4,6},{5,7},{6,4},{7,5},{8,10},{9,11},{10,... | collective-permute-start | bytes 811016 | tf_op jit(solution)/shard_map/ppermute | solution.py:457
  35.5 2.6 %collective-permute-start.8 = (bf16[528,256]{1,0:T(8,128)(2,1)S(1)}, bf16[528,256]{1,0:T(8,128)(2,1)}, u32[]{:S(2)}, u32[]{:S(2)}) collective-permute-start(bf16[528,256]{1,0:T(8,128)(2,1)S(1)} %collective-permute-done.6.refs_1_), channel_id=1, source_target_pairs={{0,2},{1,3},{2,0},{3,1},{4,6},{5,7},{6,4},{7,5},{8,10},{9,11},{10,... | collective-permute-start | bytes 811016 | tf_op jit(solution)/shard_map/ppermute | solution.py:457
  38.1 4.9 %all-to-all-start = ((bf16[4,2,2,128,512]{4,3,2,1,0:T(8,128)(2,1)}), bf16[4,2,2,128,512]{4,3,2,1,0:T(8,128)(2,1)S(1)}, u32[]{:S(2)}, u32[]{:S(2)}) async-start(bf16[4,2,2,128,512]{4,3,2,1,0:T(8,128)(2,1)} %copy-done.10), calls=%async_computation | async-start | bytes 4194304 | tf_op jit(solution)/shard_map/all_to_all | solution.py:468
  43.0 5.4 %collective-permute-done.7.refs_2_ = bf16[528,256]{1,0:T(8,128)(2,1)} collective-permute-done((bf16[528,256]{1,0:T(8,128)(2,1)S(1)}, bf16[528,256]{1,0:T(8,128)(2,1)}, u32[]{:S(2)}, u32[]{:S(2)}) %collective-permute-start.7) | collective-permute-done | bytes 270368 | tf_op jit(solution)/shard_map/ppermute | solution.py:457
  48.4 3.1 %collective-permute-done.8.refs_3_ = bf16[528,256]{1,0:T(8,128)(2,1)} collective-permute-done((bf16[528,256]{1,0:T(8,128)(2,1)S(1)}, bf16[528,256]{1,0:T(8,128)(2,1)}, u32[]{:S(2)}, u32[]{:S(2)}) %collective-permute-start.8) | collective-permute-done | bytes 270368 | tf_op jit(solution)/shard_map/ppermute | solution.py:457
  51.5 1.1 pad_maximum_fusion.1
  52.7 1.9 %collective-permute-start.13 = (bf16[528,256]{1,0:T(8,128)(2,1)}, bf16[528,256]{1,0:T(8,128)(2,1)S(1)}, u32[]{:S(2)}, u32[]{:S(2)}) collective-permute-start(bf16[528,256]{1,0:T(8,128)(2,1)} %collective-permute-done.9.refs_1_.refs_3_), channel_id=1, source_target_pairs={{0,2},{1,3},{2,0},{3,1},{4,6},{5,7},{6,4},{7,5},{8,10},{9,11},{10,... | collective-permute-start | bytes 811016 | tf_op jit(solution)/shard_map/ppermute | solution.py:457
  54.6 1.2 shard_map.86
  56.5 5.7 %collective-permute-done.13.refs_3_ = bf16[528,256]{1,0:T(8,128)(2,1)S(1)} collective-permute-done((bf16[528,256]{1,0:T(8,128)(2,1)}, bf16[528,256]{1,0:T(8,128)(2,1)S(1)}, u32[]{:S(2)}, u32[]{:S(2)}) %collective-permute-start.13) | collective-permute-done | bytes 270368 | tf_op jit(solution)/shard_map/ppermute | solution.py:457
  62.2 2.2 %collective-permute-done.11.refs_1_.refs_5_ = bf16[528,256]{1,0:T(8,128)(2,1)S(1)} collective-permute-done((bf16[528,256]{1,0:T(8,128)(2,1)S(1)}, bf16[528,256]{1,0:T(8,128)(2,1)S(1)}, u32[]{:S(2)}, u32[]{:S(2)}) %collective-permute-start.11) | collective-permute-done | bytes 270368 | tf_op jit(solution)/shard_map/ppermute | solution.py:457
  64.4 3.3 %collective-permute-done.12.refs_2_ = bf16[528,256]{1,0:T(8,128)(2,1)S(1)} collective-permute-done((bf16[528,256]{1,0:T(8,128)(2,1)S(1)}, bf16[528,256]{1,0:T(8,128)(2,1)S(1)}, u32[]{:S(2)}, u32[]{:S(2)}) %collective-permute-start.12) | collective-permute-done | bytes 270368 | tf_op jit(solution)/shard_map/ppermute | solution.py:457
  67.7 1.2 pad_maximum_fusion.2
  69.5 1.8 %collective-permute-start.16 = (bf16[528,256]{1,0:T(8,128)(2,1)S(1)}, bf16[528,256]{1,0:T(8,128)(2,1)S(1)}, u32[]{:S(2)}, u32[]{:S(2)}) collective-permute-start(bf16[528,256]{1,0:T(8,128)(2,1)S(1)} %collective-permute-done.11.refs_1_.refs_5_), channel_id=1, source_target_pairs={{0,2},{1,3},{2,0},{3,1},{4,6},{5,7},{6,4},{7,5},{8,10},{9,11},{10,... | collective-permute-start | bytes 811016 | tf_op jit(solution)/shard_map/ppermute | solution.py:457
  71.7 1.7 %shard_map.88.refs_0_.refs_1_ = bf16[4,512,512]{2,1,0:T(8,128)(2,1)S(1)} custom-call(s32[4]{0:T(128)S(1)} %pad_add_fusion.1.pick_ref, f32[8,512]{1,0:T(8,128)S(1)} %pad.4.gain_ref, bf16[528,256]{1,0:T(8,128)(2,1)S(1)} %get-tuple-element.93.refs_0_, bf16[528,256]{1,0:T(8,128)(2,1)S(1)} %collective-permute-done.6.refs_1_, ...), custom_call_target="tpu_custom_call" | custom-call | flops 2097152 | bytes 4194304 | tf_op jit(solution)/shard_map/pallas_call | solution.py:218
  73.5 1.3 %copy-done.1 = bf16[4,512,512]{2,1,0:T(8,128)(2,1)} copy-done((bf16[4,512,512]{2,1,0:T(8,128)(2,1)}, bf16[4,512,512]{2,1,0:T(8,128)(2,1)S(1)}, u32[]{:S(2)}) %copy-start.1) | copy-done | bytes 2097176
  74.8 1.3 shard_map.87.refs_0_
  76.1 1.4 %copy-done.5 = bf16[4,512,512]{2,1,0:T(8,128)(2,1)} copy-done((bf16[4,512,512]{2,1,0:T(8,128)(2,1)}, bf16[4,512,512]{2,1,0:T(8,128)(2,1)S(1)}, u32[]{:S(2)}) %copy-start.5) | copy-done | bytes 2097176
  78.0 1.8 %shard_map.89.refs_1_.refs_0_ = bf16[4,512,512]{2,1,0:T(8,128)(2,1)S(1)} custom-call(s32[4]{0:T(128)S(1)} %pad_add_fusion.1.pick_ref, f32[8,512]{1,0:T(8,128)S(1)} %pad.4.gain_ref, bf16[528,256]{1,0:T(8,128)(2,1)} %get-tuple-element.96.refs_0_.refs_2_, bf16[528,256]{1,0:T(8,128)(2,1)} %collective-permute-done.9.refs_1_.refs_3_, ...), custom_call_target="tpu_custom_call" | custom-call | flops 2097152 | bytes 4194304 | tf_op jit(solution)/shard_map/pallas_call | solution.py:218
  79.9 1.4 %copy-done.3 = bf16[4,512,512]{2,1,0:T(8,128)(2,1)} copy-done((bf16[4,512,512]{2,1,0:T(8,128)(2,1)}, bf16[4,512,512]{2,1,0:T(8,128)(2,1)S(1)}, u32[]{:S(2)}) %copy-start.3) | copy-done | bytes 2097176
  81.2 1.3 shard_map.90.refs_0_.refs_1_
  82.5 1.3 copy-done.8
  83.8 2.5 %all-to-all-done.weight_ref = bf16[4,2,2,128,512]{4,3,2,1,0:T(8,128)(2,1)S(1)} async-done(((bf16[4,2,2,128,512]{4,3,2,1,0:T(8,128)(2,1)}), bf16[4,2,2,128,512]{4,3,2,1,0:T(8,128)(2,1)S(1)}, u32[]{:S(2)}, u32[]{:S(2)}) %all-to-all-start) | async-done | bytes 2097184 | tf_op jit(solution)/shard_map/all_to_all | solution.py:468
  86.4 1.6 %copy-done.6 = bf16[4,512,512]{2,1,0:T(8,128)(2,1)S(1)} copy-done((bf16[4,512,512]{2,1,0:T(8,128)(2,1)S(1)}, bf16[4,512,512]{2,1,0:T(8,128)(2,1)}, u32[]{:S(2)}) %copy-start.6) | copy-done | bytes 2097176
  88.7 1.6 %collective-permute-start.23 = (bf16[128,512]{1,0:T(8,128)(2,1)S(1)}, bf16[128,512]{1,0:T(8,128)(2,1)S(1)}, u32[]{:S(2)}, u32[]{:S(2)}) collective-permute-start(bf16[128,512]{1,0:T(8,128)(2,1)S(1)} %get-tuple-element.131), channel_id=1, source_target_pairs={{0,4},{1,5},{2,6},{3,7},{4,0},{5,1},{6,2},{7,3},{8,12},{9,13},{10,... | collective-permute-start | bytes 393224 | tf_op jit(solution)/shard_map/ppermute | solution.py:457
  90.2 1.3 shard_map.92
  91.5 1.5 %collective-permute-start.22 = (bf16[128,1024]{1,0:T(8,128)(2,1)S(1)}, bf16[128,1024]{1,0:T(8,128)(2,1)S(1)}, u32[]{:S(2)}, u32[]{:S(2)}) collective-permute-start(bf16[128,1024]{1,0:T(8,128)(2,1)S(1)} %get-tuple-element.127), channel_id=1, source_target_pairs={{0,4},{1,5},{2,6},{3,7},{4,0},{5,1},{6,2},{7,3},{8,12},{9,13},{10,... | collective-permute-start | bytes 786440 | tf_op jit(solution)/shard_map/ppermute | solution.py:457
  93.0 1.5 %collective-permute-done.23.theirs_ref = bf16[128,512]{1,0:T(8,128)(2,1)S(1)} collective-permute-done((bf16[128,512]{1,0:T(8,128)(2,1)S(1)}, bf16[128,512]{1,0:T(8,128)(2,1)S(1)}, u32[]{:S(2)}, u32[]{:S(2)}) %collective-permute-start.23) | collective-permute-done | bytes 131104 | tf_op jit(solution)/shard_map/ppermute | solution.py:457
  95.2 1.3 %collective-permute-start.24 = (bf16[128,512]{1,0:T(8,128)(2,1)S(1)}, bf16[128,512]{1,0:T(8,128)(2,1)S(1)}, u32[]{:S(2)}, u32[]{:S(2)}) collective-permute-start(bf16[128,512]{1,0:T(8,128)(2,1)S(1)} %get-tuple-element.144), channel_id=1, source_target_pairs={{0,4},{1,5},{2,6},{3,7},{4,0},{5,1},{6,2},{7,3},{8,12},{9,13},{10,... | collective-permute-start | bytes 393224 | tf_op jit(solution)/shard_map/ppermute | solution.py:457
  97.6 1.3 shard_map.96
  99.2 1.3 shard_map.95
  100.8 1.4 %collective-permute-start.25 = (bf16[128,1024]{1,0:T(8,128)(2,1)S(1)}, bf16[128,1024]{1,0:T(8,128)(2,1)S(1)}, u32[]{:S(2)}, u32[]{:S(2)}) collective-permute-start(bf16[128,1024]{1,0:T(8,128)(2,1)S(1)} %get-tuple-element.148), channel_id=1, source_target_pairs={{0,4},{1,5},{2,6},{3,7},{4,0},{5,1},{6,2},{7,3},{8,12},{9,13},{10,... | collective-permute-start | bytes 786440 | tf_op jit(solution)/shard_map/ppermute | solution.py:457
  103.6 7.6 %shard_map.97 = (bf16[128,2048]{1,0:T(8,128)(2,1)S(1)}, bf16[128,2048]{1,0:T(8,128)(2,1)S(1)}) custom-call(f32[8]{0:T(128)S(1)} %broadcast_select_fusion.flag_ref, s32[1]{0:T(128)} %bitcast.13.first_ref, f32[128,256]{1,0:T(8,128)S(1)} %copy-done.20, f32[1,128]{1,0:T(1,128)S(1)} %dynamic-slice_bitcast_fusion.skip_ref, ...), custom_call_target="tpu_custom_call" | custom-call | flops 1610612736 | bytes 4194304 | tf_op jit(solution)/shard_map/pallas_call | solution.py:396
  111.3 1.1 shard_map.98.early_ref
  113.4 1.6 %shard_map.99 = bf16[8,128,256]{2,1,0:T(8,128)(2,1)S(1)} custom-call(bf16[128,2048]{1,0:T(8,128)(2,1)S(1)} %get-tuple-element.145.z_ref, bf16[128,2048]{1,0:T(8,128)(2,1)S(1)} %get-tuple-element.146.packed_ref, bf16[128,2048]{1,0:T(8,128)(2,1)S(1)} %shard_map.98.early_ref, f32[128,1024]{1,0:T(8,128)S(1)} %get-tuple-element.149.mine_ref, ...), custom_call_target="tpu_custom_call" | custom-call | flops 536870912 | bytes 4194304 | tf_op jit(solution)/shard_map/pallas_call | solution.py:424
  115.0 16.0 %all_to_all.10 = bf16[8,128,256]{2,1,0:T(8,128)(2,1)S(1)} all-to-all(bf16[8,128,256]{2,1,0:T(8,128)(2,1)S(1)} %shard_map.99), channel_id=1, replica_groups={{0,8,16,24,4,12,20,28},{1,9,17,25,5,13,21,29},{2,10,18,26,6,14,22,30},{..., dimensions={0} | all-to-all | bytes 1048576 | tf_op jit(solution)/shard_map/all_to_all | solution.py:577
  (96 shorter events, 18.6 us)
Async XLA Ops:
  0.0 16.0 %copy-start = (f32[1024]{0:T(1024)S(1)}, f32[1024]{0:T(1024)}, u32[]{:S(2)}) copy-start(f32[1024]{0:T(1024)} %param.14) | copy-start | bytes 12292
  0.0 26.3 %collective-permute-start.4 = (bf16[1024,256]{1,0:T(8,128)(2,1)}, bf16[1024,256]{1,0:T(8,128)(2,1)S(1)}, u32[]{:S(2)}, u32[]{:S(2)}) collective-permute-start(bf16[1024,256]{1,0:T(8,128)(2,1)} %token_ref.1), channel_id=1, source_target_pairs={{0,8},{1,9},{2,10},{3,11},{4,12},{5,13},{6,14},{7,15},{8,0},{9,1},... | collective-permute-start | bytes 1572872 | tf_op jit(solution)/shard_map/ppermute | solution.py:457
  3.0 25.9 %collective-permute-start = (bf16[1024,256]{1,0:T(8,128)(2,1)}, bf16[1024,256]{1,0:T(8,128)(2,1)}, u32[]{:S(2)}, u32[]{:S(2)}) collective-permute-start(bf16[1024,256]{1,0:T(8,128)(2,1)} %token_ref.1), channel_id=1, source_target_pairs={{0,16},{1,17},{2,18},{3,19},{4,20},{5,21},{6,22},{7,23},{8,24},{9,... | collective-permute-start | bytes 1572872 | tf_op jit(solution)/shard_map/ppermute | solution.py:457
  6.8 7.7 %collective-permute-start.1 = (bf16[528,256]{1,0:T(8,128)(2,1)S(1)}, bf16[528,256]{1,0:T(8,128)(2,1)S(1)}, u32[]{:S(2)}, u32[]{:S(2)}) collective-permute-start(bf16[528,256]{1,0:T(8,128)(2,1)S(1)} %get-tuple-element.78.after_ref), channel_id=1, source_target_pairs={{0,4},{1,5},{2,6},{3,7},{4,0},{5,1},{6,2},{7,3},{8,12},{9,13},{10,... | collective-permute-start | bytes 811016 | tf_op jit(solution)/shard_map/ppermute | solution.py:457
  8.3 14.4 %collective-permute-start.2 = (bf16[528,256]{1,0:T(8,128)(2,1)S(1)}, bf16[528,256]{1,0:T(8,128)(2,1)S(1)}, u32[]{:S(2)}, u32[]{:S(2)}) collective-permute-start(bf16[528,256]{1,0:T(8,128)(2,1)S(1)} %get-tuple-element.79.refs_0_), channel_id=1, source_target_pairs={{0,2},{1,3},{2,0},{3,1},{4,6},{5,7},{6,4},{7,5},{8,10},{9,11},{10,... | collective-permute-start | bytes 811016 | tf_op jit(solution)/shard_map/ppermute | solution.py:457
  14.5 8.2 %collective-permute-start.3 = (bf16[528,256]{1,0:T(8,128)(2,1)S(1)}, bf16[528,256]{1,0:T(8,128)(2,1)S(1)}, u32[]{:S(2)}, u32[]{:S(2)}) collective-permute-start(bf16[528,256]{1,0:T(8,128)(2,1)S(1)} %collective-permute-done.1.refs_1_), channel_id=1, source_target_pairs={{0,2},{1,3},{2,0},{3,1},{4,6},{5,7},{6,4},{7,5},{8,10},{9,11},{10,... | collective-permute-start | bytes 811016 | tf_op jit(solution)/shard_map/ppermute | solution.py:457
  16.2 1.2 copy-start.13
  17.4 1.2 copy-start.14
  19.3 1.3 %copy-start.10 = (bf16[4,2,2,128,512]{4,3,2,1,0:T(8,128)(2,1)}, bf16[4,2,2,128,512]{4,3,2,1,0:T(8,128)(2,1)S(1)}, u32[]{:S(2)}) copy-start(bf16[4,2,2,128,512]{4,3,2,1,0:T(8,128)(2,1)S(1)} %shard_map.83) | copy-start | bytes 6291460
  22.7 15.4 %copy-start.11 = (bf16[528,256]{1,0:T(8,128)(2,1)}, bf16[528,256]{1,0:T(8,128)(2,1)S(1)}, u32[]{:S(2)}) copy-start(bf16[528,256]{1,0:T(8,128)(2,1)S(1)} %collective-permute-done.3.refs_3_) | copy-start | bytes 811012
  28.9 6.6 %collective-permute-start.6 = (bf16[528,256]{1,0:T(8,128)(2,1)S(1)}, bf16[528,256]{1,0:T(8,128)(2,1)S(1)}, u32[]{:S(2)}, u32[]{:S(2)}) collective-permute-start(bf16[528,256]{1,0:T(8,128)(2,1)S(1)} %get-tuple-element.92), channel_id=1, source_target_pairs={{0,4},{1,5},{2,6},{3,7},{4,0},{5,1},{6,2},{7,3},{8,12},{9,13},{10,... | collective-permute-start | bytes 811016 | tf_op jit(solution)/shard_map/ppermute | solution.py:457
  30.4 17.9 %collective-permute-start.5 = (bf16[1024,256]{1,0:T(8,128)(2,1)}, bf16[1024,256]{1,0:T(8,128)(2,1)}, u32[]{:S(2)}, u32[]{:S(2)}) collective-permute-start(bf16[1024,256]{1,0:T(8,128)(2,1)} %collective-permute-done.token_ref), channel_id=1, source_target_pairs={{0,8},{1,9},{2,10},{3,11},{4,12},{5,13},{6,14},{7,15},{8,0},{9,1},... | collective-permute-start | bytes 1572872 | tf_op jit(solution)/shard_map/ppermute | solution.py:457
  32.8 10.2 %collective-permute-start.10 = (bf16[528,256]{1,0:T(8,128)(2,1)}, bf16[528,256]{1,0:T(8,128)(2,1)}, u32[]{:S(2)}, u32[]{:S(2)}) collective-permute-start(bf16[528,256]{1,0:T(8,128)(2,1)} %get-tuple-element.96.refs_0_.refs_2_), channel_id=1, source_target_pairs={{0,2},{1,3},{2,0},{3,1},{4,6},{5,7},{6,4},{7,5},{8,10},{9,11},{10,... | collective-permute-start | bytes 811016 | tf_op jit(solution)/shard_map/ppermute | solution.py:457
  34.3 8.6 %collective-permute-start.9 = (bf16[528,256]{1,0:T(8,128)(2,1)}, bf16[528,256]{1,0:T(8,128)(2,1)}, u32[]{:S(2)}, u32[]{:S(2)}) collective-permute-start(bf16[528,256]{1,0:T(8,128)(2,1)} %get-tuple-element.95), channel_id=1, source_target_pairs={{0,4},{1,5},{2,6},{3,7},{4,0},{5,1},{6,2},{7,3},{8,12},{9,13},{10,... | collective-permute-start | bytes 811016 | tf_op jit(solution)/shard_map/ppermute | solution.py:457
  34.9 13.5 %collective-permute-start.7 = (bf16[528,256]{1,0:T(8,128)(2,1)S(1)}, bf16[528,256]{1,0:T(8,128)(2,1)}, u32[]{:S(2)}, u32[]{:S(2)}) collective-permute-start(bf16[528,256]{1,0:T(8,128)(2,1)S(1)} %get-tuple-element.93.refs_0_), channel_id=1, source_target_pairs={{0,2},{1,3},{2,0},{3,1},{4,6},{5,7},{6,4},{7,5},{8,10},{9,11},{10,... | collective-permute-start | bytes 811016 | tf_op jit(solution)/shard_map/ppermute | solution.py:457
  35.5 16.0 %collective-permute-start.8 = (bf16[528,256]{1,0:T(8,128)(2,1)S(1)}, bf16[528,256]{1,0:T(8,128)(2,1)}, u32[]{:S(2)}, u32[]{:S(2)}) collective-permute-start(bf16[528,256]{1,0:T(8,128)(2,1)S(1)} %collective-permute-done.6.refs_1_), channel_id=1, source_target_pairs={{0,2},{1,3},{2,0},{3,1},{4,6},{5,7},{6,4},{7,5},{8,10},{9,11},{10,... | collective-permute-start | bytes 811016 | tf_op jit(solution)/shard_map/ppermute | solution.py:457
  38.1 48.3 %all-to-all-start = ((bf16[4,2,2,128,512]{4,3,2,1,0:T(8,128)(2,1)}), bf16[4,2,2,128,512]{4,3,2,1,0:T(8,128)(2,1)S(1)}, u32[]{:S(2)}, u32[]{:S(2)}) async-start(bf16[4,2,2,128,512]{4,3,2,1,0:T(8,128)(2,1)} %copy-done.10), calls=%async_computation | async-start | bytes 4194304 | tf_op jit(solution)/shard_map/all_to_all | solution.py:468
  43.0 24.7 %collective-permute-start.14 = (bf16[2112,256]{1,0:T(8,128)(2,1)}, bf16[2112,256]{1,0:T(8,128)(2,1)S(1)}, u32[]{:S(2)}, u32[]{:S(2)}) collective-permute-start(bf16[2112,256]{1,0:T(8,128)(2,1)} %pad_maximum_fusion), channel_id=1, source_target_pairs={{0,1},{1,0},{2,3},{3,2},{4,5},{5,4},{6,7},{7,6},{8,9},{9,8},{10,11... | collective-permute-start | bytes 3244040 | tf_op jit(solution)/shard_map/ppermute | solution.py:457
  52.6 15.1 %collective-permute-start.15 = (bf16[2112,256]{1,0:T(8,128)(2,1)S(1)}, bf16[2112,256]{1,0:T(8,128)(2,1)S(1)}, u32[]{:S(2)}, u32[]{:S(2)}) collective-permute-start(bf16[2112,256]{1,0:T(8,128)(2,1)S(1)} %pad_maximum_fusion.1), channel_id=1, source_target_pairs={{0,1},{1,0},{2,3},{3,2},{4,5},{5,4},{6,7},{7,6},{8,9},{9,8},{10,11... | collective-permute-start | bytes 3244040 | tf_op jit(solution)/shard_map/ppermute | solution.py:457
  52.7 9.5 %collective-permute-start.13 = (bf16[528,256]{1,0:T(8,128)(2,1)}, bf16[528,256]{1,0:T(8,128)(2,1)S(1)}, u32[]{:S(2)}, u32[]{:S(2)}) collective-permute-start(bf16[528,256]{1,0:T(8,128)(2,1)} %collective-permute-done.9.refs_1_.refs_3_), channel_id=1, source_target_pairs={{0,2},{1,3},{2,0},{3,1},{4,6},{5,7},{6,4},{7,5},{8,10},{9,11},{10,... | collective-permute-start | bytes 811016 | tf_op jit(solution)/shard_map/ppermute | solution.py:457
  55.7 25.5 %copy-start.16 = (bf16[528,256]{1,0:T(8,128)(2,1)}, bf16[528,256]{1,0:T(8,128)(2,1)S(1)}, u32[]{:S(2)}) copy-start(bf16[528,256]{1,0:T(8,128)(2,1)S(1)} %get-tuple-element.98.refs_0_.refs_4_) | copy-start | bytes 811012
  55.8 8.6 %collective-permute-start.11 = (bf16[528,256]{1,0:T(8,128)(2,1)S(1)}, bf16[528,256]{1,0:T(8,128)(2,1)S(1)}, u32[]{:S(2)}, u32[]{:S(2)}) collective-permute-start(bf16[528,256]{1,0:T(8,128)(2,1)S(1)} %get-tuple-element.99), channel_id=1, source_target_pairs={{0,4},{1,5},{2,6},{3,7},{4,0},{5,1},{6,2},{7,3},{8,12},{9,13},{10,... | collective-permute-start | bytes 811016 | tf_op jit(solution)/shard_map/ppermute | solution.py:457
  56.0 11.7 %collective-permute-start.12 = (bf16[528,256]{1,0:T(8,128)(2,1)S(1)}, bf16[528,256]{1,0:T(8,128)(2,1)S(1)}, u32[]{:S(2)}, u32[]{:S(2)}) collective-permute-start(bf16[528,256]{1,0:T(8,128)(2,1)S(1)} %get-tuple-element.98.refs_0_.refs_4_), channel_id=1, source_target_pairs={{0,2},{1,3},{2,0},{3,1},{4,6},{5,7},{6,4},{7,5},{8,10},{9,11},{10,... | collective-permute-start | bytes 811016 | tf_op jit(solution)/shard_map/ppermute | solution.py:457
  64.4 16.9 %copy-start.18 = (bf16[528,256]{1,0:T(8,128)(2,1)}, bf16[528,256]{1,0:T(8,128)(2,1)S(1)}, u32[]{:S(2)}) copy-start(bf16[528,256]{1,0:T(8,128)(2,1)S(1)} %collective-permute-done.11.refs_1_.refs_5_) | copy-start | bytes 811012
  68.9 6.0 %copy-start.12 = (bf16[528,256]{1,0:T(8,128)(2,1)S(1)}, bf16[528,256]{1,0:T(8,128)(2,1)}, u32[]{:S(2)}) copy-start(bf16[528,256]{1,0:T(8,128)(2,1)} %copy-done.11) | copy-start | bytes 811012
  68.9 9.1 %collective-permute-start.17 = (bf16[2112,256]{1,0:T(8,128)(2,1)S(1)}, bf16[2112,256]{1,0:T(8,128)(2,1)S(1)}, u32[]{:S(2)}, u32[]{:S(2)}) collective-permute-start(bf16[2112,256]{1,0:T(8,128)(2,1)S(1)} %pad_maximum_fusion.2), channel_id=1, source_target_pairs={{0,1},{1,0},{2,3},{3,2},{4,5},{5,4},{6,7},{7,6},{8,9},{9,8},{10,11... | collective-permute-start | bytes 3244040 | tf_op jit(solution)/shard_map/ppermute | solution.py:457
  69.0 8.5 %collective-permute-start.18 = (bf16[528,256]{1,0:T(8,128)(2,1)S(1)}, bf16[528,256]{1,0:T(8,128)(2,1)S(1)}, u32[]{:S(2)}, u32[]{:S(2)}) collective-permute-start(bf16[528,256]{1,0:T(8,128)(2,1)S(1)} %get-tuple-element.98.refs_0_.refs_4_), channel_id=1, source_target_pairs={{0,1},{1,0},{2,3},{3,2},{4,5},{5,4},{6,7},{7,6},{8,9},{9,8},{10,11... | collective-permute-start | bytes 811016 | tf_op jit(solution)/shard_map/ppermute | solution.py:457
  69.5 8.5 %collective-permute-start.16 = (bf16[528,256]{1,0:T(8,128)(2,1)S(1)}, bf16[528,256]{1,0:T(8,128)(2,1)S(1)}, u32[]{:S(2)}, u32[]{:S(2)}) collective-permute-start(bf16[528,256]{1,0:T(8,128)(2,1)S(1)} %collective-permute-done.11.refs_1_.refs_5_), channel_id=1, source_target_pairs={{0,2},{1,3},{2,0},{3,1},{4,6},{5,7},{6,4},{7,5},{8,10},{9,11},{10,... | collective-permute-start | bytes 811016 | tf_op jit(solution)/shard_map/ppermute | solution.py:457
  71.2 6.7 %collective-permute-start.19 = (bf16[528,256]{1,0:T(8,128)(2,1)S(1)}, bf16[528,256]{1,0:T(8,128)(2,1)S(1)}, u32[]{:S(2)}, u32[]{:S(2)}) collective-permute-start(bf16[528,256]{1,0:T(8,128)(2,1)S(1)} %collective-permute-done.12.refs_2_), channel_id=1, source_target_pairs={{0,1},{1,0},{2,3},{3,2},{4,5},{5,4},{6,7},{7,6},{8,9},{9,8},{10,11... | collective-permute-start | bytes 811016 | tf_op jit(solution)/shard_map/ppermute | solution.py:457
  71.2 6.7 %collective-permute-start.20 = (bf16[528,256]{1,0:T(8,128)(2,1)S(1)}, bf16[528,256]{1,0:T(8,128)(2,1)S(1)}, u32[]{:S(2)}, u32[]{:S(2)}) collective-permute-start(bf16[528,256]{1,0:T(8,128)(2,1)S(1)} %collective-permute-done.11.refs_1_.refs_5_), channel_id=1, source_target_pairs={{0,1},{1,0},{2,3},{3,2},{4,5},{5,4},{6,7},{7,6},{8,9},{9,8},{10,11... | collective-permute-start | bytes 811016 | tf_op jit(solution)/shard_map/ppermute | solution.py:457
  73.5 1.4 %copy-start.1 = (bf16[4,512,512]{2,1,0:T(8,128)(2,1)}, bf16[4,512,512]{2,1,0:T(8,128)(2,1)S(1)}, u32[]{:S(2)}) copy-start(bf16[4,512,512]{2,1,0:T(8,128)(2,1)S(1)} %shard_map.88.refs_0_.refs_1_) | copy-start | bytes 6291460
  76.1 1.4 %copy-start.5 = (bf16[4,512,512]{2,1,0:T(8,128)(2,1)}, bf16[4,512,512]{2,1,0:T(8,128)(2,1)S(1)}, u32[]{:S(2)}) copy-start(bf16[4,512,512]{2,1,0:T(8,128)(2,1)S(1)} %shard_map.87.refs_0_) | copy-start | bytes 6291460
  77.9 3.3 %collective-permute-start.21 = (bf16[528,256]{1,0:T(8,128)(2,1)S(1)}, bf16[528,256]{1,0:T(8,128)(2,1)S(1)}, u32[]{:S(2)}, u32[]{:S(2)}) collective-permute-start(bf16[528,256]{1,0:T(8,128)(2,1)S(1)} %collective-permute-done.16.refs_3_), channel_id=1, source_target_pairs={{0,1},{1,0},{2,3},{3,2},{4,5},{5,4},{6,7},{7,6},{8,9},{9,8},{10,11... | collective-permute-start | bytes 811016 | tf_op jit(solution)/shard_map/ppermute | solution.py:457
  79.9 1.4 %copy-start.3 = (bf16[4,512,512]{2,1,0:T(8,128)(2,1)}, bf16[4,512,512]{2,1,0:T(8,128)(2,1)S(1)}, u32[]{:S(2)}) copy-start(bf16[4,512,512]{2,1,0:T(8,128)(2,1)S(1)} %shard_map.89.refs_1_.refs_0_) | copy-start | bytes 6291460
  82.5 1.3 %copy-start.8 = (bf16[4,512,512]{2,1,0:T(8,128)(2,1)}, bf16[4,512,512]{2,1,0:T(8,128)(2,1)S(1)}, u32[]{:S(2)}) copy-start(bf16[4,512,512]{2,1,0:T(8,128)(2,1)S(1)} %shard_map.90.refs_0_.refs_1_) | copy-start | bytes 6291460
  86.4 1.6 %copy-start.6 = (bf16[4,512,512]{2,1,0:T(8,128)(2,1)S(1)}, bf16[4,512,512]{2,1,0:T(8,128)(2,1)}, u32[]{:S(2)}) copy-start(bf16[4,512,512]{2,1,0:T(8,128)(2,1)} %copy-done.5) | copy-start | bytes 6291460
  88.0 2.3 %copy-start.2 = (bf16[4,512,512]{2,1,0:T(8,128)(2,1)S(1)}, bf16[4,512,512]{2,1,0:T(8,128)(2,1)}, u32[]{:S(2)}) copy-start(bf16[4,512,512]{2,1,0:T(8,128)(2,1)} %copy-done.1) | copy-start | bytes 6291460
  88.0 2.3 %copy-start.4 = (bf16[4,512,512]{2,1,0:T(8,128)(2,1)S(1)}, bf16[4,512,512]{2,1,0:T(8,128)(2,1)}, u32[]{:S(2)}) copy-start(bf16[4,512,512]{2,1,0:T(8,128)(2,1)} %copy-done.3) | copy-start | bytes 6291460
  88.7 5.9 %collective-permute-start.23 = (bf16[128,512]{1,0:T(8,128)(2,1)S(1)}, bf16[128,512]{1,0:T(8,128)(2,1)S(1)}, u32[]{:S(2)}, u32[]{:S(2)}) collective-permute-start(bf16[128,512]{1,0:T(8,128)(2,1)S(1)} %get-tuple-element.131), channel_id=1, source_target_pairs={{0,4},{1,5},{2,6},{3,7},{4,0},{5,1},{6,2},{7,3},{8,12},{9,13},{10,... | collective-permute-start | bytes 393224 | tf_op jit(solution)/shard_map/ppermute | solution.py:457
  90.2 4.3 %copy-start.9 = (bf16[4,512,512]{2,1,0:T(8,128)(2,1)S(1)}, bf16[4,512,512]{2,1,0:T(8,128)(2,1)}, u32[]{:S(2)}) copy-start(bf16[4,512,512]{2,1,0:T(8,128)(2,1)} %copy-done.8) | copy-start | bytes 6291460
  91.5 9.3 %collective-permute-start.22 = (bf16[128,1024]{1,0:T(8,128)(2,1)S(1)}, bf16[128,1024]{1,0:T(8,128)(2,1)S(1)}, u32[]{:S(2)}, u32[]{:S(2)}) collective-permute-start(bf16[128,1024]{1,0:T(8,128)(2,1)S(1)} %get-tuple-element.127), channel_id=1, source_target_pairs={{0,4},{1,5},{2,6},{3,7},{4,0},{5,1},{6,2},{7,3},{8,12},{9,13},{10,... | collective-permute-start | bytes 786440 | tf_op jit(solution)/shard_map/ppermute | solution.py:457
  95.2 8.4 %collective-permute-start.24 = (bf16[128,512]{1,0:T(8,128)(2,1)S(1)}, bf16[128,512]{1,0:T(8,128)(2,1)S(1)}, u32[]{:S(2)}, u32[]{:S(2)}) collective-permute-start(bf16[128,512]{1,0:T(8,128)(2,1)S(1)} %get-tuple-element.144), channel_id=1, source_target_pairs={{0,4},{1,5},{2,6},{3,7},{4,0},{5,1},{6,2},{7,3},{8,12},{9,13},{10,... | collective-permute-start | bytes 393224 | tf_op jit(solution)/shard_map/ppermute | solution.py:457
  97.6 1.6 %copy-start.7 = (bf16[4,512,512]{2,1,0:T(8,128)(2,1)S(1)}, bf16[4,512,512]{2,1,0:T(8,128)(2,1)}, u32[]{:S(2)}) copy-start(bf16[4,512,512]{2,1,0:T(8,128)(2,1)} %copy-done.5) | copy-start | bytes 6291460
  99.2 4.4 %copy-start.17 = (bf16[528,256]{1,0:T(8,128)(2,1)S(1)}, bf16[528,256]{1,0:T(8,128)(2,1)}, u32[]{:S(2)}) copy-start(bf16[528,256]{1,0:T(8,128)(2,1)} %copy-done.16) | copy-start | bytes 811012
  99.2 4.4 %copy-start.19 = (bf16[528,256]{1,0:T(8,128)(2,1)S(1)}, bf16[528,256]{1,0:T(8,128)(2,1)}, u32[]{:S(2)}) copy-start(bf16[528,256]{1,0:T(8,128)(2,1)} %copy-done.18) | copy-start | bytes 811012
  99.2 4.4 %copy-start.20 = (f32[128,256]{1,0:T(8,128)S(1)}, f32[128,256]{1,0:T(8,128)}, u32[]{:S(2)}) copy-start(f32[128,256]{1,0:T(8,128)} %dynamic-slice_convert_fusion.taps_ref) | copy-start | bytes 393220
  100.8 10.4 %collective-permute-start.25 = (bf16[128,1024]{1,0:T(8,128)(2,1)S(1)}, bf16[128,1024]{1,0:T(8,128)(2,1)S(1)}, u32[]{:S(2)}, u32[]{:S(2)}) collective-permute-start(bf16[128,1024]{1,0:T(8,128)(2,1)S(1)} %get-tuple-element.148), channel_id=1, source_target_pairs={{0,4},{1,5},{2,6},{3,7},{4,0},{5,1},{6,2},{7,3},{8,12},{9,13},{10,... | collective-permute-start | bytes 786440 | tf_op jit(solution)/shard_map/ppermute | solution.py:457
  102.2 11.1 %collective-permute-start.26 = (bf16[128,1024]{1,0:T(8,128)(2,1)S(1)}, bf16[128,1024]{1,0:T(8,128)(2,1)S(1)}, u32[]{:S(2)}, u32[]{:S(2)}) collective-permute-start(bf16[128,1024]{1,0:T(8,128)(2,1)S(1)} %get-tuple-element.150), channel_id=1, source_target_pairs={{0,4},{1,5},{2,6},{3,7},{4,0},{5,1},{6,2},{7,3},{8,12},{9,13},{10,... | collective-permute-start | bytes 786440 | tf_op jit(solution)/shard_map/ppermute | solution.py:457
  (1 other events, 1.1 us)
